TPU v7x, 256 devices: a whole 4x4x8 slice. The times are simulated.
256 devices in a mesh: section: 4 (over z_hi), dp: 8 (over y, core), tensor: 8 (over x, z_lo).
Axes of the slice: x: 4, y: 4, z: 8 (z_hi: 4, z_lo: 2; z = z_hi * 2 + z_lo), core: 2. Of those that a mesh axis runs over, the one named last changes fastest.
Arguments:
- enc_out: bfloat16 [8, 512, 4096], P('dp', 'section'), may hold values from -6 to 6
- key_weight: bfloat16 [4, 4096, 4096], P('section', None, 'tensor'), may hold values from -0.09375 to 0.09375
- value_weight: bfloat16 [4, 4096, 4096], P('section', None, 'tensor'), may hold values from -0.09375 to 0.09375
- queries: bfloat16 [4, 8, 512, 4096], P('section', 'dp', None, 'tensor'), may hold values from -1024 to 1024
- ctx_grad: bfloat16 [4, 8, 512, 4096], P('section', 'dp', None, 'tensor'), may hold values from -12 to 12
- src_pad: int32 [8], P('dp'), may hold values from 0 to 384, as said below
- tgt_pad: int32 [8], P('dp'), may hold values from 0 to 256, as said below
Outputs:
- context: bfloat16 [4, 8, 512, 4096], P('section', 'dp', None, 'tensor')
- enc_grad: bfloat16 [8, 512, 4096], P('dp', 'section')
- key_weight_grad: bfloat16 [4, 4096, 4096], P('section', 'dp', 'tensor')
- value_weight_grad: bfloat16 [4, 4096, 4096], P('section', 'dp', 'tensor')
Inputs may be any that keep to these rules, and one draw needn't show every extreme that they name: `src_pad`: some sequence has no source padding and some has the most. `tgt_pad`: some sequence has no target padding and some has the most.
All inputs are finite; a program needn't handle non-finite values.
Results may differ from a plain program's by a relative error of at most 0.023.
The roundings to bfloat16 on the way count: a program that leaves them out, or rounds other values in their place, can miss the bound.
Values may be sent and summed in bfloat16 or wider, within the bound.
No kernel may reach another device: no remote copies, remote signals or barrier semaphores. Data moves between devices by JAX's collectives and lax.ppermute only.
A program may use at most 128 MiB of HBM per device.

v0:
```python
import jax
import jax.numpy as jnp
from jax import lax
from jax.sharding import PartitionSpec as P

HEAD = 256


masked_score = -1e30


def softmax_rows(scores):
    highest = jnp.max(scores, axis=-1, keepdims=True)
    shifted = jnp.exp(scores - highest)
    return shifted / jnp.sum(shifted, axis=-1, keepdims=True)


def shards(enc_out, key_weight, value_weight, queries, ctx_grad, src_pad, tgt_pad):
    seq_count = enc_out.shape[0]
    model_width = enc_out.shape[2]
    key_proj = key_weight[0]
    value_proj = value_weight[0]
    local_width = key_proj.shape[1]
    heads_here = local_width // HEAD
    target_count = queries.shape[2]
    score_scale = HEAD ** (-0.5)
    shard_rows = lax.all_gather(enc_out, "section", axis=1, tiled=True)
    key_part = jnp.einsum("bsd,dh->bsh", shard_rows, key_proj, preferred_element_type=jnp.float32)
    value_part = jnp.einsum(
        "bsd,dh->bsh", shard_rows, value_proj, preferred_element_type=jnp.float32
    )
    joined = jnp.concatenate(
        [shard_rows, key_part.astype(jnp.bfloat16), value_part.astype(jnp.bfloat16)], axis=2
    )
    total_src = joined.shape[1]
    enc_full = joined[:, :, :model_width]
    key_heads = joined[:, :, model_width : model_width + local_width].reshape(
        seq_count, total_src, heads_here, HEAD
    )
    value_heads = joined[:, :, model_width + local_width :].reshape(
        seq_count, total_src, heads_here, HEAD
    )
    query_heads = queries[0].reshape(seq_count, target_count, heads_here, HEAD)
    key_valid = jnp.arange(total_src)[None, :] < (total_src - src_pad)[:, None]
    scores = (
        jnp.einsum("bthe,bshe->bhts", query_heads, key_heads, preferred_element_type=jnp.float32)
        * score_scale
    )
    scores = jnp.where(key_valid[:, None, None, :], scores, masked_score)
    soft_weights = softmax_rows(scores)
    weights_low = soft_weights.astype(jnp.bfloat16)
    context = jnp.einsum(
        "bhts,bshe->bthe", weights_low, value_heads, preferred_element_type=jnp.float32
    )
    context = context.astype(jnp.bfloat16).reshape(1, seq_count, target_count, local_width)
    target_live = jnp.arange(target_count)[None, :] < (target_count - tgt_pad)[:, None]
    grad_in = jnp.where(target_live[:, :, None], ctx_grad[0], jnp.zeros((), jnp.bfloat16))
    grad_heads = grad_in.reshape(seq_count, target_count, heads_here, HEAD)
    prob_grad = jnp.einsum(
        "bthe,bshe->bhts", grad_heads, value_heads, preferred_element_type=jnp.float32
    )
    prob_dot = jnp.sum(soft_weights * prob_grad, axis=-1, keepdims=True)
    score_grad = (soft_weights * (prob_grad - prob_dot) * score_scale).astype(jnp.bfloat16)
    value_act = jnp.einsum(
        "bhts,bthe->bshe", weights_low, grad_heads, preferred_element_type=jnp.float32
    )
    key_act = jnp.einsum(
        "bhts,bthe->bshe", score_grad, query_heads, preferred_element_type=jnp.float32
    )
    value_act = value_act.astype(jnp.bfloat16).reshape(seq_count, total_src, local_width)
    key_act = key_act.astype(jnp.bfloat16).reshape(seq_count, total_src, local_width)
    grad_pairs = jnp.concatenate([key_act, value_act], axis=2)
    partial_value = jnp.einsum("bsh,dh->sbd", key_act, key_proj, preferred_element_type=jnp.float32)
    section_part = lax.psum_scatter(
        (
            partial_value
            + jnp.einsum("bsh,dh->sbd", value_act, value_proj, preferred_element_type=jnp.float32)
        ).astype(jnp.bfloat16),
        "section",
        scatter_dimension=0,
        tiled=True,
    )
    grad_rows = lax.psum(section_part, "tensor")
    enc_grad = jnp.transpose(grad_rows, (1, 0, 2))
    summed = lax.psum_scatter(
        jnp.einsum("bsd,bsh->dh", enc_full, grad_pairs, preferred_element_type=jnp.float32).astype(
            jnp.bfloat16
        ),
        "dp",
        scatter_dimension=0,
        tiled=True,
    ).astype(jnp.float32)
    key_weight_grad = summed[:, :local_width].astype(jnp.bfloat16)[None]
    value_weight_grad = summed[:, local_width:].astype(jnp.bfloat16)[None]
    return (context, enc_grad, key_weight_grad, value_weight_grad)


def solution(mesh):
    return jax.shard_map(
        shards,
        mesh=mesh,
        in_specs=(
            P("dp", "section", None),
            P("section", None, "tensor"),
            P("section", None, "tensor"),
            P("section", "dp", None, "tensor"),
            P("section", "dp", None, "tensor"),
            P("dp"),
            P("dp"),
        ),
        out_specs=(
            P("section", "dp", None, "tensor"),
            P("dp", "section", None),
            P("section", "dp", "tensor"),
            P("section", "dp", "tensor"),
        ),
        check_vma=False,
    )
```

profile of v0, /device:TPU:8, one launch (start us, length us, event | category | flops | bytes accessed | tf_op | source)
XLA Modules:
  0.0 364.1 jit_solution(8716023554843363507)
XLA Ops:
  7.2 0.0 copy-start
  7.2 0.0 all-gather.2.cloned.1.call-start
  7.2 0.7 all-gather.2.cloned.1.call-update
  7.9 0.0 reduce-scatter.3.cloned.1.call-start
  9.2 1.3 copy.31
  10.5 0.0 copy-done
  10.5 0.2 copy.30
  10.8 74.3 %all-gather.2.cloned.1.call-done = bf16[1,512,4096]{2,1,0:T(8,128)(2,1)} async-done(((bf16[1,128,4096]{2,1,0:T(8,128)(2,1)}), bf16[1,512,4096]{2,1,0:T(8,128)(2,1)}) %all-gather.2.cloned.1.call-update) | async-done | bytes 4194320 | tf_op jit(solution)/shard_map/all_gather | solution.py:27
  85.0 5.8 %fusion.31 = bf16[512,512]{0,1:T(8,128)(2,1)S(1)} fusion(bf16[1,4096,512]{2,1,0:T(8,128)(2,1)} %param.8, bf16[1,512,4096]{2,1,0:T(8,128)(2,1)} %all-gather.2.cloned.1.call-done), kind=kOutput, calls=%fused_computation.26 | convolution fusion | flops 2147745792 | bytes 8912896 | tf_op jit(solution)/shard_map/bsd,dh->bsh/dot_general | solution.py:28
  90.9 2.2 fusion.56
  93.1 5.8 %fusion.26 = bf16[512,512]{0,1:T(8,128)(2,1)S(1)} fusion(bf16[1,4096,512]{2,1,0:T(8,128)(2,1)} %param.9, bf16[1,512,4096]{2,1,0:T(8,128)(2,1)} %all-gather.2.cloned.1.call-done), kind=kOutput, calls=%fused_computation.25 | convolution fusion | flops 2147745792 | bytes 8912896 | tf_op jit(solution)/shard_map/bsd,dh->bsh/dot_general | solution.py:29
  98.9 0.0 copy-start.1
  98.9 0.0 copy-start.5
  99.0 0.5 fusion.44
  99.4 0.3 copy-done.1
  99.7 1.0 copy-done.5
  100.7 1.3 convolution_convert_fusion
  102.0 3.4 fusion.23
  105.4 0.0 copy-start.3
  105.4 0.0 copy-start.4
  105.4 4.7 %fusion.3 = f32[512,4096]{1,0:T(8,128)S(1)} fusion(bf16[512,512]{0,1:T(8,128)(2,1)S(1)} %bitcast.91, bf16[1,4096,512]{2,1,0:T(8,128)(2,1)} %param.8), kind=kOutput, calls=%fused_computation.5 | convolution fusion | flops 2147483648 | bytes 13107200 | tf_op jit(solution)/shard_map/bsh,dh->sbd/dot_general | solution.py:73
  110.1 0.0 copy-done.3
  110.2 0.0 copy-done.4
  110.2 4.7 %fusion.2 = bf16[512,1,4096]{2,0,1:T(8,128)(2,1)} fusion(f32[512,4096]{1,0:T(8,128)S(1)} %fusion.3, bf16[512,512]{0,1:T(8,128)(2,1)S(1)} %bitcast.98, bf16[1,4096,512]{2,1,0:T(8,128)(2,1)S(1)} %copy-done.3), kind=kOutput, calls=%fused_computation.4 | convolution fusion | flops 2151677952 | bytes 17301504 | tf_op jit(solution)/shard_map/bsh,dh->sbd/dot_general | solution.py:77
  114.8 0.0 reduce-scatter.3.cloned.1.call-update
  114.8 0.0 reduce-scatter.5.cloned.1.call-start
  114.9 9.6 %convert_bitcast_fusion = bf16[4096,1024]{0,1:T(8,128)(2,1)} fusion(bf16[1,512,4096]{2,1,0:T(8,128)(2,1)} %all-gather.2.cloned.1.call-done, bf16[1,512,512]{1,2,0:T(8,128)(2,1)S(1)} %bitcast.99, bf16[1,512,512]{1,2,0:T(8,128)(2,1)S(1)} %bitcast.92), kind=kOutput, calls=%fused_computation.2 | convolution fusion | flops 4301258752 | bytes 13631488 | tf_op jit(solution)/shard_map/bsd,bsh->dh/dot_general | solution.py:86
  124.5 0.0 copy-start.2
  124.5 0.0 copy-start.6
  124.5 0.0 reduce-scatter.5.cloned.1.call-update
  124.6 0.0 all-reduce.2.cloned.1.call-start
  124.6 87.2 %reduce-scatter.3.cloned.1.call-done = bf16[128,1,4096]{2,0,1:T(8,128)(2,1)} async-done(((bf16[512,1,4096]{2,0,1:T(8,128)(2,1)}), bf16[128,1,4096]{2,0,1:T(8,128)(2,1)}) %reduce-scatter.3.cloned.1.call-update) | async-done | bytes 1048592 | tf_op jit(solution)/shard_map/reduce_scatter | solution.py:74
  211.8 0.0 all-reduce.2.cloned.1.call-update
  211.8 0.0 copy-done.2
  211.8 0.0 copy-done.6
  211.8 0.4 convolution_convert_fusion.1
  212.3 1.0 copy.21
  213.3 52.0 %reduce-scatter.5.cloned.1.call-done = bf16[512,1024]{0,1:T(8,128)(2,1)} async-done(((bf16[4096,1024]{0,1:T(8,128)(2,1)}), bf16[512,1024]{0,1:T(8,128)(2,1)}) %reduce-scatter.5.cloned.1.call-update) | async-done | bytes 1048592 | tf_op jit(solution)/shard_map/reduce_scatter | solution.py:85
  265.3 1.3 slice_bitcast_fusion
  266.5 1.0 copy.23
  267.6 1.0 copy.22
  268.6 86.8 %all-reduce.2.cloned.1.call-done = bf16[1,128,4096]{2,1,0:T(8,128)(2,1)} async-done(((bf16[1,128,4096]{2,1,0:T(8,128)(2,1)}), bf16[1,128,4096]{2,1,0:T(8,128)(2,1)}) %all-reduce.2.cloned.1.call-update) | async-done | bytes 1048592 | tf_op jit(solution)/shard_map/psum | solution.py:83
  355.3 2.3 copy.35
  (2 shorter events, 0.0 us)
Async XLA Ops:
  7.2 3.3 copy-start
  7.2 77.9 %all-gather.2.cloned.1.call-start = ((), (), s32[]{:S(2)}) async-start(), calls=%async_computation.2 | async-start | bytes 5242880 | tf_op jit(solution)/shard_map/all_gather | solution.py:27
  7.9 203.8 %reduce-scatter.3.cloned.1.call-start = ((), (), s32[]{:S(2)}) async-start(), calls=%async_computation.3 | async-start | bytes 5242880 | tf_op jit(solution)/shard_map/reduce_scatter | solution.py:74
  98.9 0.8 copy-start.1
  98.9 1.8 copy-start.5
  105.4 4.8 %copy-start.3 = (bf16[1,4096,512]{2,1,0:T(8,128)(2,1)S(1)}, bf16[1,4096,512]{2,1,0:T(8,128)(2,1)}, u32[]{:S(2)}) copy-start(bf16[1,4096,512]{2,1,0:T(8,128)(2,1)} %param.9) | copy-start | bytes 12582916
  105.4 4.8 %copy-start.4 = (bf16[2,256,512]{2,1,0:T(8,128)(2,1)S(1)}, bf16[2,256,512]{2,1,0:T(8,128)(2,1)}, u32[]{:S(2)}) copy-start(bf16[2,256,512]{2,1,0:T(8,128)(2,1)} %convolution_convert_fusion) | copy-start | bytes 1572868
  114.8 150.4 %reduce-scatter.5.cloned.1.call-start = ((), (), s32[]{:S(2)}) async-start(), calls=%async_computation.5 | async-start | bytes 9437184 | tf_op jit(solution)/shard_map/reduce_scatter | solution.py:85
  124.5 87.3 %copy-start.2 = (bf16[512,512]{0,1:T(8,128)(2,1)S(1)}, bf16[512,512]{0,1:T(8,128)(2,1)}, u32[]{:S(2)}) copy-start(bf16[512,512]{0,1:T(8,128)(2,1)} %copy-done.1) | copy-start | bytes 1572868
  124.5 87.3 %copy-start.6 = (f32[2,512,512]{1,2,0:T(8,128)S(1)}, f32[2,512,512]{1,2,0:T(8,128)}, u32[]{:S(2)}) copy-start(f32[2,512,512]{1,2,0:T(8,128)} %get-tuple-element.11) | copy-start | bytes 6291460
  124.6 230.8 %all-reduce.2.cloned.1.call-start = ((), (), s32[]{:S(2)}) async-start(), calls=%async_computation.4 | async-start | bytes 2097152 | tf_op jit(solution)/shard_map/psum | solution.py:83
Sparse Core Ops, SparseCore 0:
  9.8 75.1 all-gather.1
  115.0 96.7 reduce-scatter.2
  214.5 50.7 reduce-scatter.4
  268.0 87.3 all-reduce.1
where the time goes:
time: 364 us
  waiting for transfers between devices  301 us (83%)
  matrix products  38.5 us (11%)
  between operations  15.2 us (4%)
  local copies, waits for them, and re-layouts  9.34 us (3%)
    reduce_scatter x1, waiting for transfers between devices, shards(): lax.psum_scatter((partial_value + jnp.einsum('bsh,dh->sbd', value_act, va...  87.2 us
    psum x1, waiting for transfers between devices, shards(): grad_rows = lax.psum(section_part, 'tensor')  86.8 us
    all_gather x1, waiting for transfers between devices, shards(): shard_rows = lax.all_gather(enc_out, 'section', axis=1, tiled=True)  74.3 us
    reduce_scatter x1, waiting for transfers between devices, shards(): lax.psum_scatter(jnp.einsum('bsd,bsh->dh', enc_full, grad_pairs, preferre...  52 us
    dot_general x1, matrix products, shards(): jnp.einsum('bsd,bsh->dh', enc_full, grad_pairs, preferred_element_type=jn...  9.63 us
  transfers between devices with their start and end apart: 4, of which 4 were waited for; matrix products, arithmetic and copies ran while one was open for 4% of the time, Pallas kernels for 0%

commit v1 on v0

v1 whole, which is shorter than its diff:
```python
import jax
import jax.numpy as jnp
from jax import lax
from jax.experimental import pallas as pl
from jax.experimental.pallas import tpu as pltpu
from jax.sharding import PartitionSpec as P

HEAD = 256
XS = 4
UNIT = 256
masked_score = -1e30
f32 = jnp.float32
bf16 = jnp.bfloat16
X, SEC, LO, Y, CORE, SRC_LIVE, TGT_LIVE = range(7)


def dot(a, b):
    return jnp.dot(a, b, preferred_element_type=f32)


def dot_t(a, b):
    return lax.dot_general(a, b, (((1,), (1,)), ((), ())), preferred_element_type=f32)


def t_dot(a, b):
    return lax.dot_general(a, b, (((0,), (0,)), ((), ())), preferred_element_type=f32)


def mod4(v):
    return lax.rem(v + 8, 4)


def params(mib):
    return pltpu.CompilerParams(vmem_limit_bytes=mib * 1024 * 1024)


def whole(a):
    return pl.BlockSpec(a.shape, lambda i, info: (0,) * a.ndim)


ANYWHERE = pl.BlockSpec(memory_space=pl.ANY)


def join_rows(parts, info):
    rows = sum(p.shape[0] for p in parts)
    out = jax.ShapeDtypeStruct((rows, parts[0].shape[1]), bf16)

    def body(info, *refs):
        at = 0
        for ref in refs[:-1]:
            refs[-1][at : at + ref.shape[0], :] = ref[...]
            at += ref.shape[0]

    return pl.pallas_call(
        body,
        grid_spec=pltpu.PrefetchScalarGridSpec(
            num_scalar_prefetch=1, grid=(1,), in_specs=[whole(p) for p in parts], out_specs=whole(out)
        ),
        out_shape=out,
        compiler_params=params(8),
    )(info, *parts)


def project(m, enc, parts, wk, wv, acc, info, last, n_sec):
    blk, width = enc.shape
    quarter = width // XS
    total = n_sec * blk
    cols = wk.shape[1]
    heads = cols // HEAD
    half = quarter // 2
    step = 64

    def body(info, enc_ref, *refs):
        n = len(parts)
        part_refs, wk_ref, wv_ref = refs[:n], refs[n], refs[n + 1]
        acc_ref = refs[n + 2] if acc is not None else None
        out_ref, rows_ref, half_ref = refs[-3:]

        @pl.when(pl.program_id(0) == 0)
        def _():
            sec = info[SEC]
            rows_ref[pl.ds(pl.multiple_of(sec * blk, blk), blk), :] = enc_ref[...]
            at = 0
            for ref in part_refs:
                for u in range(ref.shape[0] // step):
                    k, off = 1 + at // blk, at % blk
                    to = lax.rem(sec - k + n_sec, n_sec) * blk + off
                    rows_ref[pl.ds(pl.multiple_of(to, step), step), :] = ref[u * step : (u + 1) * step, :]
                    at += step
            other = pl.multiple_of((1 - info[CORE]) * half, half)
            half_ref[...] = rows_ref[:, pl.ds(other, half)]

        rows = rows_ref[...]
        k_part = dot(rows, wk_ref[...])
        v_part = dot(rows, wv_ref[...])
        if acc_ref is not None:
            k_part = k_part + acc_ref[:, :HEAD]
            v_part = v_part + acc_ref[:, HEAD:]
        out_ref[:, :HEAD] = k_part.astype(out_ref.dtype)
        out_ref[:, HEAD:] = v_part.astype(out_ref.dtype)

    def at_quarter(info):
        return mod4(info[X] - m)

    weight = pl.BlockSpec((quarter, HEAD), lambda h, info: (at_quarter(info), h))
    pair = pl.BlockSpec((total, 2 * HEAD), lambda h, info: (0, h))
    out_shape = [
        jax.ShapeDtypeStruct((total, 2 * cols), bf16 if last else f32),
        jax.ShapeDtypeStruct((total, quarter), bf16),
        jax.ShapeDtypeStruct((total, half), bf16),
    ]
    return pl.pallas_call(
        body,
        grid_spec=pltpu.PrefetchScalarGridSpec(
            num_scalar_prefetch=1,
            grid=(heads,),
            in_specs=[pl.BlockSpec((blk, quarter), lambda h, info: (0, at_quarter(info)))]
            + [whole(p) for p in parts]
            + [weight, weight]
            + ([pair] if acc is not None else []),
            out_specs=[pair, whole(out_shape[1]), whole(out_shape[2])],
        ),
        out_shape=out_shape,
        compiler_params=params(24),
        cost_estimate=pl.CostEstimate(
            flops=4 * total * quarter * cols, bytes_accessed=6 * 1024 * 1024, transcendentals=0
        ),
    )(info, enc, *parts, wk, wv, *([acc] if acc is not None else []))


def attention(kv, q, g, info):
    total, targets, width = kv.shape[0], q.shape[0], q.shape[1]
    heads = width // HEAD
    scale = HEAD ** (-0.5)

    def body(info, kv_ref, q_ref, g_ref, ctx_ref, act_ref):
        k, v, q = kv_ref[:, :HEAD], kv_ref[:, HEAD:], q_ref[...]
        place = lax.broadcasted_iota(jnp.int32, (total, 1), 0)
        scores = dot_t(k, q) * scale
        scores = jnp.where(place < info[SRC_LIVE], scores, masked_score)
        highest = jnp.max(scores, axis=0, keepdims=True)
        shifted = jnp.exp(scores - highest)
        weights = shifted * (1.0 / jnp.sum(shifted, axis=0, keepdims=True))
        low = weights.astype(bf16)
        target = lax.broadcasted_iota(jnp.int32, (targets, 1), 0)
        g = jnp.where(target < info[TGT_LIVE], g_ref[...].astype(f32), 0.0).astype(bf16)
        prob = dot_t(v, g)
        prob_dot = jnp.sum(weights * prob, axis=0, keepdims=True)
        grad = (weights * (prob - prob_dot) * scale).astype(bf16)
        act_ref[:, :HEAD] = dot(grad, q).astype(bf16)
        act_ref[:, HEAD:] = dot(low, g).astype(bf16)
        ctx_ref[...] = t_dot(low, v).astype(bf16)

    def cols(n, w):
        return pl.BlockSpec((n, w), lambda h, info: (0, h))

    return pl.pallas_call(
        body,
        grid_spec=pltpu.PrefetchScalarGridSpec(
            num_scalar_prefetch=1,
            grid=(heads,),
            in_specs=[cols(total, 2 * HEAD), cols(targets, HEAD), cols(targets, HEAD)],
            out_specs=[cols(targets, HEAD), cols(total, 2 * HEAD)],
        ),
        out_shape=[
            jax.ShapeDtypeStruct((targets, width), bf16),
            jax.ShapeDtypeStruct((total, 2 * width), bf16),
        ],
        compiler_params=params(20),
        cost_estimate=pl.CostEstimate(
            flops=12 * total * targets * width, bytes_accessed=4 * 1024 * 1024, transcendentals=total * targets * heads
        ),
    )(info, kv, q, g)


def partial_grad(act, wk, wv, info, units, dtype, after=(), add=None):
    total, cols = act.shape[0], wk.shape[1]
    heads = cols // HEAD
    n = len(units)

    def unit(i, info):
        at = units[0](info)
        for j in range(1, n):
            at = jnp.where(i == j, units[j](info), at)
        return at

    def body(info, act_ref, wk_ref, wv_ref, *refs):
        out_ref = refs[-1]
        sums = None
        for h in range(heads):
            for j, w_ref in enumerate((wk_ref, wv_ref)):
                at = (2 * h + j) * HEAD
                term = dot_t(act_ref[:, at : at + HEAD], w_ref[:, h * HEAD : (h + 1) * HEAD])
                sums = term if sums is None else sums + term
        if add is not None:
            sums = sums + refs[0][...].astype(f32)
        out_ref[...] = sums.astype(dtype)

    weight = pl.BlockSpec((UNIT, cols), lambda i, info: (unit(i, info), 0))
    block = pl.BlockSpec((total, UNIT), lambda i, info: (0, i))
    return pl.pallas_call(
        body,
        grid_spec=pltpu.PrefetchScalarGridSpec(
            num_scalar_prefetch=1,
            grid=(n,),
            in_specs=[whole(act), weight, weight]
            + ([block] if add is not None else [])
            + [ANYWHERE] * len(after),
            out_specs=block,
        ),
        out_shape=jax.ShapeDtypeStruct((total, n * UNIT), dtype),
        compiler_params=params(12),
        cost_estimate=pl.CostEstimate(
            flops=4 * total * n * UNIT * cols, bytes_accessed=2 * 1024 * 1024, transcendentals=0
        ),
    )(info, act, wk, wv, *([add] if add is not None else []), *after)


def pair_grads(rows, halves, act, act_other, info, after):
    total, quarter = rows[0].shape
    half = quarter // 2
    n = len(rows)

    def body(info, *refs):
        row_refs, half_refs, act_ref, other_ref, out_ref = refs[:n], refs[n : 2 * n], refs[2 * n], refs[2 * n + 1], refs[-1]
        for m in range(n):
            piece = t_dot(row_refs[m][...], act_ref[...]) + t_dot(half_refs[m][...], other_ref[...])
            out_ref[mod4(info[X] - info[Y] - m)] = piece.astype(bf16)

    out = jax.ShapeDtypeStruct((n, half, act.shape[1]), bf16)
    return pl.pallas_call(
        body,
        grid_spec=pltpu.PrefetchScalarGridSpec(
            num_scalar_prefetch=1,
            grid=(1,),
            in_specs=[pl.BlockSpec((total, half), lambda i, info: (0, info[CORE]))] * n
            + [whole(h) for h in halves]
            + [whole(act), whole(act_other)]
            + [ANYWHERE] * len(after),
            out_specs=whole(out),
        ),
        out_shape=out,
        compiler_params=params(28),
        cost_estimate=pl.CostEstimate(
            flops=4 * n * total * half * act.shape[1], bytes_accessed=8 * 1024 * 1024, transcendentals=0
        ),
    )(info, *rows, *halves, act, act_other, *after)


def spread(far, near_up, near_down, keep, shift):
    half = far.shape[0] // 2
    got_up = shift(far[:half], 1).astype(f32)
    got_down = shift(far[half:], -1).astype(f32)
    up = jnp.concatenate([near_up[:half].astype(f32) + got_up, near_up[half:].astype(f32)], axis=0)
    down = jnp.concatenate([near_down[:half].astype(f32), near_down[half:].astype(f32) + got_down], axis=0)
    from_below = shift(up.astype(bf16), 1).astype(f32)
    from_above = shift(down.astype(bf16), -1).astype(f32)
    return keep.astype(f32) + from_below + from_above


def make_shards(mesh):
    n_sec, n_dp, n_ten = mesh.shape["section"], mesh.shape["dp"], mesh.shape["tensor"]
    lows, cores = n_ten // XS, 2

    def shift_section(v, k):
        return lax.ppermute(v, "section", [(i, (i + k) % n_sec) for i in range(n_sec)])

    def shift_x(v, k):
        pairs = [(x * lows + l, ((x + k) % XS) * lows + l) for x in range(XS) for l in range(lows)]
        return lax.ppermute(v, "tensor", pairs)

    def swap_lo(v):
        return lax.ppermute(v, "tensor", [(i, i ^ 1) for i in range(n_ten)])

    def shift_y(v, k):
        ys = n_dp // cores
        pairs = [(y * cores + c, ((y + k) % ys) * cores + c) for y in range(ys) for c in range(cores)]
        return lax.ppermute(v, "dp", pairs)

    def swap_core(v):
        return lax.ppermute(v, "dp", [(i, i ^ 1) for i in range(n_dp)])

    def shards(enc_out, key_weight, value_weight, queries, ctx_grad, src_pad, tgt_pad):
        enc, wk, wv = enc_out[0], key_weight[0], value_weight[0]
        blk, width = enc.shape
        quarter = width // XS
        local_width = wk.shape[1]
        total_src = n_sec * blk
        ten, dp = lax.axis_index("tensor"), lax.axis_index("dp")
        x, lo = ten // lows, ten % lows
        sec = lax.axis_index("section")
        info = jnp.stack(
            [
                x,
                sec,
                lo,
                dp // cores,
                dp % cores,
                total_src - src_pad[0],
                queries.shape[2] - tgt_pad[0],
            ]
        ).astype(jnp.int32)

        mine = lax.dynamic_slice(enc, (0, x * quarter), (blk, quarter))
        g0 = join_rows([shift_section(mine, k) for k in range(1, n_sec)], info)
        mid = g0.shape[0] // 2
        g1 = shift_x(g0, 1)
        g3 = shift_x(g0, -1)
        g2a = shift_x(g1[:mid], 1)
        g2b = shift_x(g3[mid:], -1)
        parts = ([g0], [g1], [g2a, g2b], [g3])
        rows, halves = [None] * XS, [None] * XS
        acc = None
        for m in (0, 1, 3, 2):
            acc, rows[m], halves[m] = project(m, enc, parts[m], wk, wv, acc, info, m == 2, n_sec)
        halves = [swap_core(h) for h in halves]

        context, act = attention(acc, queries[0, 0], ctx_grad[0, 0], info)
        context = context[None, None]
        act_other = swap_core(act)

        per = quarter // UNIT
        a_units = per // 2

        def unit(m, j, side=None):
            def at(info):
                u = mod4(info[X] - m) * per + j
                if side is None:
                    return u
                return u + (info[LO] if side else 1 - info[LO])

            return at

        far_a = partial_grad(act, wk, wv, info, [unit(2, j) for j in range(a_units)], bf16)
        sent_b = partial_grad(
            act, wk, wv, info, [unit(m, a_units, False) for m in (2, 3, 1, 0)], bf16, (far_a,)
        )
        got_b = swap_lo(sent_b)
        near_a = partial_grad(
            act, wk, wv, info, [unit(m, j) for m in (3, 1, 0) for j in range(a_units)], f32, (sent_b,)
        )
        pieces = pair_grads(rows, halves, act, act_other, info, (near_a,))
        sum_b = partial_grad(
            act, wk, wv, info, [unit(m, a_units, True) for m in (2, 3, 1, 0)], f32, (pieces,), got_b
        )
        cols = a_units * UNIT
        total_a = spread(far_a, near_a[:, :cols], near_a[:, cols : 2 * cols], near_a[:, 2 * cols :], shift_x)
        part_b = [sum_b[:, j * UNIT : (j + 1) * UNIT] for j in range(XS)]
        total_b = spread(part_b[0].astype(bf16), part_b[1], part_b[2], part_b[3], shift_x)

        def over_sections(total):
            low = total.astype(bf16).reshape(n_sec, blk, total.shape[1])
            terms = lax.all_to_all(low, "section", 0, 0, tiled=True)
            return jnp.sum(terms.astype(f32), axis=0).astype(bf16)

        mine_a = over_sections(total_a)
        mine_b = over_sections(total_b)
        other = swap_lo(jnp.concatenate([mine_a, mine_b], axis=1))
        final_a = (mine_a.astype(f32) + other[:, :cols].astype(f32)).astype(bf16)
        low_b = jnp.where(lo == 0, mine_b, other[:, cols:])
        high_b = jnp.where(lo == 0, other[:, cols:], mine_b)
        final = jnp.concatenate([final_a, low_b, high_b], axis=1)
        gathered = jnp.stack([final] + [shift_x(final, k) for k in range(1, XS)])
        enc_grad = jnp.concatenate(
            [lax.dynamic_index_in_dim(gathered, (x - q) % XS, 0, False) for q in range(XS)], axis=1
        )[None]

        weight_grads = spread(pieces[2], pieces[1], pieces[3], pieces[0], shift_y)
        weight_grads = weight_grads.astype(bf16).reshape(quarter // cores, local_width // HEAD, 2, HEAD)
        key_weight_grad = weight_grads[:, :, 0].reshape(1, quarter // cores, local_width)
        value_weight_grad = weight_grads[:, :, 1].reshape(1, quarter // cores, local_width)
        return (context, enc_grad, key_weight_grad, value_weight_grad)

    return shards


def solution(mesh):
    return jax.shard_map(
        make_shards(mesh),
        mesh=mesh,
        in_specs=(
            P("dp", "section", None),
            P("section", None, "tensor"),
            P("section", None, "tensor"),
            P("section", "dp", None, "tensor"),
            P("section", "dp", None, "tensor"),
            P("dp"),
            P("dp"),
        ),
        out_specs=(
            P("section", "dp", None, "tensor"),
            P("dp", "section", None),
            P("section", "dp", "tensor"),
            P("section", "dp", "tensor"),
        ),
        check_vma=False,
    )
```

time: 364 us -> 194 us (0.53)
  waiting for transfers between devices: 301 us -> 86.8 us
  starting transfers between devices: 0.16 us -> 46 us
  matrix products: 38.5 us -> 0 us
  Pallas kernels: 0 us -> 31.1 us
  between operations: 15.2 us -> 2.43 us
  other arithmetic: 0.02 us -> 9.13 us
  local copies, waits for them, and re-layouts: 9.34 us -> 16.3 us
    reduce_scatter x2 -> x0, waiting for transfers between devices: 139 us -> none  [the longest x1 87.2 us: shards(): lax.psum_scatter((partial_value + jnp.einsum('bsh,dh->sbd', value_act, va...]
    psum x1 -> x0, waiting for transfers between devices: 86.8 us -> none  [shards(): grad_rows = lax.psum(section_part, 'tensor')]
    all_gather x1 -> x0, waiting for transfers between devices: 74.3 us -> none  [shards(): shard_rows = lax.all_gather(enc_out, 'section', axis=1, tiled=True)]
    ppermute x0 -> x29, waiting for transfers between devices: none -> 72.6 us  [the longest x15 27.5 us: shift_x(): return lax.ppermute(v, 'tensor', pairs)]
    ppermute x0 -> x29, starting transfers between devices: none -> 37 us  [the longest x15 20.4 us: shift_x(): return lax.ppermute(v, 'tensor', pairs)]
    dot_general x9 -> x0, matrix products: 36.3 us -> none  [the longest x1 9.63 us: shards(): jnp.einsum('bsd,bsh->dh', enc_full, grad_pairs, preferred_element_type=jn...]
    pallas_call x0 -> x11, Pallas kernels: none -> 31.1 us  [the longest x4 10.7 us: partial_grad(): pl.pallas_call(body, grid_spec=pltpu.PrefetchScalarGridSpec(num_scalar_pr...]
    all_to_all x0 -> x2, waiting for transfers between devices: none -> 14.2 us  [over_sections(): terms = lax.all_to_all(low, 'section', 0, 0, tiled=True)]
  transfers between devices with their start and end apart: 4 -> 31, of which waited for: 4 -> 15; matrix products, arithmetic and copies ran while one was open for 4% -> 5% of each run, Pallas kernels for 0% -> 16%
where the time goes in v1:
time: 194 us; the launch traced here: 192 us
  waiting for transfers between devices  86.8 us (45%)
  starting transfers between devices  46 us (24%)
  Pallas kernels  31.1 us (16%)
  local copies, waits for them, and re-layouts  16.3 us (8%)
  other arithmetic  9.13 us (5%)
  between operations  2.43 us (1%)
    ppermute x15, waiting for transfers between devices, shift_x(): return lax.ppermute(v, 'tensor', pairs)  27.5 us
    ppermute x15, starting transfers between devices, shift_x(): return lax.ppermute(v, 'tensor', pairs)  20.4 us
    ppermute x2, waiting for transfers between devices, swap_lo(): return lax.ppermute(v, 'tensor', [(i, i ^ 1) for i in range(n_ten)])  19.5 us
    ppermute x3, waiting for transfers between devices, shift_section(): lax.ppermute(v, 'section', [(i, (i + k) % n_sec) for i in range(n_sec)])  19.5 us
    all_to_all x2, waiting for transfers between devices, over_sections(): terms = lax.all_to_all(low, 'section', 0, 0, tiled=True)  14.2 us
    ppermute x3, starting transfers between devices, shift_section(): lax.ppermute(v, 'section', [(i, (i + k) % n_sec) for i in range(n_sec)])  11.4 us
    pallas_call x4, Pallas kernels, partial_grad(): pl.pallas_call(body, grid_spec=pltpu.PrefetchScalarGridSpec(num_scalar_pr...  10.7 us
    pallas_call x4, Pallas kernels, project(): pl.pallas_call(body, grid_spec=pltpu.PrefetchScalarGridSpec(num_scalar_pr...  10.3 us
  transfers between devices with their start and end apart: 31, of which 15 were waited for; matrix products, arithmetic and copies ran while one was open for 5% of the time, Pallas kernels for 16%

profile of v1, /device:TPU:8, one launch (start us, length us, event | category | flops | bytes accessed | tf_op | source)
XLA Modules:
  0.0 191.7 jit_solution(17121066721734309238)
XLA Ops:
  0.7 1.1 dynamic-slice_bitcast_fusion.4
  1.7 3.3 %collective-permute-start = (bf16[128,1024]{1,0:T(8,128)(2,1)S(1)}, bf16[128,1024]{1,0:T(8,128)(2,1)S(1)}, u32[]{:S(2)}, u32[]{:S(2)}) collective-permute-start(bf16[128,1024]{1,0:T(8,128)(2,1)S(1)} %dynamic-slice_bitcast_fusion.4), channel_id=1, source_target_pairs={{0,64},{64,128},{128,192},{192,0},{1,65},{65,129},{129,193},{193,1... | collective-permute-start | bytes 786440 | tf_op jit(solution)/shard_map/ppermute | solution.py:266
  5.1 5.4 %collective-permute-start.1 = (bf16[128,1024]{1,0:T(8,128)(2,1)S(1)}, bf16[128,1024]{1,0:T(8,128)(2,1)S(1)}, u32[]{:S(2)}, u32[]{:S(2)}) collective-permute-start(bf16[128,1024]{1,0:T(8,128)(2,1)S(1)} %dynamic-slice_bitcast_fusion.4), channel_id=1, source_target_pairs={{0,128},{64,192},{128,0},{192,64},{1,129},{65,193},{129,1},{193,65... | collective-permute-start | bytes 786440 | tf_op jit(solution)/shard_map/ppermute | solution.py:266
  10.5 2.7 %collective-permute-start.2 = (bf16[128,1024]{1,0:T(8,128)(2,1)S(1)}, bf16[128,1024]{1,0:T(8,128)(2,1)S(1)}, u32[]{:S(2)}, u32[]{:S(2)}) collective-permute-start(bf16[128,1024]{1,0:T(8,128)(2,1)S(1)} %dynamic-slice_bitcast_fusion.4), channel_id=1, source_target_pairs={{0,192},{64,0},{128,64},{192,128},{1,193},{65,1},{129,65},{193,129... | collective-permute-start | bytes 786440 | tf_op jit(solution)/shard_map/ppermute | solution.py:266
  14.5 3.0 %collective-permute-done.refs_0_ = bf16[128,1024]{1,0:T(8,128)(2,1)S(1)} collective-permute-done((bf16[128,1024]{1,0:T(8,128)(2,1)S(1)}, bf16[128,1024]{1,0:T(8,128)(2,1)S(1)}, u32[]{:S(2)}, u32[]{:S(2)}) %collective-permute-start) | collective-permute-done | bytes 262176 | tf_op jit(solution)/shard_map/ppermute | solution.py:266
  17.5 9.0 %collective-permute-done.1.refs_1_ = bf16[128,1024]{1,0:T(8,128)(2,1)S(1)} collective-permute-done((bf16[128,1024]{1,0:T(8,128)(2,1)S(1)}, bf16[128,1024]{1,0:T(8,128)(2,1)S(1)}, u32[]{:S(2)}, u32[]{:S(2)}) %collective-permute-start.1) | collective-permute-done | bytes 262176 | tf_op jit(solution)/shard_map/ppermute | solution.py:266
  26.5 7.5 %collective-permute-done.2.refs_2_ = bf16[128,1024]{1,0:T(8,128)(2,1)S(1)} collective-permute-done((bf16[128,1024]{1,0:T(8,128)(2,1)S(1)}, bf16[128,1024]{1,0:T(8,128)(2,1)S(1)}, u32[]{:S(2)}, u32[]{:S(2)}) %collective-permute-start.2) | collective-permute-done | bytes 262176 | tf_op jit(solution)/shard_map/ppermute | solution.py:266
  34.0 0.6 shard_map.102.refs_0_
  34.6 1.6 collective-permute-start.3
  36.1 1.7 collective-permute-start.5
  37.9 17.4 %collective-permute-done.3.refs_0_ = bf16[384,1024]{1,0:T(8,128)(2,1)S(1)} collective-permute-done((bf16[384,1024]{1,0:T(8,128)(2,1)S(1)}, bf16[384,1024]{1,0:T(8,128)(2,1)S(1)}, u32[]{:S(2)}, u32[]{:S(2)}) %collective-permute-start.3) | collective-permute-done | bytes 786464 | tf_op jit(solution)/shard_map/ppermute | solution.py:270
  55.4 0.4 collective-permute-start.4
  55.7 3.0 %collective-permute-start.6 = (bf16[192,1024]{1,0:T(8,128)(2,1)S(1)}, bf16[192,1024]{1,0:T(8,128)(2,1)S(1)}, u32[]{:S(2)}, u32[]{:S(2)}) collective-permute-start(bf16[192,1024]{1,0:T(8,128)(2,1)S(1)} %slice.151), channel_id=1, source_target_pairs={{0,6},{1,7},{2,0},{3,1},{4,2},{5,3},{6,4},{7,5},{8,14},{9,15},{10,... | collective-permute-start | bytes 1179656 | tf_op jit(solution)/shard_map/ppermute | solution.py:270
  58.8 2.2 %copy-done = bf16[1,4096,512]{2,1,0:T(8,128)(2,1)S(1)} copy-done((bf16[1,4096,512]{2,1,0:T(8,128)(2,1)S(1)}, bf16[1,4096,512]{2,1,0:T(8,128)(2,1)}, u32[]{:S(2)}) %copy-start) | copy-done | bytes 4194328
  61.0 2.2 %copy-done.2 = bf16[1,4096,512]{2,1,0:T(8,128)(2,1)S(1)} copy-done((bf16[1,4096,512]{2,1,0:T(8,128)(2,1)S(1)}, bf16[1,4096,512]{2,1,0:T(8,128)(2,1)}, u32[]{:S(2)}) %copy-start.2) | copy-done | bytes 4194328
  63.2 2.5 %shard_map.103 = (f32[512,1024]{1,0:T(8,128)S(1)}, bf16[512,1024]{1,0:T(8,128)(2,1)S(1)}, bf16[512,512]{1,0:T(8,128)(2,1)S(1)}) custom-call(s32[7]{0:T(128)S(1)} %stack.40.info, bf16[128,4096]{1,0:T(8,128)(2,1)S(1)} %bitcast.71, bf16[384,1024]{1,0:T(8,128)(2,1)S(1)} %shard_map.102.refs_0_, bf16[4096,512]{1,0:T(8,128)(2,1)S(1)} %bitcast.55, ...), custom_call_target="tpu_custom_call" | custom-call | flops 1073741824 | bytes 6291456 | tf_op jit(solution)/shard_map/pallas_call | solution.py:112
  65.8 0.9 copy-done.3
  66.6 2.6 %shard_map.104 = (f32[512,1024]{1,0:T(8,128)S(1)}, bf16[512,1024]{1,0:T(8,128)(2,1)S(1)}, bf16[512,512]{1,0:T(8,128)(2,1)S(1)}) custom-call(s32[7]{0:T(128)S(1)} %stack.40.info, bf16[128,4096]{1,0:T(8,128)(2,1)S(1)} %bitcast.72, bf16[384,1024]{1,0:T(8,128)(2,1)S(1)} %collective-permute-done.3.refs_0_, bf16[4096,512]{1,0:T(8,128)(2,1)S(1)} %bitcast.56, ...), custom_call_target="tpu_custom_call" | custom-call | flops 1073741824 | bytes 6291456 | tf_op jit(solution)/shard_map/pallas_call | solution.py:112
  69.3 2.6 %shard_map.105 = (f32[512,1024]{1,0:T(8,128)S(1)}, bf16[512,1024]{1,0:T(8,128)(2,1)S(1)}, bf16[512,512]{1,0:T(8,128)(2,1)S(1)}) custom-call(s32[7]{0:T(128)S(1)} %stack.40.info, bf16[128,4096]{1,0:T(8,128)(2,1)S(1)} %bitcast.73, bf16[384,1024]{1,0:T(8,128)(2,1)S(1)} %collective-permute-done.5.refs_0_, bf16[4096,512]{1,0:T(8,128)(2,1)S(1)} %bitcast.57, ...), custom_call_target="tpu_custom_call" | custom-call | flops 1073741824 | bytes 6291456 | tf_op jit(solution)/shard_map/pallas_call | solution.py:112
  72.0 2.6 %shard_map.106 = (bf16[512,1024]{1,0:T(8,128)(2,1)S(1)}, bf16[512,1024]{1,0:T(8,128)(2,1)S(1)}, bf16[512,512]{1,0:T(8,128)(2,1)S(1)}) custom-call(s32[7]{0:T(128)S(1)} %stack.40.info, bf16[128,4096]{1,0:T(8,128)(2,1)S(1)} %bitcast.74, bf16[192,1024]{1,0:T(8,128)(2,1)S(1)} %collective-permute-done.4.refs_0_, ...), custom_call_target="tpu_custom_call" | custom-call | flops 1073741824 | bytes 6291456 | tf_op jit(solution)/shard_map/pallas_call | solution.py:112
  74.6 4.4 %shard_map.107 = (bf16[512,512]{1,0:T(8,128)(2,1)}, bf16[512,1024]{1,0:T(8,128)(2,1)S(1)}) custom-call(s32[7]{0:T(128)S(1)} %stack.40.info, bf16[512,1024]{1,0:T(8,128)(2,1)S(1)} %get-tuple-element.21.kv_ref, bf16[512,512]{1,0:T(8,128)(2,1)S(1)} %bitcast.75, bf16[512,512]{1,0:T(8,128)(2,1)S(1)} %bitcast.76), custom_call_target="tpu_custom_call" | custom-call | flops 1610612736 | bytes 4194304 | tf_op jit(solution)/shard_map/pallas_call | solution.py:157
  79.0 1.6 shard_map.108.refs_0_
  81.0 3.2 %collective-permute-start.9 = (bf16[256,512]{1,0:T(8,128)(2,1)S(1)}, bf16[256,512]{1,0:T(8,128)(2,1)S(1)}, u32[]{:S(2)}, u32[]{:S(2)}) collective-permute-start(bf16[256,512]{1,0:T(8,128)(2,1)S(1)} %get-tuple-element.59), channel_id=1, source_target_pairs={{0,6},{1,7},{2,0},{3,1},{4,2},{5,3},{6,4},{7,5},{8,14},{9,15},{10,... | collective-permute-start | bytes 786440 | tf_op jit(solution)/shard_map/ppermute | solution.py:270
  84.2 2.6 %shard_map.109.refs_0_ = bf16[512,1024]{1,0:T(8,128)(2,1)S(1)} custom-call(s32[7]{0:T(128)S(1)} %stack.40.info, bf16[512,1024]{1,0:T(8,128)(2,1)S(1)} %get-tuple-element.23.act_ref.refs_8_, bf16[4096,512]{1,0:T(8,128)(2,1)S(1)} %bitcast.60, bf16[4096,512]{1,0:T(8,128)(2,1)S(1)} %bitcast.68, bf16[512,512]{1,0:T(8,128)(2,1)S(1)} %shard_map.108.refs_0_), custom_call_target="tpu_custom_call" | custom-call | flops 1073741824 | bytes 2097152 | tf_op jit(solution)/shard_map/pallas_call | solution.py:201
  86.8 3.7 %shard_map.110.refs_10_ = f32[512,1536]{1,0:T(8,128)S(1)} custom-call(s32[7]{0:T(128)S(1)} %stack.40.info, bf16[512,1024]{1,0:T(8,128)(2,1)S(1)} %get-tuple-element.23.act_ref.refs_8_, bf16[4096,512]{1,0:T(8,128)(2,1)S(1)} %bitcast.61, bf16[4096,512]{1,0:T(8,128)(2,1)S(1)} %bitcast.69, bf16[512,1024]{1,0:T(8,128)(2,1)S(1)} %shard_map.109.refs_0_), custom_call_target="tpu_custom_call" | custom-call | flops 1610612736 | bytes 2097152 | tf_op jit(solution)/shard_map/pallas_call | solution.py:201
  90.7 0.6 collective-permute-start.15
  91.9 2.4 %collective-permute-start.10 = (bf16[512,512]{1,0:T(8,128)(2,1)S(1)}, bf16[512,512]{1,0:T(8,128)(2,1)S(1)}, u32[]{:S(2)}, u32[]{:S(2)}) collective-permute-start(bf16[512,512]{1,0:T(8,128)(2,1)S(1)} %pad_maximum_fusion.4), channel_id=1, source_target_pairs={{0,6},{1,7},{2,0},{3,1},{4,2},{5,3},{6,4},{7,5},{8,14},{9,15},{10,... | collective-permute-start | bytes 1572872 | tf_op jit(solution)/shard_map/ppermute | solution.py:270
  94.3 5.1 %shard_map.111.refs_1_ = bf16[4,512,1024]{2,1,0:T(8,128)(2,1)S(1)} custom-call(s32[7]{0:T(128)S(1)} %stack.40.info, bf16[512,1024]{1,0:T(8,128)(2,1)S(1)} %get-tuple-element.24.refs_0_, bf16[512,1024]{1,0:T(8,128)(2,1)S(1)} %get-tuple-element.25.refs_1_, bf16[512,1024]{1,0:T(8,128)(2,1)S(1)} %get-tuple-element.26.refs_2_, ...), custom_call_target="tpu_custom_call" | custom-call | flops 4294967296 | bytes 8388608 | tf_op jit(solution)/shard_map/pallas_call | solution.py:231
  99.4 17.1 %collective-permute-done.11.refs_0_ = bf16[512,1024]{1,0:T(8,128)(2,1)S(1)} collective-permute-done((bf16[512,1024]{1,0:T(8,128)(2,1)S(1)}, bf16[512,1024]{1,0:T(8,128)(2,1)S(1)}, u32[]{:S(2)}, u32[]{:S(2)}) %collective-permute-start.11) | collective-permute-done | bytes 1048608 | tf_op jit(solution)/shard_map/ppermute | solution.py:273
  116.5 2.8 %shard_map.112 = f32[512,1024]{1,0:T(8,128)S(1)} custom-call(s32[7]{0:T(128)S(1)} %stack.40.info, bf16[512,1024]{1,0:T(8,128)(2,1)S(1)} %get-tuple-element.23.act_ref.refs_8_, bf16[4096,512]{1,0:T(8,128)(2,1)S(1)} %bitcast.62, bf16[4096,512]{1,0:T(8,128)(2,1)S(1)} %bitcast.70, bf16[512,1024]{1,0:T(8,128)(2,1)S(1)} %collective-permute-done.11.refs_0_, ...), custom_call_target="tpu_custom_call" | custom-call | flops 1073741824 | bytes 2097152 | tf_op jit(solution)/shard_map/pallas_call | solution.py:201
  119.7 3.2 %collective-permute-start.19 = (bf16[256,256]{1,0:T(8,128)(2,1)S(1)}, bf16[256,256]{1,0:T(8,128)(2,1)S(1)}, u32[]{:S(2)}, u32[]{:S(2)}) collective-permute-start(bf16[256,256]{1,0:T(8,128)(2,1)S(1)} %get-tuple-element.55), channel_id=1, source_target_pairs={{0,6},{1,7},{2,0},{3,1},{4,2},{5,3},{6,4},{7,5},{8,14},{9,15},{10,... | collective-permute-start | bytes 393224 | tf_op jit(solution)/shard_map/ppermute | solution.py:270
  122.9 1.0 fusion.3
  123.9 4.9 %all-to-all-start = ((bf16[4,128,512]{2,1,0:T(8,128)(2,1)}), bf16[4,128,512]{2,1,0:T(8,128)(2,1)S(1)}, u32[]{:S(2)}, u32[]{:S(2)}) async-start(bf16[4,128,512]{2,1,0:T(8,128)(2,1)} %bitcast.12), calls=%async_computation | async-start | bytes 1048576 | tf_op jit(solution)/shard_map/all_to_all | solution.py:353
  128.9 0.3 collective-permute-start.20
  129.2 2.1 %collective-permute-start.18 = (bf16[512,256]{1,0:T(8,128)(2,1)S(1)}, bf16[512,256]{1,0:T(8,128)(2,1)S(1)}, u32[]{:S(2)}, u32[]{:S(2)}) collective-permute-start(bf16[512,256]{1,0:T(8,128)(2,1)S(1)} %pad_maximum_fusion.5), channel_id=1, source_target_pairs={{0,2},{1,3},{2,4},{3,5},{4,6},{5,7},{6,0},{7,1},{8,10},{9,11},{10,... | collective-permute-start | bytes 786440 | tf_op jit(solution)/shard_map/ppermute | solution.py:270
  131.3 2.7 %slice_bitcast_fusion.5 = (bf16[256,1024]{1,0:T(8,128)(2,1)}, bf16[256,1024]{1,0:T(8,128)(2,1)}, bf16[256,1024]{1,0:T(8,128)(2,1)}, bf16[256,1024]{1,0:T(8,128)(2,1)S(1)}) fusion(bf16[4,512,1024]{2,1,0:T(8,128)(2,1)} %copy-done.5), kind=kLoop, calls=%fused_computation.19 | loop fusion | bytes 4194304 | tf_op jit(solution)/shard_map/slice | solution.py:252
  134.0 1.6 collective-permute-start.25
  135.6 0.4 collective-permute-start.27
  136.1 1.1 collective-permute-done.18
  137.2 0.8 fusion.7
  138.0 5.0 %all-to-all-done = bf16[4,128,512]{2,1,0:T(8,128)(2,1)S(1)} async-done(((bf16[4,128,512]{2,1,0:T(8,128)(2,1)}), bf16[4,128,512]{2,1,0:T(8,128)(2,1)S(1)}, u32[]{:S(2)}, u32[]{:S(2)}) %all-to-all-start) | async-done | bytes 524320 | tf_op jit(solution)/shard_map/all_to_all | solution.py:353
  143.0 4.0 %all-to-all-start.1 = ((bf16[4,128,256]{2,1,0:T(8,128)(2,1)}), bf16[4,128,256]{2,1,0:T(8,128)(2,1)S(1)}, u32[]{:S(2)}, u32[]{:S(2)}) async-start(bf16[4,128,256]{2,1,0:T(8,128)(2,1)} %bitcast.13), calls=%async_computation.1 | async-start | bytes 524288 | tf_op jit(solution)/shard_map/all_to_all | solution.py:353
  147.4 1.9 %fusion.5 = (bf16[256,1024]{1,0:T(8,128)(2,1)S(1)}, bf16[256,1024]{1,0:T(8,128)(2,1)S(1)}) fusion(bf16[256,1024]{1,0:T(8,128)(2,1)} %collective-permute-done.25, bf16[4,512,1024]{2,1,0:T(8,128)(2,1)} %copy-done.5, bf16[256,1024]{1,0:T(8,128)(2,1)} %collective-permute-done.27), kind=kLoop, calls=%fused_computation.14 | loop fusion | flops 2097152 | bytes 3145728 | tf_op jit(solution)/shard_map/convert.9
  149.3 9.2 %all-to-all-done.1 = bf16[4,128,256]{2,1,0:T(8,128)(2,1)S(1)} async-done(((bf16[4,128,256]{2,1,0:T(8,128)(2,1)}), bf16[4,128,256]{2,1,0:T(8,128)(2,1)S(1)}, u32[]{:S(2)}, u32[]{:S(2)}) %all-to-all-start.1) | async-done | bytes 262176 | tf_op jit(solution)/shard_map/all_to_all | solution.py:353
  158.7 1.1 pad_maximum_fusion.2
  159.7 0.4 collective-permute-start.28
  160.2 1.7 collective-permute-start.26
  161.9 2.4 %collective-permute-done.21 = bf16[128,768]{1,0:T(8,128)(2,1)S(1)} collective-permute-done((bf16[128,768]{1,0:T(8,128)(2,1)S(1)}, bf16[128,768]{1,0:T(8,128)(2,1)S(1)}, u32[]{:S(2)}, u32[]{:S(2)}) %collective-permute-start.21) | collective-permute-done | bytes 196640 | tf_op jit(solution)/shard_map/ppermute | solution.py:273
  164.4 0.3 collective-permute-start.24
  164.8 0.8 collective-permute-start.23
  165.6 0.9 collective-permute-start.22
  166.5 4.3 %collective-permute-done.24 = bf16[128,1024]{1,0:T(8,128)(2,1)S(1)} collective-permute-done((bf16[128,1024]{1,0:T(8,128)(2,1)S(1)}, bf16[128,1024]{1,0:T(8,128)(2,1)S(1)}, u32[]{:S(2)}, u32[]{:S(2)}) %collective-permute-start.24) | collective-permute-done | bytes 262176 | tf_op jit(solution)/shard_map/ppermute | solution.py:270
  170.9 1.9 collective-permute-done.23
  172.7 2.7 %collective-permute-done.22 = bf16[128,1024]{1,0:T(8,128)(2,1)S(1)} collective-permute-done((bf16[128,1024]{1,0:T(8,128)(2,1)S(1)}, bf16[128,1024]{1,0:T(8,128)(2,1)S(1)}, u32[]{:S(2)}, u32[]{:S(2)}) %collective-permute-start.22) | collective-permute-done | bytes 262176 | tf_op jit(solution)/shard_map/ppermute | solution.py:270
  175.7 1.0 maximum_bitcast_fusion
  176.7 4.4 %collective-permute-done.28 = bf16[512,1024]{1,0:T(8,128)(2,1)} collective-permute-done((bf16[512,1024]{1,0:T(8,128)(2,1)}, bf16[512,1024]{1,0:T(8,128)(2,1)}, u32[]{:S(2)}, u32[]{:S(2)}) %collective-permute-start.28) | collective-permute-done | bytes 1048608 | tf_op jit(solution)/shard_map/ppermute | solution.py:278
  181.2 1.4 collective-permute-done.26
  182.6 2.2 %fusion.1 = bf16[512,1024]{1,0:T(8,128)(2,1)S(1)} fusion(bf16[512,1024]{1,0:T(8,128)(2,1)} %collective-permute-done.28, bf16[512,1024]{1,0:T(8,128)(2,1)S(1)} %collective-permute-done.26, bf16[4,512,1024]{2,1,0:T(8,128)(2,1)} %copy-done.5), kind=kLoop, calls=%fused_computation.2 | loop fusion | flops 3145728 | bytes 4194304 | tf_op jit(solution)/shard_map/convert_element_type | solution.py:369
  184.8 0.8 reshape.42
  185.6 1.5 fusion.14
  187.1 1.3 copy.15
  188.4 1.0 copy.13
  189.4 1.3 copy.16
  190.7 1.0 copy.14
  (64 shorter events, 2.6 us)
Async XLA Ops:
  0.6 58.1 %copy-start.4 = (bf16[1,128,4096]{2,1,0:T(8,128)(2,1)S(1)}, bf16[1,128,4096]{2,1,0:T(8,128)(2,1)}, u32[]{:S(2)}) copy-start(bf16[1,128,4096]{2,1,0:T(8,128)(2,1)} %param.7) | copy-start | bytes 3145732
  1.7 15.8 %collective-permute-start = (bf16[128,1024]{1,0:T(8,128)(2,1)S(1)}, bf16[128,1024]{1,0:T(8,128)(2,1)S(1)}, u32[]{:S(2)}, u32[]{:S(2)}) collective-permute-start(bf16[128,1024]{1,0:T(8,128)(2,1)S(1)} %dynamic-slice_bitcast_fusion.4), channel_id=1, source_target_pairs={{0,64},{64,128},{128,192},{192,0},{1,65},{65,129},{129,193},{193,1... | collective-permute-start | bytes 786440 | tf_op jit(solution)/shard_map/ppermute | solution.py:266
  5.1 21.4 %collective-permute-start.1 = (bf16[128,1024]{1,0:T(8,128)(2,1)S(1)}, bf16[128,1024]{1,0:T(8,128)(2,1)S(1)}, u32[]{:S(2)}, u32[]{:S(2)}) collective-permute-start(bf16[128,1024]{1,0:T(8,128)(2,1)S(1)} %dynamic-slice_bitcast_fusion.4), channel_id=1, source_target_pairs={{0,128},{64,192},{128,0},{192,64},{1,129},{65,193},{129,1},{193,65... | collective-permute-start | bytes 786440 | tf_op jit(solution)/shard_map/ppermute | solution.py:266
  10.5 23.5 %collective-permute-start.2 = (bf16[128,1024]{1,0:T(8,128)(2,1)S(1)}, bf16[128,1024]{1,0:T(8,128)(2,1)S(1)}, u32[]{:S(2)}, u32[]{:S(2)}) collective-permute-start(bf16[128,1024]{1,0:T(8,128)(2,1)S(1)} %dynamic-slice_bitcast_fusion.4), channel_id=1, source_target_pairs={{0,192},{64,0},{128,64},{192,128},{1,193},{65,1},{129,65},{193,129... | collective-permute-start | bytes 786440 | tf_op jit(solution)/shard_map/ppermute | solution.py:266
  34.6 20.8 %collective-permute-start.3 = (bf16[384,1024]{1,0:T(8,128)(2,1)S(1)}, bf16[384,1024]{1,0:T(8,128)(2,1)S(1)}, u32[]{:S(2)}, u32[]{:S(2)}) collective-permute-start(bf16[384,1024]{1,0:T(8,128)(2,1)S(1)} %shard_map.102.refs_0_), channel_id=1, source_target_pairs={{0,2},{1,3},{2,4},{3,5},{4,6},{5,7},{6,0},{7,1},{8,10},{9,11},{10,... | collective-permute-start | bytes 2359304 | tf_op jit(solution)/shard_map/ppermute | solution.py:270
  36.1 19.6 %collective-permute-start.5 = (bf16[384,1024]{1,0:T(8,128)(2,1)S(1)}, bf16[384,1024]{1,0:T(8,128)(2,1)S(1)}, u32[]{:S(2)}, u32[]{:S(2)}) collective-permute-start(bf16[384,1024]{1,0:T(8,128)(2,1)S(1)} %shard_map.102.refs_0_), channel_id=1, source_target_pairs={{0,6},{1,7},{2,0},{3,1},{4,2},{5,3},{6,4},{7,5},{8,14},{9,15},{10,... | collective-permute-start | bytes 2359304 | tf_op jit(solution)/shard_map/ppermute | solution.py:270
  55.4 16.6 %collective-permute-start.4 = (bf16[192,1024]{1,0:T(8,128)(2,1)S(1)}, bf16[192,1024]{1,0:T(8,128)(2,1)S(1)}, u32[]{:S(2)}, u32[]{:S(2)}) collective-permute-start(bf16[192,1024]{1,0:T(8,128)(2,1)S(1)} %slice.150), channel_id=1, source_target_pairs={{0,2},{1,3},{2,4},{3,5},{4,6},{5,7},{6,0},{7,1},{8,10},{9,11},{10,... | collective-permute-start | bytes 1179656 | tf_op jit(solution)/shard_map/ppermute | solution.py:270
  55.7 16.2 %collective-permute-start.6 = (bf16[192,1024]{1,0:T(8,128)(2,1)S(1)}, bf16[192,1024]{1,0:T(8,128)(2,1)S(1)}, u32[]{:S(2)}, u32[]{:S(2)}) collective-permute-start(bf16[192,1024]{1,0:T(8,128)(2,1)S(1)} %slice.151), channel_id=1, source_target_pairs={{0,6},{1,7},{2,0},{3,1},{4,2},{5,3},{6,4},{7,5},{8,14},{9,15},{10,... | collective-permute-start | bytes 1179656 | tf_op jit(solution)/shard_map/ppermute | solution.py:270
  58.8 2.2 %copy-start = (bf16[1,4096,512]{2,1,0:T(8,128)(2,1)S(1)}, bf16[1,4096,512]{2,1,0:T(8,128)(2,1)}, u32[]{:S(2)}) copy-start(bf16[1,4096,512]{2,1,0:T(8,128)(2,1)} %param.8) | copy-start | bytes 12582916
  61.0 2.2 %copy-start.2 = (bf16[1,4096,512]{2,1,0:T(8,128)(2,1)S(1)}, bf16[1,4096,512]{2,1,0:T(8,128)(2,1)}, u32[]{:S(2)}) copy-start(bf16[1,4096,512]{2,1,0:T(8,128)(2,1)} %param.9) | copy-start | bytes 12582916
  63.2 2.6 %copy-start.1 = (bf16[1,4096,512]{2,1,0:T(8,128)(2,1)S(1)}, bf16[1,4096,512]{2,1,0:T(8,128)(2,1)}, u32[]{:S(2)}) copy-start(bf16[1,4096,512]{2,1,0:T(8,128)(2,1)} %param.8) | copy-start | bytes 12582916
  63.2 3.5 %copy-start.3 = (bf16[1,4096,512]{2,1,0:T(8,128)(2,1)S(1)}, bf16[1,4096,512]{2,1,0:T(8,128)(2,1)}, u32[]{:S(2)}) copy-start(bf16[1,4096,512]{2,1,0:T(8,128)(2,1)} %param.9) | copy-start | bytes 12582916
  65.7 25.1 %collective-permute-start.12 = (bf16[512,512]{1,0:T(8,128)(2,1)S(1)}, bf16[512,512]{1,0:T(8,128)(2,1)S(1)}, u32[]{:S(2)}, u32[]{:S(2)}) collective-permute-start(bf16[512,512]{1,0:T(8,128)(2,1)S(1)} %get-tuple-element.28), channel_id=1, source_target_pairs={{0,8},{8,0},{16,24},{24,16},{32,40},{40,32},{48,56},{56,48},{1,9},... | collective-permute-start | bytes 1572872 | tf_op jit(solution)/shard_map/ppermute | solution.py:281
  71.9 2.6 %copy-start.6 = (bf16[1,1,512,512]{3,2,1,0:T(8,128)(2,1)S(1)}, bf16[1,1,512,512]{3,2,1,0:T(8,128)(2,1)}, u32[]{:S(2)}) copy-start(bf16[1,1,512,512]{3,2,1,0:T(8,128)(2,1)} %param.10) | copy-start | bytes 1572868
  71.9 2.6 %copy-start.7 = (bf16[1,1,512,512]{3,2,1,0:T(8,128)(2,1)S(1)}, bf16[1,1,512,512]{3,2,1,0:T(8,128)(2,1)}, u32[]{:S(2)}) copy-start(bf16[1,1,512,512]{3,2,1,0:T(8,128)(2,1)} %param.11) | copy-start | bytes 1572868
  80.6 13.7 %collective-permute-start.16 = (bf16[512,1024]{1,0:T(8,128)(2,1)S(1)}, bf16[512,1024]{1,0:T(8,128)(2,1)S(1)}, u32[]{:S(2)}, u32[]{:S(2)}) collective-permute-start(bf16[512,1024]{1,0:T(8,128)(2,1)S(1)} %get-tuple-element.23.act_ref.refs_8_), channel_id=1, source_target_pairs={{0,8},{8,0},{16,24},{24,16},{32,40},{40,32},{48,56},{56,48},{1,9},... | collective-permute-start | bytes 3145736 | tf_op jit(solution)/shard_map/ppermute | solution.py:281
  80.7 10.6 %collective-permute-start.7 = (bf16[256,512]{1,0:T(8,128)(2,1)S(1)}, bf16[256,512]{1,0:T(8,128)(2,1)S(1)}, u32[]{:S(2)}, u32[]{:S(2)}) collective-permute-start(bf16[256,512]{1,0:T(8,128)(2,1)S(1)} %get-tuple-element.58), channel_id=1, source_target_pairs={{0,2},{1,3},{2,4},{3,5},{4,6},{5,7},{6,0},{7,1},{8,10},{9,11},{10,... | collective-permute-start | bytes 786440 | tf_op jit(solution)/shard_map/ppermute | solution.py:270
  81.0 10.3 %collective-permute-start.9 = (bf16[256,512]{1,0:T(8,128)(2,1)S(1)}, bf16[256,512]{1,0:T(8,128)(2,1)S(1)}, u32[]{:S(2)}, u32[]{:S(2)}) collective-permute-start(bf16[256,512]{1,0:T(8,128)(2,1)S(1)} %get-tuple-element.59), channel_id=1, source_target_pairs={{0,6},{1,7},{2,0},{3,1},{4,2},{5,3},{6,4},{7,5},{8,14},{9,15},{10,... | collective-permute-start | bytes 786440 | tf_op jit(solution)/shard_map/ppermute | solution.py:270
  84.2 7.6 %collective-permute-start.13 = (bf16[512,512]{1,0:T(8,128)(2,1)S(1)}, bf16[512,512]{1,0:T(8,128)(2,1)S(1)}, u32[]{:S(2)}, u32[]{:S(2)}) collective-permute-start(bf16[512,512]{1,0:T(8,128)(2,1)S(1)} %get-tuple-element.29), channel_id=1, source_target_pairs={{0,8},{8,0},{16,24},{24,16},{32,40},{40,32},{48,56},{56,48},{1,9},... | collective-permute-start | bytes 1572872 | tf_op jit(solution)/shard_map/ppermute | solution.py:281
  90.7 3.5 %collective-permute-start.15 = (bf16[512,512]{1,0:T(8,128)(2,1)S(1)}, bf16[512,512]{1,0:T(8,128)(2,1)S(1)}, u32[]{:S(2)}, u32[]{:S(2)}) collective-permute-start(bf16[512,512]{1,0:T(8,128)(2,1)S(1)} %get-tuple-element.31), channel_id=1, source_target_pairs={{0,8},{8,0},{16,24},{24,16},{32,40},{40,32},{48,56},{56,48},{1,9},... | collective-permute-start | bytes 1572872 | tf_op jit(solution)/shard_map/ppermute | solution.py:281
  91.3 25.2 %collective-permute-start.11 = (bf16[512,1024]{1,0:T(8,128)(2,1)S(1)}, bf16[512,1024]{1,0:T(8,128)(2,1)S(1)}, u32[]{:S(2)}, u32[]{:S(2)}) collective-permute-start(bf16[512,1024]{1,0:T(8,128)(2,1)S(1)} %shard_map.109.refs_0_), channel_id=1, source_target_pairs={{0,1},{1,0},{2,3},{3,2},{4,5},{5,4},{6,7},{7,6},{8,9},{9,8},{10,11... | collective-permute-start | bytes 3145736 | tf_op jit(solution)/shard_map/ppermute | solution.py:273
  91.3 2.9 %collective-permute-start.14 = (bf16[512,512]{1,0:T(8,128)(2,1)S(1)}, bf16[512,512]{1,0:T(8,128)(2,1)S(1)}, u32[]{:S(2)}, u32[]{:S(2)}) collective-permute-start(bf16[512,512]{1,0:T(8,128)(2,1)S(1)} %get-tuple-element.30), channel_id=1, source_target_pairs={{0,8},{8,0},{16,24},{24,16},{32,40},{40,32},{48,56},{56,48},{1,9},... | collective-permute-start | bytes 1572872 | tf_op jit(solution)/shard_map/ppermute | solution.py:281
  91.9 31.0 %collective-permute-start.10 = (bf16[512,512]{1,0:T(8,128)(2,1)S(1)}, bf16[512,512]{1,0:T(8,128)(2,1)S(1)}, u32[]{:S(2)}, u32[]{:S(2)}) collective-permute-start(bf16[512,512]{1,0:T(8,128)(2,1)S(1)} %pad_maximum_fusion.4), channel_id=1, source_target_pairs={{0,6},{1,7},{2,0},{3,1},{4,2},{5,3},{6,4},{7,5},{8,14},{9,15},{10,... | collective-permute-start | bytes 1572872 | tf_op jit(solution)/shard_map/ppermute | solution.py:270
  94.2 28.6 %collective-permute-start.8 = (bf16[512,512]{1,0:T(8,128)(2,1)S(1)}, bf16[512,512]{1,0:T(8,128)(2,1)S(1)}, u32[]{:S(2)}, u32[]{:S(2)}) collective-permute-start(bf16[512,512]{1,0:T(8,128)(2,1)S(1)} %pad_maximum_fusion.3), channel_id=1, source_target_pairs={{0,2},{1,3},{2,4},{3,5},{4,6},{5,7},{6,0},{7,1},{8,10},{9,11},{10,... | collective-permute-start | bytes 1572872 | tf_op jit(solution)/shard_map/ppermute | solution.py:270
  99.4 20.0 %copy-start.5 = (bf16[4,512,1024]{2,1,0:T(8,128)(2,1)}, bf16[4,512,1024]{2,1,0:T(8,128)(2,1)S(1)}, u32[]{:S(2)}) copy-start(bf16[4,512,1024]{2,1,0:T(8,128)(2,1)S(1)} %shard_map.111.refs_1_) | copy-start | bytes 12582916
  119.6 9.3 %collective-permute-start.17 = (bf16[256,256]{1,0:T(8,128)(2,1)S(1)}, bf16[256,256]{1,0:T(8,128)(2,1)S(1)}, u32[]{:S(2)}, u32[]{:S(2)}) collective-permute-start(bf16[256,256]{1,0:T(8,128)(2,1)S(1)} %get-tuple-element.54), channel_id=1, source_target_pairs={{0,2},{1,3},{2,4},{3,5},{4,6},{5,7},{6,0},{7,1},{8,10},{9,11},{10,... | collective-permute-start | bytes 393224 | tf_op jit(solution)/shard_map/ppermute | solution.py:270
  119.7 9.2 %collective-permute-start.19 = (bf16[256,256]{1,0:T(8,128)(2,1)S(1)}, bf16[256,256]{1,0:T(8,128)(2,1)S(1)}, u32[]{:S(2)}, u32[]{:S(2)}) collective-permute-start(bf16[256,256]{1,0:T(8,128)(2,1)S(1)} %get-tuple-element.55), channel_id=1, source_target_pairs={{0,6},{1,7},{2,0},{3,1},{4,2},{5,3},{6,4},{7,5},{8,14},{9,15},{10,... | collective-permute-start | bytes 393224 | tf_op jit(solution)/shard_map/ppermute | solution.py:270
  123.9 19.1 %all-to-all-start = ((bf16[4,128,512]{2,1,0:T(8,128)(2,1)}), bf16[4,128,512]{2,1,0:T(8,128)(2,1)S(1)}, u32[]{:S(2)}, u32[]{:S(2)}) async-start(bf16[4,128,512]{2,1,0:T(8,128)(2,1)} %bitcast.12), calls=%async_computation | async-start | bytes 1048576 | tf_op jit(solution)/shard_map/all_to_all | solution.py:353
  128.9 7.1 %collective-permute-start.20 = (bf16[512,256]{1,0:T(8,128)(2,1)S(1)}, bf16[512,256]{1,0:T(8,128)(2,1)S(1)}, u32[]{:S(2)}, u32[]{:S(2)}) collective-permute-start(bf16[512,256]{1,0:T(8,128)(2,1)S(1)} %pad_maximum_fusion.6), channel_id=1, source_target_pairs={{0,6},{1,7},{2,0},{3,1},{4,2},{5,3},{6,4},{7,5},{8,14},{9,15},{10,... | collective-permute-start | bytes 786440 | tf_op jit(solution)/shard_map/ppermute | solution.py:270
  129.2 7.9 %collective-permute-start.18 = (bf16[512,256]{1,0:T(8,128)(2,1)S(1)}, bf16[512,256]{1,0:T(8,128)(2,1)S(1)}, u32[]{:S(2)}, u32[]{:S(2)}) collective-permute-start(bf16[512,256]{1,0:T(8,128)(2,1)S(1)} %pad_maximum_fusion.5), channel_id=1, source_target_pairs={{0,2},{1,3},{2,4},{3,5},{4,6},{5,7},{6,0},{7,1},{8,10},{9,11},{10,... | collective-permute-start | bytes 786440 | tf_op jit(solution)/shard_map/ppermute | solution.py:270
  134.0 13.1 %collective-permute-start.25 = (bf16[256,1024]{1,0:T(8,128)(2,1)}, bf16[256,1024]{1,0:T(8,128)(2,1)}, u32[]{:S(2)}, u32[]{:S(2)}) collective-permute-start(bf16[256,1024]{1,0:T(8,128)(2,1)} %get-tuple-element.38), channel_id=1, source_target_pairs={{0,16},{8,24},{16,32},{24,40},{32,48},{40,56},{48,0},{56,8},{1,17}... | collective-permute-start | bytes 1572872 | tf_op jit(solution)/shard_map/ppermute | solution.py:278
  135.6 11.7 %collective-permute-start.27 = (bf16[256,1024]{1,0:T(8,128)(2,1)}, bf16[256,1024]{1,0:T(8,128)(2,1)}, u32[]{:S(2)}, u32[]{:S(2)}) collective-permute-start(bf16[256,1024]{1,0:T(8,128)(2,1)} %get-tuple-element.39), channel_id=1, source_target_pairs={{0,48},{8,56},{16,0},{24,8},{32,16},{40,24},{48,32},{56,40},{1,49}... | collective-permute-start | bytes 1572872 | tf_op jit(solution)/shard_map/ppermute | solution.py:278
  143.0 15.5 %all-to-all-start.1 = ((bf16[4,128,256]{2,1,0:T(8,128)(2,1)}), bf16[4,128,256]{2,1,0:T(8,128)(2,1)S(1)}, u32[]{:S(2)}, u32[]{:S(2)}) async-start(bf16[4,128,256]{2,1,0:T(8,128)(2,1)} %bitcast.13), calls=%async_computation.1 | async-start | bytes 524288 | tf_op jit(solution)/shard_map/all_to_all | solution.py:353
  147.1 11.5 %copy-start.8 = (bf16[256,1024]{1,0:T(8,128)(2,1)S(1)}, bf16[256,1024]{1,0:T(8,128)(2,1)}, u32[]{:S(2)}) copy-start(bf16[256,1024]{1,0:T(8,128)(2,1)} %get-tuple-element.40) | copy-start | bytes 1572868
  158.5 5.8 %collective-permute-start.21 = (bf16[128,768]{1,0:T(8,128)(2,1)S(1)}, bf16[128,768]{1,0:T(8,128)(2,1)S(1)}, u32[]{:S(2)}, u32[]{:S(2)}) collective-permute-start(bf16[128,768]{1,0:T(8,128)(2,1)S(1)} %pad_maximum_fusion.8), channel_id=1, source_target_pairs={{0,1},{1,0},{2,3},{3,2},{4,5},{5,4},{6,7},{7,6},{8,9},{9,8},{10,11... | collective-permute-start | bytes 589832 | tf_op jit(solution)/shard_map/ppermute | solution.py:273
  159.7 21.5 %collective-permute-start.28 = (bf16[512,1024]{1,0:T(8,128)(2,1)}, bf16[512,1024]{1,0:T(8,128)(2,1)}, u32[]{:S(2)}, u32[]{:S(2)}) collective-permute-start(bf16[512,1024]{1,0:T(8,128)(2,1)} %pad_maximum_fusion.2), channel_id=1, source_target_pairs={{0,48},{8,56},{16,0},{24,8},{32,16},{40,24},{48,32},{56,40},{1,49}... | collective-permute-start | bytes 3145736 | tf_op jit(solution)/shard_map/ppermute | solution.py:278
  160.2 22.4 %collective-permute-start.26 = (bf16[512,1024]{1,0:T(8,128)(2,1)S(1)}, bf16[512,1024]{1,0:T(8,128)(2,1)S(1)}, u32[]{:S(2)}, u32[]{:S(2)}) collective-permute-start(bf16[512,1024]{1,0:T(8,128)(2,1)S(1)} %pad_maximum_fusion.1), channel_id=1, source_target_pairs={{0,16},{8,24},{16,32},{24,40},{32,48},{40,56},{48,0},{56,8},{1,17}... | collective-permute-start | bytes 3145736 | tf_op jit(solution)/shard_map/ppermute | solution.py:278
  164.4 6.4 %collective-permute-start.24 = (bf16[128,1024]{1,0:T(8,128)(2,1)S(1)}, bf16[128,1024]{1,0:T(8,128)(2,1)S(1)}, u32[]{:S(2)}, u32[]{:S(2)}) collective-permute-start(bf16[128,1024]{1,0:T(8,128)(2,1)S(1)} %get-tuple-element.61), channel_id=1, source_target_pairs={{0,6},{1,7},{2,0},{3,1},{4,2},{5,3},{6,4},{7,5},{8,14},{9,15},{10,... | collective-permute-start | bytes 786440 | tf_op jit(solution)/shard_map/ppermute | solution.py:270
  164.8 8.0 %collective-permute-start.23 = (bf16[128,1024]{1,0:T(8,128)(2,1)S(1)}, bf16[128,1024]{1,0:T(8,128)(2,1)S(1)}, u32[]{:S(2)}, u32[]{:S(2)}) collective-permute-start(bf16[128,1024]{1,0:T(8,128)(2,1)S(1)} %get-tuple-element.61), channel_id=1, source_target_pairs={{0,4},{1,5},{2,6},{3,7},{4,0},{5,1},{6,2},{7,3},{8,12},{9,13},{10,... | collective-permute-start | bytes 786440 | tf_op jit(solution)/shard_map/ppermute | solution.py:270
  165.6 9.9 %collective-permute-start.22 = (bf16[128,1024]{1,0:T(8,128)(2,1)S(1)}, bf16[128,1024]{1,0:T(8,128)(2,1)S(1)}, u32[]{:S(2)}, u32[]{:S(2)}) collective-permute-start(bf16[128,1024]{1,0:T(8,128)(2,1)S(1)} %get-tuple-element.61), channel_id=1, source_target_pairs={{0,2},{1,3},{2,4},{3,5},{4,6},{5,7},{6,0},{7,1},{8,10},{9,11},{10,... | collective-permute-start | bytes 786440 | tf_op jit(solution)/shard_map/ppermute | solution.py:270

commit v2 on v1

--- a/solution.py
+++ b/solution.py
@@ -3,6 +3,7 @@
 from jax import lax
 from jax.experimental import pallas as pl
 from jax.experimental.pallas import tpu as pltpu
+from jax.sharding import Mesh
 from jax.sharding import PartitionSpec as P
 
 HEAD = 256
@@ -61,7 +62,7 @@
     )(info, *parts)
 
 
-def project(m, enc, parts, wk, wv, acc, info, last, n_sec):
+def project(m, enc, parts, wk, wv, acc, info, last, n_sec, after=()):
     blk, width = enc.shape
     quarter = width // XS
     total = n_sec * blk
@@ -117,7 +118,8 @@
             in_specs=[pl.BlockSpec((blk, quarter), lambda h, info: (0, at_quarter(info)))]
             + [whole(p) for p in parts]
             + [weight, weight]
-            + ([pair] if acc is not None else []),
+            + ([pair] if acc is not None else [])
+            + [ANYWHERE] * len(after),
             out_specs=[pair, whole(out_shape[1]), whole(out_shape[2])],
         ),
         out_shape=out_shape,
@@ -125,7 +127,7 @@
         cost_estimate=pl.CostEstimate(
             flops=4 * total * quarter * cols, bytes_accessed=6 * 1024 * 1024, transcendentals=0
         ),
-    )(info, enc, *parts, wk, wv, *([acc] if acc is not None else []))
+    )(info, enc, *parts, wk, wv, *([acc] if acc is not None else []), *after)
 
 
 def attention(kv, q, g, info):
@@ -173,10 +175,11 @@
     )(info, kv, q, g)
 
 
-def partial_grad(act, wk, wv, info, units, dtype, after=(), add=None):
+def partial_grad(act, wk, wv, info, units, after=(), split=False, adds=None, n_sec=1):
     total, cols = act.shape[0], wk.shape[1]
     heads = cols // HEAD
     n = len(units)
+    blk = total // n_sec
 
     def unit(i, info):
         at = units[0](info)
@@ -185,35 +188,47 @@
         return at
 
     def body(info, act_ref, wk_ref, wv_ref, *refs):
-        out_ref = refs[-1]
         sums = None
         for h in range(heads):
             for j, w_ref in enumerate((wk_ref, wv_ref)):
                 at = (2 * h + j) * HEAD
                 term = dot_t(act_ref[:, at : at + HEAD], w_ref[:, h * HEAD : (h + 1) * HEAD])
                 sums = term if sums is None else sums + term
-        if add is not None:
-            sums = sums + refs[0][...].astype(f32)
-        out_ref[...] = sums.astype(dtype)
+        if adds is not None:
+            sums = sums + refs[0][...].astype(f32) + refs[1][...].astype(f32)
+            for k in range(n_sec):
+                refs[-1][k, 0] = sums[k * blk : (k + 1) * blk].astype(bf16)
+        elif split:
+            refs[-2][...] = sums[: total // 2].astype(bf16)
+            refs[-1][...] = sums[total // 2 :].astype(bf16)
+        else:
+            refs[-1][...] = sums
 
     weight = pl.BlockSpec((UNIT, cols), lambda i, info: (unit(i, info), 0))
     block = pl.BlockSpec((total, UNIT), lambda i, info: (0, i))
+    if adds is not None:
+        out_specs = pl.BlockSpec((n_sec, 1, blk, UNIT), lambda i, info: (0, i, 0, 0))
+        out_shape = jax.ShapeDtypeStruct((n_sec, n, blk, UNIT), bf16)
+    elif split:
+        out_specs = [pl.BlockSpec((total // 2, UNIT), lambda i, info: (0, i))] * 2
+        out_shape = [jax.ShapeDtypeStruct((total // 2, n * UNIT), bf16)] * 2
+    else:
+        out_specs, out_shape = block, jax.ShapeDtypeStruct((total, n * UNIT), f32)
+    more = [] if adds is None else list(adds)
     return pl.pallas_call(
         body,
         grid_spec=pltpu.PrefetchScalarGridSpec(
             num_scalar_prefetch=1,
             grid=(n,),
-            in_specs=[whole(act), weight, weight]
-            + ([block] if add is not None else [])
-            + [ANYWHERE] * len(after),
-            out_specs=block,
-        ),
-        out_shape=jax.ShapeDtypeStruct((total, n * UNIT), dtype),
+            in_specs=[whole(act), weight, weight] + [block] * len(more) + [ANYWHERE] * len(after),
+            out_specs=out_specs,
+        ),
+        out_shape=out_shape,
         compiler_params=params(12),
         cost_estimate=pl.CostEstimate(
             flops=4 * total * n * UNIT * cols, bytes_accessed=2 * 1024 * 1024, transcendentals=0
         ),
-    )(info, act, wk, wv, *([add] if add is not None else []), *after)
+    )(info, act, wk, wv, *more, *after)
 
 
 def pair_grads(rows, halves, act, act_other, info, after):
@@ -222,12 +237,24 @@
     n = len(rows)
 
     def body(info, *refs):
-        row_refs, half_refs, act_ref, other_ref, out_ref = refs[:n], refs[n : 2 * n], refs[2 * n], refs[2 * n + 1], refs[-1]
+        row_refs, half_refs, act_ref, other_ref = refs[:n], refs[n : 2 * n], refs[2 * n], refs[2 * n + 1]
+        out_ref, top_ref, low_ref = refs[-3:]
         for m in range(n):
             piece = t_dot(row_refs[m][...], act_ref[...]) + t_dot(half_refs[m][...], other_ref[...])
-            out_ref[mod4(info[X] - info[Y] - m)] = piece.astype(bf16)
-
-    out = jax.ShapeDtypeStruct((n, half, act.shape[1]), bf16)
+            piece = piece.astype(bf16)
+            slot = mod4(info[X] - info[Y] - m)
+            out_ref[slot] = piece
+
+            @pl.when(slot == 2)
+            def _():
+                top_ref[...] = piece[: half // 2]
+                low_ref[...] = piece[half // 2 :]
+
+    out = [
+        jax.ShapeDtypeStruct((n, half, act.shape[1]), bf16),
+        jax.ShapeDtypeStruct((half // 2, act.shape[1]), bf16),
+        jax.ShapeDtypeStruct((half // 2, act.shape[1]), bf16),
+    ]
     return pl.pallas_call(
         body,
         grid_spec=pltpu.PrefetchScalarGridSpec(
@@ -237,7 +264,7 @@
             + [whole(h) for h in halves]
             + [whole(act), whole(act_other)]
             + [ANYWHERE] * len(after),
-            out_specs=whole(out),
+            out_specs=[whole(o) for o in out],
         ),
         out_shape=out,
         compiler_params=params(28),
@@ -247,30 +274,48 @@
     )(info, *rows, *halves, act, act_other, *after)
 
 
-def spread(far, near_up, near_down, keep, shift):
-    half = far.shape[0] // 2
-    got_up = shift(far[:half], 1).astype(f32)
-    got_down = shift(far[half:], -1).astype(f32)
-    up = jnp.concatenate([near_up[:half].astype(f32) + got_up, near_up[half:].astype(f32)], axis=0)
-    down = jnp.concatenate([near_down[:half].astype(f32), near_down[half:].astype(f32) + got_down], axis=0)
-    from_below = shift(up.astype(bf16), 1).astype(f32)
-    from_above = shift(down.astype(bf16), -1).astype(f32)
-    return keep.astype(f32) + from_below + from_above
-
-
-def make_shards(mesh):
-    n_sec, n_dp, n_ten = mesh.shape["section"], mesh.shape["dp"], mesh.shape["tensor"]
-    lows, cores = n_ten // XS, 2
+def small(body, ins, outs, info, after=()):
+    ins = [i if isinstance(i, tuple) else (i, whole(i)) for i in ins]
+    n = len(ins)
+
+    def run(info, *refs):
+        body(info, *refs[:n], *refs[n + len(after) :])
+
+    return pl.pallas_call(
+        run,
+        grid_spec=pltpu.PrefetchScalarGridSpec(
+            num_scalar_prefetch=1,
+            grid=(1,),
+            in_specs=[s for _, s in ins] + [ANYWHERE] * len(after),
+            out_specs=[whole(o) for o in outs],
+        ),
+        out_shape=outs,
+        compiler_params=params(24),
+        cost_estimate=pl.CostEstimate(flops=1024 * 1024, bytes_accessed=1024 * 1024, transcendentals=0),
+    )(info, *[a for a, _ in ins], *after)
+
+
+def add_near(up, down, got_up, got_down, rows, cols, info, after=()):
+    half = rows // 2
+
+    def body(info, up_ref, down_ref, got_up_ref, got_down_ref, up_out, down_out):
+        up_out[:half] = (up_ref[:half].astype(f32) + got_up_ref[...].astype(f32)).astype(bf16)
+        up_out[half:] = up_ref[half:].astype(bf16)
+        down_out[:half] = down_ref[:half].astype(bf16)
+        down_out[half:] = (down_ref[half:].astype(f32) + got_down_ref[...].astype(f32)).astype(bf16)
+
+    out = jax.ShapeDtypeStruct((rows, cols), bf16)
+    return small(body, [up, down, got_up, got_down], [out, out], info, after)
+
+
+def make_shards(n_sec, n_dp, lows):
+    cores = 2
 
     def shift_section(v, k):
         return lax.ppermute(v, "section", [(i, (i + k) % n_sec) for i in range(n_sec)])
 
     def shift_x(v, k):
-        pairs = [(x * lows + l, ((x + k) % XS) * lows + l) for x in range(XS) for l in range(lows)]
-        return lax.ppermute(v, "tensor", pairs)
-
-    def swap_lo(v):
-        return lax.ppermute(v, "tensor", [(i, i ^ 1) for i in range(n_ten)])
+        return lax.ppermute(v, "x", [(i, (i + k) % XS) for i in range(XS)])
 
     def shift_y(v, k):
         ys = n_dp // cores
@@ -286,9 +331,8 @@
         quarter = width // XS
         local_width = wk.shape[1]
         total_src = n_sec * blk
-        ten, dp = lax.axis_index("tensor"), lax.axis_index("dp")
-        x, lo = ten // lows, ten % lows
-        sec = lax.axis_index("section")
+        dp = lax.axis_index("dp")
+        x, lo, sec = lax.axis_index("x"), lax.axis_index("low"), lax.axis_index("section")
         info = jnp.stack(
             [
                 x,
@@ -306,13 +350,19 @@
         mid = g0.shape[0] // 2
         g1 = shift_x(g0, 1)
         g3 = shift_x(g0, -1)
-        g2a = shift_x(g1[:mid], 1)
-        g2b = shift_x(g3[mid:], -1)
-        parts = ([g0], [g1], [g2a, g2b], [g3])
         rows, halves = [None] * XS, [None] * XS
-        acc = None
-        for m in (0, 1, 3, 2):
-            acc, rows[m], halves[m] = project(m, enc, parts[m], wk, wv, acc, info, m == 2, n_sec)
+        acc, rows[0], halves[0] = project(0, enc, [g0], wk, wv, None, info, False, n_sec)
+        part = jax.ShapeDtypeStruct((mid, quarter), bf16)
+
+        def cut(info, g1_ref, g3_ref, top_ref, low_ref):
+            top_ref[...] = g1_ref[:mid]
+            low_ref[...] = g3_ref[mid:]
+
+        top, low = small(cut, [g1, g3], [part, part], info, (acc,))
+        g2a = shift_x(top, 1)
+        g2b = shift_x(low, -1)
+        for m, parts in ((1, [g1]), (3, [g3]), (2, [g2a, g2b])):
+            acc, rows[m], halves[m] = project(m, enc, parts, wk, wv, acc, info, m == 2, n_sec, (top,))
         halves = [swap_core(h) for h in halves]
 
         context, act = attention(acc, queries[0, 0], ctx_grad[0, 0], info)
@@ -320,78 +370,116 @@
         act_other = swap_core(act)
 
         per = quarter // UNIT
-        a_units = per // 2
-
-        def unit(m, j, side=None):
-            def at(info):
-                u = mod4(info[X] - m) * per + j
-                if side is None:
-                    return u
-                return u + (info[LO] if side else 1 - info[LO])
-
-            return at
-
-        far_a = partial_grad(act, wk, wv, info, [unit(2, j) for j in range(a_units)], bf16)
-        sent_b = partial_grad(
-            act, wk, wv, info, [unit(m, a_units, False) for m in (2, 3, 1, 0)], bf16, (far_a,)
+        span = per // 2
+        cols = span * UNIT
+
+        def units(quarters, part):
+            return [
+                lambda info, m=m, j=j: mod4(info[X] - m) * per + part * span + j
+                for m in quarters
+                for j in range(span)
+            ]
+
+        def grad(quarters, part, after=(), **more):
+            return partial_grad(act, wk, wv, info, units(quarters, part), after, n_sec=n_sec, **more)
+
+        def steer(near, got, after=()):
+            up = pl.BlockSpec((total_src, cols), lambda i, info: (0, 0))
+            down = pl.BlockSpec((total_src, cols), lambda i, info: (0, 1))
+            return add_near((near, up), (near, down), *got, total_src, cols, info, after)
+
+        far_a = grad((2,), 0, split=True)
+        got_a = shift_x(far_a[0], 1), shift_x(far_a[1], -1)
+        far_b = grad((2,), 1, far_a, split=True)
+        got_b = shift_x(far_b[0], 1), shift_x(far_b[1], -1)
+        near_a = grad((3, 1), 0, far_b)
+        out_a = steer(near_a, got_a)
+        in_a = shift_x(out_a[0], 1), shift_x(out_a[1], -1)
+
+        pieces, far_top, far_low = pair_grads(rows, halves, act, act_other, info, out_a)
+        got_y = shift_y(far_top, 1), shift_y(far_low, -1)
+
+        near_b = grad((3, 1), 1, (far_top,))
+        out_b = steer(near_b, got_b)
+        in_b = shift_x(out_b[0], 1), shift_x(out_b[1], -1)
+        total_a = grad((0,), 0, out_b, adds=in_a)
+
+        def over_sections(total):
+            flat = total.reshape(n_sec * lows, blk, UNIT)
+            return lax.all_to_all(flat, ("section", "low"), 0, 0, tiled=True)
+
+        terms_a = over_sections(total_a)
+        wide = pieces.shape[2]
+
+        def piece(i):
+            return pieces, pl.BlockSpec((None, cols, wide), lambda _, info: (i, 0, 0))
+
+        out_y = add_near(piece(1), piece(3), *got_y, cols, wide, info, (total_a,))
+        in_y = shift_y(out_y[0], 1), shift_y(out_y[1], -1)
+        total_b = grad((0,), 1, out_y, adds=in_b)
+        terms_b = over_sections(total_b)
+
+        ends = XS * lows
+        copies = jax.ShapeDtypeStruct((ends, blk, 2 * UNIT), bf16)
+
+        def collect(info, a_ref, b_ref, out_ref):
+            for j, ref in enumerate((a_ref, b_ref)):
+                sums = jnp.sum(ref[...].astype(f32), axis=0).astype(bf16)
+                for e in range(ends):
+                    out_ref[e, :, j * UNIT : (j + 1) * UNIT] = sums
+
+        (spread_out,) = small(collect, [terms_a, terms_b], [copies], info)
+        gathered = lax.all_to_all(spread_out, ("x", "low"), 0, 0, tiled=True)
+
+        def finish_y(info, keep_ref, below_ref, above_ref, key_ref, value_ref):
+            sums = keep_ref[...].astype(f32) + below_ref[...].astype(f32) + above_ref[...].astype(f32)
+            sums = sums.astype(bf16)
+            for h in range(local_width // HEAD):
+                at = 2 * h * HEAD
+                key_ref[:, h * HEAD : (h + 1) * HEAD] = sums[:, at : at + HEAD]
+                value_ref[:, h * HEAD : (h + 1) * HEAD] = sums[:, at + HEAD : at + 2 * HEAD]
+
+        shard = jax.ShapeDtypeStruct((cols, local_width), bf16)
+        key_weight_grad, value_weight_grad = small(
+            finish_y, [piece(0), *in_y], [shard, shard], info, (spread_out,)
         )
-        got_b = swap_lo(sent_b)
-        near_a = partial_grad(
-            act, wk, wv, info, [unit(m, j) for m in (3, 1, 0) for j in range(a_units)], f32, (sent_b,)
-        )
-        pieces = pair_grads(rows, halves, act, act_other, info, (near_a,))
-        sum_b = partial_grad(
-            act, wk, wv, info, [unit(m, a_units, True) for m in (2, 3, 1, 0)], f32, (pieces,), got_b
-        )
-        cols = a_units * UNIT
-        total_a = spread(far_a, near_a[:, :cols], near_a[:, cols : 2 * cols], near_a[:, 2 * cols :], shift_x)
-        part_b = [sum_b[:, j * UNIT : (j + 1) * UNIT] for j in range(XS)]
-        total_b = spread(part_b[0].astype(bf16), part_b[1], part_b[2], part_b[3], shift_x)
-
-        def over_sections(total):
-            low = total.astype(bf16).reshape(n_sec, blk, total.shape[1])
-            terms = lax.all_to_all(low, "section", 0, 0, tiled=True)
-            return jnp.sum(terms.astype(f32), axis=0).astype(bf16)
-
-        mine_a = over_sections(total_a)
-        mine_b = over_sections(total_b)
-        other = swap_lo(jnp.concatenate([mine_a, mine_b], axis=1))
-        final_a = (mine_a.astype(f32) + other[:, :cols].astype(f32)).astype(bf16)
-        low_b = jnp.where(lo == 0, mine_b, other[:, cols:])
-        high_b = jnp.where(lo == 0, other[:, cols:], mine_b)
-        final = jnp.concatenate([final_a, low_b, high_b], axis=1)
-        gathered = jnp.stack([final] + [shift_x(final, k) for k in range(1, XS)])
-        enc_grad = jnp.concatenate(
-            [lax.dynamic_index_in_dim(gathered, (x - q) % XS, 0, False) for q in range(XS)], axis=1
-        )[None]
-
-        weight_grads = spread(pieces[2], pieces[1], pieces[3], pieces[0], shift_y)
-        weight_grads = weight_grads.astype(bf16).reshape(quarter // cores, local_width // HEAD, 2, HEAD)
-        key_weight_grad = weight_grads[:, :, 0].reshape(1, quarter // cores, local_width)
-        value_weight_grad = weight_grads[:, :, 1].reshape(1, quarter // cores, local_width)
+        key_weight_grad, value_weight_grad = key_weight_grad[None], value_weight_grad[None]
+
+        def place(info, ref, out_ref):
+            for e in range(ends):
+                for j in range(2):
+                    at = (e // lows) * quarter + j * cols + (e % lows) * UNIT
+                    out_ref[:, at : at + UNIT] = ref[e, :, j * UNIT : (j + 1) * UNIT]
+
+        (enc_grad,) = small(place, [gathered], [jax.ShapeDtypeStruct((blk, width), bf16)], info)
+        enc_grad = enc_grad[None]
         return (context, enc_grad, key_weight_grad, value_weight_grad)
 
     return shards
 
 
 def solution(mesh):
+    n_sec, n_dp, n_ten = (mesh.shape[name] for name in ("section", "dp", "tensor"))
+    lows = n_ten // XS
+    fine = Mesh(mesh.devices.reshape(n_sec, n_dp, XS, lows), ("section", "dp", "x", "low"))
+    heads = ("x", "low")
     return jax.shard_map(
-        make_shards(mesh),
-        mesh=mesh,
+        make_shards(n_sec, n_dp, lows),
+        mesh=fine,
         in_specs=(
             P("dp", "section", None),
-            P("section", None, "tensor"),
-            P("section", None, "tensor"),
-            P("section", "dp", None, "tensor"),
-            P("section", "dp", None, "tensor"),
+            P("section", None, heads),
+            P("section", None, heads),
+            P("section", "dp", None, heads),
+            P("section", "dp", None, heads),
             P("dp"),
             P("dp"),
         ),
         out_specs=(
-            P("section", "dp", None, "tensor"),
+            P("section", "dp", None, heads),
             P("dp", "section", None),
-            P("section", "dp", "tensor"),
-            P("section", "dp", "tensor"),
+            P("section", "dp", heads),
+            P("section", "dp", heads),
         ),
         check_vma=False,
     )

time: 194 us -> 205 us (1.057)
  blocking collectives: 0 us -> 22 us
  waiting for transfers between devices: 86.8 us -> 68.7 us
  Pallas kernels: 31.1 us -> 42.4 us
  other arithmetic: 9.13 us -> 0 us
  starting transfers between devices: 46 us -> 53.5 us
  local copies, waits for them, and re-layouts: 16.3 us -> 13.5 us
    ppermute x17 -> x12, waiting for transfers between devices: 47 us -> 23.7 us  [shift_x(): return lax.ppermute(v, 'x', [(i, (i + k) % XS) for i in range(XS)])]
    all_to_all x0 -> x1, blocking collectives: none -> 22 us  [over_sections(): return lax.all_to_all(flat, ('section', 'low'), 0, 0, tiled=True)]
    ppermute x4, waiting for transfers between devices: 6.09 us -> 27.8 us  [shift_y(): return lax.ppermute(v, 'dp', pairs)]
    all_to_all x2, waiting for transfers between devices: 14.2 us -> 0.01 us  [the longest x1 0.01 us: over_sections(): return lax.all_to_all(flat, ('section', 'low'), 0, 0, tiled=True)]
    all_to_all x2, starting transfers between devices: 8.95 us -> 19.3 us  [the longest x1 14.4 us: over_sections(): return lax.all_to_all(flat, ('section', 'low'), 0, 0, tiled=True)]
    pallas_call x0 -> x7, Pallas kernels: none -> 8.83 us  [small(): pl.pallas_call(run, grid_spec=pltpu.PrefetchScalarGridSpec(num_scalar_pre...]
    slice x7 -> x0, local copies, waits for them, and re-layouts: 4.36 us -> none  [the longest x3 2.77 us: spread(): got_up = shift(far[:half], 1).astype(f32)]
    convert_element_type x4 -> x0, other arithmetic: 4.04 us -> none  [the longest x1 2.16 us: shards(): weight_grads.astype(bf16)]
  transfers between devices with their start and end apart: 31 -> 26, of which waited for: 15 -> 11; matrix products, arithmetic and copies ran while one was open for 5% -> 0% of each run, Pallas kernels for 16% -> 14%
where the time goes in v2:
time: 205 us; the launch traced here: 202 us
  waiting for transfers between devices  68.7 us (34%)
  starting transfers between devices  53.5 us (26%)
  Pallas kernels  42.4 us (21%)
  blocking collectives  22 us (11%)
  local copies, waits for them, and re-layouts  13.5 us (7%)
  between operations  2.21 us (1%)
    ppermute x4, waiting for transfers between devices, shift_y(): return lax.ppermute(v, 'dp', pairs)  27.8 us
    ppermute x12, waiting for transfers between devices, shift_x(): return lax.ppermute(v, 'x', [(i, (i + k) % XS) for i in range(XS)])  23.7 us
    all_to_all x1, blocking collectives, over_sections(): return lax.all_to_all(flat, ('section', 'low'), 0, 0, tiled=True)  22 us
    ppermute x12, starting transfers between devices, shift_x(): return lax.ppermute(v, 'x', [(i, (i + k) % XS) for i in range(XS)])  18 us
    ppermute x3, waiting for transfers between devices, shift_section(): lax.ppermute(v, 'section', [(i, (i + k) % n_sec) for i in range(n_sec)])  17.2 us
    all_to_all x1, starting transfers between devices, over_sections(): return lax.all_to_all(flat, ('section', 'low'), 0, 0, tiled=True)  14.4 us
    unnamed x32, local copies, waits for them, and re-layouts  12.4 us
    pallas_call x6, Pallas kernels, partial_grad(): pl.pallas_call(body, grid_spec=pltpu.PrefetchScalarGridSpec(num_scalar_pr...  12.4 us
  transfers between devices with their start and end apart: 26, of which 11 were waited for; matrix products, arithmetic and copies ran while one was open for 0% of the time, Pallas kernels for 14%

profile of v2, /device:TPU:8, one launch (start us, length us, event | category | flops | bytes accessed | tf_op | source)
XLA Modules:
  0.0 202.3 jit_solution(8842596625296843460)
XLA Ops:
  0.6 1.1 dynamic-slice_bitcast_fusion
  1.7 6.4 %collective-permute-start.2 = (bf16[128,1024]{1,0:T(8,128)(2,1)S(1)}, bf16[128,1024]{1,0:T(8,128)(2,1)S(1)}, u32[]{:S(2)}, u32[]{:S(2)}) collective-permute-start(bf16[128,1024]{1,0:T(8,128)(2,1)S(1)} %dynamic-slice_bitcast_fusion), channel_id=1, source_target_pairs={{0,192},{64,0},{128,64},{192,128},{1,193},{65,1},{129,65},{193,129... | collective-permute-start | bytes 786440 | tf_op jit(solution)/shard_map/ppermute | solution.py:315
  8.1 1.0 collective-permute-start.1
  9.1 2.8 %collective-permute-start = (bf16[128,1024]{1,0:T(8,128)(2,1)S(1)}, bf16[128,1024]{1,0:T(8,128)(2,1)S(1)}, u32[]{:S(2)}, u32[]{:S(2)}) collective-permute-start(bf16[128,1024]{1,0:T(8,128)(2,1)S(1)} %dynamic-slice_bitcast_fusion), channel_id=1, source_target_pairs={{0,64},{64,128},{128,192},{192,0},{1,65},{65,129},{129,193},{193,1... | collective-permute-start | bytes 786440 | tf_op jit(solution)/shard_map/ppermute | solution.py:315
  13.2 0.1 stack.25.info
  13.3 17.2 %collective-permute-done.2.refs_2_ = bf16[128,1024]{1,0:T(8,128)(2,1)S(1)} collective-permute-done((bf16[128,1024]{1,0:T(8,128)(2,1)S(1)}, bf16[128,1024]{1,0:T(8,128)(2,1)S(1)}, u32[]{:S(2)}, u32[]{:S(2)}) %collective-permute-start.2) | collective-permute-done | bytes 262176 | tf_op jit(solution)/shard_map/ppermute | solution.py:315
  30.5 0.0 collective-permute-done.1.refs_1_
  30.5 0.0 collective-permute-done.refs_0_
  30.5 0.6 shard_map.102.refs_0_
  31.1 2.8 %collective-permute-start.4 = (bf16[384,1024]{1,0:T(8,128)(2,1)S(1)}, bf16[384,1024]{1,0:T(8,128)(2,1)S(1)}, u32[]{:S(2)}, u32[]{:S(2)}) collective-permute-start(bf16[384,1024]{1,0:T(8,128)(2,1)S(1)} %shard_map.102.refs_0_), channel_id=1, source_target_pairs={{0,6},{2,0},{4,2},{6,4},{1,7},{3,1},{5,3},{7,5},{8,14},{10,8},{12,... | collective-permute-start | bytes 2359304 | tf_op jit(solution)/shard_map/ppermute | solution.py:318
  34.0 2.2 %copy-done = bf16[1,4096,512]{2,1,0:T(8,128)(2,1)S(1)} copy-done((bf16[1,4096,512]{2,1,0:T(8,128)(2,1)S(1)}, bf16[1,4096,512]{2,1,0:T(8,128)(2,1)}, u32[]{:S(2)}) %copy-start) | copy-done | bytes 4194328
  36.2 2.2 %copy-done.3 = bf16[1,4096,512]{2,1,0:T(8,128)(2,1)S(1)} copy-done((bf16[1,4096,512]{2,1,0:T(8,128)(2,1)S(1)}, bf16[1,4096,512]{2,1,0:T(8,128)(2,1)}, u32[]{:S(2)}) %copy-start.3) | copy-done | bytes 4194328
  38.4 2.5 %shard_map.103 = (f32[512,1024]{1,0:T(8,128)S(1)}, bf16[512,1024]{1,0:T(8,128)(2,1)S(1)}, bf16[512,512]{1,0:T(8,128)(2,1)S(1)}) custom-call(s32[7]{0:T(128)S(1)} %stack.25.info, bf16[128,4096]{1,0:T(8,128)(2,1)S(1)} %bitcast.38, bf16[384,1024]{1,0:T(8,128)(2,1)S(1)} %shard_map.102.refs_0_, bf16[4096,512]{1,0:T(8,128)(2,1)S(1)} %bitcast.18, ...), custom_call_target="tpu_custom_call" | custom-call | flops 1073741824 | bytes 6291456 | tf_op jit(solution)/shard_map/pallas_call | solution.py:113
  40.9 6.4 %collective-permute-done.4.refs_1_.refs_0_ = bf16[384,1024]{1,0:T(8,128)(2,1)S(1)} collective-permute-done((bf16[384,1024]{1,0:T(8,128)(2,1)S(1)}, bf16[384,1024]{1,0:T(8,128)(2,1)S(1)}, u32[]{:S(2)}, u32[]{:S(2)}) %collective-permute-start.4) | collective-permute-done | bytes 786464 | tf_op jit(solution)/shard_map/ppermute | solution.py:318
  47.3 3.4 %collective-permute-done.3.refs_0_ = bf16[384,1024]{1,0:T(8,128)(2,1)S(1)} collective-permute-done((bf16[384,1024]{1,0:T(8,128)(2,1)S(1)}, bf16[384,1024]{1,0:T(8,128)(2,1)S(1)}, u32[]{:S(2)}, u32[]{:S(2)}) %collective-permute-start.3) | collective-permute-done | bytes 786464 | tf_op jit(solution)/shard_map/ppermute | solution.py:318
  50.7 0.6 shard_map.104
  51.3 0.4 collective-permute-start.6
  51.7 1.7 collective-permute-start.5
  53.4 2.6 %shard_map.105 = (f32[512,1024]{1,0:T(8,128)S(1)}, bf16[512,1024]{1,0:T(8,128)(2,1)S(1)}, bf16[512,512]{1,0:T(8,128)(2,1)S(1)}) custom-call(s32[7]{0:T(128)S(1)} %stack.25.info, bf16[128,4096]{1,0:T(8,128)(2,1)S(1)} %bitcast.39, bf16[384,1024]{1,0:T(8,128)(2,1)S(1)} %collective-permute-done.3.refs_0_, bf16[4096,512]{1,0:T(8,128)(2,1)S(1)} %bitcast.19, ...), custom_call_target="tpu_custom_call" | custom-call | flops 1073741824 | bytes 6291456 | tf_op jit(solution)/shard_map/pallas_call | solution.py:113
  56.1 2.6 %shard_map.106 = (f32[512,1024]{1,0:T(8,128)S(1)}, bf16[512,1024]{1,0:T(8,128)(2,1)S(1)}, bf16[512,512]{1,0:T(8,128)(2,1)S(1)}) custom-call(s32[7]{0:T(128)S(1)} %stack.25.info, bf16[128,4096]{1,0:T(8,128)(2,1)S(1)} %bitcast.40, bf16[384,1024]{1,0:T(8,128)(2,1)S(1)} %collective-permute-done.4.refs_1_.refs_0_, bf16[4096,512]{1,0:T(8,128)(2,1)S(1)} %bitcast.20, ...), custom_call_target="tpu_custom_call" | custom-call | flops 1073741824 | bytes 6291456 | tf_op jit(solution)/shard_map/pallas_call | solution.py:113
  58.7 0.4 collective-permute-done.6.refs_1_
  59.2 1.5 collective-permute-done.5.refs_0_
  60.7 2.6 %shard_map.107 = (bf16[512,1024]{1,0:T(8,128)(2,1)S(1)}, bf16[512,1024]{1,0:T(8,128)(2,1)S(1)}, bf16[512,512]{1,0:T(8,128)(2,1)S(1)}) custom-call(s32[7]{0:T(128)S(1)} %stack.25.info, bf16[128,4096]{1,0:T(8,128)(2,1)S(1)} %bitcast.41, bf16[192,1024]{1,0:T(8,128)(2,1)S(1)} %collective-permute-done.5.refs_0_, ...), custom_call_target="tpu_custom_call" | custom-call | flops 1073741824 | bytes 6291456 | tf_op jit(solution)/shard_map/pallas_call | solution.py:113
  63.3 4.4 %shard_map.108 = (bf16[512,512]{1,0:T(8,128)(2,1)}, bf16[512,1024]{1,0:T(8,128)(2,1)S(1)}) custom-call(s32[7]{0:T(128)S(1)} %stack.25.info, bf16[512,1024]{1,0:T(8,128)(2,1)S(1)} %get-tuple-element.40.kv_ref, bf16[512,512]{1,0:T(8,128)(2,1)S(1)} %bitcast.43, bf16[512,512]{1,0:T(8,128)(2,1)S(1)} %bitcast.44), custom_call_target="tpu_custom_call" | custom-call | flops 1610612736 | bytes 4194304 | tf_op jit(solution)/shard_map/pallas_call | solution.py:159
  67.7 1.6 shard_map.109
  69.3 0.6 collective-permute-start.7
  69.9 2.7 %collective-permute-start.8 = (bf16[256,512]{1,0:T(8,128)(2,1)S(1)}, bf16[256,512]{1,0:T(8,128)(2,1)S(1)}, u32[]{:S(2)}, u32[]{:S(2)}) collective-permute-start(bf16[256,512]{1,0:T(8,128)(2,1)S(1)} %get-tuple-element.44.refs_1_), channel_id=1, source_target_pairs={{0,6},{2,0},{4,2},{6,4},{1,7},{3,1},{5,3},{7,5},{8,14},{10,8},{12,... | collective-permute-start | bytes 786440 | tf_op jit(solution)/shard_map/ppermute | solution.py:318
  72.6 0.5 collective-permute-start.12
  73.1 6.2 %collective-permute-done.7.refs_2_ = bf16[256,512]{1,0:T(8,128)(2,1)S(1)} collective-permute-done((bf16[256,512]{1,0:T(8,128)(2,1)S(1)}, bf16[256,512]{1,0:T(8,128)(2,1)S(1)}, u32[]{:S(2)}, u32[]{:S(2)}) %collective-permute-start.7) | collective-permute-done | bytes 262176 | tf_op jit(solution)/shard_map/ppermute | solution.py:318
  79.3 0.5 collective-permute-start.13
  79.8 1.6 shard_map.110
  81.4 2.6 %shard_map.111.refs_0_.refs_1_ = f32[512,1024]{1,0:T(8,128)S(1)} custom-call(s32[7]{0:T(128)S(1)} %stack.25.info, bf16[512,1024]{1,0:T(8,128)(2,1)S(1)} %get-tuple-element.42.act_ref.refs_8_, bf16[4096,512]{1,0:T(8,128)(2,1)S(1)} %bitcast.24, bf16[4096,512]{1,0:T(8,128)(2,1)S(1)} %bitcast.34, bf16[256,512]{1,0:T(8,128)(2,1)S(1)} %get-tuple-element.45.refs_0_, ...), custom_call_target="tpu_custom_call" | custom-call | flops 1073741824 | bytes 2097152 | tf_op jit(solution)/shard_map/pallas_call | solution.py:218
  84.0 0.7 shard_map.112
  84.7 0.1 collective-permute-start.9
  84.8 3.2 %collective-permute-start.10 = (bf16[512,512]{1,0:T(8,128)(2,1)S(1)}, bf16[512,512]{1,0:T(8,128)(2,1)S(1)}, u32[]{:S(2)}, u32[]{:S(2)}) collective-permute-start(bf16[512,512]{1,0:T(8,128)(2,1)S(1)} %get-tuple-element.48.refs_11_), channel_id=1, source_target_pairs={{0,6},{2,0},{4,2},{6,4},{1,7},{3,1},{5,3},{7,5},{8,14},{10,8},{12,... | collective-permute-start | bytes 1572872 | tf_op jit(solution)/shard_map/ppermute | solution.py:318
  88.1 3.2 %collective-permute-start.17 = (bf16[256,512]{1,0:T(8,128)(2,1)S(1)}, bf16[256,512]{1,0:T(8,128)(2,1)S(1)}, u32[]{:S(2)}, u32[]{:S(2)}) collective-permute-start(bf16[256,512]{1,0:T(8,128)(2,1)S(1)} %get-tuple-element.46.refs_1_), channel_id=1, source_target_pairs={{0,6},{2,0},{4,2},{6,4},{1,7},{3,1},{5,3},{7,5},{8,14},{10,8},{12,... | collective-permute-start | bytes 786440 | tf_op jit(solution)/shard_map/ppermute | solution.py:318
  91.3 5.8 %shard_map.113 = (bf16[4,512,1024]{2,1,0:T(8,128)(2,1)S(1)}, bf16[256,1024]{1,0:T(8,128)(2,1)S(1)}, bf16[256,1024]{1,0:T(8,128)(2,1)S(1)}) custom-call(s32[7]{0:T(128)S(1)} %stack.25.info, bf16[512,1024]{1,0:T(8,128)(2,1)S(1)} %get-tuple-element.49.refs_0_, bf16[512,1024]{1,0:T(8,128)(2,1)S(1)} %get-tuple-element.50.refs_1_, ...), custom_call_target="tpu_custom_call" | custom-call | flops 4294967296 | bytes 8388608 | tf_op jit(solution)/shard_map/pallas_call | solution.py:258
  97.2 2.6 %shard_map.114.refs_0_.refs_1_ = f32[512,1024]{1,0:T(8,128)S(1)} custom-call(s32[7]{0:T(128)S(1)} %stack.25.info, bf16[512,1024]{1,0:T(8,128)(2,1)S(1)} %get-tuple-element.42.act_ref.refs_8_, bf16[4096,512]{1,0:T(8,128)(2,1)S(1)} %bitcast.25, bf16[4096,512]{1,0:T(8,128)(2,1)S(1)} %bitcast.35, bf16[256,1024]{1,0:T(8,128)(2,1)S(1)} %get-tuple-element.57.refs_0_), custom_call_target="tpu_custom_call" | custom-call | flops 1073741824 | bytes 2097152 | tf_op jit(solution)/shard_map/pallas_call | solution.py:218
  99.8 5.6 %collective-permute-done.16.refs_2_ = bf16[256,512]{1,0:T(8,128)(2,1)S(1)} collective-permute-done((bf16[256,512]{1,0:T(8,128)(2,1)S(1)}, bf16[256,512]{1,0:T(8,128)(2,1)S(1)}, u32[]{:S(2)}, u32[]{:S(2)}) %collective-permute-start.16) | collective-permute-done | bytes 262176 | tf_op jit(solution)/shard_map/ppermute | solution.py:318
  105.5 1.7 shard_map.115
  107.1 2.3 %shard_map.116.refs_4_ = bf16[4,2,128,256]{3,2,1,0:T(8,128)(2,1)} custom-call(s32[7]{0:T(128)S(1)} %stack.25.info, bf16[512,1024]{1,0:T(8,128)(2,1)S(1)} %get-tuple-element.42.act_ref.refs_8_, bf16[4096,512]{1,0:T(8,128)(2,1)S(1)} %bitcast.26, bf16[4096,512]{1,0:T(8,128)(2,1)S(1)} %bitcast.36, bf16[512,512]{1,0:T(8,128)(2,1)S(1)} %collective-permute-done.9.refs_0_, ...), custom_call_target="tpu_custom_call" | custom-call | flops 536870912 | bytes 2097152 | tf_op jit(solution)/shard_map/pallas_call | solution.py:218
  109.5 14.4 %all-to-all-start = ((bf16[8,128,256]{2,1,0:T(8,128)(2,1)}), bf16[8,128,256]{2,1,0:T(8,128)(2,1)S(1)}, u32[]{:S(2)}, u32[]{:S(2)}) async-start(bf16[8,128,256]{2,1,0:T(8,128)(2,1)} %bitcast.12), calls=%async_computation | async-start | bytes 1048576 | tf_op jit(solution)/shard_map/all_to_all | solution.py:409
  123.9 0.5 collective-permute-start.21
  124.4 1.6 collective-permute-start.20
  126.0 1.1 collective-permute-start.18
  127.2 2.1 %collective-permute-start.19 = (bf16[512,512]{1,0:T(8,128)(2,1)}, bf16[512,512]{1,0:T(8,128)(2,1)S(1)}, u32[]{:S(2)}, u32[]{:S(2)}) collective-permute-start(bf16[512,512]{1,0:T(8,128)(2,1)} %get-tuple-element.59.refs_3_), channel_id=1, source_target_pairs={{0,6},{2,0},{4,2},{6,4},{1,7},{3,1},{5,3},{7,5},{8,14},{10,8},{12,... | collective-permute-start | bytes 1572872 | tf_op jit(solution)/shard_map/ppermute | solution.py:318
  129.2 7.4 %collective-permute-done.21.refs_3_ = bf16[256,1024]{1,0:T(8,128)(2,1)S(1)} collective-permute-done((bf16[256,1024]{1,0:T(8,128)(2,1)S(1)}, bf16[256,1024]{1,0:T(8,128)(2,1)S(1)}, u32[]{:S(2)}, u32[]{:S(2)}) %collective-permute-start.21) | collective-permute-done | bytes 524320 | tf_op jit(solution)/shard_map/ppermute | solution.py:323
  136.7 1.5 collective-permute-done.20.refs_2_
  138.1 2.2 %copy-done.7 = bf16[4,512,1024]{2,1,0:T(8,128)(2,1)S(1)} copy-done((bf16[4,512,1024]{2,1,0:T(8,128)(2,1)S(1)}, bf16[4,512,1024]{2,1,0:T(8,128)(2,1)}, u32[]{:S(2)}) %copy-start.7) | copy-done | bytes 4194328
  140.3 0.8 shard_map.117
  141.2 1.3 copy-done.2
  142.5 1.3 copy-done.5
  143.8 1.7 shard_map.118
  145.5 1.0 copy-done.10
  146.5 22.0 %all_to_all.15.refs_1_ = bf16[8,128,256]{2,1,0:T(8,128)(2,1)S(1)} all-to-all(bf16[8,128,256]{2,1,0:T(8,128)(2,1)S(1)} %bitcast.42), channel_id=1, replica_groups=mesh['section'=4,'dp'=8,'x'=4,'low'=2] {'section','low'}, dimensions={0} | all-to-all | bytes 1048576 | tf_op jit(solution)/shard_map/all_to_all | solution.py:409
  168.4 1.6 shard_map.119.refs_3_
  170.1 4.9 %all-to-all-start.2 = ((bf16[8,128,512]{2,1,0:T(8,128)(2,1)}), bf16[8,128,512]{2,1,0:T(8,128)(2,1)S(1)}, u32[]{:S(2)}, u32[]{:S(2)}) async-start(bf16[8,128,512]{2,1,0:T(8,128)(2,1)} %shard_map.119.refs_3_), calls=%async_computation.2 | async-start | bytes 2097152 | tf_op jit(solution)/shard_map/all_to_all | solution.py:432
  174.9 0.4 collective-permute-start.22
  175.3 2.5 %collective-permute-start.23 = (bf16[512,1024]{1,0:T(8,128)(2,1)S(1)}, bf16[512,1024]{1,0:T(8,128)(2,1)S(1)}, u32[]{:S(2)}, u32[]{:S(2)}) collective-permute-start(bf16[512,1024]{1,0:T(8,128)(2,1)S(1)} %get-tuple-element.63.refs_3_), channel_id=1, source_target_pairs={{0,48},{8,56},{16,0},{24,8},{32,16},{40,24},{48,32},{56,40},{1,49}... | collective-permute-start | bytes 3145736 | tf_op jit(solution)/shard_map/ppermute | solution.py:323
  177.8 18.5 %collective-permute-done.22.refs_1_ = bf16[512,1024]{1,0:T(8,128)(2,1)S(1)} collective-permute-done((bf16[512,1024]{1,0:T(8,128)(2,1)S(1)}, bf16[512,1024]{1,0:T(8,128)(2,1)S(1)}, u32[]{:S(2)}, u32[]{:S(2)}) %collective-permute-start.22) | collective-permute-done | bytes 1048608 | tf_op jit(solution)/shard_map/ppermute | solution.py:323
  196.2 0.4 collective-permute-done.23.refs_2_
  196.7 2.2 %copy-done.8 = bf16[4,512,1024]{2,1,0:T(8,128)(2,1)S(1)} copy-done((bf16[4,512,1024]{2,1,0:T(8,128)(2,1)S(1)}, bf16[4,512,1024]{2,1,0:T(8,128)(2,1)}, u32[]{:S(2)}) %copy-start.8) | copy-done | bytes 4194328
  198.9 1.8 shard_map.121
  200.7 1.6 shard_map.120
  (43 shorter events, 0.1 us)
Async XLA Ops:
  0.6 33.4 %copy-start.9 = (bf16[1,128,4096]{2,1,0:T(8,128)(2,1)S(1)}, bf16[1,128,4096]{2,1,0:T(8,128)(2,1)}, u32[]{:S(2)}) copy-start(bf16[1,128,4096]{2,1,0:T(8,128)(2,1)} %param.7) | copy-start | bytes 3145732
  1.7 28.8 %collective-permute-start.2 = (bf16[128,1024]{1,0:T(8,128)(2,1)S(1)}, bf16[128,1024]{1,0:T(8,128)(2,1)S(1)}, u32[]{:S(2)}, u32[]{:S(2)}) collective-permute-start(bf16[128,1024]{1,0:T(8,128)(2,1)S(1)} %dynamic-slice_bitcast_fusion), channel_id=1, source_target_pairs={{0,192},{64,0},{128,64},{192,128},{1,193},{65,1},{129,65},{193,129... | collective-permute-start | bytes 786440 | tf_op jit(solution)/shard_map/ppermute | solution.py:315
  8.1 22.5 %collective-permute-start.1 = (bf16[128,1024]{1,0:T(8,128)(2,1)S(1)}, bf16[128,1024]{1,0:T(8,128)(2,1)S(1)}, u32[]{:S(2)}, u32[]{:S(2)}) collective-permute-start(bf16[128,1024]{1,0:T(8,128)(2,1)S(1)} %dynamic-slice_bitcast_fusion), channel_id=1, source_target_pairs={{0,128},{64,192},{128,0},{192,64},{1,129},{65,193},{129,1},{193,65... | collective-permute-start | bytes 786440 | tf_op jit(solution)/shard_map/ppermute | solution.py:315
  9.1 21.5 %collective-permute-start = (bf16[128,1024]{1,0:T(8,128)(2,1)S(1)}, bf16[128,1024]{1,0:T(8,128)(2,1)S(1)}, u32[]{:S(2)}, u32[]{:S(2)}) collective-permute-start(bf16[128,1024]{1,0:T(8,128)(2,1)S(1)} %dynamic-slice_bitcast_fusion), channel_id=1, source_target_pairs={{0,64},{64,128},{128,192},{192,0},{1,65},{65,129},{129,193},{193,1... | collective-permute-start | bytes 786440 | tf_op jit(solution)/shard_map/ppermute | solution.py:315
  31.1 16.1 %collective-permute-start.4 = (bf16[384,1024]{1,0:T(8,128)(2,1)S(1)}, bf16[384,1024]{1,0:T(8,128)(2,1)S(1)}, u32[]{:S(2)}, u32[]{:S(2)}) collective-permute-start(bf16[384,1024]{1,0:T(8,128)(2,1)S(1)} %shard_map.102.refs_0_), channel_id=1, source_target_pairs={{0,6},{2,0},{4,2},{6,4},{1,7},{3,1},{5,3},{7,5},{8,14},{10,8},{12,... | collective-permute-start | bytes 2359304 | tf_op jit(solution)/shard_map/ppermute | solution.py:318
  34.0 16.7 %collective-permute-start.3 = (bf16[384,1024]{1,0:T(8,128)(2,1)S(1)}, bf16[384,1024]{1,0:T(8,128)(2,1)S(1)}, u32[]{:S(2)}, u32[]{:S(2)}) collective-permute-start(bf16[384,1024]{1,0:T(8,128)(2,1)S(1)} %shard_map.102.refs_0_), channel_id=1, source_target_pairs={{0,2},{2,4},{4,6},{6,0},{1,3},{3,5},{5,7},{7,1},{8,10},{10,12},{12... | collective-permute-start | bytes 2359304 | tf_op jit(solution)/shard_map/ppermute | solution.py:318
  34.0 2.2 %copy-start = (bf16[1,4096,512]{2,1,0:T(8,128)(2,1)S(1)}, bf16[1,4096,512]{2,1,0:T(8,128)(2,1)}, u32[]{:S(2)}) copy-start(bf16[1,4096,512]{2,1,0:T(8,128)(2,1)} %param.8) | copy-start | bytes 12582916
  36.2 2.2 %copy-start.3 = (bf16[1,4096,512]{2,1,0:T(8,128)(2,1)S(1)}, bf16[1,4096,512]{2,1,0:T(8,128)(2,1)}, u32[]{:S(2)}) copy-start(bf16[1,4096,512]{2,1,0:T(8,128)(2,1)} %param.9) | copy-start | bytes 12582916
  38.4 15.1 %copy-start.1 = (bf16[1,4096,512]{2,1,0:T(8,128)(2,1)S(1)}, bf16[1,4096,512]{2,1,0:T(8,128)(2,1)}, u32[]{:S(2)}) copy-start(bf16[1,4096,512]{2,1,0:T(8,128)(2,1)} %param.8) | copy-start | bytes 12582916
  38.4 15.1 %copy-start.4 = (bf16[1,4096,512]{2,1,0:T(8,128)(2,1)S(1)}, bf16[1,4096,512]{2,1,0:T(8,128)(2,1)}, u32[]{:S(2)}) copy-start(bf16[1,4096,512]{2,1,0:T(8,128)(2,1)} %param.9) | copy-start | bytes 12582916
  51.3 7.9 %collective-permute-start.6 = (bf16[192,1024]{1,0:T(8,128)(2,1)S(1)}, bf16[192,1024]{1,0:T(8,128)(2,1)S(1)}, u32[]{:S(2)}, u32[]{:S(2)}) collective-permute-start(bf16[192,1024]{1,0:T(8,128)(2,1)S(1)} %get-tuple-element.37), channel_id=1, source_target_pairs={{0,6},{2,0},{4,2},{6,4},{1,7},{3,1},{5,3},{7,5},{8,14},{10,8},{12,... | collective-permute-start | bytes 1179656 | tf_op jit(solution)/shard_map/ppermute | solution.py:318
  51.7 9.0 %collective-permute-start.5 = (bf16[192,1024]{1,0:T(8,128)(2,1)S(1)}, bf16[192,1024]{1,0:T(8,128)(2,1)S(1)}, u32[]{:S(2)}, u32[]{:S(2)}) collective-permute-start(bf16[192,1024]{1,0:T(8,128)(2,1)S(1)} %get-tuple-element.36.refs_4_.refs_5_), channel_id=1, source_target_pairs={{0,2},{2,4},{4,6},{6,0},{1,3},{3,5},{5,7},{7,1},{8,10},{10,12},{12... | collective-permute-start | bytes 1179656 | tf_op jit(solution)/shard_map/ppermute | solution.py:318
  60.7 2.6 %copy-start.12 = (bf16[1,1,512,512]{3,2,1,0:T(8,128)(2,1)S(1)}, bf16[1,1,512,512]{3,2,1,0:T(8,128)(2,1)}, u32[]{:S(2)}) copy-start(bf16[1,1,512,512]{3,2,1,0:T(8,128)(2,1)} %param.10) | copy-start | bytes 1572868
  60.7 2.6 %copy-start.13 = (bf16[1,1,512,512]{3,2,1,0:T(8,128)(2,1)S(1)}, bf16[1,1,512,512]{3,2,1,0:T(8,128)(2,1)}, u32[]{:S(2)}) copy-start(bf16[1,1,512,512]{3,2,1,0:T(8,128)(2,1)} %param.11) | copy-start | bytes 1572868
  67.7 23.6 %collective-permute-start.15 = (bf16[512,1024]{1,0:T(8,128)(2,1)S(1)}, bf16[512,1024]{1,0:T(8,128)(2,1)S(1)}, u32[]{:S(2)}, u32[]{:S(2)}) collective-permute-start(bf16[512,1024]{1,0:T(8,128)(2,1)S(1)} %get-tuple-element.42.act_ref.refs_8_), channel_id=1, source_target_pairs={{0,8},{8,0},{16,24},{24,16},{32,40},{40,32},{48,56},{56,48},{1,9},... | collective-permute-start | bytes 3145736 | tf_op jit(solution)/shard_map/ppermute | solution.py:326
  69.3 10.0 %collective-permute-start.7 = (bf16[256,512]{1,0:T(8,128)(2,1)S(1)}, bf16[256,512]{1,0:T(8,128)(2,1)S(1)}, u32[]{:S(2)}, u32[]{:S(2)}) collective-permute-start(bf16[256,512]{1,0:T(8,128)(2,1)S(1)} %get-tuple-element.43.refs_0_), channel_id=1, source_target_pairs={{0,2},{2,4},{4,6},{6,0},{1,3},{3,5},{5,7},{7,1},{8,10},{10,12},{12... | collective-permute-start | bytes 786440 | tf_op jit(solution)/shard_map/ppermute | solution.py:318
  69.9 9.4 %collective-permute-start.8 = (bf16[256,512]{1,0:T(8,128)(2,1)S(1)}, bf16[256,512]{1,0:T(8,128)(2,1)S(1)}, u32[]{:S(2)}, u32[]{:S(2)}) collective-permute-start(bf16[256,512]{1,0:T(8,128)(2,1)S(1)} %get-tuple-element.44.refs_1_), channel_id=1, source_target_pairs={{0,6},{2,0},{4,2},{6,4},{1,7},{3,1},{5,3},{7,5},{8,14},{10,8},{12,... | collective-permute-start | bytes 786440 | tf_op jit(solution)/shard_map/ppermute | solution.py:318
  72.6 12.1 %collective-permute-start.11 = (bf16[512,512]{1,0:T(8,128)(2,1)S(1)}, bf16[512,512]{1,0:T(8,128)(2,1)S(1)}, u32[]{:S(2)}, u32[]{:S(2)}) collective-permute-start(bf16[512,512]{1,0:T(8,128)(2,1)S(1)} %get-tuple-element.53), channel_id=1, source_target_pairs={{0,8},{8,0},{16,24},{24,16},{32,40},{40,32},{48,56},{56,48},{1,9},... | collective-permute-start | bytes 1572872 | tf_op jit(solution)/shard_map/ppermute | solution.py:326
  72.6 12.2 %collective-permute-start.12 = (bf16[512,512]{1,0:T(8,128)(2,1)S(1)}, bf16[512,512]{1,0:T(8,128)(2,1)S(1)}, u32[]{:S(2)}, u32[]{:S(2)}) collective-permute-start(bf16[512,512]{1,0:T(8,128)(2,1)S(1)} %get-tuple-element.54), channel_id=1, source_target_pairs={{0,8},{8,0},{16,24},{24,16},{32,40},{40,32},{48,56},{56,48},{1,9},... | collective-permute-start | bytes 1572872 | tf_op jit(solution)/shard_map/ppermute | solution.py:326
  79.3 8.7 %collective-permute-start.14 = (bf16[512,512]{1,0:T(8,128)(2,1)S(1)}, bf16[512,512]{1,0:T(8,128)(2,1)S(1)}, u32[]{:S(2)}, u32[]{:S(2)}) collective-permute-start(bf16[512,512]{1,0:T(8,128)(2,1)S(1)} %get-tuple-element.56), channel_id=1, source_target_pairs={{0,8},{8,0},{16,24},{24,16},{32,40},{40,32},{48,56},{56,48},{1,9},... | collective-permute-start | bytes 1572872 | tf_op jit(solution)/shard_map/ppermute | solution.py:326
  79.3 8.7 %collective-permute-start.13 = (bf16[512,512]{1,0:T(8,128)(2,1)S(1)}, bf16[512,512]{1,0:T(8,128)(2,1)S(1)}, u32[]{:S(2)}, u32[]{:S(2)}) collective-permute-start(bf16[512,512]{1,0:T(8,128)(2,1)S(1)} %get-tuple-element.55), channel_id=1, source_target_pairs={{0,8},{8,0},{16,24},{24,16},{32,40},{40,32},{48,56},{56,48},{1,9},... | collective-permute-start | bytes 1572872 | tf_op jit(solution)/shard_map/ppermute | solution.py:326
  84.7 22.4 %collective-permute-start.9 = (bf16[512,512]{1,0:T(8,128)(2,1)S(1)}, bf16[512,512]{1,0:T(8,128)(2,1)S(1)}, u32[]{:S(2)}, u32[]{:S(2)}) collective-permute-start(bf16[512,512]{1,0:T(8,128)(2,1)S(1)} %get-tuple-element.47.refs_10_), channel_id=1, source_target_pairs={{0,2},{2,4},{4,6},{6,0},{1,3},{3,5},{5,7},{7,1},{8,10},{10,12},{12... | collective-permute-start | bytes 1572872 | tf_op jit(solution)/shard_map/ppermute | solution.py:318
  84.8 22.3 %collective-permute-start.10 = (bf16[512,512]{1,0:T(8,128)(2,1)S(1)}, bf16[512,512]{1,0:T(8,128)(2,1)S(1)}, u32[]{:S(2)}, u32[]{:S(2)}) collective-permute-start(bf16[512,512]{1,0:T(8,128)(2,1)S(1)} %get-tuple-element.48.refs_11_), channel_id=1, source_target_pairs={{0,6},{2,0},{4,2},{6,4},{1,7},{3,1},{5,3},{7,5},{8,14},{10,8},{12,... | collective-permute-start | bytes 1572872 | tf_op jit(solution)/shard_map/ppermute | solution.py:318
  88.1 17.4 %collective-permute-start.16 = (bf16[256,512]{1,0:T(8,128)(2,1)S(1)}, bf16[256,512]{1,0:T(8,128)(2,1)S(1)}, u32[]{:S(2)}, u32[]{:S(2)}) collective-permute-start(bf16[256,512]{1,0:T(8,128)(2,1)S(1)} %get-tuple-element.45.refs_0_), channel_id=1, source_target_pairs={{0,2},{2,4},{4,6},{6,0},{1,3},{3,5},{5,7},{7,1},{8,10},{10,12},{12... | collective-permute-start | bytes 786440 | tf_op jit(solution)/shard_map/ppermute | solution.py:318
  88.1 17.4 %collective-permute-start.17 = (bf16[256,512]{1,0:T(8,128)(2,1)S(1)}, bf16[256,512]{1,0:T(8,128)(2,1)S(1)}, u32[]{:S(2)}, u32[]{:S(2)}) collective-permute-start(bf16[256,512]{1,0:T(8,128)(2,1)S(1)} %get-tuple-element.46.refs_1_), channel_id=1, source_target_pairs={{0,6},{2,0},{4,2},{6,4},{1,7},{3,1},{5,3},{7,5},{8,14},{10,8},{12,... | collective-permute-start | bytes 786440 | tf_op jit(solution)/shard_map/ppermute | solution.py:318
  97.2 2.7 %copy-start.6 = (bf16[4,512,1024]{2,1,0:T(8,128)(2,1)}, bf16[4,512,1024]{2,1,0:T(8,128)(2,1)S(1)}, u32[]{:S(2)}) copy-start(bf16[4,512,1024]{2,1,0:T(8,128)(2,1)S(1)} %get-tuple-element.60.refs_0_.refs_1_) | copy-start | bytes 12582916
  97.2 2.7 %copy-start.14 = (bf16[256,1024]{1,0:T(8,128)(2,1)}, bf16[256,1024]{1,0:T(8,128)(2,1)S(1)}, u32[]{:S(2)}) copy-start(bf16[256,1024]{1,0:T(8,128)(2,1)S(1)} %get-tuple-element.61) | copy-start | bytes 1572868
  107.1 16.8 %copy-start.15 = (bf16[256,1024]{1,0:T(8,128)(2,1)S(1)}, bf16[256,1024]{1,0:T(8,128)(2,1)}, u32[]{:S(2)}) copy-start(bf16[256,1024]{1,0:T(8,128)(2,1)} %copy-done.14) | copy-start | bytes 1572868
  109.5 37.0 %all-to-all-start = ((bf16[8,128,256]{2,1,0:T(8,128)(2,1)}), bf16[8,128,256]{2,1,0:T(8,128)(2,1)S(1)}, u32[]{:S(2)}, u32[]{:S(2)}) async-start(bf16[8,128,256]{2,1,0:T(8,128)(2,1)} %bitcast.12), calls=%async_computation | async-start | bytes 1048576 | tf_op jit(solution)/shard_map/all_to_all | solution.py:409
  123.9 12.8 %collective-permute-start.21 = (bf16[256,1024]{1,0:T(8,128)(2,1)S(1)}, bf16[256,1024]{1,0:T(8,128)(2,1)S(1)}, u32[]{:S(2)}, u32[]{:S(2)}) collective-permute-start(bf16[256,1024]{1,0:T(8,128)(2,1)S(1)} %copy-done.15), channel_id=1, source_target_pairs={{0,48},{8,56},{16,0},{24,8},{32,16},{40,24},{48,32},{56,40},{1,49}... | collective-permute-start | bytes 1572872 | tf_op jit(solution)/shard_map/ppermute | solution.py:323
  124.4 13.7 %collective-permute-start.20 = (bf16[256,1024]{1,0:T(8,128)(2,1)S(1)}, bf16[256,1024]{1,0:T(8,128)(2,1)S(1)}, u32[]{:S(2)}, u32[]{:S(2)}) collective-permute-start(bf16[256,1024]{1,0:T(8,128)(2,1)S(1)} %get-tuple-element.57.refs_0_), channel_id=1, source_target_pairs={{0,16},{8,24},{16,32},{24,40},{32,48},{40,56},{48,0},{56,8},{1,17}... | collective-permute-start | bytes 1572872 | tf_op jit(solution)/shard_map/ppermute | solution.py:323
  126.0 15.1 %collective-permute-start.18 = (bf16[512,512]{1,0:T(8,128)(2,1)}, bf16[512,512]{1,0:T(8,128)(2,1)S(1)}, u32[]{:S(2)}, u32[]{:S(2)}) collective-permute-start(bf16[512,512]{1,0:T(8,128)(2,1)} %get-tuple-element.58.refs_2_), channel_id=1, source_target_pairs={{0,2},{2,4},{4,6},{6,0},{1,3},{3,5},{5,7},{7,1},{8,10},{10,12},{12... | collective-permute-start | bytes 1572872 | tf_op jit(solution)/shard_map/ppermute | solution.py:318
  127.2 14.0 %collective-permute-start.19 = (bf16[512,512]{1,0:T(8,128)(2,1)}, bf16[512,512]{1,0:T(8,128)(2,1)S(1)}, u32[]{:S(2)}, u32[]{:S(2)}) collective-permute-start(bf16[512,512]{1,0:T(8,128)(2,1)} %get-tuple-element.59.refs_3_), channel_id=1, source_target_pairs={{0,6},{2,0},{4,2},{6,4},{1,7},{3,1},{5,3},{7,5},{8,14},{10,8},{12,... | collective-permute-start | bytes 1572872 | tf_op jit(solution)/shard_map/ppermute | solution.py:318
  138.1 2.2 %copy-start.7 = (bf16[4,512,1024]{2,1,0:T(8,128)(2,1)S(1)}, bf16[4,512,1024]{2,1,0:T(8,128)(2,1)}, u32[]{:S(2)}) copy-start(bf16[4,512,1024]{2,1,0:T(8,128)(2,1)} %copy-done.6) | copy-start | bytes 12582916
  140.3 2.2 %copy-start.2 = (bf16[1,4096,512]{2,1,0:T(8,128)(2,1)S(1)}, bf16[1,4096,512]{2,1,0:T(8,128)(2,1)}, u32[]{:S(2)}) copy-start(bf16[1,4096,512]{2,1,0:T(8,128)(2,1)} %param.8) | copy-start | bytes 12582916
  140.3 3.5 %copy-start.5 = (bf16[1,4096,512]{2,1,0:T(8,128)(2,1)S(1)}, bf16[1,4096,512]{2,1,0:T(8,128)(2,1)}, u32[]{:S(2)}) copy-start(bf16[1,4096,512]{2,1,0:T(8,128)(2,1)} %param.9) | copy-start | bytes 12582916
  145.5 1.0 copy-start.10
  170.1 4.9 %copy-start.11 = (bf16[512,1024]{1,0:T(8,128)(2,1)S(1)}, bf16[512,1024]{1,0:T(8,128)(2,1)}, u32[]{:S(2)}) copy-start(bf16[512,1024]{1,0:T(8,128)(2,1)} %copy-done.10) | copy-start | bytes 3145732
  170.1 30.6 %all-to-all-start.2 = ((bf16[8,128,512]{2,1,0:T(8,128)(2,1)}), bf16[8,128,512]{2,1,0:T(8,128)(2,1)S(1)}, u32[]{:S(2)}, u32[]{:S(2)}) async-start(bf16[8,128,512]{2,1,0:T(8,128)(2,1)} %shard_map.119.refs_3_), calls=%async_computation.2 | async-start | bytes 2097152 | tf_op jit(solution)/shard_map/all_to_all | solution.py:432
  174.9 21.3 %collective-permute-start.22 = (bf16[512,1024]{1,0:T(8,128)(2,1)S(1)}, bf16[512,1024]{1,0:T(8,128)(2,1)S(1)}, u32[]{:S(2)}, u32[]{:S(2)}) collective-permute-start(bf16[512,1024]{1,0:T(8,128)(2,1)S(1)} %copy-done.11), channel_id=1, source_target_pairs={{0,16},{8,24},{16,32},{24,40},{32,48},{40,56},{48,0},{56,8},{1,17}... | collective-permute-start | bytes 3145736 | tf_op jit(solution)/shard_map/ppermute | solution.py:323
  175.3 21.3 %collective-permute-start.23 = (bf16[512,1024]{1,0:T(8,128)(2,1)S(1)}, bf16[512,1024]{1,0:T(8,128)(2,1)S(1)}, u32[]{:S(2)}, u32[]{:S(2)}) collective-permute-start(bf16[512,1024]{1,0:T(8,128)(2,1)S(1)} %get-tuple-element.63.refs_3_), channel_id=1, source_target_pairs={{0,48},{8,56},{16,0},{24,8},{32,16},{40,24},{48,32},{56,40},{1,49}... | collective-permute-start | bytes 3145736 | tf_op jit(solution)/shard_map/ppermute | solution.py:323
  196.7 2.2 %copy-start.8 = (bf16[4,512,1024]{2,1,0:T(8,128)(2,1)S(1)}, bf16[4,512,1024]{2,1,0:T(8,128)(2,1)}, u32[]{:S(2)}) copy-start(bf16[4,512,1024]{2,1,0:T(8,128)(2,1)} %copy-done.6) | copy-start | bytes 12582916

commit v3 on v1

v3 whole, which is shorter than its diff:
```python
import jax
import jax.numpy as jnp
from jax import lax
from jax.experimental import pallas as pl
from jax.experimental.pallas import tpu as pltpu
from jax.sharding import Mesh
from jax.sharding import PartitionSpec as P

HEAD = 256
XS = 4
UNIT = 256
masked_score = -1e30
f32 = jnp.float32
bf16 = jnp.bfloat16
X, SEC, LO, Y, CORE, SRC_LIVE, TGT_LIVE = range(7)


def dot(a, b):
    return jnp.dot(a, b, preferred_element_type=f32)


def dot_t(a, b):
    return lax.dot_general(a, b, (((1,), (1,)), ((), ())), preferred_element_type=f32)


def t_dot(a, b):
    return lax.dot_general(a, b, (((0,), (0,)), ((), ())), preferred_element_type=f32)


def mod4(v):
    return lax.rem(v + 8, 4)


def params(mib):
    return pltpu.CompilerParams(vmem_limit_bytes=mib * 1024 * 1024)


def whole(a):
    return pl.BlockSpec(a.shape, lambda i, info: (0,) * a.ndim)


ANYWHERE = pl.BlockSpec(memory_space=pl.ANY)
LIGHT = pl.CostEstimate(flops=1, bytes_accessed=1, transcendentals=0)


def project(m, enc, parts, wk, wv, acc, info, last, n_sec, after=()):
    blk, width = enc.shape
    quarter = width // XS
    total = n_sec * blk
    cols = wk.shape[1]
    heads = cols // HEAD

    def body(info, enc_ref, *refs):
        n = len(parts)
        part_refs, wk_ref, wv_ref = refs[:n], refs[n], refs[n + 1]
        acc_ref = refs[n + 2] if acc is not None else None
        out_ref, rows_ref = refs[-2:]

        @pl.when(pl.program_id(0) == 0)
        def _():
            rows_ref[pl.ds(pl.multiple_of(info[SEC] * blk, blk), blk), :] = enc_ref[...]
            for ref, (_, pieces) in zip(part_refs, parts):
                for at, count, block, off in pieces:
                    to = block_of(info, block, n_sec) * blk + off
                    rows_ref[pl.ds(pl.multiple_of(to, count), count), :] = ref[at : at + count, :]

        rows = rows_ref[...]
        k_part = dot(rows, wk_ref[...])
        v_part = dot(rows, wv_ref[...])
        if acc_ref is not None:
            k_part = k_part + acc_ref[:, :HEAD]
            v_part = v_part + acc_ref[:, HEAD:]
        out_ref[:, :HEAD] = k_part.astype(out_ref.dtype)
        out_ref[:, HEAD:] = v_part.astype(out_ref.dtype)

    def at_quarter(info):
        return mod4(info[X] - m)

    weight = pl.BlockSpec((quarter, HEAD), lambda h, info: (at_quarter(info), h))
    pair = pl.BlockSpec((total, 2 * HEAD), lambda h, info: (0, h))
    out_shape = [
        jax.ShapeDtypeStruct((total, 2 * cols), bf16 if last else f32),
        jax.ShapeDtypeStruct((total, quarter), bf16),
    ]
    return pl.pallas_call(
        body,
        grid_spec=pltpu.PrefetchScalarGridSpec(
            num_scalar_prefetch=1,
            grid=(heads,),
            in_specs=[pl.BlockSpec((blk, quarter), lambda h, info: (0, at_quarter(info)))]
            + [whole(p) for p, _ in parts]
            + [weight, weight]
            + ([pair] if acc is not None else [])
            + [ANYWHERE] * len(after),
            out_specs=[pair, whole(out_shape[1])],
        ),
        out_shape=out_shape,
        compiler_params=params(24),
        cost_estimate=LIGHT,
    )(info, enc, *[p for p, _ in parts], wk, wv, *([acc] if acc is not None else []), *after)


def attention(kv, q, g, info, after):
    total, targets, width = kv.shape[0], q.shape[0], q.shape[1]
    heads = width // HEAD
    scale = HEAD ** (-0.5)

    def body(info, kv_ref, q_ref, g_ref, *refs):
        ctx_ref, act_ref = refs[-2:]
        k, v, q = kv_ref[:, :HEAD], kv_ref[:, HEAD:], q_ref[...]
        place = lax.broadcasted_iota(jnp.int32, (total, 1), 0)
        scores = dot_t(k, q) * scale
        scores = jnp.where(place < info[SRC_LIVE], scores, masked_score)
        highest = jnp.max(scores, axis=0, keepdims=True)
        shifted = jnp.exp(scores - highest)
        weights = shifted * (1.0 / jnp.sum(shifted, axis=0, keepdims=True))
        low = weights.astype(bf16)
        target = lax.broadcasted_iota(jnp.int32, (targets, 1), 0)
        g = jnp.where(target < info[TGT_LIVE], g_ref[...].astype(f32), 0.0).astype(bf16)
        prob = dot_t(v, g)
        prob_dot = jnp.sum(weights * prob, axis=0, keepdims=True)
        grad = (weights * (prob - prob_dot) * scale).astype(bf16)
        act_ref[:, :HEAD] = dot(grad, q).astype(bf16)
        act_ref[:, HEAD:] = dot(low, g).astype(bf16)
        ctx_ref[...] = t_dot(low, v).astype(bf16)

    def cols(n, w):
        return pl.BlockSpec((n, w), lambda h, info: (0, h))

    return pl.pallas_call(
        body,
        grid_spec=pltpu.PrefetchScalarGridSpec(
            num_scalar_prefetch=1,
            grid=(heads,),
            in_specs=[cols(total, 2 * HEAD), cols(targets, HEAD), cols(targets, HEAD)] + [ANYWHERE] * len(after),
            out_specs=[cols(targets, HEAD), cols(total, 2 * HEAD)],
        ),
        out_shape=[
            jax.ShapeDtypeStruct((targets, width), bf16),
            jax.ShapeDtypeStruct((total, 2 * width), bf16),
        ],
        compiler_params=params(20),
        cost_estimate=LIGHT,
    )(info, kv, q, g, *after)


def block_of(info, which, n_sec):
    back = (0, 1 + 2 * info[LO], 3 - 2 * info[LO], 2)[which]
    return lax.rem(info[SEC] - back + n_sec, n_sec)


def partial_grad(act, wk, wv, info, quarters, dtype, after=(), first=None):
    total, cols = act.shape[0], wk.shape[1]
    width = wk.shape[0]
    heads = cols // HEAD
    per = width // XS // UNIT
    n = per * len(quarters)

    def unit(i, info):
        quarter = i // per
        m = quarters[0]
        for j, other in enumerate(quarters[1:]):
            m = jnp.where(quarter == j + 1, other, m)
        return mod4(info[X] - m) * per + i % per

    def body(info, act_ref, wk_ref, wv_ref, *refs):
        sums = None
        for h in range(heads):
            for j, w_ref in enumerate((wk_ref, wv_ref)):
                at = (2 * h + j) * HEAD
                term = dot_t(act_ref[:, at : at + HEAD], w_ref[:, h * HEAD : (h + 1) * HEAD])
                sums = term if sums is None else sums + term
        if first is None:
            refs[-1][...] = sums.astype(dtype)
        else:
            out_ref, up_ref, down_ref = refs[-3:]
            out_ref[...] = sums.astype(dtype)
            n_sec, blk = first
            at = block_of(info, 3, n_sec) * blk
            up_ref[...] = out_ref[pl.ds(pl.multiple_of(at, blk), blk // 2), :]
            down_ref[...] = out_ref[pl.ds(pl.multiple_of(at + blk // 2, blk // 2), blk // 2), :]

    weight = pl.BlockSpec((UNIT, cols), lambda i, info: (unit(i, info), 0))
    block = pl.BlockSpec((total, UNIT), lambda i, info: (0, i))
    out_specs, out_shape = [block], [jax.ShapeDtypeStruct((total, n * UNIT), dtype)]
    if first is not None:
        rows = first[1] // 2
        out_specs += [pl.BlockSpec((rows, UNIT), lambda i, info: (0, i))] * 2
        out_shape += [jax.ShapeDtypeStruct((rows, n * UNIT), dtype)] * 2
    return pl.pallas_call(
        body,
        grid_spec=pltpu.PrefetchScalarGridSpec(
            num_scalar_prefetch=1,
            grid=(n,),
            in_specs=[whole(act), weight, weight] + [ANYWHERE] * len(after),
            out_specs=out_specs,
        ),
        out_shape=out_shape,
        compiler_params=params(12),
        cost_estimate=LIGHT,
    )(info, act, wk, wv, *after)


def pair_grads(kept, got, act, act_other, info, after):
    width = act.shape[1]
    counts = (2, 1, 1)
    half = kept.shape[1] // sum(counts)

    def body(info, kept_ref, got_ref, act_ref, other_ref, *refs):
        at = 0
        for ref, count in zip(refs[-3:], counts):
            for j in range(count):
                here = slice(at, at + half)
                term = t_dot(kept_ref[:, here], act_ref[...]) + t_dot(got_ref[:, here], other_ref[...])
                ref[j * half : (j + 1) * half, :] = term.astype(bf16)
                at += half

    out = [jax.ShapeDtypeStruct((count * half, width), bf16) for count in counts]
    return small(body, [kept, got, act, act_other], out, info, after)


def small(body, ins, outs, info, after=()):
    ins = [i if isinstance(i, tuple) else (i, whole(i)) for i in ins]
    n = len(ins)

    def run(info, *refs):
        body(info, *refs[:n], *refs[n + len(after) :])

    return pl.pallas_call(
        run,
        grid_spec=pltpu.PrefetchScalarGridSpec(
            num_scalar_prefetch=1,
            grid=(1,),
            in_specs=[s for _, s in ins] + [ANYWHERE] * len(after),
            out_specs=[whole(o) for o in outs],
        ),
        out_shape=[jax.ShapeDtypeStruct(o.shape, o.dtype) for o in outs],
        compiler_params=params(28),
        cost_estimate=LIGHT,
    )(info, *[a for a, _ in ins], *after)


def make_shards(n_sec):

    def shift_x(v, k):
        return lax.ppermute(v, "x", [(i, (i + k) % XS) for i in range(XS)])

    def swap_core(v):
        return lax.ppermute(v, "core", [(0, 1), (1, 0)])

    def swap_low(v):
        return lax.ppermute(v, "low", [(0, 1), (1, 0)])

    def cross(v):
        n = 2 * n_sec
        return lax.ppermute(v, ("section", "low"), [(z, (z + (1 if z % 2 else -1)) % n) for z in range(n)])

    def shift_y(v):
        n = 2 * XS
        return lax.ppermute(v, ("y", "core"), [(i, (i + (-2 if i % 2 else 2)) % n) for i in range(n)])

    def shards(enc_out, key_weight, value_weight, queries, ctx_grad, src_pad, tgt_pad):
        enc, wk, wv = enc_out[0], key_weight[0], value_weight[0]
        blk, width = enc.shape
        quarter = width // XS
        local_width = wk.shape[1]
        total_src = n_sec * blk
        x, lo, sec = lax.axis_index("x"), lax.axis_index("low"), lax.axis_index("section")
        info = jnp.stack(
            [
                x,
                sec,
                lo,
                lax.axis_index("y"),
                lax.axis_index("core"),
                total_src - src_pad[0],
                queries.shape[2] - tgt_pad[0],
            ]
        ).astype(jnp.int32)

        mine = lax.dynamic_slice(enc, (0, x * quarter), (blk, quarter))
        mid = blk // 2

        def both(up, down):
            return shift_x(up, 1), shift_x(down, -1)

        def with_half(block, up, down, after=()):
            out = jax.ShapeDtypeStruct((blk + mid, quarter), bf16)

            def body(info, block_ref, up_ref, down_ref, up_out, down_out):
                up_out[:blk] = block_ref[...]
                up_out[blk:] = up_ref[:mid]
                down_out[:blk] = block_ref[...]
                down_out[blk:] = down_ref[mid:blk]

            return small(body, [block, up, down], [out, out], info, after)

        b1 = cross(mine)
        b2 = swap_low(b1)
        u1, d1 = both(b1, b1)
        b3 = cross(b2)
        u2, d2 = both(*with_half(b2, u1, d1))
        out3 = with_half(b3, u2, d2)
        u3, d3 = both(*out3)
        rows = [None] * XS
        acc, rows[0] = project(
            0, enc, [(b, [(0, blk, i + 1, 0)]) for i, b in enumerate((b1, b2, b3))], wk, wv, None, info, False, n_sec, out3
        )

        def cut(info, up_ref, down_ref, up_out, down_out):
            up_out[...] = up_ref[:mid]
            down_out[...] = down_ref[mid:blk]

        out4 = small(cut, [u3, d3], [jax.ShapeDtypeStruct((mid, quarter), bf16)] * 2, info, (acc,))
        u4, d4 = both(*out4)
        for m, got in ((1, (u1, u2, u3)), (3, (d1, d2, d3))):
            acc, rows[m] = project(
                m, enc, [(g, [(0, blk, i + 1, 0)]) for i, g in enumerate(got)], wk, wv, acc, info, False, n_sec, out4
            )
        last = [(u2, [(blk, mid, 1, 0)]), (d2, [(blk, mid, 1, mid)]), (u3, [(blk, mid, 2, 0)]), (d3, [(blk, mid, 2, mid)])]
        last += [(u4, [(0, mid, 3, 0)]), (d4, [(0, mid, 3, mid)])]
        acc, rows[2] = project(2, enc, last, wk, wv, acc, info, True, n_sec)

        half = quarter // 2

        def pack(info, *refs):
            core = info[CORE]
            row_refs, (kept_ref, sent_ref) = refs[:XS], refs[XS:]
            for m, ref in enumerate(row_refs):
                step = mod4(info[X] - info[Y] - m)
                for out_ref, side in ((kept_ref, core), (sent_ref, 1 - core)):

                    @pl.when(step == 1 + 2 * side)
                    def _():
                        out_ref[:, :quarter] = ref[...]

                    for place, at in ((2, quarter), (0, quarter + half)):

                        @pl.when(step == place)
                        def _():
                            out_ref[:, at : at + half] = ref[:, pl.ds(pl.multiple_of(side * half, half), half)]

        packed = jax.ShapeDtypeStruct((total_src, 2 * quarter), bf16)
        kept, sent = small(pack, rows, [packed, packed], info)
        got = swap_core(sent)

        context, act = attention(acc, queries[0, 0], ctx_grad[0, 0], info, (sent,))
        context = context[None, None]
        act_other = swap_core(act)

        far, up, down = partial_grad(act, wk, wv, info, (2,), bf16, first=(n_sec, blk))
        up, down = both(up, down)
        (near,) = partial_grad(act, wk, wv, info, (3, 1), f32, (far,))
        (keep,) = partial_grad(act, wk, wv, info, (0,), f32, (near,))
        def stage(done, sent, following, up, down, carried, after=(), through=None):
            ins, outs = [up, down], []
            if done is not None:
                ins.append((keep, pl.BlockSpec((blk, quarter), lambda i, info: (block_of(info, done, n_sec), 0))))
                outs.append(jax.ShapeDtypeStruct((blk, quarter), bf16))
            if carried is not None:
                ins.append(carried)
            if sent is not None:
                ins.append((near, pl.BlockSpec((blk, 2 * quarter), lambda i, info: (block_of(info, sent, n_sec), 0))))
                size = blk if following is None else blk + mid
                outs += [jax.ShapeDtypeStruct((size, quarter), bf16)] * 2
            if following is not None:
                ins.append((far, pl.BlockSpec((blk, quarter), lambda i, info: (block_of(info, following, n_sec), 0))))

            if through is not None:
                ins.append(through)
                outs.append(through)

            def body(info, *refs):
                refs = list(refs)
                if through is not None:
                    refs.pop()[...] = refs.pop(len(ins) - 1)[...]
                up_ref, down_ref = refs.pop(0), refs.pop(0)
                if done is not None:
                    sums = refs.pop(0)[...] + up_ref[:blk].astype(f32) + down_ref[:blk].astype(f32)
                    if carried is not None:
                        sums = sums + refs.pop(0)[...].astype(f32)
                near_ref = refs.pop(0) if sent is not None else None
                far_ref = refs.pop(0) if following is not None else None
                if done is not None:
                    refs.pop(0)[...] = sums.astype(bf16)
                if sent is not None:
                    up_out, down_out = refs
                    at = blk if done is not None else 0
                    half_up, half_down = up_ref[at : at + mid].astype(f32), down_ref[at : at + mid].astype(f32)
                    up_out[:mid] = (near_ref[:mid, :quarter] + half_up).astype(bf16)
                    up_out[mid:blk] = near_ref[mid:, :quarter].astype(bf16)
                    down_out[:mid] = near_ref[:mid, quarter:].astype(bf16)
                    down_out[mid:blk] = (near_ref[mid:, quarter:] + half_down).astype(bf16)
                    if following is not None:
                        up_out[blk:] = far_ref[:mid]
                        down_out[blk:] = far_ref[mid:]

            return small(body, ins, outs, info, after)

        out = stage(None, 3, 2, up, down, None)
        up, down = both(*out)
        near_y, far_y, keep_y = pair_grads(kept, got, act, act_other, info, out)
        total, up, down, far_y = stage(3, 2, 1, up, down, None, through=far_y)
        got_y = shift_y(far_y)
        (up, down), carried = both(up, down), cross(total)
        total, up, down = stage(2, 1, 0, up, down, carried)
        (up, down), carried = both(up, down), swap_low(total)
        def add_y(info, near_ref, got_ref, out_ref):
            out_ref[...] = near_ref[...]
            at = pl.ds(pl.multiple_of(info[CORE] * half, half), half)
            out_ref[at, :] = (near_ref[at, :].astype(f32) + got_ref[...].astype(f32)).astype(bf16)

        (out_y,) = small(add_y, [near_y, got_y], [near_y], info, (total,))
        in_y = shift_y(out_y)
        total, up, down = stage(1, 0, None, up, down, carried, (out_y,))
        (up, down), carried = both(up, down), cross(total)
        (mine,) = stage(0, None, None, up, down, carried)
        other = swap_low(mine)
        part = mine

        def add_two(info, one_ref, two_ref, out_ref):
            out_ref[...] = (one_ref[...].astype(f32) + two_ref[...].astype(f32)).astype(bf16)

        (final,) = small(add_two, [mine, other], [part], info)
        gathered = [final] + [shift_x(final, k) for k in range(1, XS)]

        def halve(info, in_ref, out_ref):
            out_ref[...] = in_ref[pl.ds(pl.multiple_of((1 - info[CORE]) * half, half), half), :]

        (away_y,) = small(halve, [in_y], [keep_y], info, (final,))
        home_y = swap_core(away_y)

        def place(info, *refs):
            for k in range(XS):
                at = mod4(info[X] - k) * quarter
                refs[-1][:, pl.ds(pl.multiple_of(at, quarter), quarter)] = refs[k][...]

        (enc_grad,) = small(place, gathered, [jax.ShapeDtypeStruct((blk, width), bf16)], info, (away_y,))
        enc_grad = enc_grad[None]

        def finish(info, keep_ref, in_ref, home_ref, key_ref, value_ref):
            at = pl.ds(pl.multiple_of(info[CORE] * half, half), half)
            sums = keep_ref[...].astype(f32) + in_ref[at, :].astype(f32) + home_ref[...].astype(f32)
            sums = sums.astype(bf16)
            for h in range(local_width // HEAD):
                at = 2 * h * HEAD
                key_ref[:, h * HEAD : (h + 1) * HEAD] = sums[:, at : at + HEAD]
                value_ref[:, h * HEAD : (h + 1) * HEAD] = sums[:, at + HEAD : at + 2 * HEAD]

        shard = jax.ShapeDtypeStruct((half, local_width), bf16)
        key_weight_grad, value_weight_grad = small(finish, [keep_y, in_y, home_y], [shard, shard], info)
        key_weight_grad, value_weight_grad = key_weight_grad[None], value_weight_grad[None]
        return (context, enc_grad, key_weight_grad, value_weight_grad)

    return shards


def solution(mesh):
    n_sec, n_dp, n_ten = (mesh.shape[name] for name in ("section", "dp", "tensor"))
    fine = Mesh(
        mesh.devices.reshape(n_sec, n_dp // 2, 2, XS, n_ten // XS), ("section", "y", "core", "x", "low")
    )
    dp, heads = ("y", "core"), ("x", "low")
    return jax.shard_map(
        make_shards(n_sec),
        mesh=fine,
        in_specs=(
            P(dp, "section", None),
            P("section", None, heads),
            P("section", None, heads),
            P("section", dp, None, heads),
            P("section", dp, None, heads),
            P(dp),
            P(dp),
        ),
        out_specs=(
            P("section", dp, None, heads),
            P(dp, "section", None),
            P("section", dp, heads),
            P("section", dp, heads),
        ),
        check_vma=False,
    )
```

time: 194 us -> 160 us (0.82)
  the two profiles are of different devices: /device:TPU:8 before, /device:TPU:1 now
where the time goes in v3:
time: 160 us
  waiting for transfers between devices  55.6 us (35%)
  starting transfers between devices  54.9 us (34%)
  Pallas kernels  41.7 us (26%)
  local copies, waits for them, and re-layouts  5.54 us (3%)
  between operations  2.27 us (1%)
    ppermute x21, starting transfers between devices, shift_x(): return lax.ppermute(v, 'x', [(i, (i + k) % XS) for i in range(XS)])  26.2 us
    ppermute x21, waiting for transfers between devices, shift_x(): return lax.ppermute(v, 'x', [(i, (i + k) % XS) for i in range(XS)])  25.7 us
    ppermute x4, waiting for transfers between devices, cross(): lax.ppermute(v, ('section', 'low'), [(z, (z + (1 if z % 2 else -1)) % n)...  18.1 us
    pallas_call x15, Pallas kernels, small(): pl.pallas_call(run, grid_spec=pltpu.PrefetchScalarGridSpec(num_scalar_pre...  17 us
    ppermute x4, starting transfers between devices, cross(): lax.ppermute(v, ('section', 'low'), [(z, (z + (1 if z % 2 else -1)) % n)...  13.3 us
    ppermute x3, waiting for transfers between devices, swap_low(): return lax.ppermute(v, 'low', [(0, 1), (1, 0)])  11.7 us
    pallas_call x4, Pallas kernels, project(): pl.pallas_call(body, grid_spec=pltpu.PrefetchScalarGridSpec(num_scalar_pr...  10.2 us
    pallas_call x3, Pallas kernels, partial_grad(): pl.pallas_call(body, grid_spec=pltpu.PrefetchScalarGridSpec(num_scalar_pr...  9.99 us
  transfers between devices with their start and end apart: 33, of which 15 were waited for; matrix products, arithmetic and copies ran while one was open for 0% of the time, Pallas kernels for 20%

profile of v3, /device:TPU:1, one launch (start us, length us, event | category | flops | bytes accessed | tf_op | source)
XLA Modules:
  0.0 159.9 jit_solution(144563328904006113)
XLA Ops:
  0.6 1.1 dynamic-slice_bitcast_fusion
  1.7 6.5 %collective-permute-start = (bf16[128,1024]{1,0:T(8,128)(2,1)S(1)}, bf16[128,1024]{1,0:T(8,128)(2,1)S(1)}, u32[]{:S(2)}, u32[]{:S(2)}) collective-permute-start(bf16[128,1024]{1,0:T(8,128)(2,1)S(1)} %dynamic-slice_bitcast_fusion), channel_id=1, source_target_pairs={{0,193},{1,64},{64,1},{65,128},{128,65},{129,192},{192,129},{193,0... | collective-permute-start | bytes 786440 | tf_op jit(solution)/shard_map/ppermute | solution.py:256
  8.2 6.0 %collective-permute-done.refs_0_ = bf16[128,1024]{1,0:T(8,128)(2,1)S(1)} collective-permute-done((bf16[128,1024]{1,0:T(8,128)(2,1)S(1)}, bf16[128,1024]{1,0:T(8,128)(2,1)S(1)}, u32[]{:S(2)}, u32[]{:S(2)}) %collective-permute-start) | collective-permute-done | bytes 262176 | tf_op jit(solution)/shard_map/ppermute | solution.py:256
  14.2 2.5 %collective-permute-start.3 = (bf16[128,1024]{1,0:T(8,128)(2,1)S(1)}, bf16[128,1024]{1,0:T(8,128)(2,1)S(1)}, u32[]{:S(2)}, u32[]{:S(2)}) collective-permute-start(bf16[128,1024]{1,0:T(8,128)(2,1)S(1)} %collective-permute-done.refs_0_), channel_id=1, source_target_pairs={{0,6},{2,0},{4,2},{6,4},{1,7},{3,1},{5,3},{7,5},{8,14},{10,8},{12,... | collective-permute-start | bytes 786440 | tf_op jit(solution)/shard_map/ppermute | solution.py:246
  18.0 0.1 stack.25.info
  18.1 3.0 %collective-permute-done.3.refs_2_.refs_0_ = bf16[128,1024]{1,0:T(8,128)(2,1)S(1)} collective-permute-done((bf16[128,1024]{1,0:T(8,128)(2,1)S(1)}, bf16[128,1024]{1,0:T(8,128)(2,1)S(1)}, u32[]{:S(2)}, u32[]{:S(2)}) %collective-permute-start.3) | collective-permute-done | bytes 262176 | tf_op jit(solution)/shard_map/ppermute | solution.py:246
  21.1 3.1 %collective-permute-done.2.refs_1_.refs_0_ = bf16[128,1024]{1,0:T(8,128)(2,1)S(1)} collective-permute-done((bf16[128,1024]{1,0:T(8,128)(2,1)S(1)}, bf16[128,1024]{1,0:T(8,128)(2,1)S(1)}, u32[]{:S(2)}, u32[]{:S(2)}) %collective-permute-start.2) | collective-permute-done | bytes 262176 | tf_op jit(solution)/shard_map/ppermute | solution.py:246
  24.2 0.6 shard_map.102
  24.8 0.1 collective-permute-start.4
  24.9 2.7 %collective-permute-start.5 = (bf16[192,1024]{1,0:T(8,128)(2,1)S(1)}, bf16[192,1024]{1,0:T(8,128)(2,1)S(1)}, u32[]{:S(2)}, u32[]{:S(2)}) collective-permute-start(bf16[192,1024]{1,0:T(8,128)(2,1)S(1)} %get-tuple-element.43), channel_id=1, source_target_pairs={{0,6},{2,0},{4,2},{6,4},{1,7},{3,1},{5,3},{7,5},{8,14},{10,8},{12,... | collective-permute-start | bytes 1179656 | tf_op jit(solution)/shard_map/ppermute | solution.py:246
  27.6 2.0 %collective-permute-start.6 = (bf16[128,1024]{1,0:T(8,128)(2,1)S(1)}, bf16[128,1024]{1,0:T(8,128)(2,1)S(1)}, u32[]{:S(2)}, u32[]{:S(2)}) collective-permute-start(bf16[128,1024]{1,0:T(8,128)(2,1)S(1)} %collective-permute-done.1.refs_0_.refs_1_), channel_id=1, source_target_pairs={{0,193},{1,64},{64,1},{65,128},{128,65},{129,192},{192,129},{193,0... | collective-permute-start | bytes 786440 | tf_op jit(solution)/shard_map/ppermute | solution.py:256
  29.6 4.7 %collective-permute-done.6.refs_0_.refs_2_ = bf16[128,1024]{1,0:T(8,128)(2,1)S(1)} collective-permute-done((bf16[128,1024]{1,0:T(8,128)(2,1)S(1)}, bf16[128,1024]{1,0:T(8,128)(2,1)S(1)}, u32[]{:S(2)}, u32[]{:S(2)}) %collective-permute-start.6) | collective-permute-done | bytes 262176 | tf_op jit(solution)/shard_map/ppermute | solution.py:256
  34.3 0.6 shard_map.103
  35.0 2.7 %collective-permute-start.8 = (bf16[192,1024]{1,0:T(8,128)(2,1)S(1)}, bf16[192,1024]{1,0:T(8,128)(2,1)S(1)}, u32[]{:S(2)}, u32[]{:S(2)}) collective-permute-start(bf16[192,1024]{1,0:T(8,128)(2,1)S(1)} %get-tuple-element.45.refs_6_), channel_id=1, source_target_pairs={{0,6},{2,0},{4,2},{6,4},{1,7},{3,1},{5,3},{7,5},{8,14},{10,8},{12,... | collective-permute-start | bytes 1179656 | tf_op jit(solution)/shard_map/ppermute | solution.py:246
  37.7 2.2 %copy-done = bf16[1,4096,512]{2,1,0:T(8,128)(2,1)S(1)} copy-done((bf16[1,4096,512]{2,1,0:T(8,128)(2,1)S(1)}, bf16[1,4096,512]{2,1,0:T(8,128)(2,1)}, u32[]{:S(2)}) %copy-start) | copy-done | bytes 4194328
  39.9 2.2 %copy-done.2 = bf16[1,4096,512]{2,1,0:T(8,128)(2,1)S(1)} copy-done((bf16[1,4096,512]{2,1,0:T(8,128)(2,1)S(1)}, bf16[1,4096,512]{2,1,0:T(8,128)(2,1)}, u32[]{:S(2)}) %copy-start.2) | copy-done | bytes 4194328
  42.0 2.4 %shard_map.104 = (f32[512,1024]{1,0:T(8,128)S(1)}, bf16[512,1024]{1,0:T(8,128)(2,1)S(1)}) custom-call(s32[7]{0:T(128)S(1)} %stack.25.info, bf16[128,4096]{1,0:T(8,128)(2,1)S(1)} %bitcast.30, bf16[128,1024]{1,0:T(8,128)(2,1)S(1)} %collective-permute-done.refs_0_, bf16[128,1024]{1,0:T(8,128)(2,1)S(1)} %collective-permute-done.1.refs_0_.refs_1_, ...), custom_call_target="tpu_custom_call" | custom-call | flops 1 | bytes 1 | tf_op jit(solution)/shard_map/pallas_call | solution.py:85
  44.5 0.6 shard_map.105
  45.2 2.7 %collective-permute-start.10 = (bf16[64,1024]{1,0:T(8,128)(2,1)S(1)}, bf16[64,1024]{1,0:T(8,128)(2,1)S(1)}, u32[]{:S(2)}, u32[]{:S(2)}) collective-permute-start(bf16[64,1024]{1,0:T(8,128)(2,1)S(1)} %get-tuple-element.48.refs_7_), channel_id=1, source_target_pairs={{0,6},{2,0},{4,2},{6,4},{1,7},{3,1},{5,3},{7,5},{8,14},{10,8},{12,... | collective-permute-start | bytes 393224 | tf_op jit(solution)/shard_map/ppermute | solution.py:246
  47.8 2.6 %shard_map.106 = (f32[512,1024]{1,0:T(8,128)S(1)}, bf16[512,1024]{1,0:T(8,128)(2,1)S(1)}) custom-call(s32[7]{0:T(128)S(1)} %stack.25.info, bf16[128,4096]{1,0:T(8,128)(2,1)S(1)} %bitcast.31, bf16[128,1024]{1,0:T(8,128)(2,1)S(1)} %collective-permute-done.2.refs_1_.refs_0_, bf16[192,1024]{1,0:T(8,128)(2,1)S(1)} %collective-permute-done.4.refs_1_.refs_0_, ...), custom_call_target="tpu_custom_call" | custom-call | flops 1 | bytes 1 | tf_op jit(solution)/shard_map/pallas_call | solution.py:85
  50.5 2.6 %shard_map.107 = (f32[512,1024]{1,0:T(8,128)S(1)}, bf16[512,1024]{1,0:T(8,128)(2,1)S(1)}) custom-call(s32[7]{0:T(128)S(1)} %stack.25.info, bf16[128,4096]{1,0:T(8,128)(2,1)S(1)} %bitcast.32, bf16[128,1024]{1,0:T(8,128)(2,1)S(1)} %collective-permute-done.3.refs_2_.refs_0_, bf16[192,1024]{1,0:T(8,128)(2,1)S(1)} %collective-permute-done.5.refs_2_.refs_1_, ...), custom_call_target="tpu_custom_call" | custom-call | flops 1 | bytes 1 | tf_op jit(solution)/shard_map/pallas_call | solution.py:85
  53.1 2.5 %shard_map.108 = (bf16[512,1024]{1,0:T(8,128)(2,1)S(1)}, bf16[512,1024]{1,0:T(8,128)(2,1)S(1)}) custom-call(s32[7]{0:T(128)S(1)} %stack.25.info, bf16[128,4096]{1,0:T(8,128)(2,1)S(1)} %bitcast.33, bf16[192,1024]{1,0:T(8,128)(2,1)S(1)} %collective-permute-done.4.refs_1_.refs_0_, bf16[192,1024]{1,0:T(8,128)(2,1)S(1)} %collective-permute-done.5.refs_2_.refs_1_, ...), custom_call_target="tpu_custom_call" | custom-call | flops 1 | bytes 1 | tf_op jit(solution)/shard_map/pallas_call | solution.py:85
  55.7 1.1 shard_map.109
  56.8 5.0 %collective-permute-start.15 = (bf16[512,2048]{1,0:T(8,128)(2,1)S(1)}, bf16[512,2048]{1,0:T(8,128)(2,1)S(1)}, u32[]{:S(2)}, u32[]{:S(2)}) collective-permute-start(bf16[512,2048]{1,0:T(8,128)(2,1)S(1)} %get-tuple-element.56.refs_0_), channel_id=1, source_target_pairs={{0,8},{8,0},{1,9},{9,1},{2,10},{10,2},{3,11},{11,3},{4,12},{12,4},... | collective-permute-start | bytes 6291464 | tf_op jit(solution)/shard_map/ppermute | solution.py:249
  61.9 4.4 %shard_map.110 = (bf16[512,512]{1,0:T(8,128)(2,1)}, bf16[512,1024]{1,0:T(8,128)(2,1)S(1)}) custom-call(s32[7]{0:T(128)S(1)} %stack.25.info, bf16[512,1024]{1,0:T(8,128)(2,1)S(1)} %get-tuple-element.51.kv_ref, bf16[512,512]{1,0:T(8,128)(2,1)S(1)} %bitcast.34, bf16[512,512]{1,0:T(8,128)(2,1)S(1)} %bitcast.35, bf16[512,2048]{1,0:T(8,128)(2,1)S(1)} %get-tuple-element.56.refs_0_), custom_call_target="tpu_custom_call" | custom-call | flops 1 | bytes 1 | tf_op jit(solution)/shard_map/pallas_call | solution.py:130
  66.3 2.7 %shard_map.111 = (bf16[512,1024]{1,0:T(8,128)(2,1)S(1)}, bf16[64,1024]{1,0:T(8,128)(2,1)S(1)}, bf16[64,1024]{1,0:T(8,128)(2,1)S(1)}) custom-call(s32[7]{0:T(128)S(1)} %stack.25.info, bf16[512,1024]{1,0:T(8,128)(2,1)S(1)} %get-tuple-element.58.act_ref.refs_2_, bf16[4096,512]{1,0:T(8,128)(2,1)S(1)} %bitcast.20, bf16[4096,512]{1,0:T(8,128)(2,1)S(1)} %bitcast.27), custom_call_target="tpu_custom_call" | custom-call | flops 1 | bytes 1 | tf_op jit(solution)/shard_map/pallas_call | solution.py:190
  69.1 2.7 %collective-permute-start.12 = (bf16[64,1024]{1,0:T(8,128)(2,1)S(1)}, bf16[64,1024]{1,0:T(8,128)(2,1)S(1)}, u32[]{:S(2)}, u32[]{:S(2)}) collective-permute-start(bf16[64,1024]{1,0:T(8,128)(2,1)S(1)} %get-tuple-element.60), channel_id=1, source_target_pairs={{0,6},{2,0},{4,2},{6,4},{1,7},{3,1},{5,3},{7,5},{8,14},{10,8},{12,... | collective-permute-start | bytes 393224 | tf_op jit(solution)/shard_map/ppermute | solution.py:246
  71.8 4.7 %shard_map.112.refs_2_.refs_0_.refs_3_.refs_4_ = f32[512,2048]{1,0:T(8,128)S(1)} custom-call(s32[7]{0:T(128)S(1)} %stack.25.info, bf16[512,1024]{1,0:T(8,128)(2,1)S(1)} %get-tuple-element.58.act_ref.refs_2_, bf16[4096,512]{1,0:T(8,128)(2,1)S(1)} %bitcast.21, bf16[4096,512]{1,0:T(8,128)(2,1)S(1)} %bitcast.28, ...), custom_call_target="tpu_custom_call" | custom-call | flops 1 | bytes 1 | tf_op jit(solution)/shard_map/pallas_call | solution.py:190
  76.5 0.6 shard_map.113
  77.2 2.7 %collective-permute-start.14 = (bf16[192,1024]{1,0:T(8,128)(2,1)S(1)}, bf16[192,1024]{1,0:T(8,128)(2,1)S(1)}, u32[]{:S(2)}, u32[]{:S(2)}) collective-permute-start(bf16[192,1024]{1,0:T(8,128)(2,1)S(1)} %get-tuple-element.63.refs_5_), channel_id=1, source_target_pairs={{0,6},{2,0},{4,2},{6,4},{1,7},{3,1},{5,3},{7,5},{8,14},{10,8},{12,... | collective-permute-start | bytes 1179656 | tf_op jit(solution)/shard_map/ppermute | solution.py:246
  79.9 2.6 %shard_map.114.refs_2_ = f32[512,1024]{1,0:T(8,128)S(1)} custom-call(s32[7]{0:T(128)S(1)} %stack.25.info, bf16[512,1024]{1,0:T(8,128)(2,1)S(1)} %get-tuple-element.58.act_ref.refs_2_, bf16[4096,512]{1,0:T(8,128)(2,1)S(1)} %bitcast.22, bf16[4096,512]{1,0:T(8,128)(2,1)S(1)} %bitcast.29, f32[512,2048]{1,0:T(8,128)S(1)} %shard_map.112.refs_2_.refs_0_.refs_3_.refs_4_), custom_call_target="tpu_custom_call" | custom-call | flops 1 | bytes 1 | tf_op jit(solution)/shard_map/pallas_call | solution.py:190
  82.5 5.1 %shard_map.115 = (bf16[1024,1024]{1,0:T(8,128)(2,1)S(1)}, bf16[512,1024]{1,0:T(8,128)(2,1)S(1)}, bf16[512,1024]{1,0:T(8,128)(2,1)S(1)}) custom-call(s32[7]{0:T(128)S(1)} %stack.25.info, bf16[512,2048]{1,0:T(8,128)(2,1)S(1)} %get-tuple-element.64.refs_0_, bf16[512,2048]{1,0:T(8,128)(2,1)S(1)} %collective-permute-done.15.refs_1_, ...), custom_call_target="tpu_custom_call" | custom-call | flops 1 | bytes 1 | tf_op jit(solution)/shard_map/pallas_call | solution.py:229
  87.6 0.4 collective-permute-done.13.refs_0_
  88.0 0.8 shard_map.116
  88.8 2.8 %collective-permute-start.23 = (bf16[512,1024]{1,0:T(8,128)(2,1)S(1)}, bf16[512,1024]{1,0:T(8,128)(2,1)S(1)}, u32[]{:S(2)}, u32[]{:S(2)}) collective-permute-start(bf16[512,1024]{1,0:T(8,128)(2,1)S(1)} %get-tuple-element.73), channel_id=1, source_target_pairs={{0,16},{8,56},{16,32},{24,8},{32,48},{40,24},{48,0},{56,40},{1,17}... | collective-permute-start | bytes 3145736 | tf_op jit(solution)/shard_map/ppermute | solution.py:260
  91.6 2.7 %collective-permute-start.18 = (bf16[192,1024]{1,0:T(8,128)(2,1)S(1)}, bf16[192,1024]{1,0:T(8,128)(2,1)S(1)}, u32[]{:S(2)}, u32[]{:S(2)}) collective-permute-start(bf16[192,1024]{1,0:T(8,128)(2,1)S(1)} %get-tuple-element.67), channel_id=1, source_target_pairs={{0,6},{2,0},{4,2},{6,4},{1,7},{3,1},{5,3},{7,5},{8,14},{10,8},{12,... | collective-permute-start | bytes 1179656 | tf_op jit(solution)/shard_map/ppermute | solution.py:246
  94.2 2.4 %collective-permute-start.19 = (bf16[128,1024]{1,0:T(8,128)(2,1)S(1)}, bf16[128,1024]{1,0:T(8,128)(2,1)S(1)}, u32[]{:S(2)}, u32[]{:S(2)}) collective-permute-start(bf16[128,1024]{1,0:T(8,128)(2,1)S(1)} %get-tuple-element.68), channel_id=1, source_target_pairs={{0,193},{1,64},{64,1},{65,128},{128,65},{129,192},{192,129},{193,0... | collective-permute-start | bytes 786440 | tf_op jit(solution)/shard_map/ppermute | solution.py:256
  96.6 5.3 %collective-permute-done.19.refs_3_ = bf16[128,1024]{1,0:T(8,128)(2,1)S(1)} collective-permute-done((bf16[128,1024]{1,0:T(8,128)(2,1)S(1)}, bf16[128,1024]{1,0:T(8,128)(2,1)S(1)}, u32[]{:S(2)}, u32[]{:S(2)}) %collective-permute-start.19) | collective-permute-done | bytes 262176 | tf_op jit(solution)/shard_map/ppermute | solution.py:256
  101.9 0.7 collective-permute-done.17.refs_0_
  102.6 0.7 shard_map.117
  103.4 0.9 shard_map.118.refs_5_
  104.3 3.1 %collective-permute-start.31 = (bf16[1024,1024]{1,0:T(8,128)(2,1)S(1)}, bf16[1024,1024]{1,0:T(8,128)(2,1)S(1)}, u32[]{:S(2)}, u32[]{:S(2)}) collective-permute-start(bf16[1024,1024]{1,0:T(8,128)(2,1)S(1)} %shard_map.118.refs_5_), channel_id=1, source_target_pairs={{0,16},{8,56},{16,32},{24,8},{32,48},{40,24},{48,0},{56,40},{1,17}... | collective-permute-start | bytes 6291464 | tf_op jit(solution)/shard_map/ppermute | solution.py:260
  107.4 2.7 %collective-permute-start.21 = (bf16[192,1024]{1,0:T(8,128)(2,1)S(1)}, bf16[192,1024]{1,0:T(8,128)(2,1)S(1)}, u32[]{:S(2)}, u32[]{:S(2)}) collective-permute-start(bf16[192,1024]{1,0:T(8,128)(2,1)S(1)} %get-tuple-element.70), channel_id=1, source_target_pairs={{0,6},{2,0},{4,2},{6,4},{1,7},{3,1},{5,3},{7,5},{8,14},{10,8},{12,... | collective-permute-start | bytes 1179656 | tf_op jit(solution)/shard_map/ppermute | solution.py:246
  110.1 6.5 %collective-permute-done.22.refs_3_ = bf16[128,1024]{1,0:T(8,128)(2,1)S(1)} collective-permute-done((bf16[128,1024]{1,0:T(8,128)(2,1)S(1)}, bf16[128,1024]{1,0:T(8,128)(2,1)S(1)}, u32[]{:S(2)}, u32[]{:S(2)}) %collective-permute-start.22) | collective-permute-done | bytes 262176 | tf_op jit(solution)/shard_map/ppermute | solution.py:252
  116.6 1.9 %collective-permute-done.20.refs_0_ = bf16[192,1024]{1,0:T(8,128)(2,1)S(1)} collective-permute-done((bf16[192,1024]{1,0:T(8,128)(2,1)S(1)}, bf16[192,1024]{1,0:T(8,128)(2,1)S(1)}, u32[]{:S(2)}, u32[]{:S(2)}) %collective-permute-start.20) | collective-permute-done | bytes 393248 | tf_op jit(solution)/shard_map/ppermute | solution.py:246
  118.5 0.7 shard_map.119
  119.3 0.3 collective-permute-start.24
  119.6 2.4 %collective-permute-start.25 = (bf16[128,1024]{1,0:T(8,128)(2,1)S(1)}, bf16[128,1024]{1,0:T(8,128)(2,1)S(1)}, u32[]{:S(2)}, u32[]{:S(2)}) collective-permute-start(bf16[128,1024]{1,0:T(8,128)(2,1)S(1)} %get-tuple-element.75), channel_id=1, source_target_pairs={{0,6},{2,0},{4,2},{6,4},{1,7},{3,1},{5,3},{7,5},{8,14},{10,8},{12,... | collective-permute-start | bytes 786440 | tf_op jit(solution)/shard_map/ppermute | solution.py:246
  122.0 2.4 %collective-permute-start.26 = (bf16[128,1024]{1,0:T(8,128)(2,1)S(1)}, bf16[128,1024]{1,0:T(8,128)(2,1)S(1)}, u32[]{:S(2)}, u32[]{:S(2)}) collective-permute-start(bf16[128,1024]{1,0:T(8,128)(2,1)S(1)} %get-tuple-element.76), channel_id=1, source_target_pairs={{0,193},{1,64},{64,1},{65,128},{128,65},{129,192},{192,129},{193,0... | collective-permute-start | bytes 786440 | tf_op jit(solution)/shard_map/ppermute | solution.py:256
  124.4 2.3 %collective-permute-done.24.refs_0_ = bf16[128,1024]{1,0:T(8,128)(2,1)S(1)} collective-permute-done((bf16[128,1024]{1,0:T(8,128)(2,1)S(1)}, bf16[128,1024]{1,0:T(8,128)(2,1)S(1)}, u32[]{:S(2)}, u32[]{:S(2)}) %collective-permute-start.24) | collective-permute-done | bytes 262176 | tf_op jit(solution)/shard_map/ppermute | solution.py:246
  126.7 2.1 %collective-permute-done.26.refs_3_ = bf16[128,1024]{1,0:T(8,128)(2,1)S(1)} collective-permute-done((bf16[128,1024]{1,0:T(8,128)(2,1)S(1)}, bf16[128,1024]{1,0:T(8,128)(2,1)S(1)}, u32[]{:S(2)}, u32[]{:S(2)}) %collective-permute-start.26) | collective-permute-done | bytes 262176 | tf_op jit(solution)/shard_map/ppermute | solution.py:256
  128.8 0.7 shard_map.120.refs_0_
  129.5 0.1 collective-permute-start.27
  129.6 5.2 %collective-permute-done.27.refs_1_ = bf16[128,1024]{1,0:T(8,128)(2,1)S(1)} collective-permute-done((bf16[128,1024]{1,0:T(8,128)(2,1)S(1)}, bf16[128,1024]{1,0:T(8,128)(2,1)S(1)}, u32[]{:S(2)}, u32[]{:S(2)}) %collective-permute-start.27) | collective-permute-done | bytes 262176 | tf_op jit(solution)/shard_map/ppermute | solution.py:252
  134.8 0.6 shard_map.121.refs_1_.refs_0_
  135.4 0.6 shard_map.122.refs_4_
  136.1 4.3 %collective-permute-start.32 = (bf16[512,1024]{1,0:T(8,128)(2,1)S(1)}, bf16[512,1024]{1,0:T(8,128)(2,1)S(1)}, u32[]{:S(2)}, u32[]{:S(2)}) collective-permute-start(bf16[512,1024]{1,0:T(8,128)(2,1)S(1)} %shard_map.122.refs_4_), channel_id=1, source_target_pairs={{0,8},{8,0},{1,9},{9,1},{2,10},{10,2},{3,11},{11,3},{4,12},{12,4},... | collective-permute-start | bytes 3145736 | tf_op jit(solution)/shard_map/ppermute | solution.py:249
  140.4 1.3 collective-permute-start.30
  141.7 0.6 collective-permute-start.28
  142.3 6.0 %collective-permute-done.30.refs_3_ = bf16[128,1024]{1,0:T(8,128)(2,1)S(1)} collective-permute-done((bf16[128,1024]{1,0:T(8,128)(2,1)S(1)}, bf16[128,1024]{1,0:T(8,128)(2,1)S(1)}, u32[]{:S(2)}, u32[]{:S(2)}) %collective-permute-start.30) | collective-permute-done | bytes 262176 | tf_op jit(solution)/shard_map/ppermute | solution.py:246
  148.3 2.5 %collective-permute-done.29.refs_2_ = bf16[128,1024]{1,0:T(8,128)(2,1)S(1)} collective-permute-done((bf16[128,1024]{1,0:T(8,128)(2,1)S(1)}, bf16[128,1024]{1,0:T(8,128)(2,1)S(1)}, u32[]{:S(2)}, u32[]{:S(2)}) %collective-permute-start.29) | collective-permute-done | bytes 262176 | tf_op jit(solution)/shard_map/ppermute | solution.py:246
  150.8 5.7 %collective-permute-done.28.refs_1_ = bf16[128,1024]{1,0:T(8,128)(2,1)S(1)} collective-permute-done((bf16[128,1024]{1,0:T(8,128)(2,1)S(1)}, bf16[128,1024]{1,0:T(8,128)(2,1)S(1)}, u32[]{:S(2)}, u32[]{:S(2)}) %collective-permute-start.28) | collective-permute-done | bytes 262176 | tf_op jit(solution)/shard_map/ppermute | solution.py:246
  156.5 1.6 shard_map.123
  158.1 1.8 %shard_map.124 = (bf16[512,512]{1,0:T(8,128)(2,1)}, bf16[512,512]{1,0:T(8,128)(2,1)}) custom-call(s32[7]{0:T(128)S(1)} %stack.25.info, bf16[512,1024]{1,0:T(8,128)(2,1)S(1)} %get-tuple-element.77.refs_0_, bf16[1024,1024]{1,0:T(8,128)(2,1)S(1)} %collective-permute-done.31.refs_0_.refs_1_, bf16[512,1024]{1,0:T(8,128)(2,1)S(1)} %collective-permute-done.32.refs_2_), custom_call_target="tpu_custom_call" | custom-call | flops 1 | bytes 1 | tf_op jit(solution)/shard_map/pallas_call | solution.py:229
  (41 shorter events, 0.4 us)
Async XLA Ops:
  0.6 37.0 %copy-start.4 = (bf16[1,128,4096]{2,1,0:T(8,128)(2,1)S(1)}, bf16[1,128,4096]{2,1,0:T(8,128)(2,1)}, u32[]{:S(2)}) copy-start(bf16[1,128,4096]{2,1,0:T(8,128)(2,1)} %param.7) | copy-start | bytes 3145732
  1.7 12.5 %collective-permute-start = (bf16[128,1024]{1,0:T(8,128)(2,1)S(1)}, bf16[128,1024]{1,0:T(8,128)(2,1)S(1)}, u32[]{:S(2)}, u32[]{:S(2)}) collective-permute-start(bf16[128,1024]{1,0:T(8,128)(2,1)S(1)} %dynamic-slice_bitcast_fusion), channel_id=1, source_target_pairs={{0,193},{1,64},{64,1},{65,128},{128,65},{129,192},{192,129},{193,0... | collective-permute-start | bytes 786440 | tf_op jit(solution)/shard_map/ppermute | solution.py:256
  14.2 6.8 %collective-permute-start.3 = (bf16[128,1024]{1,0:T(8,128)(2,1)S(1)}, bf16[128,1024]{1,0:T(8,128)(2,1)S(1)}, u32[]{:S(2)}, u32[]{:S(2)}) collective-permute-start(bf16[128,1024]{1,0:T(8,128)(2,1)S(1)} %collective-permute-done.refs_0_), channel_id=1, source_target_pairs={{0,6},{2,0},{4,2},{6,4},{1,7},{3,1},{5,3},{7,5},{8,14},{10,8},{12,... | collective-permute-start | bytes 786440 | tf_op jit(solution)/shard_map/ppermute | solution.py:246
  16.7 7.5 %collective-permute-start.2 = (bf16[128,1024]{1,0:T(8,128)(2,1)S(1)}, bf16[128,1024]{1,0:T(8,128)(2,1)S(1)}, u32[]{:S(2)}, u32[]{:S(2)}) collective-permute-start(bf16[128,1024]{1,0:T(8,128)(2,1)S(1)} %collective-permute-done.refs_0_), channel_id=1, source_target_pairs={{0,2},{2,4},{4,6},{6,0},{1,3},{3,5},{5,7},{7,1},{8,10},{10,12},{12... | collective-permute-start | bytes 786440 | tf_op jit(solution)/shard_map/ppermute | solution.py:246
  16.7 7.5 %collective-permute-start.1 = (bf16[128,1024]{1,0:T(8,128)(2,1)S(1)}, bf16[128,1024]{1,0:T(8,128)(2,1)S(1)}, u32[]{:S(2)}, u32[]{:S(2)}) collective-permute-start(bf16[128,1024]{1,0:T(8,128)(2,1)S(1)} %collective-permute-done.refs_0_), channel_id=1, source_target_pairs={{0,1},{1,0},{2,3},{3,2},{4,5},{5,4},{6,7},{7,6},{8,9},{9,8},{10,11... | collective-permute-start | bytes 786440 | tf_op jit(solution)/shard_map/ppermute | solution.py:252
  24.8 9.5 %collective-permute-start.4 = (bf16[192,1024]{1,0:T(8,128)(2,1)S(1)}, bf16[192,1024]{1,0:T(8,128)(2,1)S(1)}, u32[]{:S(2)}, u32[]{:S(2)}) collective-permute-start(bf16[192,1024]{1,0:T(8,128)(2,1)S(1)} %get-tuple-element.42), channel_id=1, source_target_pairs={{0,2},{2,4},{4,6},{6,0},{1,3},{3,5},{5,7},{7,1},{8,10},{10,12},{12... | collective-permute-start | bytes 1179656 | tf_op jit(solution)/shard_map/ppermute | solution.py:246
  24.9 9.4 %collective-permute-start.5 = (bf16[192,1024]{1,0:T(8,128)(2,1)S(1)}, bf16[192,1024]{1,0:T(8,128)(2,1)S(1)}, u32[]{:S(2)}, u32[]{:S(2)}) collective-permute-start(bf16[192,1024]{1,0:T(8,128)(2,1)S(1)} %get-tuple-element.43), channel_id=1, source_target_pairs={{0,6},{2,0},{4,2},{6,4},{1,7},{3,1},{5,3},{7,5},{8,14},{10,8},{12,... | collective-permute-start | bytes 1179656 | tf_op jit(solution)/shard_map/ppermute | solution.py:246
  27.6 6.7 %collective-permute-start.6 = (bf16[128,1024]{1,0:T(8,128)(2,1)S(1)}, bf16[128,1024]{1,0:T(8,128)(2,1)S(1)}, u32[]{:S(2)}, u32[]{:S(2)}) collective-permute-start(bf16[128,1024]{1,0:T(8,128)(2,1)S(1)} %collective-permute-done.1.refs_0_.refs_1_), channel_id=1, source_target_pairs={{0,193},{1,64},{64,1},{65,128},{128,65},{129,192},{192,129},{193,0... | collective-permute-start | bytes 786440 | tf_op jit(solution)/shard_map/ppermute | solution.py:256
  34.9 9.6 %collective-permute-start.7 = (bf16[192,1024]{1,0:T(8,128)(2,1)S(1)}, bf16[192,1024]{1,0:T(8,128)(2,1)S(1)}, u32[]{:S(2)}, u32[]{:S(2)}) collective-permute-start(bf16[192,1024]{1,0:T(8,128)(2,1)S(1)} %get-tuple-element.44.refs_5_), channel_id=1, source_target_pairs={{0,2},{2,4},{4,6},{6,0},{1,3},{3,5},{5,7},{7,1},{8,10},{10,12},{12... | collective-permute-start | bytes 1179656 | tf_op jit(solution)/shard_map/ppermute | solution.py:246
  35.0 9.5 %collective-permute-start.8 = (bf16[192,1024]{1,0:T(8,128)(2,1)S(1)}, bf16[192,1024]{1,0:T(8,128)(2,1)S(1)}, u32[]{:S(2)}, u32[]{:S(2)}) collective-permute-start(bf16[192,1024]{1,0:T(8,128)(2,1)S(1)} %get-tuple-element.45.refs_6_), channel_id=1, source_target_pairs={{0,6},{2,0},{4,2},{6,4},{1,7},{3,1},{5,3},{7,5},{8,14},{10,8},{12,... | collective-permute-start | bytes 1179656 | tf_op jit(solution)/shard_map/ppermute | solution.py:246
  37.7 2.2 %copy-start = (bf16[1,4096,512]{2,1,0:T(8,128)(2,1)S(1)}, bf16[1,4096,512]{2,1,0:T(8,128)(2,1)}, u32[]{:S(2)}) copy-start(bf16[1,4096,512]{2,1,0:T(8,128)(2,1)} %param.8) | copy-start | bytes 12582916
  39.9 2.2 %copy-start.2 = (bf16[1,4096,512]{2,1,0:T(8,128)(2,1)S(1)}, bf16[1,4096,512]{2,1,0:T(8,128)(2,1)}, u32[]{:S(2)}) copy-start(bf16[1,4096,512]{2,1,0:T(8,128)(2,1)} %param.9) | copy-start | bytes 12582916
  42.0 5.8 %copy-start.1 = (bf16[1,4096,512]{2,1,0:T(8,128)(2,1)S(1)}, bf16[1,4096,512]{2,1,0:T(8,128)(2,1)}, u32[]{:S(2)}) copy-start(bf16[1,4096,512]{2,1,0:T(8,128)(2,1)} %param.8) | copy-start | bytes 12582916
  42.0 5.8 %copy-start.3 = (bf16[1,4096,512]{2,1,0:T(8,128)(2,1)S(1)}, bf16[1,4096,512]{2,1,0:T(8,128)(2,1)}, u32[]{:S(2)}) copy-start(bf16[1,4096,512]{2,1,0:T(8,128)(2,1)} %param.9) | copy-start | bytes 12582916
  45.1 8.0 %collective-permute-start.9 = (bf16[64,1024]{1,0:T(8,128)(2,1)S(1)}, bf16[64,1024]{1,0:T(8,128)(2,1)S(1)}, u32[]{:S(2)}, u32[]{:S(2)}) collective-permute-start(bf16[64,1024]{1,0:T(8,128)(2,1)S(1)} %get-tuple-element.47.refs_6_), channel_id=1, source_target_pairs={{0,2},{2,4},{4,6},{6,0},{1,3},{3,5},{5,7},{7,1},{8,10},{10,12},{12... | collective-permute-start | bytes 393224 | tf_op jit(solution)/shard_map/ppermute | solution.py:246
  45.2 7.9 %collective-permute-start.10 = (bf16[64,1024]{1,0:T(8,128)(2,1)S(1)}, bf16[64,1024]{1,0:T(8,128)(2,1)S(1)}, u32[]{:S(2)}, u32[]{:S(2)}) collective-permute-start(bf16[64,1024]{1,0:T(8,128)(2,1)S(1)} %get-tuple-element.48.refs_7_), channel_id=1, source_target_pairs={{0,6},{2,0},{4,2},{6,4},{1,7},{3,1},{5,3},{7,5},{8,14},{10,8},{12,... | collective-permute-start | bytes 393224 | tf_op jit(solution)/shard_map/ppermute | solution.py:246
  55.7 6.2 %copy-start.5 = (bf16[1,1,512,512]{3,2,1,0:T(8,128)(2,1)S(1)}, bf16[1,1,512,512]{3,2,1,0:T(8,128)(2,1)}, u32[]{:S(2)}) copy-start(bf16[1,1,512,512]{3,2,1,0:T(8,128)(2,1)} %param.10) | copy-start | bytes 1572868
  55.7 6.2 %copy-start.6 = (bf16[1,1,512,512]{3,2,1,0:T(8,128)(2,1)S(1)}, bf16[1,1,512,512]{3,2,1,0:T(8,128)(2,1)}, u32[]{:S(2)}) copy-start(bf16[1,1,512,512]{3,2,1,0:T(8,128)(2,1)} %param.11) | copy-start | bytes 1572868
  56.8 25.7 %collective-permute-start.15 = (bf16[512,2048]{1,0:T(8,128)(2,1)S(1)}, bf16[512,2048]{1,0:T(8,128)(2,1)S(1)}, u32[]{:S(2)}, u32[]{:S(2)}) collective-permute-start(bf16[512,2048]{1,0:T(8,128)(2,1)S(1)} %get-tuple-element.56.refs_0_), channel_id=1, source_target_pairs={{0,8},{8,0},{1,9},{9,1},{2,10},{10,2},{3,11},{11,3},{4,12},{12,4},... | collective-permute-start | bytes 6291464 | tf_op jit(solution)/shard_map/ppermute | solution.py:249
  66.3 16.2 %collective-permute-start.16 = (bf16[512,1024]{1,0:T(8,128)(2,1)S(1)}, bf16[512,1024]{1,0:T(8,128)(2,1)S(1)}, u32[]{:S(2)}, u32[]{:S(2)}) collective-permute-start(bf16[512,1024]{1,0:T(8,128)(2,1)S(1)} %get-tuple-element.58.act_ref.refs_2_), channel_id=1, source_target_pairs={{0,8},{8,0},{1,9},{9,1},{2,10},{10,2},{3,11},{11,3},{4,12},{12,4},... | collective-permute-start | bytes 3145736 | tf_op jit(solution)/shard_map/ppermute | solution.py:249
  69.0 7.5 %collective-permute-start.11 = (bf16[64,1024]{1,0:T(8,128)(2,1)S(1)}, bf16[64,1024]{1,0:T(8,128)(2,1)S(1)}, u32[]{:S(2)}, u32[]{:S(2)}) collective-permute-start(bf16[64,1024]{1,0:T(8,128)(2,1)S(1)} %get-tuple-element.59), channel_id=1, source_target_pairs={{0,2},{2,4},{4,6},{6,0},{1,3},{3,5},{5,7},{7,1},{8,10},{10,12},{12... | collective-permute-start | bytes 393224 | tf_op jit(solution)/shard_map/ppermute | solution.py:246
  69.1 7.4 %collective-permute-start.12 = (bf16[64,1024]{1,0:T(8,128)(2,1)S(1)}, bf16[64,1024]{1,0:T(8,128)(2,1)S(1)}, u32[]{:S(2)}, u32[]{:S(2)}) collective-permute-start(bf16[64,1024]{1,0:T(8,128)(2,1)S(1)} %get-tuple-element.60), channel_id=1, source_target_pairs={{0,6},{2,0},{4,2},{6,4},{1,7},{3,1},{5,3},{7,5},{8,14},{10,8},{12,... | collective-permute-start | bytes 393224 | tf_op jit(solution)/shard_map/ppermute | solution.py:246
  77.1 10.9 %collective-permute-start.13 = (bf16[192,1024]{1,0:T(8,128)(2,1)S(1)}, bf16[192,1024]{1,0:T(8,128)(2,1)S(1)}, u32[]{:S(2)}, u32[]{:S(2)}) collective-permute-start(bf16[192,1024]{1,0:T(8,128)(2,1)S(1)} %get-tuple-element.62.refs_4_), channel_id=1, source_target_pairs={{0,2},{2,4},{4,6},{6,0},{1,3},{3,5},{5,7},{7,1},{8,10},{10,12},{12... | collective-permute-start | bytes 1179656 | tf_op jit(solution)/shard_map/ppermute | solution.py:246
  77.2 10.8 %collective-permute-start.14 = (bf16[192,1024]{1,0:T(8,128)(2,1)S(1)}, bf16[192,1024]{1,0:T(8,128)(2,1)S(1)}, u32[]{:S(2)}, u32[]{:S(2)}) collective-permute-start(bf16[192,1024]{1,0:T(8,128)(2,1)S(1)} %get-tuple-element.63.refs_5_), channel_id=1, source_target_pairs={{0,6},{2,0},{4,2},{6,4},{1,7},{3,1},{5,3},{7,5},{8,14},{10,8},{12,... | collective-permute-start | bytes 1179656 | tf_op jit(solution)/shard_map/ppermute | solution.py:246
  88.8 14.6 %collective-permute-start.23 = (bf16[512,1024]{1,0:T(8,128)(2,1)S(1)}, bf16[512,1024]{1,0:T(8,128)(2,1)S(1)}, u32[]{:S(2)}, u32[]{:S(2)}) collective-permute-start(bf16[512,1024]{1,0:T(8,128)(2,1)S(1)} %get-tuple-element.73), channel_id=1, source_target_pairs={{0,16},{8,56},{16,32},{24,8},{32,48},{40,24},{48,0},{56,40},{1,17}... | collective-permute-start | bytes 3145736 | tf_op jit(solution)/shard_map/ppermute | solution.py:260
  91.6 11.0 %collective-permute-start.17 = (bf16[192,1024]{1,0:T(8,128)(2,1)S(1)}, bf16[192,1024]{1,0:T(8,128)(2,1)S(1)}, u32[]{:S(2)}, u32[]{:S(2)}) collective-permute-start(bf16[192,1024]{1,0:T(8,128)(2,1)S(1)} %get-tuple-element.66), channel_id=1, source_target_pairs={{0,2},{2,4},{4,6},{6,0},{1,3},{3,5},{5,7},{7,1},{8,10},{10,12},{12... | collective-permute-start | bytes 1179656 | tf_op jit(solution)/shard_map/ppermute | solution.py:246
  91.6 11.0 %collective-permute-start.18 = (bf16[192,1024]{1,0:T(8,128)(2,1)S(1)}, bf16[192,1024]{1,0:T(8,128)(2,1)S(1)}, u32[]{:S(2)}, u32[]{:S(2)}) collective-permute-start(bf16[192,1024]{1,0:T(8,128)(2,1)S(1)} %get-tuple-element.67), channel_id=1, source_target_pairs={{0,6},{2,0},{4,2},{6,4},{1,7},{3,1},{5,3},{7,5},{8,14},{10,8},{12,... | collective-permute-start | bytes 1179656 | tf_op jit(solution)/shard_map/ppermute | solution.py:246
  94.2 7.6 %collective-permute-start.19 = (bf16[128,1024]{1,0:T(8,128)(2,1)S(1)}, bf16[128,1024]{1,0:T(8,128)(2,1)S(1)}, u32[]{:S(2)}, u32[]{:S(2)}) collective-permute-start(bf16[128,1024]{1,0:T(8,128)(2,1)S(1)} %get-tuple-element.68), channel_id=1, source_target_pairs={{0,193},{1,64},{64,1},{65,128},{128,65},{129,192},{192,129},{193,0... | collective-permute-start | bytes 786440 | tf_op jit(solution)/shard_map/ppermute | solution.py:256
  104.3 31.1 %collective-permute-start.31 = (bf16[1024,1024]{1,0:T(8,128)(2,1)S(1)}, bf16[1024,1024]{1,0:T(8,128)(2,1)S(1)}, u32[]{:S(2)}, u32[]{:S(2)}) collective-permute-start(bf16[1024,1024]{1,0:T(8,128)(2,1)S(1)} %shard_map.118.refs_5_), channel_id=1, source_target_pairs={{0,16},{8,56},{16,32},{24,8},{32,48},{40,24},{48,0},{56,40},{1,17}... | collective-permute-start | bytes 6291464 | tf_op jit(solution)/shard_map/ppermute | solution.py:260
  107.4 11.1 %collective-permute-start.20 = (bf16[192,1024]{1,0:T(8,128)(2,1)S(1)}, bf16[192,1024]{1,0:T(8,128)(2,1)S(1)}, u32[]{:S(2)}, u32[]{:S(2)}) collective-permute-start(bf16[192,1024]{1,0:T(8,128)(2,1)S(1)} %get-tuple-element.69), channel_id=1, source_target_pairs={{0,2},{2,4},{4,6},{6,0},{1,3},{3,5},{5,7},{7,1},{8,10},{10,12},{12... | collective-permute-start | bytes 1179656 | tf_op jit(solution)/shard_map/ppermute | solution.py:246
  107.4 11.1 %collective-permute-start.21 = (bf16[192,1024]{1,0:T(8,128)(2,1)S(1)}, bf16[192,1024]{1,0:T(8,128)(2,1)S(1)}, u32[]{:S(2)}, u32[]{:S(2)}) collective-permute-start(bf16[192,1024]{1,0:T(8,128)(2,1)S(1)} %get-tuple-element.70), channel_id=1, source_target_pairs={{0,6},{2,0},{4,2},{6,4},{1,7},{3,1},{5,3},{7,5},{8,14},{10,8},{12,... | collective-permute-start | bytes 1179656 | tf_op jit(solution)/shard_map/ppermute | solution.py:246
  110.1 6.5 %collective-permute-start.22 = (bf16[128,1024]{1,0:T(8,128)(2,1)S(1)}, bf16[128,1024]{1,0:T(8,128)(2,1)S(1)}, u32[]{:S(2)}, u32[]{:S(2)}) collective-permute-start(bf16[128,1024]{1,0:T(8,128)(2,1)S(1)} %get-tuple-element.71.refs_2_), channel_id=1, source_target_pairs={{0,1},{1,0},{2,3},{3,2},{4,5},{5,4},{6,7},{7,6},{8,9},{9,8},{10,11... | collective-permute-start | bytes 786440 | tf_op jit(solution)/shard_map/ppermute | solution.py:252
  119.3 7.5 %collective-permute-start.24 = (bf16[128,1024]{1,0:T(8,128)(2,1)S(1)}, bf16[128,1024]{1,0:T(8,128)(2,1)S(1)}, u32[]{:S(2)}, u32[]{:S(2)}) collective-permute-start(bf16[128,1024]{1,0:T(8,128)(2,1)S(1)} %get-tuple-element.74), channel_id=1, source_target_pairs={{0,2},{2,4},{4,6},{6,0},{1,3},{3,5},{5,7},{7,1},{8,10},{10,12},{12... | collective-permute-start | bytes 786440 | tf_op jit(solution)/shard_map/ppermute | solution.py:246
  119.6 7.1 %collective-permute-start.25 = (bf16[128,1024]{1,0:T(8,128)(2,1)S(1)}, bf16[128,1024]{1,0:T(8,128)(2,1)S(1)}, u32[]{:S(2)}, u32[]{:S(2)}) collective-permute-start(bf16[128,1024]{1,0:T(8,128)(2,1)S(1)} %get-tuple-element.75), channel_id=1, source_target_pairs={{0,6},{2,0},{4,2},{6,4},{1,7},{3,1},{5,3},{7,5},{8,14},{10,8},{12,... | collective-permute-start | bytes 786440 | tf_op jit(solution)/shard_map/ppermute | solution.py:246
  122.0 6.8 %collective-permute-start.26 = (bf16[128,1024]{1,0:T(8,128)(2,1)S(1)}, bf16[128,1024]{1,0:T(8,128)(2,1)S(1)}, u32[]{:S(2)}, u32[]{:S(2)}) collective-permute-start(bf16[128,1024]{1,0:T(8,128)(2,1)S(1)} %get-tuple-element.76), channel_id=1, source_target_pairs={{0,193},{1,64},{64,1},{65,128},{128,65},{129,192},{192,129},{193,0... | collective-permute-start | bytes 786440 | tf_op jit(solution)/shard_map/ppermute | solution.py:256
  129.5 5.3 %collective-permute-start.27 = (bf16[128,1024]{1,0:T(8,128)(2,1)S(1)}, bf16[128,1024]{1,0:T(8,128)(2,1)S(1)}, u32[]{:S(2)}, u32[]{:S(2)}) collective-permute-start(bf16[128,1024]{1,0:T(8,128)(2,1)S(1)} %shard_map.120.refs_0_), channel_id=1, source_target_pairs={{0,1},{1,0},{2,3},{3,2},{4,5},{5,4},{6,7},{7,6},{8,9},{9,8},{10,11... | collective-permute-start | bytes 786440 | tf_op jit(solution)/shard_map/ppermute | solution.py:252
  136.1 22.0 %collective-permute-start.32 = (bf16[512,1024]{1,0:T(8,128)(2,1)S(1)}, bf16[512,1024]{1,0:T(8,128)(2,1)S(1)}, u32[]{:S(2)}, u32[]{:S(2)}) collective-permute-start(bf16[512,1024]{1,0:T(8,128)(2,1)S(1)} %shard_map.122.refs_4_), channel_id=1, source_target_pairs={{0,8},{8,0},{1,9},{9,1},{2,10},{10,2},{3,11},{11,3},{4,12},{12,4},... | collective-permute-start | bytes 3145736 | tf_op jit(solution)/shard_map/ppermute | solution.py:249
  140.4 7.9 %collective-permute-start.30 = (bf16[128,1024]{1,0:T(8,128)(2,1)S(1)}, bf16[128,1024]{1,0:T(8,128)(2,1)S(1)}, u32[]{:S(2)}, u32[]{:S(2)}) collective-permute-start(bf16[128,1024]{1,0:T(8,128)(2,1)S(1)} %shard_map.121.refs_1_.refs_0_), channel_id=1, source_target_pairs={{0,6},{2,0},{4,2},{6,4},{1,7},{3,1},{5,3},{7,5},{8,14},{10,8},{12,... | collective-permute-start | bytes 786440 | tf_op jit(solution)/shard_map/ppermute | solution.py:246
  141.7 9.1 %collective-permute-start.29 = (bf16[128,1024]{1,0:T(8,128)(2,1)S(1)}, bf16[128,1024]{1,0:T(8,128)(2,1)S(1)}, u32[]{:S(2)}, u32[]{:S(2)}) collective-permute-start(bf16[128,1024]{1,0:T(8,128)(2,1)S(1)} %shard_map.121.refs_1_.refs_0_), channel_id=1, source_target_pairs={{0,4},{2,6},{4,0},{6,2},{1,5},{3,7},{5,1},{7,3},{8,12},{10,14},{12... | collective-permute-start | bytes 786440 | tf_op jit(solution)/shard_map/ppermute | solution.py:246
  141.7 14.8 %collective-permute-start.28 = (bf16[128,1024]{1,0:T(8,128)(2,1)S(1)}, bf16[128,1024]{1,0:T(8,128)(2,1)S(1)}, u32[]{:S(2)}, u32[]{:S(2)}) collective-permute-start(bf16[128,1024]{1,0:T(8,128)(2,1)S(1)} %shard_map.121.refs_1_.refs_0_), channel_id=1, source_target_pairs={{0,2},{2,4},{4,6},{6,0},{1,3},{3,5},{5,7},{7,1},{8,10},{10,12},{12... | collective-permute-start | bytes 786440 | tf_op jit(solution)/shard_map/ppermute | solution.py:246

commit v4 on v3

--- a/solution.py
+++ b/solution.py
@@ -8,7 +8,7 @@
 
 HEAD = 256
 XS = 4
-UNIT = 256
+UNIT = 512
 masked_score = -1e30
 f32 = jnp.float32
 bf16 = jnp.bfloat16
@@ -43,105 +43,104 @@
 LIGHT = pl.CostEstimate(flops=1, bytes_accessed=1, transcendentals=0)
 
 
-def project(m, enc, parts, wk, wv, acc, info, last, n_sec, after=()):
+def project(quarters, enc, wk, wv, acc, info, n_sec, after=(), queries=None):
     blk, width = enc.shape
     quarter = width // XS
     total = n_sec * blk
     cols = wk.shape[1]
     heads = cols // HEAD
-
-    def body(info, enc_ref, *refs):
-        n = len(parts)
-        part_refs, wk_ref, wv_ref = refs[:n], refs[n], refs[n + 1]
-        acc_ref = refs[n + 2] if acc is not None else None
-        out_ref, rows_ref = refs[-2:]
+    parts = [part for _, some in quarters for part in some]
+    extra = ([] if acc is None else [acc]) + list(queries or ())
+    n = len(quarters)
+
+    def body(info, *refs):
+        refs = list(refs)
+        enc_refs = [refs.pop(0) for _ in quarters]
+        part_refs = [refs.pop(0) for _ in parts]
+        weight_refs = [refs.pop(0) for _ in range(2 * n)]
+        acc_ref = refs.pop(0) if acc is not None else None
+        rows_refs = refs[-n:]
 
         @pl.when(pl.program_id(0) == 0)
         def _():
-            rows_ref[pl.ds(pl.multiple_of(info[SEC] * blk, blk), blk), :] = enc_ref[...]
-            for ref, (_, pieces) in zip(part_refs, parts):
-                for at, count, block, off in pieces:
-                    to = block_of(info, block, n_sec) * blk + off
-                    rows_ref[pl.ds(pl.multiple_of(to, count), count), :] = ref[at : at + count, :]
-
-        rows = rows_ref[...]
-        k_part = dot(rows, wk_ref[...])
-        v_part = dot(rows, wv_ref[...])
-        if acc_ref is not None:
-            k_part = k_part + acc_ref[:, :HEAD]
-            v_part = v_part + acc_ref[:, HEAD:]
-        out_ref[:, :HEAD] = k_part.astype(out_ref.dtype)
-        out_ref[:, HEAD:] = v_part.astype(out_ref.dtype)
-
-    def at_quarter(info):
-        return mod4(info[X] - m)
-
-    weight = pl.BlockSpec((quarter, HEAD), lambda h, info: (at_quarter(info), h))
-    pair = pl.BlockSpec((total, 2 * HEAD), lambda h, info: (0, h))
-    out_shape = [
-        jax.ShapeDtypeStruct((total, 2 * cols), bf16 if last else f32),
-        jax.ShapeDtypeStruct((total, quarter), bf16),
-    ]
+            left = list(part_refs)
+            for rows_ref, enc_ref, (_, some) in zip(rows_refs, enc_refs, quarters):
+                rows_ref[pl.ds(pl.multiple_of(info[SEC] * blk, blk), blk), :] = enc_ref[...]
+                for _, pieces in some:
+                    ref = left.pop(0)
+                    for at, count, block, off in pieces:
+                        to = block_of(info, block, n_sec) * blk + off
+                        rows_ref[pl.ds(pl.multiple_of(to, count), count), :] = ref[at : at + count, :]
+
+        sums = [None if acc_ref is None else acc_ref[:, j * HEAD : (j + 1) * HEAD] for j in range(2)]
+        for i, rows_ref in enumerate(rows_refs):
+            rows = rows_ref[...]
+            for j in range(2):
+                term = dot(rows, weight_refs[2 * i + j][...])
+                sums[j] = term if sums[j] is None else sums[j] + term
+        if queries is None:
+            refs[-n - 1][:, :HEAD] = sums[0]
+            refs[-n - 1][:, HEAD:] = sums[1]
+        else:
+            k, v = (one.astype(bf16) for one in sums)
+            attend(k, v, refs[0][...], refs[1][...], info, refs[-n - 2], refs[-n - 1])
+
+    def head(rows, count):
+        return pl.BlockSpec((rows, count * HEAD), lambda h, info: (0, h))
+
+    def enc_block(m):
+        return pl.BlockSpec((blk, quarter), lambda h, info: (0, mod4(info[X] - m)))
+
+    def weight(m):
+        return pl.BlockSpec((quarter, HEAD), lambda h, info: (mod4(info[X] - m), h))
+
+    rows_out = jax.ShapeDtypeStruct((total, quarter), bf16)
+    if queries is None:
+        targets = 0
+        out_shape, out_specs = [jax.ShapeDtypeStruct((total, 2 * cols), f32)], [head(total, 2)]
+    else:
+        targets = queries[0].shape[0]
+        out_shape = [
+            jax.ShapeDtypeStruct((targets, cols), bf16),
+            jax.ShapeDtypeStruct((total, 2 * cols), bf16),
+        ]
+        out_specs = [head(targets, 1), head(total, 2)]
     return pl.pallas_call(
         body,
         grid_spec=pltpu.PrefetchScalarGridSpec(
             num_scalar_prefetch=1,
             grid=(heads,),
-            in_specs=[pl.BlockSpec((blk, quarter), lambda h, info: (0, at_quarter(info)))]
+            in_specs=[enc_block(m) for m, _ in quarters]
             + [whole(p) for p, _ in parts]
-            + [weight, weight]
-            + ([pair] if acc is not None else [])
+            + [weight(m) for m, _ in quarters for _ in range(2)]
+            + ([] if acc is None else [head(total, 2)])
+            + ([] if queries is None else [head(targets, 1)] * 2)
             + [ANYWHERE] * len(after),
-            out_specs=[pair, whole(out_shape[1])],
+            out_specs=out_specs + [whole(rows_out)] * n,
         ),
-        out_shape=out_shape,
+        out_shape=out_shape + [rows_out] * n,
         compiler_params=params(24),
         cost_estimate=LIGHT,
-    )(info, enc, *[p for p, _ in parts], wk, wv, *([acc] if acc is not None else []), *after)
-
-
-def attention(kv, q, g, info, after):
-    total, targets, width = kv.shape[0], q.shape[0], q.shape[1]
-    heads = width // HEAD
+    )(info, *[enc] * n, *[p for p, _ in parts], *[wk, wv] * n, *extra, *after)
+
+
+def attend(k, v, q, g, info, ctx_ref, act_ref):
     scale = HEAD ** (-0.5)
-
-    def body(info, kv_ref, q_ref, g_ref, *refs):
-        ctx_ref, act_ref = refs[-2:]
-        k, v, q = kv_ref[:, :HEAD], kv_ref[:, HEAD:], q_ref[...]
-        place = lax.broadcasted_iota(jnp.int32, (total, 1), 0)
-        scores = dot_t(k, q) * scale
-        scores = jnp.where(place < info[SRC_LIVE], scores, masked_score)
-        highest = jnp.max(scores, axis=0, keepdims=True)
-        shifted = jnp.exp(scores - highest)
-        weights = shifted * (1.0 / jnp.sum(shifted, axis=0, keepdims=True))
-        low = weights.astype(bf16)
-        target = lax.broadcasted_iota(jnp.int32, (targets, 1), 0)
-        g = jnp.where(target < info[TGT_LIVE], g_ref[...].astype(f32), 0.0).astype(bf16)
-        prob = dot_t(v, g)
-        prob_dot = jnp.sum(weights * prob, axis=0, keepdims=True)
-        grad = (weights * (prob - prob_dot) * scale).astype(bf16)
-        act_ref[:, :HEAD] = dot(grad, q).astype(bf16)
-        act_ref[:, HEAD:] = dot(low, g).astype(bf16)
-        ctx_ref[...] = t_dot(low, v).astype(bf16)
-
-    def cols(n, w):
-        return pl.BlockSpec((n, w), lambda h, info: (0, h))
-
-    return pl.pallas_call(
-        body,
-        grid_spec=pltpu.PrefetchScalarGridSpec(
-            num_scalar_prefetch=1,
-            grid=(heads,),
-            in_specs=[cols(total, 2 * HEAD), cols(targets, HEAD), cols(targets, HEAD)] + [ANYWHERE] * len(after),
-            out_specs=[cols(targets, HEAD), cols(total, 2 * HEAD)],
-        ),
-        out_shape=[
-            jax.ShapeDtypeStruct((targets, width), bf16),
-            jax.ShapeDtypeStruct((total, 2 * width), bf16),
-        ],
-        compiler_params=params(20),
-        cost_estimate=LIGHT,
-    )(info, kv, q, g, *after)
+    place = lax.broadcasted_iota(jnp.int32, (k.shape[0], 1), 0)
+    scores = dot_t(k, q) * scale
+    scores = jnp.where(place < info[SRC_LIVE], scores, masked_score)
+    highest = jnp.max(scores, axis=0, keepdims=True)
+    shifted = jnp.exp(scores - highest)
+    weights = shifted * (1.0 / jnp.sum(shifted, axis=0, keepdims=True))
+    low = weights.astype(bf16)
+    target = lax.broadcasted_iota(jnp.int32, (q.shape[0], 1), 0)
+    g = jnp.where(target < info[TGT_LIVE], g.astype(f32), 0.0).astype(bf16)
+    prob = dot_t(v, g)
+    prob_dot = jnp.sum(weights * prob, axis=0, keepdims=True)
+    grad = (weights * (prob - prob_dot) * scale).astype(bf16)
+    act_ref[:, :HEAD] = dot(grad, q).astype(bf16)
+    act_ref[:, HEAD:] = dot(low, g).astype(bf16)
+    ctx_ref[...] = t_dot(low, v).astype(bf16)
 
 
 def block_of(info, which, n_sec):
@@ -255,9 +254,10 @@
         n = 2 * n_sec
         return lax.ppermute(v, ("section", "low"), [(z, (z + (1 if z % 2 else -1)) % n) for z in range(n)])
 
-    def shift_y(v):
+    def shift_y(v, change=False):
         n = 2 * XS
-        return lax.ppermute(v, ("y", "core"), [(i, (i + (-2 if i % 2 else 2)) % n) for i in range(n)])
+        pairs = [(i, (i + (-2 if i % 2 else 2)) % n) for i in range(n)]
+        return lax.ppermute(v, ("y", "core"), [(i, j ^ 1 if change else j) for i, j in pairs])
 
     def shards(enc_out, key_weight, value_weight, queries, ctx_grad, src_pad, tgt_pad):
         enc, wk, wv = enc_out[0], key_weight[0], value_weight[0]
@@ -303,9 +303,11 @@
         out3 = with_half(b3, u2, d2)
         u3, d3 = both(*out3)
         rows = [None] * XS
-        acc, rows[0] = project(
-            0, enc, [(b, [(0, blk, i + 1, 0)]) for i, b in enumerate((b1, b2, b3))], wk, wv, None, info, False, n_sec, out3
-        )
+
+        def parts(*got):
+            return [(g, [(0, blk, i + 1, 0)]) for i, g in enumerate(got)]
+
+        acc, rows[0] = project([(0, parts(b1, b2, b3))], enc, wk, wv, None, info, n_sec, out3)
 
         def cut(info, up_ref, down_ref, up_out, down_out):
             up_out[...] = up_ref[:mid]
@@ -313,44 +315,42 @@
 
         out4 = small(cut, [u3, d3], [jax.ShapeDtypeStruct((mid, quarter), bf16)] * 2, info, (acc,))
         u4, d4 = both(*out4)
-        for m, got in ((1, (u1, u2, u3)), (3, (d1, d2, d3))):
-            acc, rows[m] = project(
-                m, enc, [(g, [(0, blk, i + 1, 0)]) for i, g in enumerate(got)], wk, wv, acc, info, False, n_sec, out4
-            )
+        beside = [(1, parts(u1, u2, u3)), (3, parts(d1, d2, d3))]
+        acc, rows[1], rows[3] = project(beside, enc, wk, wv, acc, info, n_sec, out4)
         last = [(u2, [(blk, mid, 1, 0)]), (d2, [(blk, mid, 1, mid)]), (u3, [(blk, mid, 2, 0)]), (d3, [(blk, mid, 2, mid)])]
         last += [(u4, [(0, mid, 3, 0)]), (d4, [(0, mid, 3, mid)])]
-        acc, rows[2] = project(2, enc, last, wk, wv, acc, info, True, n_sec)
+        asked = (queries[0, 0], ctx_grad[0, 0])
+        context, act, rows[2] = project([(2, last)], enc, wk, wv, acc, info, n_sec, queries=asked)
+        context = context[None, None]
+        act_other = swap_core(act)
 
         half = quarter // 2
 
-        def pack(info, *refs):
-            core = info[CORE]
-            row_refs, (kept_ref, sent_ref) = refs[:XS], refs[XS:]
-            for m, ref in enumerate(row_refs):
-                step = mod4(info[X] - info[Y] - m)
-                for out_ref, side in ((kept_ref, core), (sent_ref, 1 - core)):
+        def pack(own, after=()):
+            def body(info, *refs):
+                side = info[CORE] if own else 1 - info[CORE]
+                for m, ref in enumerate(refs[:-1]):
+                    step = mod4(info[X] - info[Y] - m)
 
                     @pl.when(step == 1 + 2 * side)
                     def _():
-                        out_ref[:, :quarter] = ref[...]
+                        refs[-1][:, :quarter] = ref[...]
 
                     for place, at in ((2, quarter), (0, quarter + half)):
 
                         @pl.when(step == place)
                         def _():
-                            out_ref[:, at : at + half] = ref[:, pl.ds(pl.multiple_of(side * half, half), half)]
-
-        packed = jax.ShapeDtypeStruct((total_src, 2 * quarter), bf16)
-        kept, sent = small(pack, rows, [packed, packed], info)
+                            refs[-1][:, at : at + half] = ref[:, pl.ds(pl.multiple_of(side * half, half), half)]
+
+            return small(body, rows, [jax.ShapeDtypeStruct((total_src, 2 * quarter), bf16)], info, after)[0]
+
+        sent = pack(False)
         got = swap_core(sent)
-
-        context, act = attention(acc, queries[0, 0], ctx_grad[0, 0], info, (sent,))
-        context = context[None, None]
-        act_other = swap_core(act)
 
         far, up, down = partial_grad(act, wk, wv, info, (2,), bf16, first=(n_sec, blk))
         up, down = both(up, down)
         (near,) = partial_grad(act, wk, wv, info, (3, 1), f32, (far,))
+        kept = pack(True, (near,))
         (keep,) = partial_grad(act, wk, wv, info, (0,), f32, (near,))
         def stage(done, sent, following, up, down, carried, after=(), through=None):
             ins, outs = [up, down], []
@@ -405,14 +405,16 @@
         (up, down), carried = both(up, down), cross(total)
         total, up, down = stage(2, 1, 0, up, down, carried)
         (up, down), carried = both(up, down), swap_low(total)
-        def add_y(info, near_ref, got_ref, out_ref):
-            out_ref[...] = near_ref[...]
-            at = pl.ds(pl.multiple_of(info[CORE] * half, half), half)
-            out_ref[at, :] = (near_ref[at, :].astype(f32) + got_ref[...].astype(f32)).astype(bf16)
-
-        (out_y,) = small(add_y, [near_y, got_y], [near_y], info, (total,))
-        in_y = shift_y(out_y)
-        total, up, down = stage(1, 0, None, up, down, carried, (out_y,))
+        total, up, down = stage(1, 0, None, up, down, carried)
+
+        def add_y(info, near_ref, got_ref, same_ref, other_ref):
+            here = pl.ds(pl.multiple_of(info[CORE] * half, half), half)
+            there = pl.ds(pl.multiple_of((1 - info[CORE]) * half, half), half)
+            same_ref[...] = (near_ref[here, :].astype(f32) + got_ref[...].astype(f32)).astype(bf16)
+            other_ref[...] = near_ref[there, :]
+
+        same_y, other_y = small(add_y, [near_y, got_y], [keep_y, keep_y], info, (total,))
+        in_y = shift_y(same_y), shift_y(other_y, True)
         (up, down), carried = both(up, down), cross(total)
         (mine,) = stage(0, None, None, up, down, carried)
         other = swap_low(mine)
@@ -424,23 +426,8 @@
         (final,) = small(add_two, [mine, other], [part], info)
         gathered = [final] + [shift_x(final, k) for k in range(1, XS)]
 
-        def halve(info, in_ref, out_ref):
-            out_ref[...] = in_ref[pl.ds(pl.multiple_of((1 - info[CORE]) * half, half), half), :]
-
-        (away_y,) = small(halve, [in_y], [keep_y], info, (final,))
-        home_y = swap_core(away_y)
-
-        def place(info, *refs):
-            for k in range(XS):
-                at = mod4(info[X] - k) * quarter
-                refs[-1][:, pl.ds(pl.multiple_of(at, quarter), quarter)] = refs[k][...]
-
-        (enc_grad,) = small(place, gathered, [jax.ShapeDtypeStruct((blk, width), bf16)], info, (away_y,))
-        enc_grad = enc_grad[None]
-
-        def finish(info, keep_ref, in_ref, home_ref, key_ref, value_ref):
-            at = pl.ds(pl.multiple_of(info[CORE] * half, half), half)
-            sums = keep_ref[...].astype(f32) + in_ref[at, :].astype(f32) + home_ref[...].astype(f32)
+        def finish(info, keep_ref, one_ref, two_ref, key_ref, value_ref):
+            sums = keep_ref[...].astype(f32) + one_ref[...].astype(f32) + two_ref[...].astype(f32)
             sums = sums.astype(bf16)
             for h in range(local_width // HEAD):
                 at = 2 * h * HEAD
@@ -448,8 +435,16 @@
                 value_ref[:, h * HEAD : (h + 1) * HEAD] = sums[:, at + HEAD : at + 2 * HEAD]
 
         shard = jax.ShapeDtypeStruct((half, local_width), bf16)
-        key_weight_grad, value_weight_grad = small(finish, [keep_y, in_y, home_y], [shard, shard], info)
+        key_weight_grad, value_weight_grad = small(finish, [keep_y, *in_y], [shard, shard], info)
         key_weight_grad, value_weight_grad = key_weight_grad[None], value_weight_grad[None]
+        def place(info, *refs):
+            for k in range(XS):
+                at = mod4(info[X] - k) * quarter
+                refs[-1][:, pl.ds(pl.multiple_of(at, quarter), quarter)] = refs[k][...]
+
+        (enc_grad,) = small(place, gathered, [jax.ShapeDtypeStruct((blk, width), bf16)], info, (key_weight_grad,))
+        enc_grad = enc_grad[None]
+
         return (context, enc_grad, key_weight_grad, value_weight_grad)
 
     return shards

time: 160 us -> 156 us (0.975)
  the two profiles are of different devices: /device:TPU:1 before, /device:TPU:8 now
where the time goes in v4:
time: 156 us; the launch traced here: 153 us
  waiting for transfers between devices  57.8 us (37%)
  starting transfers between devices  48.8 us (31%)
  Pallas kernels  37.3 us (24%)
  local copies, waits for them, and re-layouts  6.59 us (4%)
  between operations  2.29 us (1%)
    ppermute x21, starting transfers between devices, shift_x(): return lax.ppermute(v, 'x', [(i, (i + k) % XS) for i in range(XS)])  31.3 us
    ppermute x21, waiting for transfers between devices, shift_x(): return lax.ppermute(v, 'x', [(i, (i + k) % XS) for i in range(XS)])  22.4 us
    ppermute x4, waiting for transfers between devices, cross(): lax.ppermute(v, ('section', 'low'), [(z, (z + (1 if z % 2 else -1)) % n)...  20.1 us
    pallas_call x15, Pallas kernels, small(): pl.pallas_call(run, grid_spec=pltpu.PrefetchScalarGridSpec(num_scalar_pre...  16.9 us
    ppermute x3, waiting for transfers between devices, swap_low(): return lax.ppermute(v, 'low', [(0, 1), (1, 0)])  15.2 us
    ppermute x4, starting transfers between devices, cross(): lax.ppermute(v, ('section', 'low'), [(z, (z + (1 if z % 2 else -1)) % n)...  13.8 us
    pallas_call x3, Pallas kernels, project(): pl.pallas_call(body, grid_spec=pltpu.PrefetchScalarGridSpec(num_scalar_pr...  12.2 us
    pallas_call x3, Pallas kernels, partial_grad(): pl.pallas_call(body, grid_spec=pltpu.PrefetchScalarGridSpec(num_scalar_pr...  8.18 us
  transfers between devices with their start and end apart: 33, of which 13 were waited for; matrix products, arithmetic and copies ran while one was open for 0% of the time, Pallas kernels for 17%

profile of v4, /device:TPU:8, one launch (start us, length us, event | category | flops | bytes accessed | tf_op | source)
XLA Modules:
  0.0 152.7 jit_solution(1784809760200216656)
XLA Ops:
  0.6 1.1 dynamic-slice_bitcast_fusion
  1.7 5.9 %collective-permute-start = (bf16[128,1024]{1,0:T(8,128)(2,1)S(1)}, bf16[128,1024]{1,0:T(8,128)(2,1)S(1)}, u32[]{:S(2)}, u32[]{:S(2)}) collective-permute-start(bf16[128,1024]{1,0:T(8,128)(2,1)S(1)} %dynamic-slice_bitcast_fusion), channel_id=1, source_target_pairs={{0,193},{1,64},{64,1},{65,128},{128,65},{129,192},{192,129},{193,0... | collective-permute-start | bytes 786440 | tf_op jit(solution)/shard_map/ppermute | solution.py:255
  7.7 6.3 %collective-permute-done.refs_1_ = bf16[128,1024]{1,0:T(8,128)(2,1)S(1)} collective-permute-done((bf16[128,1024]{1,0:T(8,128)(2,1)S(1)}, bf16[128,1024]{1,0:T(8,128)(2,1)S(1)}, u32[]{:S(2)}, u32[]{:S(2)}) %collective-permute-start) | collective-permute-done | bytes 262176 | tf_op jit(solution)/shard_map/ppermute | solution.py:255
  14.0 2.8 %collective-permute-start.3 = (bf16[128,1024]{1,0:T(8,128)(2,1)S(1)}, bf16[128,1024]{1,0:T(8,128)(2,1)S(1)}, u32[]{:S(2)}, u32[]{:S(2)}) collective-permute-start(bf16[128,1024]{1,0:T(8,128)(2,1)S(1)} %collective-permute-done.refs_1_), channel_id=1, source_target_pairs={{0,6},{2,0},{4,2},{6,4},{1,7},{3,1},{5,3},{7,5},{8,14},{10,8},{12,... | collective-permute-start | bytes 786440 | tf_op jit(solution)/shard_map/ppermute | solution.py:245
  18.0 0.1 stack.25.info
  18.1 3.6 %collective-permute-done.3.refs_2_.refs_5_ = bf16[128,1024]{1,0:T(8,128)(2,1)S(1)} collective-permute-done((bf16[128,1024]{1,0:T(8,128)(2,1)S(1)}, bf16[128,1024]{1,0:T(8,128)(2,1)S(1)}, u32[]{:S(2)}, u32[]{:S(2)}) %collective-permute-start.3) | collective-permute-done | bytes 262176 | tf_op jit(solution)/shard_map/ppermute | solution.py:245
  21.7 3.4 %collective-permute-done.2.refs_1_.refs_2_ = bf16[128,1024]{1,0:T(8,128)(2,1)S(1)} collective-permute-done((bf16[128,1024]{1,0:T(8,128)(2,1)S(1)}, bf16[128,1024]{1,0:T(8,128)(2,1)S(1)}, u32[]{:S(2)}, u32[]{:S(2)}) %collective-permute-start.2) | collective-permute-done | bytes 262176 | tf_op jit(solution)/shard_map/ppermute | solution.py:245
  25.1 0.6 shard_map.102
  25.7 0.1 collective-permute-start.4
  25.8 3.2 %collective-permute-start.5 = (bf16[192,1024]{1,0:T(8,128)(2,1)S(1)}, bf16[192,1024]{1,0:T(8,128)(2,1)S(1)}, u32[]{:S(2)}, u32[]{:S(2)}) collective-permute-start(bf16[192,1024]{1,0:T(8,128)(2,1)S(1)} %get-tuple-element.41), channel_id=1, source_target_pairs={{0,6},{2,0},{4,2},{6,4},{1,7},{3,1},{5,3},{7,5},{8,14},{10,8},{12,... | collective-permute-start | bytes 1179656 | tf_op jit(solution)/shard_map/ppermute | solution.py:245
  29.1 2.6 %collective-permute-start.6 = (bf16[128,1024]{1,0:T(8,128)(2,1)S(1)}, bf16[128,1024]{1,0:T(8,128)(2,1)S(1)}, u32[]{:S(2)}, u32[]{:S(2)}) collective-permute-start(bf16[128,1024]{1,0:T(8,128)(2,1)S(1)} %collective-permute-done.1.refs_0_.refs_2_), channel_id=1, source_target_pairs={{0,193},{1,64},{64,1},{65,128},{128,65},{129,192},{192,129},{193,0... | collective-permute-start | bytes 786440 | tf_op jit(solution)/shard_map/ppermute | solution.py:255
  31.7 5.0 %collective-permute-done.6.refs_0_.refs_3_ = bf16[128,1024]{1,0:T(8,128)(2,1)S(1)} collective-permute-done((bf16[128,1024]{1,0:T(8,128)(2,1)S(1)}, bf16[128,1024]{1,0:T(8,128)(2,1)S(1)}, u32[]{:S(2)}, u32[]{:S(2)}) %collective-permute-start.6) | collective-permute-done | bytes 262176 | tf_op jit(solution)/shard_map/ppermute | solution.py:255
  36.6 0.6 shard_map.103
  37.3 3.2 %collective-permute-start.8 = (bf16[192,1024]{1,0:T(8,128)(2,1)S(1)}, bf16[192,1024]{1,0:T(8,128)(2,1)S(1)}, u32[]{:S(2)}, u32[]{:S(2)}) collective-permute-start(bf16[192,1024]{1,0:T(8,128)(2,1)S(1)} %get-tuple-element.43.refs_7_), channel_id=1, source_target_pairs={{0,6},{2,0},{4,2},{6,4},{1,7},{3,1},{5,3},{7,5},{8,14},{10,8},{12,... | collective-permute-start | bytes 1179656 | tf_op jit(solution)/shard_map/ppermute | solution.py:245
  40.6 2.2 %copy-done = bf16[1,4096,512]{2,1,0:T(8,128)(2,1)S(1)} copy-done((bf16[1,4096,512]{2,1,0:T(8,128)(2,1)S(1)}, bf16[1,4096,512]{2,1,0:T(8,128)(2,1)}, u32[]{:S(2)}) %copy-start) | copy-done | bytes 4194328
  42.8 2.2 %copy-done.2 = bf16[1,4096,512]{2,1,0:T(8,128)(2,1)S(1)} copy-done((bf16[1,4096,512]{2,1,0:T(8,128)(2,1)S(1)}, bf16[1,4096,512]{2,1,0:T(8,128)(2,1)}, u32[]{:S(2)}) %copy-start.2) | copy-done | bytes 4194328
  44.9 2.4 %shard_map.104 = (f32[512,1024]{1,0:T(8,128)S(1)}, bf16[512,1024]{1,0:T(8,128)(2,1)S(1)}) custom-call(s32[7]{0:T(128)S(1)} %stack.25.info, bf16[128,4096]{1,0:T(8,128)(2,1)S(1)} %bitcast.30, bf16[128,1024]{1,0:T(8,128)(2,1)S(1)} %collective-permute-done.refs_1_, bf16[128,1024]{1,0:T(8,128)(2,1)S(1)} %collective-permute-done.1.refs_0_.refs_2_, ...), custom_call_target="tpu_custom_call" | custom-call | flops 1 | bytes 1 | tf_op jit(solution)/shard_map/pallas_call | solution.py:108
  47.4 0.6 shard_map.105
  48.0 0.1 collective-permute-start.9
  48.1 3.2 %collective-permute-start.10 = (bf16[64,1024]{1,0:T(8,128)(2,1)S(1)}, bf16[64,1024]{1,0:T(8,128)(2,1)S(1)}, u32[]{:S(2)}, u32[]{:S(2)}) collective-permute-start(bf16[64,1024]{1,0:T(8,128)(2,1)S(1)} %get-tuple-element.46.refs_14_), channel_id=1, source_target_pairs={{0,6},{2,0},{4,2},{6,4},{1,7},{3,1},{5,3},{7,5},{8,14},{10,8},{12,... | collective-permute-start | bytes 393224 | tf_op jit(solution)/shard_map/ppermute | solution.py:245
  51.3 4.0 %shard_map.106 = (f32[512,1024]{1,0:T(8,128)S(1)}, bf16[512,1024]{1,0:T(8,128)(2,1)S(1)}, bf16[512,1024]{1,0:T(8,128)(2,1)S(1)}) custom-call(s32[7]{0:T(128)S(1)} %stack.25.info, bf16[128,4096]{1,0:T(8,128)(2,1)S(1)} %bitcast.31, bf16[128,4096]{1,0:T(8,128)(2,1)S(1)} %bitcast.32, bf16[128,1024]{1,0:T(8,128)(2,1)S(1)} %collective-permute-done.2.refs_1_.refs_2_, ...), custom_call_target="tpu_custom_call" | custom-call | flops 1 | bytes 1 | tf_op jit(solution)/shard_map/pallas_call | solution.py:108
  55.4 5.7 %shard_map.107 = (bf16[512,512]{1,0:T(8,128)(2,1)}, bf16[512,1024]{1,0:T(8,128)(2,1)S(1)}, bf16[512,1024]{1,0:T(8,128)(2,1)S(1)}) custom-call(s32[7]{0:T(128)S(1)} %stack.25.info, bf16[128,4096]{1,0:T(8,128)(2,1)S(1)} %bitcast.33, bf16[192,1024]{1,0:T(8,128)(2,1)S(1)} %collective-permute-done.4.refs_1_.refs_3_, ...), custom_call_target="tpu_custom_call" | custom-call | flops 1 | bytes 1 | tf_op jit(solution)/shard_map/pallas_call | solution.py:108
  61.1 0.8 shard_map.113
  61.9 0.1 collective-permute-start.15
  62.0 0.5 collective-permute-start.16
  62.5 2.2 %shard_map.108 = (bf16[512,1024]{1,0:T(8,128)(2,1)S(1)}, bf16[64,1024]{1,0:T(8,128)(2,1)S(1)}, bf16[64,1024]{1,0:T(8,128)(2,1)S(1)}) custom-call(s32[7]{0:T(128)S(1)} %stack.25.info, bf16[512,1024]{1,0:T(8,128)(2,1)S(1)} %get-tuple-element.49.act_ref.refs_2_, bf16[4096,512]{1,0:T(8,128)(2,1)S(1)} %bitcast.20, bf16[4096,512]{1,0:T(8,128)(2,1)S(1)} %bitcast.27), custom_call_target="tpu_custom_call" | custom-call | flops 1 | bytes 1 | tf_op jit(solution)/shard_map/pallas_call | solution.py:189
  64.7 0.1 collective-permute-start.11
  64.8 3.2 %collective-permute-start.12 = (bf16[64,1024]{1,0:T(8,128)(2,1)S(1)}, bf16[64,1024]{1,0:T(8,128)(2,1)S(1)}, u32[]{:S(2)}, u32[]{:S(2)}) collective-permute-start(bf16[64,1024]{1,0:T(8,128)(2,1)S(1)} %get-tuple-element.51), channel_id=1, source_target_pairs={{0,6},{2,0},{4,2},{6,4},{1,7},{3,1},{5,3},{7,5},{8,14},{10,8},{12,... | collective-permute-start | bytes 393224 | tf_op jit(solution)/shard_map/ppermute | solution.py:245
  68.0 3.8 %shard_map.109.refs_2_.refs_0_.refs_4_.refs_3_ = f32[512,2048]{1,0:T(8,128)S(1)} custom-call(s32[7]{0:T(128)S(1)} %stack.25.info, bf16[512,1024]{1,0:T(8,128)(2,1)S(1)} %get-tuple-element.49.act_ref.refs_2_, bf16[4096,512]{1,0:T(8,128)(2,1)S(1)} %bitcast.21, bf16[4096,512]{1,0:T(8,128)(2,1)S(1)} %bitcast.28, ...), custom_call_target="tpu_custom_call" | custom-call | flops 1 | bytes 1 | tf_op jit(solution)/shard_map/pallas_call | solution.py:189
  71.8 0.6 shard_map.110
  72.5 3.2 %collective-permute-start.14 = (bf16[192,1024]{1,0:T(8,128)(2,1)S(1)}, bf16[192,1024]{1,0:T(8,128)(2,1)S(1)}, u32[]{:S(2)}, u32[]{:S(2)}) collective-permute-start(bf16[192,1024]{1,0:T(8,128)(2,1)S(1)} %get-tuple-element.54.refs_5_), channel_id=1, source_target_pairs={{0,6},{2,0},{4,2},{6,4},{1,7},{3,1},{5,3},{7,5},{8,14},{10,8},{12,... | collective-permute-start | bytes 1179656 | tf_op jit(solution)/shard_map/ppermute | solution.py:245
  75.8 1.0 shard_map.112.refs_0_
  76.8 2.2 %shard_map.111.refs_2_ = f32[512,1024]{1,0:T(8,128)S(1)} custom-call(s32[7]{0:T(128)S(1)} %stack.25.info, bf16[512,1024]{1,0:T(8,128)(2,1)S(1)} %get-tuple-element.49.act_ref.refs_2_, bf16[4096,512]{1,0:T(8,128)(2,1)S(1)} %bitcast.22, bf16[4096,512]{1,0:T(8,128)(2,1)S(1)} %bitcast.29, f32[512,2048]{1,0:T(8,128)S(1)} %shard_map.109.refs_2_.refs_0_.refs_4_.refs_3_), custom_call_target="tpu_custom_call" | custom-call | flops 1 | bytes 1 | tf_op jit(solution)/shard_map/pallas_call | solution.py:189
  79.0 5.1 %shard_map.114 = (bf16[1024,1024]{1,0:T(8,128)(2,1)S(1)}, bf16[512,1024]{1,0:T(8,128)(2,1)S(1)}, bf16[512,1024]{1,0:T(8,128)(2,1)S(1)}) custom-call(s32[7]{0:T(128)S(1)} %stack.25.info, bf16[512,2048]{1,0:T(8,128)(2,1)S(1)} %shard_map.112.refs_0_, bf16[512,2048]{1,0:T(8,128)(2,1)S(1)} %collective-permute-done.15.refs_1_, ...), custom_call_target="tpu_custom_call" | custom-call | flops 1 | bytes 1 | tf_op jit(solution)/shard_map/pallas_call | solution.py:228
  84.1 0.2 collective-permute-done.13.refs_0_
  84.3 0.8 shard_map.115
  85.1 1.7 %collective-permute-start.30 = (bf16[512,1024]{1,0:T(8,128)(2,1)S(1)}, bf16[512,1024]{1,0:T(8,128)(2,1)S(1)}, u32[]{:S(2)}, u32[]{:S(2)}) collective-permute-start(bf16[512,1024]{1,0:T(8,128)(2,1)S(1)} %get-tuple-element.71), channel_id=1, source_target_pairs={{0,16},{8,56},{16,32},{24,8},{32,48},{40,24},{48,0},{56,40},{1,17}... | collective-permute-start | bytes 3145736 | tf_op jit(solution)/shard_map/ppermute | solution.py:260
  86.7 0.2 collective-permute-start.17
  86.9 3.1 %collective-permute-start.18 = (bf16[192,1024]{1,0:T(8,128)(2,1)S(1)}, bf16[192,1024]{1,0:T(8,128)(2,1)S(1)}, u32[]{:S(2)}, u32[]{:S(2)}) collective-permute-start(bf16[192,1024]{1,0:T(8,128)(2,1)S(1)} %get-tuple-element.61), channel_id=1, source_target_pairs={{0,6},{2,0},{4,2},{6,4},{1,7},{3,1},{5,3},{7,5},{8,14},{10,8},{12,... | collective-permute-start | bytes 1179656 | tf_op jit(solution)/shard_map/ppermute | solution.py:245
  90.0 2.6 %collective-permute-start.19 = (bf16[128,1024]{1,0:T(8,128)(2,1)S(1)}, bf16[128,1024]{1,0:T(8,128)(2,1)S(1)}, u32[]{:S(2)}, u32[]{:S(2)}) collective-permute-start(bf16[128,1024]{1,0:T(8,128)(2,1)S(1)} %get-tuple-element.62), channel_id=1, source_target_pairs={{0,193},{1,64},{64,1},{65,128},{128,65},{129,192},{192,129},{193,0... | collective-permute-start | bytes 786440 | tf_op jit(solution)/shard_map/ppermute | solution.py:255
  92.6 5.0 %collective-permute-done.19.refs_3_ = bf16[128,1024]{1,0:T(8,128)(2,1)S(1)} collective-permute-done((bf16[128,1024]{1,0:T(8,128)(2,1)S(1)}, bf16[128,1024]{1,0:T(8,128)(2,1)S(1)}, u32[]{:S(2)}, u32[]{:S(2)}) %collective-permute-start.19) | collective-permute-done | bytes 262176 | tf_op jit(solution)/shard_map/ppermute | solution.py:255
  97.6 0.7 shard_map.116
  98.3 0.1 collective-permute-start.20
  98.4 3.2 %collective-permute-start.21 = (bf16[192,1024]{1,0:T(8,128)(2,1)S(1)}, bf16[192,1024]{1,0:T(8,128)(2,1)S(1)}, u32[]{:S(2)}, u32[]{:S(2)}) collective-permute-start(bf16[192,1024]{1,0:T(8,128)(2,1)S(1)} %get-tuple-element.64), channel_id=1, source_target_pairs={{0,6},{2,0},{4,2},{6,4},{1,7},{3,1},{5,3},{7,5},{8,14},{10,8},{12,... | collective-permute-start | bytes 1179656 | tf_op jit(solution)/shard_map/ppermute | solution.py:245
  101.6 6.4 %collective-permute-done.22.refs_3_ = bf16[128,1024]{1,0:T(8,128)(2,1)S(1)} collective-permute-done((bf16[128,1024]{1,0:T(8,128)(2,1)S(1)}, bf16[128,1024]{1,0:T(8,128)(2,1)S(1)}, u32[]{:S(2)}, u32[]{:S(2)}) %collective-permute-start.22) | collective-permute-done | bytes 262176 | tf_op jit(solution)/shard_map/ppermute | solution.py:251
  108.0 0.7 shard_map.117
  108.7 0.8 shard_map.120
  109.6 1.4 collective-permute-start.31
  110.9 3.2 %collective-permute-start.24 = (bf16[128,1024]{1,0:T(8,128)(2,1)S(1)}, bf16[128,1024]{1,0:T(8,128)(2,1)S(1)}, u32[]{:S(2)}, u32[]{:S(2)}) collective-permute-start(bf16[128,1024]{1,0:T(8,128)(2,1)S(1)} %get-tuple-element.67), channel_id=1, source_target_pairs={{0,6},{2,0},{4,2},{6,4},{1,7},{3,1},{5,3},{7,5},{8,14},{10,8},{12,... | collective-permute-start | bytes 786440 | tf_op jit(solution)/shard_map/ppermute | solution.py:245
  114.2 2.6 %collective-permute-start.25 = (bf16[128,1024]{1,0:T(8,128)(2,1)S(1)}, bf16[128,1024]{1,0:T(8,128)(2,1)S(1)}, u32[]{:S(2)}, u32[]{:S(2)}) collective-permute-start(bf16[128,1024]{1,0:T(8,128)(2,1)S(1)} %get-tuple-element.68.refs_2_), channel_id=1, source_target_pairs={{0,193},{1,64},{64,1},{65,128},{128,65},{129,192},{192,129},{193,0... | collective-permute-start | bytes 786440 | tf_op jit(solution)/shard_map/ppermute | solution.py:255
  116.8 3.0 %collective-permute-done.23.refs_0_ = bf16[128,1024]{1,0:T(8,128)(2,1)S(1)} collective-permute-done((bf16[128,1024]{1,0:T(8,128)(2,1)S(1)}, bf16[128,1024]{1,0:T(8,128)(2,1)S(1)}, u32[]{:S(2)}, u32[]{:S(2)}) %collective-permute-start.23) | collective-permute-done | bytes 262176 | tf_op jit(solution)/shard_map/ppermute | solution.py:245
  119.8 3.9 %collective-permute-done.25.refs_3_ = bf16[128,1024]{1,0:T(8,128)(2,1)S(1)} collective-permute-done((bf16[128,1024]{1,0:T(8,128)(2,1)S(1)}, bf16[128,1024]{1,0:T(8,128)(2,1)S(1)}, u32[]{:S(2)}, u32[]{:S(2)}) %collective-permute-start.25) | collective-permute-done | bytes 262176 | tf_op jit(solution)/shard_map/ppermute | solution.py:255
  123.7 0.7 shard_map.118.refs_0_
  124.4 0.1 collective-permute-start.26
  124.5 8.9 %collective-permute-done.26.refs_1_ = bf16[128,1024]{1,0:T(8,128)(2,1)S(1)} collective-permute-done((bf16[128,1024]{1,0:T(8,128)(2,1)S(1)}, bf16[128,1024]{1,0:T(8,128)(2,1)S(1)}, u32[]{:S(2)}, u32[]{:S(2)}) %collective-permute-start.26) | collective-permute-done | bytes 262176 | tf_op jit(solution)/shard_map/ppermute | solution.py:251
  133.3 0.6 shard_map.119.refs_0_
  133.9 1.3 collective-permute-start.29
  135.2 1.0 collective-permute-start.27
  136.2 1.8 %shard_map.121 = (bf16[512,512]{1,0:T(8,128)(2,1)}, bf16[512,512]{1,0:T(8,128)(2,1)}) custom-call(s32[7]{0:T(128)S(1)} %stack.25.info, bf16[512,1024]{1,0:T(8,128)(2,1)S(1)} %get-tuple-element.69.refs_0_, bf16[512,1024]{1,0:T(8,128)(2,1)S(1)} %collective-permute-done.31.refs_1_, bf16[512,1024]{1,0:T(8,128)(2,1)S(1)} %collective-permute-done.32.refs_2_), custom_call_target="tpu_custom_call" | custom-call | flops 1 | bytes 1 | tf_op jit(solution)/shard_map/pallas_call | solution.py:228
  138.0 5.2 %collective-permute-done.29.refs_3_ = bf16[128,1024]{1,0:T(8,128)(2,1)S(1)} collective-permute-done((bf16[128,1024]{1,0:T(8,128)(2,1)S(1)}, bf16[128,1024]{1,0:T(8,128)(2,1)S(1)}, u32[]{:S(2)}, u32[]{:S(2)}) %collective-permute-start.29) | collective-permute-done | bytes 262176 | tf_op jit(solution)/shard_map/ppermute | solution.py:245
  143.2 2.7 %collective-permute-done.28.refs_2_ = bf16[128,1024]{1,0:T(8,128)(2,1)S(1)} collective-permute-done((bf16[128,1024]{1,0:T(8,128)(2,1)S(1)}, bf16[128,1024]{1,0:T(8,128)(2,1)S(1)}, u32[]{:S(2)}, u32[]{:S(2)}) %collective-permute-start.28) | collective-permute-done | bytes 262176 | tf_op jit(solution)/shard_map/ppermute | solution.py:245
  145.9 4.2 %collective-permute-done.27.refs_1_ = bf16[128,1024]{1,0:T(8,128)(2,1)S(1)} collective-permute-done((bf16[128,1024]{1,0:T(8,128)(2,1)S(1)}, bf16[128,1024]{1,0:T(8,128)(2,1)S(1)}, u32[]{:S(2)}, u32[]{:S(2)}) %collective-permute-start.27) | collective-permute-done | bytes 262176 | tf_op jit(solution)/shard_map/ppermute | solution.py:245
  150.1 1.0 copy-done.7
  151.1 1.6 %shard_map.122 = bf16[128,4096]{1,0:T(8,128)(2,1)} custom-call(s32[7]{0:T(128)S(1)} %stack.25.info, bf16[128,1024]{1,0:T(8,128)(2,1)S(1)} %shard_map.119.refs_0_, bf16[128,1024]{1,0:T(8,128)(2,1)S(1)} %collective-permute-done.27.refs_1_, bf16[128,1024]{1,0:T(8,128)(2,1)S(1)} %collective-permute-done.28.refs_2_, ...), custom_call_target="tpu_custom_call" | custom-call | flops 1 | bytes 1 | tf_op jit(solution)/shard_map/pallas_call | solution.py:228
  (41 shorter events, 0.3 us)
Async XLA Ops:
  0.6 39.9 %copy-start.4 = (bf16[1,128,4096]{2,1,0:T(8,128)(2,1)S(1)}, bf16[1,128,4096]{2,1,0:T(8,128)(2,1)}, u32[]{:S(2)}) copy-start(bf16[1,128,4096]{2,1,0:T(8,128)(2,1)} %param.7) | copy-start | bytes 3145732
  1.7 12.2 %collective-permute-start = (bf16[128,1024]{1,0:T(8,128)(2,1)S(1)}, bf16[128,1024]{1,0:T(8,128)(2,1)S(1)}, u32[]{:S(2)}, u32[]{:S(2)}) collective-permute-start(bf16[128,1024]{1,0:T(8,128)(2,1)S(1)} %dynamic-slice_bitcast_fusion), channel_id=1, source_target_pairs={{0,193},{1,64},{64,1},{65,128},{128,65},{129,192},{192,129},{193,0... | collective-permute-start | bytes 786440 | tf_op jit(solution)/shard_map/ppermute | solution.py:255
  14.0 7.8 %collective-permute-start.3 = (bf16[128,1024]{1,0:T(8,128)(2,1)S(1)}, bf16[128,1024]{1,0:T(8,128)(2,1)S(1)}, u32[]{:S(2)}, u32[]{:S(2)}) collective-permute-start(bf16[128,1024]{1,0:T(8,128)(2,1)S(1)} %collective-permute-done.refs_1_), channel_id=1, source_target_pairs={{0,6},{2,0},{4,2},{6,4},{1,7},{3,1},{5,3},{7,5},{8,14},{10,8},{12,... | collective-permute-start | bytes 786440 | tf_op jit(solution)/shard_map/ppermute | solution.py:245
  16.7 8.4 %collective-permute-start.2 = (bf16[128,1024]{1,0:T(8,128)(2,1)S(1)}, bf16[128,1024]{1,0:T(8,128)(2,1)S(1)}, u32[]{:S(2)}, u32[]{:S(2)}) collective-permute-start(bf16[128,1024]{1,0:T(8,128)(2,1)S(1)} %collective-permute-done.refs_1_), channel_id=1, source_target_pairs={{0,2},{2,4},{4,6},{6,0},{1,3},{3,5},{5,7},{7,1},{8,10},{10,12},{12... | collective-permute-start | bytes 786440 | tf_op jit(solution)/shard_map/ppermute | solution.py:245
  16.7 8.4 %collective-permute-start.1 = (bf16[128,1024]{1,0:T(8,128)(2,1)S(1)}, bf16[128,1024]{1,0:T(8,128)(2,1)S(1)}, u32[]{:S(2)}, u32[]{:S(2)}) collective-permute-start(bf16[128,1024]{1,0:T(8,128)(2,1)S(1)} %collective-permute-done.refs_1_), channel_id=1, source_target_pairs={{0,1},{1,0},{2,3},{3,2},{4,5},{5,4},{6,7},{7,6},{8,9},{9,8},{10,11... | collective-permute-start | bytes 786440 | tf_op jit(solution)/shard_map/ppermute | solution.py:251
  25.7 10.9 %collective-permute-start.4 = (bf16[192,1024]{1,0:T(8,128)(2,1)S(1)}, bf16[192,1024]{1,0:T(8,128)(2,1)S(1)}, u32[]{:S(2)}, u32[]{:S(2)}) collective-permute-start(bf16[192,1024]{1,0:T(8,128)(2,1)S(1)} %get-tuple-element.40), channel_id=1, source_target_pairs={{0,2},{2,4},{4,6},{6,0},{1,3},{3,5},{5,7},{7,1},{8,10},{10,12},{12... | collective-permute-start | bytes 1179656 | tf_op jit(solution)/shard_map/ppermute | solution.py:245
  25.8 10.8 %collective-permute-start.5 = (bf16[192,1024]{1,0:T(8,128)(2,1)S(1)}, bf16[192,1024]{1,0:T(8,128)(2,1)S(1)}, u32[]{:S(2)}, u32[]{:S(2)}) collective-permute-start(bf16[192,1024]{1,0:T(8,128)(2,1)S(1)} %get-tuple-element.41), channel_id=1, source_target_pairs={{0,6},{2,0},{4,2},{6,4},{1,7},{3,1},{5,3},{7,5},{8,14},{10,8},{12,... | collective-permute-start | bytes 1179656 | tf_op jit(solution)/shard_map/ppermute | solution.py:245
  29.1 7.6 %collective-permute-start.6 = (bf16[128,1024]{1,0:T(8,128)(2,1)S(1)}, bf16[128,1024]{1,0:T(8,128)(2,1)S(1)}, u32[]{:S(2)}, u32[]{:S(2)}) collective-permute-start(bf16[128,1024]{1,0:T(8,128)(2,1)S(1)} %collective-permute-done.1.refs_0_.refs_2_), channel_id=1, source_target_pairs={{0,193},{1,64},{64,1},{65,128},{128,65},{129,192},{192,129},{193,0... | collective-permute-start | bytes 786440 | tf_op jit(solution)/shard_map/ppermute | solution.py:255
  37.2 10.2 %collective-permute-start.7 = (bf16[192,1024]{1,0:T(8,128)(2,1)S(1)}, bf16[192,1024]{1,0:T(8,128)(2,1)S(1)}, u32[]{:S(2)}, u32[]{:S(2)}) collective-permute-start(bf16[192,1024]{1,0:T(8,128)(2,1)S(1)} %get-tuple-element.42.refs_6_), channel_id=1, source_target_pairs={{0,2},{2,4},{4,6},{6,0},{1,3},{3,5},{5,7},{7,1},{8,10},{10,12},{12... | collective-permute-start | bytes 1179656 | tf_op jit(solution)/shard_map/ppermute | solution.py:245
  37.3 10.1 %collective-permute-start.8 = (bf16[192,1024]{1,0:T(8,128)(2,1)S(1)}, bf16[192,1024]{1,0:T(8,128)(2,1)S(1)}, u32[]{:S(2)}, u32[]{:S(2)}) collective-permute-start(bf16[192,1024]{1,0:T(8,128)(2,1)S(1)} %get-tuple-element.43.refs_7_), channel_id=1, source_target_pairs={{0,6},{2,0},{4,2},{6,4},{1,7},{3,1},{5,3},{7,5},{8,14},{10,8},{12,... | collective-permute-start | bytes 1179656 | tf_op jit(solution)/shard_map/ppermute | solution.py:245
  40.6 2.2 %copy-start = (bf16[1,4096,512]{2,1,0:T(8,128)(2,1)S(1)}, bf16[1,4096,512]{2,1,0:T(8,128)(2,1)}, u32[]{:S(2)}) copy-start(bf16[1,4096,512]{2,1,0:T(8,128)(2,1)} %param.8) | copy-start | bytes 12582916
  42.8 2.2 %copy-start.2 = (bf16[1,4096,512]{2,1,0:T(8,128)(2,1)S(1)}, bf16[1,4096,512]{2,1,0:T(8,128)(2,1)}, u32[]{:S(2)}) copy-start(bf16[1,4096,512]{2,1,0:T(8,128)(2,1)} %param.9) | copy-start | bytes 12582916
  44.9 6.4 %copy-start.1 = (bf16[1,4096,512]{2,1,0:T(8,128)(2,1)S(1)}, bf16[1,4096,512]{2,1,0:T(8,128)(2,1)}, u32[]{:S(2)}) copy-start(bf16[1,4096,512]{2,1,0:T(8,128)(2,1)} %param.8) | copy-start | bytes 12582916
  44.9 6.4 %copy-start.3 = (bf16[1,4096,512]{2,1,0:T(8,128)(2,1)S(1)}, bf16[1,4096,512]{2,1,0:T(8,128)(2,1)}, u32[]{:S(2)}) copy-start(bf16[1,4096,512]{2,1,0:T(8,128)(2,1)} %param.9) | copy-start | bytes 12582916
  48.0 7.3 %collective-permute-start.9 = (bf16[64,1024]{1,0:T(8,128)(2,1)S(1)}, bf16[64,1024]{1,0:T(8,128)(2,1)S(1)}, u32[]{:S(2)}, u32[]{:S(2)}) collective-permute-start(bf16[64,1024]{1,0:T(8,128)(2,1)S(1)} %get-tuple-element.45.refs_13_), channel_id=1, source_target_pairs={{0,2},{2,4},{4,6},{6,0},{1,3},{3,5},{5,7},{7,1},{8,10},{10,12},{12... | collective-permute-start | bytes 393224 | tf_op jit(solution)/shard_map/ppermute | solution.py:245
  48.1 7.3 %copy-start.5 = (bf16[1,1,512,512]{3,2,1,0:T(8,128)(2,1)S(1)}, bf16[1,1,512,512]{3,2,1,0:T(8,128)(2,1)}, u32[]{:S(2)}) copy-start(bf16[1,1,512,512]{3,2,1,0:T(8,128)(2,1)} %param.10) | copy-start | bytes 1572868
  48.1 7.3 %copy-start.6 = (bf16[1,1,512,512]{3,2,1,0:T(8,128)(2,1)S(1)}, bf16[1,1,512,512]{3,2,1,0:T(8,128)(2,1)}, u32[]{:S(2)}) copy-start(bf16[1,1,512,512]{3,2,1,0:T(8,128)(2,1)} %param.11) | copy-start | bytes 1572868
  48.1 7.2 %collective-permute-start.10 = (bf16[64,1024]{1,0:T(8,128)(2,1)S(1)}, bf16[64,1024]{1,0:T(8,128)(2,1)S(1)}, u32[]{:S(2)}, u32[]{:S(2)}) collective-permute-start(bf16[64,1024]{1,0:T(8,128)(2,1)S(1)} %get-tuple-element.46.refs_14_), channel_id=1, source_target_pairs={{0,6},{2,0},{4,2},{6,4},{1,7},{3,1},{5,3},{7,5},{8,14},{10,8},{12,... | collective-permute-start | bytes 393224 | tf_op jit(solution)/shard_map/ppermute | solution.py:245
  61.9 17.1 %collective-permute-start.15 = (bf16[512,2048]{1,0:T(8,128)(2,1)S(1)}, bf16[512,2048]{1,0:T(8,128)(2,1)S(1)}, u32[]{:S(2)}, u32[]{:S(2)}) collective-permute-start(bf16[512,2048]{1,0:T(8,128)(2,1)S(1)} %shard_map.113), channel_id=1, source_target_pairs={{0,8},{8,0},{1,9},{9,1},{2,10},{10,2},{3,11},{11,3},{4,12},{12,4},... | collective-permute-start | bytes 6291464 | tf_op jit(solution)/shard_map/ppermute | solution.py:248
  62.0 17.0 %collective-permute-start.16 = (bf16[512,1024]{1,0:T(8,128)(2,1)S(1)}, bf16[512,1024]{1,0:T(8,128)(2,1)S(1)}, u32[]{:S(2)}, u32[]{:S(2)}) collective-permute-start(bf16[512,1024]{1,0:T(8,128)(2,1)S(1)} %get-tuple-element.49.act_ref.refs_2_), channel_id=1, source_target_pairs={{0,8},{8,0},{1,9},{9,1},{2,10},{10,2},{3,11},{11,3},{4,12},{12,4},... | collective-permute-start | bytes 3145736 | tf_op jit(solution)/shard_map/ppermute | solution.py:248
  64.7 7.1 %collective-permute-start.11 = (bf16[64,1024]{1,0:T(8,128)(2,1)S(1)}, bf16[64,1024]{1,0:T(8,128)(2,1)S(1)}, u32[]{:S(2)}, u32[]{:S(2)}) collective-permute-start(bf16[64,1024]{1,0:T(8,128)(2,1)S(1)} %get-tuple-element.50), channel_id=1, source_target_pairs={{0,2},{2,4},{4,6},{6,0},{1,3},{3,5},{5,7},{7,1},{8,10},{10,12},{12... | collective-permute-start | bytes 393224 | tf_op jit(solution)/shard_map/ppermute | solution.py:245
  64.8 7.1 %collective-permute-start.12 = (bf16[64,1024]{1,0:T(8,128)(2,1)S(1)}, bf16[64,1024]{1,0:T(8,128)(2,1)S(1)}, u32[]{:S(2)}, u32[]{:S(2)}) collective-permute-start(bf16[64,1024]{1,0:T(8,128)(2,1)S(1)} %get-tuple-element.51), channel_id=1, source_target_pairs={{0,6},{2,0},{4,2},{6,4},{1,7},{3,1},{5,3},{7,5},{8,14},{10,8},{12,... | collective-permute-start | bytes 393224 | tf_op jit(solution)/shard_map/ppermute | solution.py:245
  72.5 11.8 %collective-permute-start.13 = (bf16[192,1024]{1,0:T(8,128)(2,1)S(1)}, bf16[192,1024]{1,0:T(8,128)(2,1)S(1)}, u32[]{:S(2)}, u32[]{:S(2)}) collective-permute-start(bf16[192,1024]{1,0:T(8,128)(2,1)S(1)} %get-tuple-element.53.refs_4_), channel_id=1, source_target_pairs={{0,2},{2,4},{4,6},{6,0},{1,3},{3,5},{5,7},{7,1},{8,10},{10,12},{12... | collective-permute-start | bytes 1179656 | tf_op jit(solution)/shard_map/ppermute | solution.py:245
  72.5 11.8 %collective-permute-start.14 = (bf16[192,1024]{1,0:T(8,128)(2,1)S(1)}, bf16[192,1024]{1,0:T(8,128)(2,1)S(1)}, u32[]{:S(2)}, u32[]{:S(2)}) collective-permute-start(bf16[192,1024]{1,0:T(8,128)(2,1)S(1)} %get-tuple-element.54.refs_5_), channel_id=1, source_target_pairs={{0,6},{2,0},{4,2},{6,4},{1,7},{3,1},{5,3},{7,5},{8,14},{10,8},{12,... | collective-permute-start | bytes 1179656 | tf_op jit(solution)/shard_map/ppermute | solution.py:245
  85.1 23.6 %collective-permute-start.30 = (bf16[512,1024]{1,0:T(8,128)(2,1)S(1)}, bf16[512,1024]{1,0:T(8,128)(2,1)S(1)}, u32[]{:S(2)}, u32[]{:S(2)}) collective-permute-start(bf16[512,1024]{1,0:T(8,128)(2,1)S(1)} %get-tuple-element.71), channel_id=1, source_target_pairs={{0,16},{8,56},{16,32},{24,8},{32,48},{40,24},{48,0},{56,40},{1,17}... | collective-permute-start | bytes 3145736 | tf_op jit(solution)/shard_map/ppermute | solution.py:260
  86.7 10.8 %collective-permute-start.17 = (bf16[192,1024]{1,0:T(8,128)(2,1)S(1)}, bf16[192,1024]{1,0:T(8,128)(2,1)S(1)}, u32[]{:S(2)}, u32[]{:S(2)}) collective-permute-start(bf16[192,1024]{1,0:T(8,128)(2,1)S(1)} %get-tuple-element.60), channel_id=1, source_target_pairs={{0,2},{2,4},{4,6},{6,0},{1,3},{3,5},{5,7},{7,1},{8,10},{10,12},{12... | collective-permute-start | bytes 1179656 | tf_op jit(solution)/shard_map/ppermute | solution.py:245
  86.9 10.7 %collective-permute-start.18 = (bf16[192,1024]{1,0:T(8,128)(2,1)S(1)}, bf16[192,1024]{1,0:T(8,128)(2,1)S(1)}, u32[]{:S(2)}, u32[]{:S(2)}) collective-permute-start(bf16[192,1024]{1,0:T(8,128)(2,1)S(1)} %get-tuple-element.61), channel_id=1, source_target_pairs={{0,6},{2,0},{4,2},{6,4},{1,7},{3,1},{5,3},{7,5},{8,14},{10,8},{12,... | collective-permute-start | bytes 1179656 | tf_op jit(solution)/shard_map/ppermute | solution.py:245
  90.0 7.6 %collective-permute-start.19 = (bf16[128,1024]{1,0:T(8,128)(2,1)S(1)}, bf16[128,1024]{1,0:T(8,128)(2,1)S(1)}, u32[]{:S(2)}, u32[]{:S(2)}) collective-permute-start(bf16[128,1024]{1,0:T(8,128)(2,1)S(1)} %get-tuple-element.62), channel_id=1, source_target_pairs={{0,193},{1,64},{64,1},{65,128},{128,65},{129,192},{192,129},{193,0... | collective-permute-start | bytes 786440 | tf_op jit(solution)/shard_map/ppermute | solution.py:255
  98.3 9.7 %collective-permute-start.20 = (bf16[192,1024]{1,0:T(8,128)(2,1)S(1)}, bf16[192,1024]{1,0:T(8,128)(2,1)S(1)}, u32[]{:S(2)}, u32[]{:S(2)}) collective-permute-start(bf16[192,1024]{1,0:T(8,128)(2,1)S(1)} %get-tuple-element.63), channel_id=1, source_target_pairs={{0,2},{2,4},{4,6},{6,0},{1,3},{3,5},{5,7},{7,1},{8,10},{10,12},{12... | collective-permute-start | bytes 1179656 | tf_op jit(solution)/shard_map/ppermute | solution.py:245
  98.4 9.6 %collective-permute-start.21 = (bf16[192,1024]{1,0:T(8,128)(2,1)S(1)}, bf16[192,1024]{1,0:T(8,128)(2,1)S(1)}, u32[]{:S(2)}, u32[]{:S(2)}) collective-permute-start(bf16[192,1024]{1,0:T(8,128)(2,1)S(1)} %get-tuple-element.64), channel_id=1, source_target_pairs={{0,6},{2,0},{4,2},{6,4},{1,7},{3,1},{5,3},{7,5},{8,14},{10,8},{12,... | collective-permute-start | bytes 1179656 | tf_op jit(solution)/shard_map/ppermute | solution.py:245
  101.6 6.4 %collective-permute-start.22 = (bf16[128,1024]{1,0:T(8,128)(2,1)S(1)}, bf16[128,1024]{1,0:T(8,128)(2,1)S(1)}, u32[]{:S(2)}, u32[]{:S(2)}) collective-permute-start(bf16[128,1024]{1,0:T(8,128)(2,1)S(1)} %get-tuple-element.65), channel_id=1, source_target_pairs={{0,1},{1,0},{2,3},{3,2},{4,5},{5,4},{6,7},{7,6},{8,9},{9,8},{10,11... | collective-permute-start | bytes 786440 | tf_op jit(solution)/shard_map/ppermute | solution.py:251
  109.6 26.6 %collective-permute-start.31 = (bf16[512,1024]{1,0:T(8,128)(2,1)S(1)}, bf16[512,1024]{1,0:T(8,128)(2,1)S(1)}, u32[]{:S(2)}, u32[]{:S(2)}) collective-permute-start(bf16[512,1024]{1,0:T(8,128)(2,1)S(1)} %get-tuple-element.72), channel_id=1, source_target_pairs={{0,16},{8,56},{16,32},{24,8},{32,48},{40,24},{48,0},{56,40},{1,17}... | collective-permute-start | bytes 3145736 | tf_op jit(solution)/shard_map/ppermute | solution.py:260
  110.9 25.3 %collective-permute-start.32 = (bf16[512,1024]{1,0:T(8,128)(2,1)S(1)}, bf16[512,1024]{1,0:T(8,128)(2,1)S(1)}, u32[]{:S(2)}, u32[]{:S(2)}) collective-permute-start(bf16[512,1024]{1,0:T(8,128)(2,1)S(1)} %get-tuple-element.73), channel_id=1, source_target_pairs={{0,24},{8,48},{16,40},{24,0},{32,56},{40,16},{48,8},{56,32},{1,25}... | collective-permute-start | bytes 3145736 | tf_op jit(solution)/shard_map/ppermute | solution.py:260
  110.9 8.9 %collective-permute-start.23 = (bf16[128,1024]{1,0:T(8,128)(2,1)S(1)}, bf16[128,1024]{1,0:T(8,128)(2,1)S(1)}, u32[]{:S(2)}, u32[]{:S(2)}) collective-permute-start(bf16[128,1024]{1,0:T(8,128)(2,1)S(1)} %get-tuple-element.66), channel_id=1, source_target_pairs={{0,2},{2,4},{4,6},{6,0},{1,3},{3,5},{5,7},{7,1},{8,10},{10,12},{12... | collective-permute-start | bytes 786440 | tf_op jit(solution)/shard_map/ppermute | solution.py:245
  110.9 8.9 %collective-permute-start.24 = (bf16[128,1024]{1,0:T(8,128)(2,1)S(1)}, bf16[128,1024]{1,0:T(8,128)(2,1)S(1)}, u32[]{:S(2)}, u32[]{:S(2)}) collective-permute-start(bf16[128,1024]{1,0:T(8,128)(2,1)S(1)} %get-tuple-element.67), channel_id=1, source_target_pairs={{0,6},{2,0},{4,2},{6,4},{1,7},{3,1},{5,3},{7,5},{8,14},{10,8},{12,... | collective-permute-start | bytes 786440 | tf_op jit(solution)/shard_map/ppermute | solution.py:245
  114.2 9.5 %collective-permute-start.25 = (bf16[128,1024]{1,0:T(8,128)(2,1)S(1)}, bf16[128,1024]{1,0:T(8,128)(2,1)S(1)}, u32[]{:S(2)}, u32[]{:S(2)}) collective-permute-start(bf16[128,1024]{1,0:T(8,128)(2,1)S(1)} %get-tuple-element.68.refs_2_), channel_id=1, source_target_pairs={{0,193},{1,64},{64,1},{65,128},{128,65},{129,192},{192,129},{193,0... | collective-permute-start | bytes 786440 | tf_op jit(solution)/shard_map/ppermute | solution.py:255
  124.4 9.0 %collective-permute-start.26 = (bf16[128,1024]{1,0:T(8,128)(2,1)S(1)}, bf16[128,1024]{1,0:T(8,128)(2,1)S(1)}, u32[]{:S(2)}, u32[]{:S(2)}) collective-permute-start(bf16[128,1024]{1,0:T(8,128)(2,1)S(1)} %shard_map.118.refs_0_), channel_id=1, source_target_pairs={{0,1},{1,0},{2,3},{3,2},{4,5},{5,4},{6,7},{7,6},{8,9},{9,8},{10,11... | collective-permute-start | bytes 786440 | tf_op jit(solution)/shard_map/ppermute | solution.py:251
  133.9 9.3 %collective-permute-start.29 = (bf16[128,1024]{1,0:T(8,128)(2,1)S(1)}, bf16[128,1024]{1,0:T(8,128)(2,1)S(1)}, u32[]{:S(2)}, u32[]{:S(2)}) collective-permute-start(bf16[128,1024]{1,0:T(8,128)(2,1)S(1)} %shard_map.119.refs_0_), channel_id=1, source_target_pairs={{0,6},{2,0},{4,2},{6,4},{1,7},{3,1},{5,3},{7,5},{8,14},{10,8},{12,... | collective-permute-start | bytes 786440 | tf_op jit(solution)/shard_map/ppermute | solution.py:245
  135.2 10.7 %collective-permute-start.28 = (bf16[128,1024]{1,0:T(8,128)(2,1)S(1)}, bf16[128,1024]{1,0:T(8,128)(2,1)S(1)}, u32[]{:S(2)}, u32[]{:S(2)}) collective-permute-start(bf16[128,1024]{1,0:T(8,128)(2,1)S(1)} %shard_map.119.refs_0_), channel_id=1, source_target_pairs={{0,4},{2,6},{4,0},{6,2},{1,5},{3,7},{5,1},{7,3},{8,12},{10,14},{12... | collective-permute-start | bytes 786440 | tf_op jit(solution)/shard_map/ppermute | solution.py:245
  135.2 14.9 %collective-permute-start.27 = (bf16[128,1024]{1,0:T(8,128)(2,1)S(1)}, bf16[128,1024]{1,0:T(8,128)(2,1)S(1)}, u32[]{:S(2)}, u32[]{:S(2)}) collective-permute-start(bf16[128,1024]{1,0:T(8,128)(2,1)S(1)} %shard_map.119.refs_0_), channel_id=1, source_target_pairs={{0,2},{2,4},{4,6},{6,0},{1,3},{3,5},{5,7},{7,1},{8,10},{10,12},{12... | collective-permute-start | bytes 786440 | tf_op jit(solution)/shard_map/ppermute | solution.py:245
  150.1 1.0 copy-start.7

commit v5 on v4

--- a/solution.py
+++ b/solution.py
@@ -174,16 +174,18 @@
         else:
             out_ref, up_ref, down_ref = refs[-3:]
             out_ref[...] = sums.astype(dtype)
-            n_sec, blk = first
-            at = block_of(info, 3, n_sec) * blk
-            up_ref[...] = out_ref[pl.ds(pl.multiple_of(at, blk), blk // 2), :]
-            down_ref[...] = out_ref[pl.ds(pl.multiple_of(at + blk // 2, blk // 2), blk // 2), :]
+            n_sec, blk, blocks = first
+            mid = blk // 2
+            for i, which in enumerate(blocks):
+                at = block_of(info, which, n_sec) * blk
+                up_ref[i * mid : (i + 1) * mid, :] = out_ref[pl.ds(pl.multiple_of(at, blk), mid), :]
+                down_ref[i * mid : (i + 1) * mid, :] = out_ref[pl.ds(pl.multiple_of(at + mid, mid), mid), :]
 
     weight = pl.BlockSpec((UNIT, cols), lambda i, info: (unit(i, info), 0))
     block = pl.BlockSpec((total, UNIT), lambda i, info: (0, i))
     out_specs, out_shape = [block], [jax.ShapeDtypeStruct((total, n * UNIT), dtype)]
     if first is not None:
-        rows = first[1] // 2
+        rows = first[1] // 2 * len(first[2])
         out_specs += [pl.BlockSpec((rows, UNIT), lambda i, info: (0, i))] * 2
         out_shape += [jax.ShapeDtypeStruct((rows, n * UNIT), dtype)] * 2
     return pl.pallas_call(
@@ -200,21 +202,18 @@
     )(info, act, wk, wv, *after)
 
 
-def pair_grads(kept, got, act, act_other, info, after):
+def pair_grads(kept, got, act, act_other, info, blocks, after=()):
     width = act.shape[1]
-    counts = (2, 1, 1)
-    half = kept.shape[1] // sum(counts)
+    half = kept.shape[1] // XS
 
     def body(info, kept_ref, got_ref, act_ref, other_ref, *refs):
-        at = 0
-        for ref, count in zip(refs[-3:], counts):
-            for j in range(count):
-                here = slice(at, at + half)
+        for ref, group in zip(refs, blocks):
+            for j, at in enumerate(group):
+                here = slice(at * half, (at + 1) * half)
                 term = t_dot(kept_ref[:, here], act_ref[...]) + t_dot(got_ref[:, here], other_ref[...])
                 ref[j * half : (j + 1) * half, :] = term.astype(bf16)
-                at += half
-
-    out = [jax.ShapeDtypeStruct((count * half, width), bf16) for count in counts]
+
+    out = [jax.ShapeDtypeStruct((len(group) * half, width), bf16) for group in blocks]
     return small(body, [kept, got, act, act_other], out, info, after)
 
 
@@ -253,6 +252,10 @@
     def cross(v):
         n = 2 * n_sec
         return lax.ppermute(v, ("section", "low"), [(z, (z + (1 if z % 2 else -1)) % n) for z in range(n)])
+
+    def jump(v, k):
+        n = 2 * n_sec
+        return lax.ppermute(v, ("section", "low"), [(z, (z + (-2 * k if z % 2 else 2 * k)) % n) for z in range(n)])
 
     def shift_y(v, change=False):
         n = 2 * XS
@@ -284,23 +287,25 @@
         def both(up, down):
             return shift_x(up, 1), shift_x(down, -1)
 
-        def with_half(block, up, down, after=()):
-            out = jax.ShapeDtypeStruct((blk + mid, quarter), bf16)
-
-            def body(info, block_ref, up_ref, down_ref, up_out, down_out):
+        def with_halves(block, ups, downs, after=()):
+            out = jax.ShapeDtypeStruct((blk + mid * len(ups), quarter), bf16)
+
+            def body(info, block_ref, *refs):
+                up_out, down_out = refs[-2:]
                 up_out[:blk] = block_ref[...]
-                up_out[blk:] = up_ref[:mid]
                 down_out[:blk] = block_ref[...]
-                down_out[blk:] = down_ref[mid:blk]
-
-            return small(body, [block, up, down], [out, out], info, after)
-
-        b1 = cross(mine)
-        b2 = swap_low(b1)
+                for i in range(len(ups)):
+                    at = blk + i * mid
+                    up_out[at : at + mid] = refs[i][:mid]
+                    down_out[at : at + mid] = refs[len(ups) + i][mid:blk]
+
+            return small(body, [block, *ups, *downs], [out, out], info, after)
+
+        b1, b2 = cross(mine), jump(mine, -1)
         u1, d1 = both(b1, b1)
+        u2, d2 = both(b2, b2)
         b3 = cross(b2)
-        u2, d2 = both(*with_half(b2, u1, d1))
-        out3 = with_half(b3, u2, d2)
+        out3 = with_halves(b3, (u1, u2), (d1, d2))
         u3, d3 = both(*out3)
         rows = [None] * XS
 
@@ -317,7 +322,7 @@
         u4, d4 = both(*out4)
         beside = [(1, parts(u1, u2, u3)), (3, parts(d1, d2, d3))]
         acc, rows[1], rows[3] = project(beside, enc, wk, wv, acc, info, n_sec, out4)
-        last = [(u2, [(blk, mid, 1, 0)]), (d2, [(blk, mid, 1, mid)]), (u3, [(blk, mid, 2, 0)]), (d3, [(blk, mid, 2, mid)])]
+        last = [(u3, [(blk, mid, 1, 0), (blk + mid, mid, 2, 0)]), (d3, [(blk, mid, 1, mid), (blk + mid, mid, 2, mid)])]
         last += [(u4, [(0, mid, 3, 0)]), (d4, [(0, mid, 3, mid)])]
         asked = (queries[0, 0], ctx_grad[0, 0])
         context, act, rows[2] = project([(2, last)], enc, wk, wv, acc, info, n_sec, queries=asked)
@@ -347,65 +352,65 @@
         sent = pack(False)
         got = swap_core(sent)
 
-        far, up, down = partial_grad(act, wk, wv, info, (2,), bf16, first=(n_sec, blk))
-        up, down = both(up, down)
-        (near,) = partial_grad(act, wk, wv, info, (3, 1), f32, (far,))
+        far, up, down = partial_grad(act, wk, wv, info, (2,), bf16, first=(n_sec, blk, (3, 0)))
+        halves = both(up, down)
+        (near,) = partial_grad(act, wk, wv, info, (3, 1), bf16, (far,))
         kept = pack(True, (near,))
+        (far_y,) = pair_grads(kept, got, act, act_other, info, [(2,)], (near,))
         (keep,) = partial_grad(act, wk, wv, info, (0,), f32, (near,))
-        def stage(done, sent, following, up, down, carried, after=(), through=None):
-            ins, outs = [up, down], []
-            if done is not None:
-                ins.append((keep, pl.BlockSpec((blk, quarter), lambda i, info: (block_of(info, done, n_sec), 0))))
+
+        def rows_of(v, which):
+            return v, pl.BlockSpec((blk, v.shape[1]), lambda i, info: (block_of(info, which, n_sec), 0))
+
+        def stage(done, sent, ahead, after=(), through=()):
+            ins, outs = [], []
+            for which, (up, down), _, more in done:
+                ins += [rows_of(keep, which), up, down, *more]
                 outs.append(jax.ShapeDtypeStruct((blk, quarter), bf16))
-            if carried is not None:
-                ins.append(carried)
-            if sent is not None:
-                ins.append((near, pl.BlockSpec((blk, 2 * quarter), lambda i, info: (block_of(info, sent, n_sec), 0))))
-                size = blk if following is None else blk + mid
-                outs += [jax.ShapeDtypeStruct((size, quarter), bf16)] * 2
-            if following is not None:
-                ins.append((far, pl.BlockSpec((blk, quarter), lambda i, info: (block_of(info, following, n_sec), 0))))
-
-            if through is not None:
-                ins.append(through)
-                outs.append(through)
+            for which, (up, down), _ in sent:
+                ins += [rows_of(near, which), up, down]
+            ins += [rows_of(far, which) for which in ahead] + list(through)
+            size = blk * len(sent) + mid * len(ahead)
+            outs += [jax.ShapeDtypeStruct((size, quarter), bf16)] * (2 if size else 0) + list(through)
 
             def body(info, *refs):
-                refs = list(refs)
-                if through is not None:
-                    refs.pop()[...] = refs.pop(len(ins) - 1)[...]
-                up_ref, down_ref = refs.pop(0), refs.pop(0)
-                if done is not None:
-                    sums = refs.pop(0)[...] + up_ref[:blk].astype(f32) + down_ref[:blk].astype(f32)
-                    if carried is not None:
+                refs, out_refs = list(refs[: len(ins)]), list(refs[len(ins) :])
+                for _, _, at, more in done:
+                    sums = refs.pop(0)[...]
+                    for _ in range(2):
+                        sums = sums + refs.pop(0)[at : at + blk].astype(f32)
+                    for _ in more:
                         sums = sums + refs.pop(0)[...].astype(f32)
-                near_ref = refs.pop(0) if sent is not None else None
-                far_ref = refs.pop(0) if following is not None else None
-                if done is not None:
-                    refs.pop(0)[...] = sums.astype(bf16)
-                if sent is not None:
-                    up_out, down_out = refs
-                    at = blk if done is not None else 0
+                    out_refs.pop(0)[...] = sums.astype(bf16)
+                to = 0
+                if size:
+                    up_out, down_out = out_refs.pop(0), out_refs.pop(0)
+                for _, _, at in sent:
+                    near_ref, up_ref, down_ref = (refs.pop(0) for _ in range(3))
                     half_up, half_down = up_ref[at : at + mid].astype(f32), down_ref[at : at + mid].astype(f32)
-                    up_out[:mid] = (near_ref[:mid, :quarter] + half_up).astype(bf16)
-                    up_out[mid:blk] = near_ref[mid:, :quarter].astype(bf16)
-                    down_out[:mid] = near_ref[:mid, quarter:].astype(bf16)
-                    down_out[mid:blk] = (near_ref[mid:, quarter:] + half_down).astype(bf16)
-                    if following is not None:
-                        up_out[blk:] = far_ref[:mid]
-                        down_out[blk:] = far_ref[mid:]
+                    up_out[to : to + mid] = (near_ref[:mid, :quarter].astype(f32) + half_up).astype(bf16)
+                    up_out[to + mid : to + blk] = near_ref[mid:, :quarter]
+                    down_out[to : to + mid] = near_ref[:mid, quarter:]
+                    down_out[to + mid : to + blk] = (near_ref[mid:, quarter:].astype(f32) + half_down).astype(bf16)
+                    to += blk
+                for _ in ahead:
+                    far_ref = refs.pop(0)
+                    up_out[to : to + mid] = far_ref[:mid]
+                    down_out[to : to + mid] = far_ref[mid:]
+                    to += mid
+                for ref, out_ref in zip(refs, out_refs):
+                    out_ref[...] = ref[...]
 
             return small(body, ins, outs, info, after)
 
-        out = stage(None, 3, 2, up, down, None)
-        up, down = both(*out)
-        near_y, far_y, keep_y = pair_grads(kept, got, act, act_other, info, out)
-        total, up, down, far_y = stage(3, 2, 1, up, down, None, through=far_y)
+        up, down, far_y = stage([], [(3, halves, 0)], [2, 1], through=[far_y])
         got_y = shift_y(far_y)
-        (up, down), carried = both(up, down), cross(total)
-        total, up, down = stage(2, 1, 0, up, down, carried)
-        (up, down), carried = both(up, down), swap_low(total)
-        total, up, down = stage(1, 0, None, up, down, carried)
+        near_y, keep_y = pair_grads(kept, got, act, act_other, info, [(0, 1), (3,)], (up,))
+        side = both(up, down)
+        total3, up, down = stage([(3, side, 0, [])], [(2, side, blk), (1, side, blk + mid)], [])
+        carried = cross(total3)
+        side = both(up, down)
+        total2, total1, up, down = stage([(2, side, 0, [carried]), (1, side, blk, [])], [(0, halves, mid)], [])
 
         def add_y(info, near_ref, got_ref, same_ref, other_ref):
             here = pl.ds(pl.multiple_of(info[CORE] * half, half), half)
@@ -413,10 +418,12 @@
             same_ref[...] = (near_ref[here, :].astype(f32) + got_ref[...].astype(f32)).astype(bf16)
             other_ref[...] = near_ref[there, :]
 
-        same_y, other_y = small(add_y, [near_y, got_y], [keep_y, keep_y], info, (total,))
-        in_y = shift_y(same_y), shift_y(other_y, True)
-        (up, down), carried = both(up, down), cross(total)
-        (mine,) = stage(0, None, None, up, down, carried)
+        same_y, other_y = small(add_y, [near_y, got_y], [keep_y, keep_y], info, (total1,))
+        same_y = shift_y(same_y)
+        side = both(up, down)
+        carried = [cross(total1), jump(total2, 1)]
+        mine, other_y = stage([(0, side, 0, carried)], [], [], through=[other_y])
+        in_y = same_y, shift_y(other_y, True)
         other = swap_low(mine)
         part = mine
 
@@ -424,7 +431,10 @@
             out_ref[...] = (one_ref[...].astype(f32) + two_ref[...].astype(f32)).astype(bf16)
 
         (final,) = small(add_two, [mine, other], [part], info)
-        gathered = [final] + [shift_x(final, k) for k in range(1, XS)]
+        below, above = both(final, final)
+        half_part = jax.ShapeDtypeStruct((mid, quarter), bf16)
+        passed = small(cut, [below, above], [half_part, half_part], info)
+        top, low = both(*passed)
 
         def finish(info, keep_ref, one_ref, two_ref, key_ref, value_ref):
             sums = keep_ref[...].astype(f32) + one_ref[...].astype(f32) + two_ref[...].astype(f32)
@@ -435,17 +445,36 @@
                 value_ref[:, h * HEAD : (h + 1) * HEAD] = sums[:, at + HEAD : at + 2 * HEAD]
 
         shard = jax.ShapeDtypeStruct((half, local_width), bf16)
-        key_weight_grad, value_weight_grad = small(finish, [keep_y, *in_y], [shard, shard], info)
-        key_weight_grad, value_weight_grad = key_weight_grad[None], value_weight_grad[None]
+        key_weight_grad, value_weight_grad = small(finish, [keep_y, *in_y], [shard, shard], info, (passed[0],))
+
         def place(info, *refs):
-            for k in range(XS):
+            for ref, k in zip(refs[:-1], (0, 1, 3)):
                 at = mod4(info[X] - k) * quarter
-                refs[-1][:, pl.ds(pl.multiple_of(at, quarter), quarter)] = refs[k][...]
-
-        (enc_grad,) = small(place, gathered, [jax.ShapeDtypeStruct((blk, width), bf16)], info, (key_weight_grad,))
+                refs[-1][:, pl.ds(pl.multiple_of(at, quarter), quarter)] = ref[...]
+
+        whole_rows = jax.ShapeDtypeStruct((blk, width), bf16)
+        (enc_grad,) = small(place, [final, below, above], [whole_rows], info, (key_weight_grad,))
+
+        def place_last(info, top_ref, low_ref, _, out_ref):
+            out_ref[:mid] = top_ref[...]
+            out_ref[mid:] = low_ref[...]
+
+        enc_grad = pl.pallas_call(
+            place_last,
+            grid_spec=pltpu.PrefetchScalarGridSpec(
+                num_scalar_prefetch=1,
+                grid=(1,),
+                in_specs=[whole(half_part), whole(half_part), ANYWHERE],
+                out_specs=pl.BlockSpec((blk, quarter), lambda i, info: (0, mod4(info[X] - 2))),
+            ),
+            out_shape=whole_rows,
+            input_output_aliases={3: 0},
+            compiler_params=params(8),
+            cost_estimate=LIGHT,
+        )(info, top, low, enc_grad)
         enc_grad = enc_grad[None]
 
-        return (context, enc_grad, key_weight_grad, value_weight_grad)
+        return (context, enc_grad, key_weight_grad[None], value_weight_grad[None])
 
     return shards
 

time: 156 us -> 149 us (0.955); the launches traced: 153 us -> 148 us
  waiting for transfers between devices: 57.8 us -> 53.5 us
  starting transfers between devices: 48.8 us -> 47.2 us
    ppermute x4, starting transfers between devices: 13.8 us -> 3.56 us  [cross(): lax.ppermute(v, ('section', 'low'), [(z, (z + (1 if z % 2 else -1)) % n)...]
    ppermute x4, waiting for transfers between devices: 20.1 us -> 12.2 us  [cross(): lax.ppermute(v, ('section', 'low'), [(z, (z + (1 if z % 2 else -1)) % n)...]
    ppermute x0 -> x2, starting transfers between devices: none -> 6.87 us  [jump(): lax.ppermute(v, ('section', 'low'), [(z, (z + (-2 * k if z % 2 else 2 * k...]
    ppermute x0 -> x2, waiting for transfers between devices: none -> 6.71 us  [jump(): lax.ppermute(v, ('section', 'low'), [(z, (z + (-2 * k if z % 2 else 2 * k...]
    ppermute x3 -> x1, waiting for transfers between devices: 15.2 us -> 8.57 us  [swap_low(): return lax.ppermute(v, 'low', [(0, 1), (1, 0)])]
    ppermute x21 -> x20, waiting for transfers between devices: 22.4 us -> 26.1 us  [shift_x(): return lax.ppermute(v, 'x', [(i, (i + k) % XS) for i in range(XS)])]
    ppermute x21 -> x20, starting transfers between devices: 31.3 us -> 32.6 us  [shift_x(): return lax.ppermute(v, 'x', [(i, (i + k) % XS) for i in range(XS)])]
  transfers between devices with their start and end apart: 33 -> 32, of which waited for: 13 -> 13; matrix products, arithmetic and copies ran while one was open for 0% -> 0% of each run, Pallas kernels for 17% -> 19%
where the time goes in v5:
time: 149 us; the launch traced here: 148 us
  waiting for transfers between devices  53.5 us (36%)
  starting transfers between devices  47.2 us (32%)
  Pallas kernels  38.4 us (26%)
  local copies, waits for them, and re-layouts  6.58 us (4%)
  between operations  2.21 us (1%)
    ppermute x20, starting transfers between devices, shift_x(): return lax.ppermute(v, 'x', [(i, (i + k) % XS) for i in range(XS)])  32.6 us
    ppermute x20, waiting for transfers between devices, shift_x(): return lax.ppermute(v, 'x', [(i, (i + k) % XS) for i in range(XS)])  26.1 us
    pallas_call x15, Pallas kernels, small(): pl.pallas_call(run, grid_spec=pltpu.PrefetchScalarGridSpec(num_scalar_pre...  16.9 us
    pallas_call x3, Pallas kernels, project(): pl.pallas_call(body, grid_spec=pltpu.PrefetchScalarGridSpec(num_scalar_pr...  12.2 us
    ppermute x4, waiting for transfers between devices, cross(): lax.ppermute(v, ('section', 'low'), [(z, (z + (1 if z % 2 else -1)) % n)...  12.2 us
    ppermute x1, waiting for transfers between devices, swap_low(): return lax.ppermute(v, 'low', [(0, 1), (1, 0)])  8.57 us
    pallas_call x3, Pallas kernels, partial_grad(): pl.pallas_call(body, grid_spec=pltpu.PrefetchScalarGridSpec(num_scalar_pr...  8.12 us
    ppermute x2, starting transfers between devices, jump(): lax.ppermute(v, ('section', 'low'), [(z, (z + (-2 * k if z % 2 else 2 * k...  6.87 us
  transfers between devices with their start and end apart: 32, of which 13 were waited for; matrix products, arithmetic and copies ran while one was open for 0% of the time, Pallas kernels for 19%

profile of v5, /device:TPU:8, one launch (start us, length us, event | category | flops | bytes accessed | tf_op | source)
XLA Modules:
  0.0 147.9 jit_solution(6543460083290560104)
XLA Ops:
  0.6 1.1 dynamic-slice_bitcast_fusion
  1.7 6.4 %collective-permute-start = (bf16[128,1024]{1,0:T(8,128)(2,1)S(1)}, bf16[128,1024]{1,0:T(8,128)(2,1)S(1)}, u32[]{:S(2)}, u32[]{:S(2)}) collective-permute-start(bf16[128,1024]{1,0:T(8,128)(2,1)S(1)} %dynamic-slice_bitcast_fusion), channel_id=1, source_target_pairs={{0,192},{1,65},{64,0},{65,129},{128,64},{129,193},{192,128},{193,1... | collective-permute-start | bytes 786440 | tf_op jit(solution)/shard_map/ppermute | solution.py:258
  8.1 6.7 %collective-permute-done.refs_2_ = bf16[128,1024]{1,0:T(8,128)(2,1)S(1)} collective-permute-done((bf16[128,1024]{1,0:T(8,128)(2,1)S(1)}, bf16[128,1024]{1,0:T(8,128)(2,1)S(1)}, u32[]{:S(2)}, u32[]{:S(2)}) %collective-permute-start) | collective-permute-done | bytes 262176 | tf_op jit(solution)/shard_map/ppermute | solution.py:258
  14.8 2.9 %collective-permute-start.1 = (bf16[128,1024]{1,0:T(8,128)(2,1)S(1)}, bf16[128,1024]{1,0:T(8,128)(2,1)S(1)}, u32[]{:S(2)}, u32[]{:S(2)}) collective-permute-start(bf16[128,1024]{1,0:T(8,128)(2,1)S(1)} %collective-permute-done.refs_2_), channel_id=1, source_target_pairs={{0,193},{1,64},{64,1},{65,128},{128,65},{129,192},{192,129},{193,0... | collective-permute-start | bytes 786440 | tf_op jit(solution)/shard_map/ppermute | solution.py:254
  17.7 1.5 %collective-permute-start.4 = (bf16[128,1024]{1,0:T(8,128)(2,1)S(1)}, bf16[128,1024]{1,0:T(8,128)(2,1)S(1)}, u32[]{:S(2)}, u32[]{:S(2)}) collective-permute-start(bf16[128,1024]{1,0:T(8,128)(2,1)S(1)} %collective-permute-done.refs_2_), channel_id=1, source_target_pairs={{0,2},{2,4},{4,6},{6,0},{1,3},{3,5},{5,7},{7,1},{8,10},{10,12},{12... | collective-permute-start | bytes 786440 | tf_op jit(solution)/shard_map/ppermute | solution.py:244
  19.2 1.7 %collective-permute-start.6 = (bf16[128,1024]{1,0:T(8,128)(2,1)S(1)}, bf16[128,1024]{1,0:T(8,128)(2,1)S(1)}, u32[]{:S(2)}, u32[]{:S(2)}) collective-permute-start(bf16[128,1024]{1,0:T(8,128)(2,1)S(1)} %collective-permute-done.refs_2_), channel_id=1, source_target_pairs={{0,6},{2,0},{4,2},{6,4},{1,7},{3,1},{5,3},{7,5},{8,14},{10,8},{12,... | collective-permute-start | bytes 786440 | tf_op jit(solution)/shard_map/ppermute | solution.py:244
  21.0 0.9 collective-permute-start.3
  21.9 2.3 %collective-permute-start.5 = (bf16[128,1024]{1,0:T(8,128)(2,1)S(1)}, bf16[128,1024]{1,0:T(8,128)(2,1)S(1)}, u32[]{:S(2)}, u32[]{:S(2)}) collective-permute-start(bf16[128,1024]{1,0:T(8,128)(2,1)S(1)} %collective-permute-done.2.refs_1_), channel_id=1, source_target_pairs={{0,6},{2,0},{4,2},{6,4},{1,7},{3,1},{5,3},{7,5},{8,14},{10,8},{12,... | collective-permute-start | bytes 786440 | tf_op jit(solution)/shard_map/ppermute | solution.py:244
  25.6 2.4 %collective-permute-done.4.refs_2_.refs_3_ = bf16[128,1024]{1,0:T(8,128)(2,1)S(1)} collective-permute-done((bf16[128,1024]{1,0:T(8,128)(2,1)S(1)}, bf16[128,1024]{1,0:T(8,128)(2,1)S(1)}, u32[]{:S(2)}, u32[]{:S(2)}) %collective-permute-start.4) | collective-permute-done | bytes 262176 | tf_op jit(solution)/shard_map/ppermute | solution.py:244
  28.0 0.3 collective-permute-done.6.refs_4_.refs_6_
  28.3 2.7 %collective-permute-done.3.refs_1_.refs_2_ = bf16[128,1024]{1,0:T(8,128)(2,1)S(1)} collective-permute-done((bf16[128,1024]{1,0:T(8,128)(2,1)S(1)}, bf16[128,1024]{1,0:T(8,128)(2,1)S(1)}, u32[]{:S(2)}, u32[]{:S(2)}) %collective-permute-start.3) | collective-permute-done | bytes 262176 | tf_op jit(solution)/shard_map/ppermute | solution.py:244
  30.9 0.1 collective-permute-done.5.refs_3_.refs_5_
  31.1 0.6 shard_map.102
  31.7 1.6 %collective-permute-start.7 = (bf16[256,1024]{1,0:T(8,128)(2,1)S(1)}, bf16[256,1024]{1,0:T(8,128)(2,1)S(1)}, u32[]{:S(2)}, u32[]{:S(2)}) collective-permute-start(bf16[256,1024]{1,0:T(8,128)(2,1)S(1)} %get-tuple-element.39.refs_6_), channel_id=1, source_target_pairs={{0,2},{2,4},{4,6},{6,0},{1,3},{3,5},{5,7},{7,1},{8,10},{10,12},{12... | collective-permute-start | bytes 1572872 | tf_op jit(solution)/shard_map/ppermute | solution.py:244
  33.3 1.7 %collective-permute-start.8 = (bf16[256,1024]{1,0:T(8,128)(2,1)S(1)}, bf16[256,1024]{1,0:T(8,128)(2,1)S(1)}, u32[]{:S(2)}, u32[]{:S(2)}) collective-permute-start(bf16[256,1024]{1,0:T(8,128)(2,1)S(1)} %get-tuple-element.40.refs_7_), channel_id=1, source_target_pairs={{0,6},{2,0},{4,2},{6,4},{1,7},{3,1},{5,3},{7,5},{8,14},{10,8},{12,... | collective-permute-start | bytes 1572872 | tf_op jit(solution)/shard_map/ppermute | solution.py:244
  35.0 2.2 %copy-done = bf16[1,4096,512]{2,1,0:T(8,128)(2,1)S(1)} copy-done((bf16[1,4096,512]{2,1,0:T(8,128)(2,1)S(1)}, bf16[1,4096,512]{2,1,0:T(8,128)(2,1)}, u32[]{:S(2)}) %copy-start) | copy-done | bytes 4194328
  37.2 2.2 %copy-done.2 = bf16[1,4096,512]{2,1,0:T(8,128)(2,1)S(1)} copy-done((bf16[1,4096,512]{2,1,0:T(8,128)(2,1)S(1)}, bf16[1,4096,512]{2,1,0:T(8,128)(2,1)}, u32[]{:S(2)}) %copy-start.2) | copy-done | bytes 4194328
  39.4 2.4 %shard_map.103 = (f32[512,1024]{1,0:T(8,128)S(1)}, bf16[512,1024]{1,0:T(8,128)(2,1)S(1)}) custom-call(s32[7]{0:T(128)S(1)} %stack.25.info, bf16[128,4096]{1,0:T(8,128)(2,1)S(1)} %bitcast.30, bf16[128,1024]{1,0:T(8,128)(2,1)S(1)} %collective-permute-done.2.refs_1_, bf16[128,1024]{1,0:T(8,128)(2,1)S(1)} %collective-permute-done.refs_2_, ...), custom_call_target="tpu_custom_call" | custom-call | flops 1 | bytes 1 | tf_op jit(solution)/shard_map/pallas_call | solution.py:108
  41.8 2.3 %collective-permute-done.7.refs_0_.refs_4_.refs_1_ = bf16[256,1024]{1,0:T(8,128)(2,1)S(1)} collective-permute-done((bf16[256,1024]{1,0:T(8,128)(2,1)S(1)}, bf16[256,1024]{1,0:T(8,128)(2,1)S(1)}, u32[]{:S(2)}, u32[]{:S(2)}) %collective-permute-start.7) | collective-permute-done | bytes 524320 | tf_op jit(solution)/shard_map/ppermute | solution.py:244
  44.1 0.6 shard_map.104
  44.7 3.0 %collective-permute-start.10 = (bf16[64,1024]{1,0:T(8,128)(2,1)S(1)}, bf16[64,1024]{1,0:T(8,128)(2,1)S(1)}, u32[]{:S(2)}, u32[]{:S(2)}) collective-permute-start(bf16[64,1024]{1,0:T(8,128)(2,1)S(1)} %get-tuple-element.43.refs_14_), channel_id=1, source_target_pairs={{0,6},{2,0},{4,2},{6,4},{1,7},{3,1},{5,3},{7,5},{8,14},{10,8},{12,... | collective-permute-start | bytes 393224 | tf_op jit(solution)/shard_map/ppermute | solution.py:244
  47.7 4.0 %shard_map.105 = (f32[512,1024]{1,0:T(8,128)S(1)}, bf16[512,1024]{1,0:T(8,128)(2,1)S(1)}, bf16[512,1024]{1,0:T(8,128)(2,1)S(1)}) custom-call(s32[7]{0:T(128)S(1)} %stack.25.info, bf16[128,4096]{1,0:T(8,128)(2,1)S(1)} %bitcast.31, bf16[128,4096]{1,0:T(8,128)(2,1)S(1)} %bitcast.32, bf16[128,1024]{1,0:T(8,128)(2,1)S(1)} %collective-permute-done.3.refs_1_.refs_2_, ...), custom_call_target="tpu_custom_call" | custom-call | flops 1 | bytes 1 | tf_op jit(solution)/shard_map/pallas_call | solution.py:108
  51.8 2.1 %collective-permute-done.9.refs_3_ = bf16[64,1024]{1,0:T(8,128)(2,1)S(1)} collective-permute-done((bf16[64,1024]{1,0:T(8,128)(2,1)S(1)}, bf16[64,1024]{1,0:T(8,128)(2,1)S(1)}, u32[]{:S(2)}, u32[]{:S(2)}) %collective-permute-start.9) | collective-permute-done | bytes 131104 | tf_op jit(solution)/shard_map/ppermute | solution.py:244
  53.9 5.7 %shard_map.106 = (bf16[512,512]{1,0:T(8,128)(2,1)}, bf16[512,1024]{1,0:T(8,128)(2,1)S(1)}, bf16[512,1024]{1,0:T(8,128)(2,1)S(1)}) custom-call(s32[7]{0:T(128)S(1)} %stack.25.info, bf16[128,4096]{1,0:T(8,128)(2,1)S(1)} %bitcast.33, bf16[256,1024]{1,0:T(8,128)(2,1)S(1)} %collective-permute-done.7.refs_0_.refs_4_.refs_1_, ...), custom_call_target="tpu_custom_call" | custom-call | flops 1 | bytes 1 | tf_op jit(solution)/shard_map/pallas_call | solution.py:108
  59.6 0.8 shard_map.111
  60.4 0.1 collective-permute-start.13
  60.5 0.5 collective-permute-start.14
  61.0 2.2 %shard_map.107 = (bf16[512,1024]{1,0:T(8,128)(2,1)S(1)}, bf16[128,1024]{1,0:T(8,128)(2,1)S(1)}, bf16[128,1024]{1,0:T(8,128)(2,1)S(1)}) custom-call(s32[7]{0:T(128)S(1)} %stack.25.info, bf16[512,1024]{1,0:T(8,128)(2,1)S(1)} %get-tuple-element.46.act_ref.refs_2_, bf16[4096,512]{1,0:T(8,128)(2,1)S(1)} %bitcast.20, bf16[4096,512]{1,0:T(8,128)(2,1)S(1)} %bitcast.27), custom_call_target="tpu_custom_call" | custom-call | flops 1 | bytes 1 | tf_op jit(solution)/shard_map/pallas_call | solution.py:191
  63.3 3.2 %collective-permute-start.12 = (bf16[128,1024]{1,0:T(8,128)(2,1)S(1)}, bf16[128,1024]{1,0:T(8,128)(2,1)S(1)}, u32[]{:S(2)}, u32[]{:S(2)}) collective-permute-start(bf16[128,1024]{1,0:T(8,128)(2,1)S(1)} %get-tuple-element.49), channel_id=1, source_target_pairs={{0,6},{2,0},{4,2},{6,4},{1,7},{3,1},{5,3},{7,5},{8,14},{10,8},{12,... | collective-permute-start | bytes 786440 | tf_op jit(solution)/shard_map/ppermute | solution.py:244
  66.6 3.7 %shard_map.108.refs_0_.refs_4_.refs_3_.refs_6_.refs_7_ = bf16[512,2048]{1,0:T(8,128)(2,1)S(1)} custom-call(s32[7]{0:T(128)S(1)} %stack.25.info, bf16[512,1024]{1,0:T(8,128)(2,1)S(1)} %get-tuple-element.46.act_ref.refs_2_, bf16[4096,512]{1,0:T(8,128)(2,1)S(1)} %bitcast.21, bf16[4096,512]{1,0:T(8,128)(2,1)S(1)} %bitcast.28, ...), custom_call_target="tpu_custom_call" | custom-call | flops 1 | bytes 1 | tf_op jit(solution)/shard_map/pallas_call | solution.py:191
  70.3 0.8 shard_map.110.refs_0_
  71.1 1.8 %shard_map.112.refs_5_ = bf16[512,1024]{1,0:T(8,128)(2,1)S(1)} custom-call(s32[7]{0:T(128)S(1)} %stack.25.info, bf16[512,2048]{1,0:T(8,128)(2,1)S(1)} %shard_map.110.refs_0_, bf16[512,2048]{1,0:T(8,128)(2,1)S(1)} %collective-permute-done.13.refs_1_, bf16[512,1024]{1,0:T(8,128)(2,1)S(1)} %get-tuple-element.46.act_ref.refs_2_, ...), custom_call_target="tpu_custom_call" | custom-call | flops 1 | bytes 1 | tf_op jit(solution)/shard_map/pallas_call | solution.py:227
  72.9 0.7 shard_map.113
  73.7 3.2 %collective-permute-start.16 = (bf16[256,1024]{1,0:T(8,128)(2,1)S(1)}, bf16[256,1024]{1,0:T(8,128)(2,1)S(1)}, u32[]{:S(2)}, u32[]{:S(2)}) collective-permute-start(bf16[256,1024]{1,0:T(8,128)(2,1)S(1)} %get-tuple-element.55), channel_id=1, source_target_pairs={{0,6},{2,0},{4,2},{6,4},{1,7},{3,1},{5,3},{7,5},{8,14},{10,8},{12,... | collective-permute-start | bytes 1572872 | tf_op jit(solution)/shard_map/ppermute | solution.py:244
  76.9 1.6 %collective-permute-start.24 = (bf16[512,1024]{1,0:T(8,128)(2,1)S(1)}, bf16[512,1024]{1,0:T(8,128)(2,1)S(1)}, u32[]{:S(2)}, u32[]{:S(2)}) collective-permute-start(bf16[512,1024]{1,0:T(8,128)(2,1)S(1)} %get-tuple-element.64), channel_id=1, source_target_pairs={{0,16},{8,56},{16,32},{24,8},{32,48},{40,24},{48,0},{56,40},{1,17}... | collective-permute-start | bytes 3145736 | tf_op jit(solution)/shard_map/ppermute | solution.py:263
  78.5 2.2 %shard_map.109.refs_0_.refs_4_ = f32[512,1024]{1,0:T(8,128)S(1)} custom-call(s32[7]{0:T(128)S(1)} %stack.25.info, bf16[512,1024]{1,0:T(8,128)(2,1)S(1)} %get-tuple-element.46.act_ref.refs_2_, bf16[4096,512]{1,0:T(8,128)(2,1)S(1)} %bitcast.22, bf16[4096,512]{1,0:T(8,128)(2,1)S(1)} %bitcast.29, ...), custom_call_target="tpu_custom_call" | custom-call | flops 1 | bytes 1 | tf_op jit(solution)/shard_map/pallas_call | solution.py:191
  80.7 7.6 %collective-permute-done.15.refs_1_.refs_4_.refs_7_ = bf16[256,1024]{1,0:T(8,128)(2,1)S(1)} collective-permute-done((bf16[256,1024]{1,0:T(8,128)(2,1)S(1)}, bf16[256,1024]{1,0:T(8,128)(2,1)S(1)}, u32[]{:S(2)}, u32[]{:S(2)}) %collective-permute-start.15) | collective-permute-done | bytes 524320 | tf_op jit(solution)/shard_map/ppermute | solution.py:244
  88.3 0.8 shard_map.114
  89.0 0.5 collective-permute-start.17
  89.6 2.8 %collective-permute-start.18 = (bf16[256,1024]{1,0:T(8,128)(2,1)S(1)}, bf16[256,1024]{1,0:T(8,128)(2,1)S(1)}, u32[]{:S(2)}, u32[]{:S(2)}) collective-permute-start(bf16[256,1024]{1,0:T(8,128)(2,1)S(1)} %get-tuple-element.57), channel_id=1, source_target_pairs={{0,6},{2,0},{4,2},{6,4},{1,7},{3,1},{5,3},{7,5},{8,14},{10,8},{12,... | collective-permute-start | bytes 1572872 | tf_op jit(solution)/shard_map/ppermute | solution.py:244
  92.3 0.3 collective-permute-start.19
  92.6 7.3 %collective-permute-done.19.refs_3_ = bf16[128,1024]{1,0:T(8,128)(2,1)S(1)} collective-permute-done((bf16[128,1024]{1,0:T(8,128)(2,1)S(1)}, bf16[128,1024]{1,0:T(8,128)(2,1)S(1)}, u32[]{:S(2)}, u32[]{:S(2)}) %collective-permute-start.19) | collective-permute-done | bytes 262176 | tf_op jit(solution)/shard_map/ppermute | solution.py:254
  99.9 2.8 %collective-permute-done.17.refs_1_.refs_5_ = bf16[256,1024]{1,0:T(8,128)(2,1)S(1)} collective-permute-done((bf16[256,1024]{1,0:T(8,128)(2,1)S(1)}, bf16[256,1024]{1,0:T(8,128)(2,1)S(1)}, u32[]{:S(2)}, u32[]{:S(2)}) %collective-permute-start.17) | collective-permute-done | bytes 524320 | tf_op jit(solution)/shard_map/ppermute | solution.py:244
  102.8 0.8 shard_map.115
  103.6 0.9 collective-permute-start.20
  104.5 2.4 %collective-permute-start.21 = (bf16[128,1024]{1,0:T(8,128)(2,1)S(1)}, bf16[128,1024]{1,0:T(8,128)(2,1)S(1)}, u32[]{:S(2)}, u32[]{:S(2)}) collective-permute-start(bf16[128,1024]{1,0:T(8,128)(2,1)S(1)} %get-tuple-element.60), channel_id=1, source_target_pairs={{0,6},{2,0},{4,2},{6,4},{1,7},{3,1},{5,3},{7,5},{8,14},{10,8},{12,... | collective-permute-start | bytes 786440 | tf_op jit(solution)/shard_map/ppermute | solution.py:244
  106.9 0.3 collective-permute-start.22
  107.2 0.5 collective-permute-start.23
  107.7 4.0 %shard_map.116 = (bf16[1024,1024]{1,0:T(8,128)(2,1)S(1)}, bf16[512,1024]{1,0:T(8,128)(2,1)S(1)}) custom-call(s32[7]{0:T(128)S(1)} %stack.25.info, bf16[512,2048]{1,0:T(8,128)(2,1)S(1)} %shard_map.110.refs_0_, bf16[512,2048]{1,0:T(8,128)(2,1)S(1)} %collective-permute-done.13.refs_1_, bf16[512,1024]{1,0:T(8,128)(2,1)S(1)} %get-tuple-element.46.act_ref.refs_2_, ...), custom_call_target="tpu_custom_call" | custom-call | flops 1 | bytes 1 | tf_op jit(solution)/shard_map/pallas_call | solution.py:227
  111.7 0.8 shard_map.117
  112.5 1.6 %collective-permute-start.30 = (bf16[512,1024]{1,0:T(8,128)(2,1)S(1)}, bf16[512,1024]{1,0:T(8,128)(2,1)S(1)}, u32[]{:S(2)}, u32[]{:S(2)}) collective-permute-start(bf16[512,1024]{1,0:T(8,128)(2,1)S(1)} %get-tuple-element.70), channel_id=1, source_target_pairs={{0,16},{8,56},{16,32},{24,8},{32,48},{40,24},{48,0},{56,40},{1,17}... | collective-permute-start | bytes 3145736 | tf_op jit(solution)/shard_map/ppermute | solution.py:263
  114.2 4.9 %collective-permute-done.22.refs_3_ = bf16[128,1024]{1,0:T(8,128)(2,1)S(1)} collective-permute-done((bf16[128,1024]{1,0:T(8,128)(2,1)S(1)}, bf16[128,1024]{1,0:T(8,128)(2,1)S(1)}, u32[]{:S(2)}, u32[]{:S(2)}) %collective-permute-start.22) | collective-permute-done | bytes 262176 | tf_op jit(solution)/shard_map/ppermute | solution.py:254
  119.1 0.7 shard_map.118
  119.8 0.3 collective-permute-start.31
  120.1 8.6 %collective-permute-done.25.refs_1_ = bf16[128,1024]{1,0:T(8,128)(2,1)S(1)} collective-permute-done((bf16[128,1024]{1,0:T(8,128)(2,1)S(1)}, bf16[128,1024]{1,0:T(8,128)(2,1)S(1)}, u32[]{:S(2)}, u32[]{:S(2)}) %collective-permute-start.25) | collective-permute-done | bytes 262176 | tf_op jit(solution)/shard_map/ppermute | solution.py:250
  128.7 0.6 shard_map.119.refs_0_
  129.4 3.2 %collective-permute-start.27 = (bf16[128,1024]{1,0:T(8,128)(2,1)S(1)}, bf16[128,1024]{1,0:T(8,128)(2,1)S(1)}, u32[]{:S(2)}, u32[]{:S(2)}) collective-permute-start(bf16[128,1024]{1,0:T(8,128)(2,1)S(1)} %shard_map.119.refs_0_), channel_id=1, source_target_pairs={{0,6},{2,0},{4,2},{6,4},{1,7},{3,1},{5,3},{7,5},{8,14},{10,8},{12,... | collective-permute-start | bytes 786440 | tf_op jit(solution)/shard_map/ppermute | solution.py:244
  132.6 5.7 %collective-permute-done.26.refs_0_.refs_1_ = bf16[128,1024]{1,0:T(8,128)(2,1)S(1)} collective-permute-done((bf16[128,1024]{1,0:T(8,128)(2,1)S(1)}, bf16[128,1024]{1,0:T(8,128)(2,1)S(1)}, u32[]{:S(2)}, u32[]{:S(2)}) %collective-permute-start.26) | collective-permute-done | bytes 262176 | tf_op jit(solution)/shard_map/ppermute | solution.py:244
  138.3 0.6 shard_map.120
  139.0 3.2 %collective-permute-start.29 = (bf16[64,1024]{1,0:T(8,128)(2,1)S(1)}, bf16[64,1024]{1,0:T(8,128)(2,1)S(1)}, u32[]{:S(2)}, u32[]{:S(2)}) collective-permute-start(bf16[64,1024]{1,0:T(8,128)(2,1)S(1)} %get-tuple-element.68), channel_id=1, source_target_pairs={{0,6},{2,0},{4,2},{6,4},{1,7},{3,1},{5,3},{7,5},{8,14},{10,8},{12,... | collective-permute-start | bytes 393224 | tf_op jit(solution)/shard_map/ppermute | solution.py:244
  142.2 1.8 %shard_map.121 = (bf16[512,512]{1,0:T(8,128)(2,1)}, bf16[512,512]{1,0:T(8,128)(2,1)}) custom-call(s32[7]{0:T(128)S(1)} %stack.25.info, bf16[512,1024]{1,0:T(8,128)(2,1)S(1)} %get-tuple-element.69.refs_0_, bf16[512,1024]{1,0:T(8,128)(2,1)S(1)} %collective-permute-done.30.refs_1_, bf16[512,1024]{1,0:T(8,128)(2,1)S(1)} %collective-permute-done.31.refs_2_, ...), custom_call_target="tpu_custom_call" | custom-call | flops 1 | bytes 1 | tf_op jit(solution)/shard_map/pallas_call | solution.py:227
  144.0 1.0 copy-done.7
  145.1 1.6 %shard_map.122._ = bf16[128,4096]{1,0:T(8,128)(2,1)} custom-call(s32[7]{0:T(128)S(1)} %stack.25.info, bf16[128,1024]{1,0:T(8,128)(2,1)S(1)} %shard_map.119.refs_0_, bf16[128,1024]{1,0:T(8,128)(2,1)S(1)} %collective-permute-done.26.refs_0_.refs_1_, bf16[128,1024]{1,0:T(8,128)(2,1)S(1)} %collective-permute-done.27.refs_1_.refs_2_, bf16[512,512]{1,0:T(8,128)(2,1)S(1)} %copy-done.7), custom_call_target="tpu_custom_call" | custom-call | flops 1 | bytes 1 | tf_op jit(solution)/shard_map/pallas_call | solution.py:227
  146.6 1.3 shard_map.123
  (40 shorter events, 0.5 us)
Async XLA Ops:
  0.6 34.4 %copy-start.4 = (bf16[1,128,4096]{2,1,0:T(8,128)(2,1)S(1)}, bf16[1,128,4096]{2,1,0:T(8,128)(2,1)}, u32[]{:S(2)}) copy-start(bf16[1,128,4096]{2,1,0:T(8,128)(2,1)} %param.7) | copy-start | bytes 3145732
  1.7 13.1 %collective-permute-start = (bf16[128,1024]{1,0:T(8,128)(2,1)S(1)}, bf16[128,1024]{1,0:T(8,128)(2,1)S(1)}, u32[]{:S(2)}, u32[]{:S(2)}) collective-permute-start(bf16[128,1024]{1,0:T(8,128)(2,1)S(1)} %dynamic-slice_bitcast_fusion), channel_id=1, source_target_pairs={{0,192},{1,65},{64,0},{65,129},{128,64},{129,193},{192,128},{193,1... | collective-permute-start | bytes 786440 | tf_op jit(solution)/shard_map/ppermute | solution.py:258
  8.1 12.9 %collective-permute-start.2 = (bf16[128,1024]{1,0:T(8,128)(2,1)S(1)}, bf16[128,1024]{1,0:T(8,128)(2,1)S(1)}, u32[]{:S(2)}, u32[]{:S(2)}) collective-permute-start(bf16[128,1024]{1,0:T(8,128)(2,1)S(1)} %dynamic-slice_bitcast_fusion), channel_id=1, source_target_pairs={{0,193},{1,64},{64,1},{65,128},{128,65},{129,192},{192,129},{193,0... | collective-permute-start | bytes 786440 | tf_op jit(solution)/shard_map/ppermute | solution.py:254
  14.8 10.8 %collective-permute-start.1 = (bf16[128,1024]{1,0:T(8,128)(2,1)S(1)}, bf16[128,1024]{1,0:T(8,128)(2,1)S(1)}, u32[]{:S(2)}, u32[]{:S(2)}) collective-permute-start(bf16[128,1024]{1,0:T(8,128)(2,1)S(1)} %collective-permute-done.refs_2_), channel_id=1, source_target_pairs={{0,193},{1,64},{64,1},{65,128},{128,65},{129,192},{192,129},{193,0... | collective-permute-start | bytes 786440 | tf_op jit(solution)/shard_map/ppermute | solution.py:254
  17.7 10.2 %collective-permute-start.4 = (bf16[128,1024]{1,0:T(8,128)(2,1)S(1)}, bf16[128,1024]{1,0:T(8,128)(2,1)S(1)}, u32[]{:S(2)}, u32[]{:S(2)}) collective-permute-start(bf16[128,1024]{1,0:T(8,128)(2,1)S(1)} %collective-permute-done.refs_2_), channel_id=1, source_target_pairs={{0,2},{2,4},{4,6},{6,0},{1,3},{3,5},{5,7},{7,1},{8,10},{10,12},{12... | collective-permute-start | bytes 786440 | tf_op jit(solution)/shard_map/ppermute | solution.py:244
  19.2 9.0 %collective-permute-start.6 = (bf16[128,1024]{1,0:T(8,128)(2,1)S(1)}, bf16[128,1024]{1,0:T(8,128)(2,1)S(1)}, u32[]{:S(2)}, u32[]{:S(2)}) collective-permute-start(bf16[128,1024]{1,0:T(8,128)(2,1)S(1)} %collective-permute-done.refs_2_), channel_id=1, source_target_pairs={{0,6},{2,0},{4,2},{6,4},{1,7},{3,1},{5,3},{7,5},{8,14},{10,8},{12,... | collective-permute-start | bytes 786440 | tf_op jit(solution)/shard_map/ppermute | solution.py:244
  21.0 10.0 %collective-permute-start.3 = (bf16[128,1024]{1,0:T(8,128)(2,1)S(1)}, bf16[128,1024]{1,0:T(8,128)(2,1)S(1)}, u32[]{:S(2)}, u32[]{:S(2)}) collective-permute-start(bf16[128,1024]{1,0:T(8,128)(2,1)S(1)} %collective-permute-done.2.refs_1_), channel_id=1, source_target_pairs={{0,2},{2,4},{4,6},{6,0},{1,3},{3,5},{5,7},{7,1},{8,10},{10,12},{12... | collective-permute-start | bytes 786440 | tf_op jit(solution)/shard_map/ppermute | solution.py:244
  21.9 9.2 %collective-permute-start.5 = (bf16[128,1024]{1,0:T(8,128)(2,1)S(1)}, bf16[128,1024]{1,0:T(8,128)(2,1)S(1)}, u32[]{:S(2)}, u32[]{:S(2)}) collective-permute-start(bf16[128,1024]{1,0:T(8,128)(2,1)S(1)} %collective-permute-done.2.refs_1_), channel_id=1, source_target_pairs={{0,6},{2,0},{4,2},{6,4},{1,7},{3,1},{5,3},{7,5},{8,14},{10,8},{12,... | collective-permute-start | bytes 786440 | tf_op jit(solution)/shard_map/ppermute | solution.py:244
  31.7 12.4 %collective-permute-start.7 = (bf16[256,1024]{1,0:T(8,128)(2,1)S(1)}, bf16[256,1024]{1,0:T(8,128)(2,1)S(1)}, u32[]{:S(2)}, u32[]{:S(2)}) collective-permute-start(bf16[256,1024]{1,0:T(8,128)(2,1)S(1)} %get-tuple-element.39.refs_6_), channel_id=1, source_target_pairs={{0,2},{2,4},{4,6},{6,0},{1,3},{3,5},{5,7},{7,1},{8,10},{10,12},{12... | collective-permute-start | bytes 1572872 | tf_op jit(solution)/shard_map/ppermute | solution.py:244
  33.3 10.9 %collective-permute-start.8 = (bf16[256,1024]{1,0:T(8,128)(2,1)S(1)}, bf16[256,1024]{1,0:T(8,128)(2,1)S(1)}, u32[]{:S(2)}, u32[]{:S(2)}) collective-permute-start(bf16[256,1024]{1,0:T(8,128)(2,1)S(1)} %get-tuple-element.40.refs_7_), channel_id=1, source_target_pairs={{0,6},{2,0},{4,2},{6,4},{1,7},{3,1},{5,3},{7,5},{8,14},{10,8},{12,... | collective-permute-start | bytes 1572872 | tf_op jit(solution)/shard_map/ppermute | solution.py:244
  35.0 2.2 %copy-start = (bf16[1,4096,512]{2,1,0:T(8,128)(2,1)S(1)}, bf16[1,4096,512]{2,1,0:T(8,128)(2,1)}, u32[]{:S(2)}) copy-start(bf16[1,4096,512]{2,1,0:T(8,128)(2,1)} %param.8) | copy-start | bytes 12582916
  37.2 2.2 %copy-start.2 = (bf16[1,4096,512]{2,1,0:T(8,128)(2,1)S(1)}, bf16[1,4096,512]{2,1,0:T(8,128)(2,1)}, u32[]{:S(2)}) copy-start(bf16[1,4096,512]{2,1,0:T(8,128)(2,1)} %param.9) | copy-start | bytes 12582916
  39.4 8.3 %copy-start.1 = (bf16[1,4096,512]{2,1,0:T(8,128)(2,1)S(1)}, bf16[1,4096,512]{2,1,0:T(8,128)(2,1)}, u32[]{:S(2)}) copy-start(bf16[1,4096,512]{2,1,0:T(8,128)(2,1)} %param.8) | copy-start | bytes 12582916
  39.4 8.3 %copy-start.3 = (bf16[1,4096,512]{2,1,0:T(8,128)(2,1)S(1)}, bf16[1,4096,512]{2,1,0:T(8,128)(2,1)}, u32[]{:S(2)}) copy-start(bf16[1,4096,512]{2,1,0:T(8,128)(2,1)} %param.9) | copy-start | bytes 12582916
  44.7 7.0 %collective-permute-start.10 = (bf16[64,1024]{1,0:T(8,128)(2,1)S(1)}, bf16[64,1024]{1,0:T(8,128)(2,1)S(1)}, u32[]{:S(2)}, u32[]{:S(2)}) collective-permute-start(bf16[64,1024]{1,0:T(8,128)(2,1)S(1)} %get-tuple-element.43.refs_14_), channel_id=1, source_target_pairs={{0,6},{2,0},{4,2},{6,4},{1,7},{3,1},{5,3},{7,5},{8,14},{10,8},{12,... | collective-permute-start | bytes 393224 | tf_op jit(solution)/shard_map/ppermute | solution.py:244
  47.7 6.2 %copy-start.5 = (bf16[1,1,512,512]{3,2,1,0:T(8,128)(2,1)S(1)}, bf16[1,1,512,512]{3,2,1,0:T(8,128)(2,1)}, u32[]{:S(2)}) copy-start(bf16[1,1,512,512]{3,2,1,0:T(8,128)(2,1)} %param.10) | copy-start | bytes 1572868
  47.7 6.2 %copy-start.6 = (bf16[1,1,512,512]{3,2,1,0:T(8,128)(2,1)S(1)}, bf16[1,1,512,512]{3,2,1,0:T(8,128)(2,1)}, u32[]{:S(2)}) copy-start(bf16[1,1,512,512]{3,2,1,0:T(8,128)(2,1)} %param.11) | copy-start | bytes 1572868
  47.7 6.2 %collective-permute-start.9 = (bf16[64,1024]{1,0:T(8,128)(2,1)S(1)}, bf16[64,1024]{1,0:T(8,128)(2,1)S(1)}, u32[]{:S(2)}, u32[]{:S(2)}) collective-permute-start(bf16[64,1024]{1,0:T(8,128)(2,1)S(1)} %get-tuple-element.42.refs_13_), channel_id=1, source_target_pairs={{0,2},{2,4},{4,6},{6,0},{1,3},{3,5},{5,7},{7,1},{8,10},{10,12},{12... | collective-permute-start | bytes 393224 | tf_op jit(solution)/shard_map/ppermute | solution.py:244
  60.4 10.6 %collective-permute-start.13 = (bf16[512,2048]{1,0:T(8,128)(2,1)S(1)}, bf16[512,2048]{1,0:T(8,128)(2,1)S(1)}, u32[]{:S(2)}, u32[]{:S(2)}) collective-permute-start(bf16[512,2048]{1,0:T(8,128)(2,1)S(1)} %shard_map.111), channel_id=1, source_target_pairs={{0,8},{8,0},{1,9},{9,1},{2,10},{10,2},{3,11},{11,3},{4,12},{12,4},... | collective-permute-start | bytes 6291464 | tf_op jit(solution)/shard_map/ppermute | solution.py:247
  60.5 10.5 %collective-permute-start.14 = (bf16[512,1024]{1,0:T(8,128)(2,1)S(1)}, bf16[512,1024]{1,0:T(8,128)(2,1)S(1)}, u32[]{:S(2)}, u32[]{:S(2)}) collective-permute-start(bf16[512,1024]{1,0:T(8,128)(2,1)S(1)} %get-tuple-element.46.act_ref.refs_2_), channel_id=1, source_target_pairs={{0,8},{8,0},{1,9},{9,1},{2,10},{10,2},{3,11},{11,3},{4,12},{12,4},... | collective-permute-start | bytes 3145736 | tf_op jit(solution)/shard_map/ppermute | solution.py:247
  63.2 9.7 %collective-permute-start.11 = (bf16[128,1024]{1,0:T(8,128)(2,1)S(1)}, bf16[128,1024]{1,0:T(8,128)(2,1)S(1)}, u32[]{:S(2)}, u32[]{:S(2)}) collective-permute-start(bf16[128,1024]{1,0:T(8,128)(2,1)S(1)} %get-tuple-element.48), channel_id=1, source_target_pairs={{0,2},{2,4},{4,6},{6,0},{1,3},{3,5},{5,7},{7,1},{8,10},{10,12},{12... | collective-permute-start | bytes 786440 | tf_op jit(solution)/shard_map/ppermute | solution.py:244
  63.3 9.6 %collective-permute-start.12 = (bf16[128,1024]{1,0:T(8,128)(2,1)S(1)}, bf16[128,1024]{1,0:T(8,128)(2,1)S(1)}, u32[]{:S(2)}, u32[]{:S(2)}) collective-permute-start(bf16[128,1024]{1,0:T(8,128)(2,1)S(1)} %get-tuple-element.49), channel_id=1, source_target_pairs={{0,6},{2,0},{4,2},{6,4},{1,7},{3,1},{5,3},{7,5},{8,14},{10,8},{12,... | collective-permute-start | bytes 786440 | tf_op jit(solution)/shard_map/ppermute | solution.py:244
  73.6 14.7 %collective-permute-start.15 = (bf16[256,1024]{1,0:T(8,128)(2,1)S(1)}, bf16[256,1024]{1,0:T(8,128)(2,1)S(1)}, u32[]{:S(2)}, u32[]{:S(2)}) collective-permute-start(bf16[256,1024]{1,0:T(8,128)(2,1)S(1)} %get-tuple-element.54.refs_4_), channel_id=1, source_target_pairs={{0,2},{2,4},{4,6},{6,0},{1,3},{3,5},{5,7},{7,1},{8,10},{10,12},{12... | collective-permute-start | bytes 1572872 | tf_op jit(solution)/shard_map/ppermute | solution.py:244
  73.7 14.6 %collective-permute-start.16 = (bf16[256,1024]{1,0:T(8,128)(2,1)S(1)}, bf16[256,1024]{1,0:T(8,128)(2,1)S(1)}, u32[]{:S(2)}, u32[]{:S(2)}) collective-permute-start(bf16[256,1024]{1,0:T(8,128)(2,1)S(1)} %get-tuple-element.55), channel_id=1, source_target_pairs={{0,6},{2,0},{4,2},{6,4},{1,7},{3,1},{5,3},{7,5},{8,14},{10,8},{12,... | collective-permute-start | bytes 1572872 | tf_op jit(solution)/shard_map/ppermute | solution.py:244
  76.9 34.8 %collective-permute-start.24 = (bf16[512,1024]{1,0:T(8,128)(2,1)S(1)}, bf16[512,1024]{1,0:T(8,128)(2,1)S(1)}, u32[]{:S(2)}, u32[]{:S(2)}) collective-permute-start(bf16[512,1024]{1,0:T(8,128)(2,1)S(1)} %get-tuple-element.64), channel_id=1, source_target_pairs={{0,16},{8,56},{16,32},{24,8},{32,48},{40,24},{48,0},{56,40},{1,17}... | collective-permute-start | bytes 3145736 | tf_op jit(solution)/shard_map/ppermute | solution.py:263
  89.0 13.7 %collective-permute-start.17 = (bf16[256,1024]{1,0:T(8,128)(2,1)S(1)}, bf16[256,1024]{1,0:T(8,128)(2,1)S(1)}, u32[]{:S(2)}, u32[]{:S(2)}) collective-permute-start(bf16[256,1024]{1,0:T(8,128)(2,1)S(1)} %get-tuple-element.56), channel_id=1, source_target_pairs={{0,2},{2,4},{4,6},{6,0},{1,3},{3,5},{5,7},{7,1},{8,10},{10,12},{12... | collective-permute-start | bytes 1572872 | tf_op jit(solution)/shard_map/ppermute | solution.py:244
  89.6 13.2 %collective-permute-start.18 = (bf16[256,1024]{1,0:T(8,128)(2,1)S(1)}, bf16[256,1024]{1,0:T(8,128)(2,1)S(1)}, u32[]{:S(2)}, u32[]{:S(2)}) collective-permute-start(bf16[256,1024]{1,0:T(8,128)(2,1)S(1)} %get-tuple-element.57), channel_id=1, source_target_pairs={{0,6},{2,0},{4,2},{6,4},{1,7},{3,1},{5,3},{7,5},{8,14},{10,8},{12,... | collective-permute-start | bytes 1572872 | tf_op jit(solution)/shard_map/ppermute | solution.py:244
  92.3 7.6 %collective-permute-start.19 = (bf16[128,1024]{1,0:T(8,128)(2,1)S(1)}, bf16[128,1024]{1,0:T(8,128)(2,1)S(1)}, u32[]{:S(2)}, u32[]{:S(2)}) collective-permute-start(bf16[128,1024]{1,0:T(8,128)(2,1)S(1)} %get-tuple-element.58), channel_id=1, source_target_pairs={{0,193},{1,64},{64,1},{65,128},{128,65},{129,192},{192,129},{193,0... | collective-permute-start | bytes 786440 | tf_op jit(solution)/shard_map/ppermute | solution.py:254
  103.6 10.6 %collective-permute-start.20 = (bf16[128,1024]{1,0:T(8,128)(2,1)S(1)}, bf16[128,1024]{1,0:T(8,128)(2,1)S(1)}, u32[]{:S(2)}, u32[]{:S(2)}) collective-permute-start(bf16[128,1024]{1,0:T(8,128)(2,1)S(1)} %get-tuple-element.59), channel_id=1, source_target_pairs={{0,2},{2,4},{4,6},{6,0},{1,3},{3,5},{5,7},{7,1},{8,10},{10,12},{12... | collective-permute-start | bytes 786440 | tf_op jit(solution)/shard_map/ppermute | solution.py:244
  104.5 9.7 %collective-permute-start.21 = (bf16[128,1024]{1,0:T(8,128)(2,1)S(1)}, bf16[128,1024]{1,0:T(8,128)(2,1)S(1)}, u32[]{:S(2)}, u32[]{:S(2)}) collective-permute-start(bf16[128,1024]{1,0:T(8,128)(2,1)S(1)} %get-tuple-element.60), channel_id=1, source_target_pairs={{0,6},{2,0},{4,2},{6,4},{1,7},{3,1},{5,3},{7,5},{8,14},{10,8},{12,... | collective-permute-start | bytes 786440 | tf_op jit(solution)/shard_map/ppermute | solution.py:244
  106.9 12.2 %collective-permute-start.22 = (bf16[128,1024]{1,0:T(8,128)(2,1)S(1)}, bf16[128,1024]{1,0:T(8,128)(2,1)S(1)}, u32[]{:S(2)}, u32[]{:S(2)}) collective-permute-start(bf16[128,1024]{1,0:T(8,128)(2,1)S(1)} %get-tuple-element.61.refs_2_), channel_id=1, source_target_pairs={{0,193},{1,64},{64,1},{65,128},{128,65},{129,192},{192,129},{193,0... | collective-permute-start | bytes 786440 | tf_op jit(solution)/shard_map/ppermute | solution.py:254
  107.2 11.9 %collective-permute-start.23 = (bf16[128,1024]{1,0:T(8,128)(2,1)S(1)}, bf16[128,1024]{1,0:T(8,128)(2,1)S(1)}, u32[]{:S(2)}, u32[]{:S(2)}) collective-permute-start(bf16[128,1024]{1,0:T(8,128)(2,1)S(1)} %get-tuple-element.62), channel_id=1, source_target_pairs={{0,64},{1,193},{64,128},{65,1},{128,192},{129,65},{192,0},{193,129... | collective-permute-start | bytes 786440 | tf_op jit(solution)/shard_map/ppermute | solution.py:258
  112.5 29.7 %collective-permute-start.30 = (bf16[512,1024]{1,0:T(8,128)(2,1)S(1)}, bf16[512,1024]{1,0:T(8,128)(2,1)S(1)}, u32[]{:S(2)}, u32[]{:S(2)}) collective-permute-start(bf16[512,1024]{1,0:T(8,128)(2,1)S(1)} %get-tuple-element.70), channel_id=1, source_target_pairs={{0,16},{8,56},{16,32},{24,8},{32,48},{40,24},{48,0},{56,40},{1,17}... | collective-permute-start | bytes 3145736 | tf_op jit(solution)/shard_map/ppermute | solution.py:263
  119.8 22.4 %collective-permute-start.31 = (bf16[512,1024]{1,0:T(8,128)(2,1)S(1)}, bf16[512,1024]{1,0:T(8,128)(2,1)S(1)}, u32[]{:S(2)}, u32[]{:S(2)}) collective-permute-start(bf16[512,1024]{1,0:T(8,128)(2,1)S(1)} %get-tuple-element.71), channel_id=1, source_target_pairs={{0,24},{8,48},{16,40},{24,0},{32,56},{40,16},{48,8},{56,32},{1,25}... | collective-permute-start | bytes 3145736 | tf_op jit(solution)/shard_map/ppermute | solution.py:263
  120.1 8.6 %collective-permute-start.25 = (bf16[128,1024]{1,0:T(8,128)(2,1)S(1)}, bf16[128,1024]{1,0:T(8,128)(2,1)S(1)}, u32[]{:S(2)}, u32[]{:S(2)}) collective-permute-start(bf16[128,1024]{1,0:T(8,128)(2,1)S(1)} %get-tuple-element.66.refs_0_), channel_id=1, source_target_pairs={{0,1},{1,0},{2,3},{3,2},{4,5},{5,4},{6,7},{7,6},{8,9},{9,8},{10,11... | collective-permute-start | bytes 786440 | tf_op jit(solution)/shard_map/ppermute | solution.py:250
  129.3 9.0 %collective-permute-start.26 = (bf16[128,1024]{1,0:T(8,128)(2,1)S(1)}, bf16[128,1024]{1,0:T(8,128)(2,1)S(1)}, u32[]{:S(2)}, u32[]{:S(2)}) collective-permute-start(bf16[128,1024]{1,0:T(8,128)(2,1)S(1)} %shard_map.119.refs_0_), channel_id=1, source_target_pairs={{0,2},{2,4},{4,6},{6,0},{1,3},{3,5},{5,7},{7,1},{8,10},{10,12},{12... | collective-permute-start | bytes 786440 | tf_op jit(solution)/shard_map/ppermute | solution.py:244
  129.4 9.0 %collective-permute-start.27 = (bf16[128,1024]{1,0:T(8,128)(2,1)S(1)}, bf16[128,1024]{1,0:T(8,128)(2,1)S(1)}, u32[]{:S(2)}, u32[]{:S(2)}) collective-permute-start(bf16[128,1024]{1,0:T(8,128)(2,1)S(1)} %shard_map.119.refs_0_), channel_id=1, source_target_pairs={{0,6},{2,0},{4,2},{6,4},{1,7},{3,1},{5,3},{7,5},{8,14},{10,8},{12,... | collective-permute-start | bytes 786440 | tf_op jit(solution)/shard_map/ppermute | solution.py:244
  138.9 7.8 %collective-permute-start.28 = (bf16[64,1024]{1,0:T(8,128)(2,1)S(1)}, bf16[64,1024]{1,0:T(8,128)(2,1)S(1)}, u32[]{:S(2)}, u32[]{:S(2)}) collective-permute-start(bf16[64,1024]{1,0:T(8,128)(2,1)S(1)} %get-tuple-element.67.refs_3_), channel_id=1, source_target_pairs={{0,2},{2,4},{4,6},{6,0},{1,3},{3,5},{5,7},{7,1},{8,10},{10,12},{12... | collective-permute-start | bytes 393224 | tf_op jit(solution)/shard_map/ppermute | solution.py:244
  139.0 7.7 %collective-permute-start.29 = (bf16[64,1024]{1,0:T(8,128)(2,1)S(1)}, bf16[64,1024]{1,0:T(8,128)(2,1)S(1)}, u32[]{:S(2)}, u32[]{:S(2)}) collective-permute-start(bf16[64,1024]{1,0:T(8,128)(2,1)S(1)} %get-tuple-element.68), channel_id=1, source_target_pairs={{0,6},{2,0},{4,2},{6,4},{1,7},{3,1},{5,3},{7,5},{8,14},{10,8},{12,... | collective-permute-start | bytes 393224 | tf_op jit(solution)/shard_map/ppermute | solution.py:244
  144.0 1.0 copy-start.7

commit v6 on v5

--- a/solution.py
+++ b/solution.py
@@ -127,18 +127,17 @@
 def attend(k, v, q, g, info, ctx_ref, act_ref):
     scale = HEAD ** (-0.5)
     place = lax.broadcasted_iota(jnp.int32, (k.shape[0], 1), 0)
-    scores = dot_t(k, q) * scale
-    scores = jnp.where(place < info[SRC_LIVE], scores, masked_score)
+    scores = jnp.where(place < info[SRC_LIVE], dot_t(k, q), masked_score / scale)
     highest = jnp.max(scores, axis=0, keepdims=True)
-    shifted = jnp.exp(scores - highest)
+    shifted = jnp.exp((scores - highest) * scale)
     weights = shifted * (1.0 / jnp.sum(shifted, axis=0, keepdims=True))
     low = weights.astype(bf16)
     target = lax.broadcasted_iota(jnp.int32, (q.shape[0], 1), 0)
     g = jnp.where(target < info[TGT_LIVE], g.astype(f32), 0.0).astype(bf16)
     prob = dot_t(v, g)
     prob_dot = jnp.sum(weights * prob, axis=0, keepdims=True)
-    grad = (weights * (prob - prob_dot) * scale).astype(bf16)
-    act_ref[:, :HEAD] = dot(grad, q).astype(bf16)
+    grad = (weights * (prob - prob_dot)).astype(bf16)
+    act_ref[:, :HEAD] = (dot(grad, q) * scale).astype(bf16)
     act_ref[:, HEAD:] = dot(low, g).astype(bf16)
     ctx_ref[...] = t_dot(low, v).astype(bf16)
 
@@ -352,7 +351,7 @@
         sent = pack(False)
         got = swap_core(sent)
 
-        far, up, down = partial_grad(act, wk, wv, info, (2,), bf16, first=(n_sec, blk, (3, 0)))
+        far, up, down = partial_grad(act, wk, wv, info, (2,), bf16, first=(n_sec, blk, (3, 0, 2)))
         halves = both(up, down)
         (near,) = partial_grad(act, wk, wv, info, (3, 1), bf16, (far,))
         kept = pack(True, (near,))
@@ -403,11 +402,11 @@
 
             return small(body, ins, outs, info, after)
 
-        up, down, far_y = stage([], [(3, halves, 0)], [2, 1], through=[far_y])
+        up, down, far_y = stage([], [(3, halves, 0)], [1], through=[far_y])
         got_y = shift_y(far_y)
         near_y, keep_y = pair_grads(kept, got, act, act_other, info, [(0, 1), (3,)], (up,))
         side = both(up, down)
-        total3, up, down = stage([(3, side, 0, [])], [(2, side, blk), (1, side, blk + mid)], [])
+        total3, up, down = stage([(3, side, 0, [])], [(2, halves, 2 * mid), (1, side, blk)], [])
         carried = cross(total3)
         side = both(up, down)
         total2, total1, up, down = stage([(2, side, 0, [carried]), (1, side, blk, [])], [(0, halves, mid)], [])
@@ -420,23 +419,30 @@
 
         same_y, other_y = small(add_y, [near_y, got_y], [keep_y, keep_y], info, (total1,))
         same_y = shift_y(same_y)
+        carried = [jump(total2, 1), cross(total1)]
         side = both(up, down)
-        carried = [cross(total1), jump(total2, 1)]
         mine, other_y = stage([(0, side, 0, carried)], [], [], through=[other_y])
         in_y = same_y, shift_y(other_y, True)
         other = swap_low(mine)
         part = mine
 
-        def add_two(info, one_ref, two_ref, out_ref):
+        def add_two(info, one_ref, two_ref, out_ref, top_ref):
             out_ref[...] = (one_ref[...].astype(f32) + two_ref[...].astype(f32)).astype(bf16)
-
-        (final,) = small(add_two, [mine, other], [part], info)
+            top_ref[...] = out_ref[:mid]
+
+        half_part = jax.ShapeDtypeStruct((mid, quarter), bf16)
+        final, top = small(add_two, [mine, other], [part, half_part], info)
         below, above = both(final, final)
-        half_part = jax.ShapeDtypeStruct((mid, quarter), bf16)
-        passed = small(cut, [below, above], [half_part, half_part], info)
-        top, low = both(*passed)
-
-        def finish(info, keep_ref, one_ref, two_ref, key_ref, value_ref):
+        far_top = shift_x(top, 2)
+
+        def cut_low(info, in_ref, out_ref):
+            out_ref[...] = in_ref[mid:]
+
+        (low,) = small(cut_low, [above], [half_part], info)
+        far_low = shift_x(low, -1)
+
+        def finish(info, keep_ref, one_ref, two_ref, key_ref, value_ref, end_ref):
+            end_ref[...] = jnp.zeros_like(end_ref)
             sums = keep_ref[...].astype(f32) + one_ref[...].astype(f32) + two_ref[...].astype(f32)
             sums = sums.astype(bf16)
             for h in range(local_width // HEAD):
@@ -445,7 +451,8 @@
                 value_ref[:, h * HEAD : (h + 1) * HEAD] = sums[:, at + HEAD : at + 2 * HEAD]
 
         shard = jax.ShapeDtypeStruct((half, local_width), bf16)
-        key_weight_grad, value_weight_grad = small(finish, [keep_y, *in_y], [shard, shard], info, (passed[0],))
+        end = jax.ShapeDtypeStruct((16, 128), bf16)
+        key_weight_grad, value_weight_grad, end = small(finish, [keep_y, *in_y], [shard, shard, end], info, (low,))
 
         def place(info, *refs):
             for ref, k in zip(refs[:-1], (0, 1, 3)):
@@ -453,9 +460,9 @@
                 refs[-1][:, pl.ds(pl.multiple_of(at, quarter), quarter)] = ref[...]
 
         whole_rows = jax.ShapeDtypeStruct((blk, width), bf16)
-        (enc_grad,) = small(place, [final, below, above], [whole_rows], info, (key_weight_grad,))
-
-        def place_last(info, top_ref, low_ref, _, out_ref):
+        (enc_grad,) = small(place, [final, below, above], [whole_rows], info, (low,))
+
+        def place_last(info, top_ref, low_ref, _, __, out_ref):
             out_ref[:mid] = top_ref[...]
             out_ref[mid:] = low_ref[...]
 
@@ -464,14 +471,14 @@
             grid_spec=pltpu.PrefetchScalarGridSpec(
                 num_scalar_prefetch=1,
                 grid=(1,),
-                in_specs=[whole(half_part), whole(half_part), ANYWHERE],
+                in_specs=[whole(half_part), whole(half_part), ANYWHERE, ANYWHERE],
                 out_specs=pl.BlockSpec((blk, quarter), lambda i, info: (0, mod4(info[X] - 2))),
             ),
             out_shape=whole_rows,
             input_output_aliases={3: 0},
             compiler_params=params(8),
             cost_estimate=LIGHT,
-        )(info, top, low, enc_grad)
+        )(info, far_top, far_low, enc_grad, end)
         enc_grad = enc_grad[None]
 
         return (context, enc_grad, key_weight_grad[None], value_weight_grad[None])

time: 149 us -> 147 us (0.987)
  waiting for transfers between devices: 53.5 us -> 51.2 us
  starting transfers between devices: 47.2 us -> 48.8 us
    ppermute x4, waiting for transfers between devices: 12.2 us -> 9.58 us  [cross(): lax.ppermute(v, ('section', 'low'), [(z, (z + (1 if z % 2 else -1)) % n)...]
    ppermute x4, starting transfers between devices: 3.56 us -> 6.04 us  [cross(): lax.ppermute(v, ('section', 'low'), [(z, (z + (1 if z % 2 else -1)) % n)...]
    unnamed x16 -> x14, local copies, waits for them, and re-layouts: 5.44 us -> 4.39 us
  transfers between devices with their start and end apart: 32 -> 32, of which waited for: 13 -> 15; matrix products, arithmetic and copies ran while one was open for 0% -> 0% of each run, Pallas kernels for 19% -> 20%
where the time goes in v6:
time: 147 us; the launch traced here: 146 us
  waiting for transfers between devices  51.2 us (35%)
  starting transfers between devices  48.8 us (33%)
  Pallas kernels  38.6 us (26%)
  local copies, waits for them, and re-layouts  5.54 us (4%)
  between operations  2.2 us (1%)
    ppermute x20, starting transfers between devices, shift_x(): return lax.ppermute(v, 'x', [(i, (i + k) % XS) for i in range(XS)])  32.1 us
    ppermute x20, waiting for transfers between devices, shift_x(): return lax.ppermute(v, 'x', [(i, (i + k) % XS) for i in range(XS)])  26.3 us
    pallas_call x15, Pallas kernels, small(): pl.pallas_call(run, grid_spec=pltpu.PrefetchScalarGridSpec(num_scalar_pre...  16.9 us
    pallas_call x3, Pallas kernels, project(): pl.pallas_call(body, grid_spec=pltpu.PrefetchScalarGridSpec(num_scalar_pr...  12.3 us
    ppermute x4, waiting for transfers between devices, cross(): lax.ppermute(v, ('section', 'low'), [(z, (z + (1 if z % 2 else -1)) % n)...  9.58 us
    ppermute x1, waiting for transfers between devices, swap_low(): return lax.ppermute(v, 'low', [(0, 1), (1, 0)])  8.64 us
    pallas_call x3, Pallas kernels, partial_grad(): pl.pallas_call(body, grid_spec=pltpu.PrefetchScalarGridSpec(num_scalar_pr...  8.15 us
    ppermute x2, waiting for transfers between devices, jump(): lax.ppermute(v, ('section', 'low'), [(z, (z + (-2 * k if z % 2 else 2 * k...  6.71 us
  transfers between devices with their start and end apart: 32, of which 15 were waited for; matrix products, arithmetic and copies ran while one was open for 0% of the time, Pallas kernels for 20%

profile of v6, /device:TPU:8, one launch (start us, length us, event | category | flops | bytes accessed | tf_op | source)
XLA Modules:
  0.0 146.3 jit_solution(1157416725717628367)
XLA Ops:
  0.6 1.1 dynamic-slice_bitcast_fusion
  1.7 6.4 %collective-permute-start = (bf16[128,1024]{1,0:T(8,128)(2,1)S(1)}, bf16[128,1024]{1,0:T(8,128)(2,1)S(1)}, u32[]{:S(2)}, u32[]{:S(2)}) collective-permute-start(bf16[128,1024]{1,0:T(8,128)(2,1)S(1)} %dynamic-slice_bitcast_fusion), channel_id=1, source_target_pairs={{0,192},{1,65},{64,0},{65,129},{128,64},{129,193},{192,128},{193,1... | collective-permute-start | bytes 786440 | tf_op jit(solution)/shard_map/ppermute | solution.py:257
  8.1 6.7 %collective-permute-done.refs_2_ = bf16[128,1024]{1,0:T(8,128)(2,1)S(1)} collective-permute-done((bf16[128,1024]{1,0:T(8,128)(2,1)S(1)}, bf16[128,1024]{1,0:T(8,128)(2,1)S(1)}, u32[]{:S(2)}, u32[]{:S(2)}) %collective-permute-start) | collective-permute-done | bytes 262176 | tf_op jit(solution)/shard_map/ppermute | solution.py:257
  14.8 2.9 %collective-permute-start.1 = (bf16[128,1024]{1,0:T(8,128)(2,1)S(1)}, bf16[128,1024]{1,0:T(8,128)(2,1)S(1)}, u32[]{:S(2)}, u32[]{:S(2)}) collective-permute-start(bf16[128,1024]{1,0:T(8,128)(2,1)S(1)} %collective-permute-done.refs_2_), channel_id=1, source_target_pairs={{0,193},{1,64},{64,1},{65,128},{128,65},{129,192},{192,129},{193,0... | collective-permute-start | bytes 786440 | tf_op jit(solution)/shard_map/ppermute | solution.py:253
  17.7 1.5 %collective-permute-start.4 = (bf16[128,1024]{1,0:T(8,128)(2,1)S(1)}, bf16[128,1024]{1,0:T(8,128)(2,1)S(1)}, u32[]{:S(2)}, u32[]{:S(2)}) collective-permute-start(bf16[128,1024]{1,0:T(8,128)(2,1)S(1)} %collective-permute-done.refs_2_), channel_id=1, source_target_pairs={{0,2},{2,4},{4,6},{6,0},{1,3},{3,5},{5,7},{7,1},{8,10},{10,12},{12... | collective-permute-start | bytes 786440 | tf_op jit(solution)/shard_map/ppermute | solution.py:243
  19.2 1.7 %collective-permute-start.6 = (bf16[128,1024]{1,0:T(8,128)(2,1)S(1)}, bf16[128,1024]{1,0:T(8,128)(2,1)S(1)}, u32[]{:S(2)}, u32[]{:S(2)}) collective-permute-start(bf16[128,1024]{1,0:T(8,128)(2,1)S(1)} %collective-permute-done.refs_2_), channel_id=1, source_target_pairs={{0,6},{2,0},{4,2},{6,4},{1,7},{3,1},{5,3},{7,5},{8,14},{10,8},{12,... | collective-permute-start | bytes 786440 | tf_op jit(solution)/shard_map/ppermute | solution.py:243
  21.0 0.9 collective-permute-start.3
  21.9 2.3 %collective-permute-start.5 = (bf16[128,1024]{1,0:T(8,128)(2,1)S(1)}, bf16[128,1024]{1,0:T(8,128)(2,1)S(1)}, u32[]{:S(2)}, u32[]{:S(2)}) collective-permute-start(bf16[128,1024]{1,0:T(8,128)(2,1)S(1)} %collective-permute-done.2.refs_1_), channel_id=1, source_target_pairs={{0,6},{2,0},{4,2},{6,4},{1,7},{3,1},{5,3},{7,5},{8,14},{10,8},{12,... | collective-permute-start | bytes 786440 | tf_op jit(solution)/shard_map/ppermute | solution.py:243
  25.6 2.4 %collective-permute-done.4.refs_2_.refs_3_ = bf16[128,1024]{1,0:T(8,128)(2,1)S(1)} collective-permute-done((bf16[128,1024]{1,0:T(8,128)(2,1)S(1)}, bf16[128,1024]{1,0:T(8,128)(2,1)S(1)}, u32[]{:S(2)}, u32[]{:S(2)}) %collective-permute-start.4) | collective-permute-done | bytes 262176 | tf_op jit(solution)/shard_map/ppermute | solution.py:243
  28.0 0.3 collective-permute-done.6.refs_4_.refs_6_
  28.3 2.7 %collective-permute-done.3.refs_1_.refs_2_ = bf16[128,1024]{1,0:T(8,128)(2,1)S(1)} collective-permute-done((bf16[128,1024]{1,0:T(8,128)(2,1)S(1)}, bf16[128,1024]{1,0:T(8,128)(2,1)S(1)}, u32[]{:S(2)}, u32[]{:S(2)}) %collective-permute-start.3) | collective-permute-done | bytes 262176 | tf_op jit(solution)/shard_map/ppermute | solution.py:243
  31.1 0.6 shard_map.102
  31.7 1.6 %collective-permute-start.7 = (bf16[256,1024]{1,0:T(8,128)(2,1)S(1)}, bf16[256,1024]{1,0:T(8,128)(2,1)S(1)}, u32[]{:S(2)}, u32[]{:S(2)}) collective-permute-start(bf16[256,1024]{1,0:T(8,128)(2,1)S(1)} %get-tuple-element.40.refs_6_), channel_id=1, source_target_pairs={{0,2},{2,4},{4,6},{6,0},{1,3},{3,5},{5,7},{7,1},{8,10},{10,12},{12... | collective-permute-start | bytes 1572872 | tf_op jit(solution)/shard_map/ppermute | solution.py:243
  33.3 1.7 %collective-permute-start.8 = (bf16[256,1024]{1,0:T(8,128)(2,1)S(1)}, bf16[256,1024]{1,0:T(8,128)(2,1)S(1)}, u32[]{:S(2)}, u32[]{:S(2)}) collective-permute-start(bf16[256,1024]{1,0:T(8,128)(2,1)S(1)} %get-tuple-element.41.refs_7_), channel_id=1, source_target_pairs={{0,6},{2,0},{4,2},{6,4},{1,7},{3,1},{5,3},{7,5},{8,14},{10,8},{12,... | collective-permute-start | bytes 1572872 | tf_op jit(solution)/shard_map/ppermute | solution.py:243
  35.0 2.2 %copy-done = bf16[1,4096,512]{2,1,0:T(8,128)(2,1)S(1)} copy-done((bf16[1,4096,512]{2,1,0:T(8,128)(2,1)S(1)}, bf16[1,4096,512]{2,1,0:T(8,128)(2,1)}, u32[]{:S(2)}) %copy-start) | copy-done | bytes 4194328
  37.2 2.2 %copy-done.2 = bf16[1,4096,512]{2,1,0:T(8,128)(2,1)S(1)} copy-done((bf16[1,4096,512]{2,1,0:T(8,128)(2,1)S(1)}, bf16[1,4096,512]{2,1,0:T(8,128)(2,1)}, u32[]{:S(2)}) %copy-start.2) | copy-done | bytes 4194328
  39.4 2.4 %shard_map.103 = (f32[512,1024]{1,0:T(8,128)S(1)}, bf16[512,1024]{1,0:T(8,128)(2,1)S(1)}) custom-call(s32[7]{0:T(128)S(1)} %stack.25.info, bf16[128,4096]{1,0:T(8,128)(2,1)S(1)} %bitcast.30, bf16[128,1024]{1,0:T(8,128)(2,1)S(1)} %collective-permute-done.2.refs_1_, bf16[128,1024]{1,0:T(8,128)(2,1)S(1)} %collective-permute-done.refs_2_, ...), custom_call_target="tpu_custom_call" | custom-call | flops 1 | bytes 1 | tf_op jit(solution)/shard_map/pallas_call | solution.py:108
  41.8 2.3 %collective-permute-done.7.refs_0_.refs_4_.refs_1_ = bf16[256,1024]{1,0:T(8,128)(2,1)S(1)} collective-permute-done((bf16[256,1024]{1,0:T(8,128)(2,1)S(1)}, bf16[256,1024]{1,0:T(8,128)(2,1)S(1)}, u32[]{:S(2)}, u32[]{:S(2)}) %collective-permute-start.7) | collective-permute-done | bytes 524320 | tf_op jit(solution)/shard_map/ppermute | solution.py:243
  44.1 0.6 shard_map.104
  44.7 3.0 %collective-permute-start.10 = (bf16[64,1024]{1,0:T(8,128)(2,1)S(1)}, bf16[64,1024]{1,0:T(8,128)(2,1)S(1)}, u32[]{:S(2)}, u32[]{:S(2)}) collective-permute-start(bf16[64,1024]{1,0:T(8,128)(2,1)S(1)} %get-tuple-element.44.refs_14_), channel_id=1, source_target_pairs={{0,6},{2,0},{4,2},{6,4},{1,7},{3,1},{5,3},{7,5},{8,14},{10,8},{12,... | collective-permute-start | bytes 393224 | tf_op jit(solution)/shard_map/ppermute | solution.py:243
  47.7 4.0 %shard_map.105 = (f32[512,1024]{1,0:T(8,128)S(1)}, bf16[512,1024]{1,0:T(8,128)(2,1)S(1)}, bf16[512,1024]{1,0:T(8,128)(2,1)S(1)}) custom-call(s32[7]{0:T(128)S(1)} %stack.25.info, bf16[128,4096]{1,0:T(8,128)(2,1)S(1)} %bitcast.31, bf16[128,4096]{1,0:T(8,128)(2,1)S(1)} %bitcast.32, bf16[128,1024]{1,0:T(8,128)(2,1)S(1)} %collective-permute-done.3.refs_1_.refs_2_, ...), custom_call_target="tpu_custom_call" | custom-call | flops 1 | bytes 1 | tf_op jit(solution)/shard_map/pallas_call | solution.py:108
  51.8 2.1 %collective-permute-done.9.refs_3_ = bf16[64,1024]{1,0:T(8,128)(2,1)S(1)} collective-permute-done((bf16[64,1024]{1,0:T(8,128)(2,1)S(1)}, bf16[64,1024]{1,0:T(8,128)(2,1)S(1)}, u32[]{:S(2)}, u32[]{:S(2)}) %collective-permute-start.9) | collective-permute-done | bytes 131104 | tf_op jit(solution)/shard_map/ppermute | solution.py:243
  53.9 5.8 %shard_map.106 = (bf16[512,512]{1,0:T(8,128)(2,1)}, bf16[512,1024]{1,0:T(8,128)(2,1)S(1)}, bf16[512,1024]{1,0:T(8,128)(2,1)S(1)}) custom-call(s32[7]{0:T(128)S(1)} %stack.25.info, bf16[128,4096]{1,0:T(8,128)(2,1)S(1)} %bitcast.33, bf16[256,1024]{1,0:T(8,128)(2,1)S(1)} %collective-permute-done.7.refs_0_.refs_4_.refs_1_, ...), custom_call_target="tpu_custom_call" | custom-call | flops 1 | bytes 1 | tf_op jit(solution)/shard_map/pallas_call | solution.py:108
  59.7 0.8 shard_map.111
  60.6 0.5 collective-permute-start.14
  61.1 2.3 %shard_map.107 = (bf16[512,1024]{1,0:T(8,128)(2,1)S(1)}, bf16[192,1024]{1,0:T(8,128)(2,1)S(1)}, bf16[192,1024]{1,0:T(8,128)(2,1)S(1)}) custom-call(s32[7]{0:T(128)S(1)} %stack.25.info, bf16[512,1024]{1,0:T(8,128)(2,1)S(1)} %get-tuple-element.47.act_ref.refs_2_, bf16[4096,512]{1,0:T(8,128)(2,1)S(1)} %bitcast.20, bf16[4096,512]{1,0:T(8,128)(2,1)S(1)} %bitcast.27), custom_call_target="tpu_custom_call" | custom-call | flops 1 | bytes 1 | tf_op jit(solution)/shard_map/pallas_call | solution.py:190
  63.4 3.2 %collective-permute-start.12 = (bf16[192,1024]{1,0:T(8,128)(2,1)S(1)}, bf16[192,1024]{1,0:T(8,128)(2,1)S(1)}, u32[]{:S(2)}, u32[]{:S(2)}) collective-permute-start(bf16[192,1024]{1,0:T(8,128)(2,1)S(1)} %get-tuple-element.50), channel_id=1, source_target_pairs={{0,6},{2,0},{4,2},{6,4},{1,7},{3,1},{5,3},{7,5},{8,14},{10,8},{12,... | collective-permute-start | bytes 1179656 | tf_op jit(solution)/shard_map/ppermute | solution.py:243
  66.7 3.7 %shard_map.108.refs_0_.refs_4_.refs_3_.refs_6_.refs_7_ = bf16[512,2048]{1,0:T(8,128)(2,1)S(1)} custom-call(s32[7]{0:T(128)S(1)} %stack.25.info, bf16[512,1024]{1,0:T(8,128)(2,1)S(1)} %get-tuple-element.47.act_ref.refs_2_, bf16[4096,512]{1,0:T(8,128)(2,1)S(1)} %bitcast.21, bf16[4096,512]{1,0:T(8,128)(2,1)S(1)} %bitcast.28, ...), custom_call_target="tpu_custom_call" | custom-call | flops 1 | bytes 1 | tf_op jit(solution)/shard_map/pallas_call | solution.py:190
  70.4 0.8 shard_map.110.refs_0_
  71.2 1.8 %shard_map.112.refs_4_ = bf16[512,1024]{1,0:T(8,128)(2,1)S(1)} custom-call(s32[7]{0:T(128)S(1)} %stack.25.info, bf16[512,2048]{1,0:T(8,128)(2,1)S(1)} %shard_map.110.refs_0_, bf16[512,2048]{1,0:T(8,128)(2,1)S(1)} %collective-permute-done.13.refs_1_, bf16[512,1024]{1,0:T(8,128)(2,1)S(1)} %get-tuple-element.47.act_ref.refs_2_, ...), custom_call_target="tpu_custom_call" | custom-call | flops 1 | bytes 1 | tf_op jit(solution)/shard_map/pallas_call | solution.py:226
  73.0 2.8 %collective-permute-done.11.refs_1_.refs_4_.refs_8_ = bf16[192,1024]{1,0:T(8,128)(2,1)S(1)} collective-permute-done((bf16[192,1024]{1,0:T(8,128)(2,1)S(1)}, bf16[192,1024]{1,0:T(8,128)(2,1)S(1)}, u32[]{:S(2)}, u32[]{:S(2)}) %collective-permute-start.11) | collective-permute-done | bytes 393248 | tf_op jit(solution)/shard_map/ppermute | solution.py:243
  75.8 0.7 shard_map.113
  76.5 3.2 %collective-permute-start.16 = (bf16[192,1024]{1,0:T(8,128)(2,1)S(1)}, bf16[192,1024]{1,0:T(8,128)(2,1)S(1)}, u32[]{:S(2)}, u32[]{:S(2)}) collective-permute-start(bf16[192,1024]{1,0:T(8,128)(2,1)S(1)} %get-tuple-element.56), channel_id=1, source_target_pairs={{0,6},{2,0},{4,2},{6,4},{1,7},{3,1},{5,3},{7,5},{8,14},{10,8},{12,... | collective-permute-start | bytes 1179656 | tf_op jit(solution)/shard_map/ppermute | solution.py:243
  79.8 1.6 %collective-permute-start.24 = (bf16[512,1024]{1,0:T(8,128)(2,1)S(1)}, bf16[512,1024]{1,0:T(8,128)(2,1)S(1)}, u32[]{:S(2)}, u32[]{:S(2)}) collective-permute-start(bf16[512,1024]{1,0:T(8,128)(2,1)S(1)} %get-tuple-element.65), channel_id=1, source_target_pairs={{0,16},{8,56},{16,32},{24,8},{32,48},{40,24},{48,0},{56,40},{1,17}... | collective-permute-start | bytes 3145736 | tf_op jit(solution)/shard_map/ppermute | solution.py:262
  81.3 2.2 %shard_map.109.refs_0_.refs_4_ = f32[512,1024]{1,0:T(8,128)S(1)} custom-call(s32[7]{0:T(128)S(1)} %stack.25.info, bf16[512,1024]{1,0:T(8,128)(2,1)S(1)} %get-tuple-element.47.act_ref.refs_2_, bf16[4096,512]{1,0:T(8,128)(2,1)S(1)} %bitcast.22, bf16[4096,512]{1,0:T(8,128)(2,1)S(1)} %bitcast.29, ...), custom_call_target="tpu_custom_call" | custom-call | flops 1 | bytes 1 | tf_op jit(solution)/shard_map/pallas_call | solution.py:190
  83.5 4.5 %collective-permute-done.15.refs_1_.refs_7_ = bf16[192,1024]{1,0:T(8,128)(2,1)S(1)} collective-permute-done((bf16[192,1024]{1,0:T(8,128)(2,1)S(1)}, bf16[192,1024]{1,0:T(8,128)(2,1)S(1)}, u32[]{:S(2)}, u32[]{:S(2)}) %collective-permute-start.15) | collective-permute-done | bytes 393248 | tf_op jit(solution)/shard_map/ppermute | solution.py:243
  88.0 0.8 shard_map.114
  88.8 0.9 collective-permute-start.17
  89.7 2.4 %collective-permute-start.18 = (bf16[256,1024]{1,0:T(8,128)(2,1)S(1)}, bf16[256,1024]{1,0:T(8,128)(2,1)S(1)}, u32[]{:S(2)}, u32[]{:S(2)}) collective-permute-start(bf16[256,1024]{1,0:T(8,128)(2,1)S(1)} %get-tuple-element.58), channel_id=1, source_target_pairs={{0,6},{2,0},{4,2},{6,4},{1,7},{3,1},{5,3},{7,5},{8,14},{10,8},{12,... | collective-permute-start | bytes 1572872 | tf_op jit(solution)/shard_map/ppermute | solution.py:243
  92.1 0.3 collective-permute-start.19
  92.4 7.3 %collective-permute-done.19.refs_3_ = bf16[128,1024]{1,0:T(8,128)(2,1)S(1)} collective-permute-done((bf16[128,1024]{1,0:T(8,128)(2,1)S(1)}, bf16[128,1024]{1,0:T(8,128)(2,1)S(1)}, u32[]{:S(2)}, u32[]{:S(2)}) %collective-permute-start.19) | collective-permute-done | bytes 262176 | tf_op jit(solution)/shard_map/ppermute | solution.py:253
  99.7 2.6 %collective-permute-done.17.refs_1_.refs_5_ = bf16[256,1024]{1,0:T(8,128)(2,1)S(1)} collective-permute-done((bf16[256,1024]{1,0:T(8,128)(2,1)S(1)}, bf16[256,1024]{1,0:T(8,128)(2,1)S(1)}, u32[]{:S(2)}, u32[]{:S(2)}) %collective-permute-start.17) | collective-permute-done | bytes 524320 | tf_op jit(solution)/shard_map/ppermute | solution.py:243
  102.2 0.8 shard_map.115
  103.1 0.9 collective-permute-start.20
  104.0 2.4 %collective-permute-start.21 = (bf16[128,1024]{1,0:T(8,128)(2,1)S(1)}, bf16[128,1024]{1,0:T(8,128)(2,1)S(1)}, u32[]{:S(2)}, u32[]{:S(2)}) collective-permute-start(bf16[128,1024]{1,0:T(8,128)(2,1)S(1)} %get-tuple-element.61), channel_id=1, source_target_pairs={{0,6},{2,0},{4,2},{6,4},{1,7},{3,1},{5,3},{7,5},{8,14},{10,8},{12,... | collective-permute-start | bytes 786440 | tf_op jit(solution)/shard_map/ppermute | solution.py:243
  106.4 0.3 collective-permute-start.22
  106.7 2.8 %collective-permute-start.23 = (bf16[128,1024]{1,0:T(8,128)(2,1)S(1)}, bf16[128,1024]{1,0:T(8,128)(2,1)S(1)}, u32[]{:S(2)}, u32[]{:S(2)}) collective-permute-start(bf16[128,1024]{1,0:T(8,128)(2,1)S(1)} %get-tuple-element.63.refs_2_), channel_id=1, source_target_pairs={{0,193},{1,64},{64,1},{65,128},{128,65},{129,192},{192,129},{193,0... | collective-permute-start | bytes 786440 | tf_op jit(solution)/shard_map/ppermute | solution.py:253
  109.4 4.0 %shard_map.116 = (bf16[1024,1024]{1,0:T(8,128)(2,1)S(1)}, bf16[512,1024]{1,0:T(8,128)(2,1)S(1)}) custom-call(s32[7]{0:T(128)S(1)} %stack.25.info, bf16[512,2048]{1,0:T(8,128)(2,1)S(1)} %shard_map.110.refs_0_, bf16[512,2048]{1,0:T(8,128)(2,1)S(1)} %collective-permute-done.13.refs_1_, bf16[512,1024]{1,0:T(8,128)(2,1)S(1)} %get-tuple-element.47.act_ref.refs_2_, ...), custom_call_target="tpu_custom_call" | custom-call | flops 1 | bytes 1 | tf_op jit(solution)/shard_map/pallas_call | solution.py:226
  113.5 0.8 shard_map.117
  114.3 1.7 %collective-permute-start.30 = (bf16[512,1024]{1,0:T(8,128)(2,1)S(1)}, bf16[512,1024]{1,0:T(8,128)(2,1)S(1)}, u32[]{:S(2)}, u32[]{:S(2)}) collective-permute-start(bf16[512,1024]{1,0:T(8,128)(2,1)S(1)} %get-tuple-element.71), channel_id=1, source_target_pairs={{0,16},{8,56},{16,32},{24,8},{32,48},{40,24},{48,0},{56,40},{1,17}... | collective-permute-start | bytes 3145736 | tf_op jit(solution)/shard_map/ppermute | solution.py:262
  116.0 2.3 %collective-permute-done.23.refs_4_ = bf16[128,1024]{1,0:T(8,128)(2,1)S(1)} collective-permute-done((bf16[128,1024]{1,0:T(8,128)(2,1)S(1)}, bf16[128,1024]{1,0:T(8,128)(2,1)S(1)}, u32[]{:S(2)}, u32[]{:S(2)}) %collective-permute-start.23) | collective-permute-done | bytes 262176 | tf_op jit(solution)/shard_map/ppermute | solution.py:253
  118.3 0.7 shard_map.118
  119.2 8.6 %collective-permute-done.25.refs_1_ = bf16[128,1024]{1,0:T(8,128)(2,1)S(1)} collective-permute-done((bf16[128,1024]{1,0:T(8,128)(2,1)S(1)}, bf16[128,1024]{1,0:T(8,128)(2,1)S(1)}, u32[]{:S(2)}, u32[]{:S(2)}) %collective-permute-start.25) | collective-permute-done | bytes 262176 | tf_op jit(solution)/shard_map/ppermute | solution.py:249
  127.9 0.7 shard_map.119
  128.5 1.5 %collective-permute-start.27 = (bf16[128,1024]{1,0:T(8,128)(2,1)S(1)}, bf16[128,1024]{1,0:T(8,128)(2,1)S(1)}, u32[]{:S(2)}, u32[]{:S(2)}) collective-permute-start(bf16[128,1024]{1,0:T(8,128)(2,1)S(1)} %get-tuple-element.69.refs_0_), channel_id=1, source_target_pairs={{0,6},{2,0},{4,2},{6,4},{1,7},{3,1},{5,3},{7,5},{8,14},{10,8},{12,... | collective-permute-start | bytes 786440 | tf_op jit(solution)/shard_map/ppermute | solution.py:243
  130.1 0.6 collective-permute-start.29
  130.6 1.2 collective-permute-start.26
  131.8 6.0 %collective-permute-done.27.refs_0_.refs_2_ = bf16[128,1024]{1,0:T(8,128)(2,1)S(1)} collective-permute-done((bf16[128,1024]{1,0:T(8,128)(2,1)S(1)}, bf16[128,1024]{1,0:T(8,128)(2,1)S(1)}, u32[]{:S(2)}, u32[]{:S(2)}) %collective-permute-start.27) | collective-permute-done | bytes 262176 | tf_op jit(solution)/shard_map/ppermute | solution.py:243
  137.8 0.5 shard_map.120.refs_3_
  138.4 2.8 %collective-permute-start.28 = (bf16[64,1024]{1,0:T(8,128)(2,1)S(1)}, bf16[64,1024]{1,0:T(8,128)(2,1)S(1)}, u32[]{:S(2)}, u32[]{:S(2)}) collective-permute-start(bf16[64,1024]{1,0:T(8,128)(2,1)S(1)} %shard_map.120.refs_3_), channel_id=1, source_target_pairs={{0,6},{2,0},{4,2},{6,4},{1,7},{3,1},{5,3},{7,5},{8,14},{10,8},{12,... | collective-permute-start | bytes 393224 | tf_op jit(solution)/shard_map/ppermute | solution.py:243
  141.1 0.5 collective-permute-done.29.refs_1_
  141.7 1.6 %shard_map.121._ = bf16[128,4096]{1,0:T(8,128)(2,1)} custom-call(s32[7]{0:T(128)S(1)} %stack.25.info, bf16[128,1024]{1,0:T(8,128)(2,1)S(1)} %get-tuple-element.69.refs_0_, bf16[128,1024]{1,0:T(8,128)(2,1)S(1)} %collective-permute-done.29.refs_1_, bf16[128,1024]{1,0:T(8,128)(2,1)S(1)} %collective-permute-done.27.refs_0_.refs_2_, ...), custom_call_target="tpu_custom_call" | custom-call | flops 1 | bytes 1 | tf_op jit(solution)/shard_map/pallas_call | solution.py:226
  143.2 1.8 %shard_map.122 = (bf16[512,512]{1,0:T(8,128)(2,1)}, bf16[512,512]{1,0:T(8,128)(2,1)}, bf16[16,128]{1,0:T(8,128)(2,1)S(1)}) custom-call(s32[7]{0:T(128)S(1)} %stack.25.info, bf16[512,1024]{1,0:T(8,128)(2,1)S(1)} %get-tuple-element.70.refs_0_, bf16[512,1024]{1,0:T(8,128)(2,1)S(1)} %collective-permute-done.30.refs_1_, ...), custom_call_target="tpu_custom_call" | custom-call | flops 1 | bytes 1 | tf_op jit(solution)/shard_map/pallas_call | solution.py:226
  145.1 1.3 shard_map.123
  (38 shorter events, 0.8 us)
Async XLA Ops:
  0.6 34.4 %copy-start.4 = (bf16[1,128,4096]{2,1,0:T(8,128)(2,1)S(1)}, bf16[1,128,4096]{2,1,0:T(8,128)(2,1)}, u32[]{:S(2)}) copy-start(bf16[1,128,4096]{2,1,0:T(8,128)(2,1)} %param.7) | copy-start | bytes 3145732
  1.7 13.1 %collective-permute-start = (bf16[128,1024]{1,0:T(8,128)(2,1)S(1)}, bf16[128,1024]{1,0:T(8,128)(2,1)S(1)}, u32[]{:S(2)}, u32[]{:S(2)}) collective-permute-start(bf16[128,1024]{1,0:T(8,128)(2,1)S(1)} %dynamic-slice_bitcast_fusion), channel_id=1, source_target_pairs={{0,192},{1,65},{64,0},{65,129},{128,64},{129,193},{192,128},{193,1... | collective-permute-start | bytes 786440 | tf_op jit(solution)/shard_map/ppermute | solution.py:257
  8.1 12.9 %collective-permute-start.2 = (bf16[128,1024]{1,0:T(8,128)(2,1)S(1)}, bf16[128,1024]{1,0:T(8,128)(2,1)S(1)}, u32[]{:S(2)}, u32[]{:S(2)}) collective-permute-start(bf16[128,1024]{1,0:T(8,128)(2,1)S(1)} %dynamic-slice_bitcast_fusion), channel_id=1, source_target_pairs={{0,193},{1,64},{64,1},{65,128},{128,65},{129,192},{192,129},{193,0... | collective-permute-start | bytes 786440 | tf_op jit(solution)/shard_map/ppermute | solution.py:253
  14.8 10.8 %collective-permute-start.1 = (bf16[128,1024]{1,0:T(8,128)(2,1)S(1)}, bf16[128,1024]{1,0:T(8,128)(2,1)S(1)}, u32[]{:S(2)}, u32[]{:S(2)}) collective-permute-start(bf16[128,1024]{1,0:T(8,128)(2,1)S(1)} %collective-permute-done.refs_2_), channel_id=1, source_target_pairs={{0,193},{1,64},{64,1},{65,128},{128,65},{129,192},{192,129},{193,0... | collective-permute-start | bytes 786440 | tf_op jit(solution)/shard_map/ppermute | solution.py:253
  17.7 10.2 %collective-permute-start.4 = (bf16[128,1024]{1,0:T(8,128)(2,1)S(1)}, bf16[128,1024]{1,0:T(8,128)(2,1)S(1)}, u32[]{:S(2)}, u32[]{:S(2)}) collective-permute-start(bf16[128,1024]{1,0:T(8,128)(2,1)S(1)} %collective-permute-done.refs_2_), channel_id=1, source_target_pairs={{0,2},{2,4},{4,6},{6,0},{1,3},{3,5},{5,7},{7,1},{8,10},{10,12},{12... | collective-permute-start | bytes 786440 | tf_op jit(solution)/shard_map/ppermute | solution.py:243
  19.2 9.0 %collective-permute-start.6 = (bf16[128,1024]{1,0:T(8,128)(2,1)S(1)}, bf16[128,1024]{1,0:T(8,128)(2,1)S(1)}, u32[]{:S(2)}, u32[]{:S(2)}) collective-permute-start(bf16[128,1024]{1,0:T(8,128)(2,1)S(1)} %collective-permute-done.refs_2_), channel_id=1, source_target_pairs={{0,6},{2,0},{4,2},{6,4},{1,7},{3,1},{5,3},{7,5},{8,14},{10,8},{12,... | collective-permute-start | bytes 786440 | tf_op jit(solution)/shard_map/ppermute | solution.py:243
  21.0 10.0 %collective-permute-start.3 = (bf16[128,1024]{1,0:T(8,128)(2,1)S(1)}, bf16[128,1024]{1,0:T(8,128)(2,1)S(1)}, u32[]{:S(2)}, u32[]{:S(2)}) collective-permute-start(bf16[128,1024]{1,0:T(8,128)(2,1)S(1)} %collective-permute-done.2.refs_1_), channel_id=1, source_target_pairs={{0,2},{2,4},{4,6},{6,0},{1,3},{3,5},{5,7},{7,1},{8,10},{10,12},{12... | collective-permute-start | bytes 786440 | tf_op jit(solution)/shard_map/ppermute | solution.py:243
  21.9 9.2 %collective-permute-start.5 = (bf16[128,1024]{1,0:T(8,128)(2,1)S(1)}, bf16[128,1024]{1,0:T(8,128)(2,1)S(1)}, u32[]{:S(2)}, u32[]{:S(2)}) collective-permute-start(bf16[128,1024]{1,0:T(8,128)(2,1)S(1)} %collective-permute-done.2.refs_1_), channel_id=1, source_target_pairs={{0,6},{2,0},{4,2},{6,4},{1,7},{3,1},{5,3},{7,5},{8,14},{10,8},{12,... | collective-permute-start | bytes 786440 | tf_op jit(solution)/shard_map/ppermute | solution.py:243
  31.7 12.4 %collective-permute-start.7 = (bf16[256,1024]{1,0:T(8,128)(2,1)S(1)}, bf16[256,1024]{1,0:T(8,128)(2,1)S(1)}, u32[]{:S(2)}, u32[]{:S(2)}) collective-permute-start(bf16[256,1024]{1,0:T(8,128)(2,1)S(1)} %get-tuple-element.40.refs_6_), channel_id=1, source_target_pairs={{0,2},{2,4},{4,6},{6,0},{1,3},{3,5},{5,7},{7,1},{8,10},{10,12},{12... | collective-permute-start | bytes 1572872 | tf_op jit(solution)/shard_map/ppermute | solution.py:243
  33.3 10.9 %collective-permute-start.8 = (bf16[256,1024]{1,0:T(8,128)(2,1)S(1)}, bf16[256,1024]{1,0:T(8,128)(2,1)S(1)}, u32[]{:S(2)}, u32[]{:S(2)}) collective-permute-start(bf16[256,1024]{1,0:T(8,128)(2,1)S(1)} %get-tuple-element.41.refs_7_), channel_id=1, source_target_pairs={{0,6},{2,0},{4,2},{6,4},{1,7},{3,1},{5,3},{7,5},{8,14},{10,8},{12,... | collective-permute-start | bytes 1572872 | tf_op jit(solution)/shard_map/ppermute | solution.py:243
  35.0 2.2 %copy-start = (bf16[1,4096,512]{2,1,0:T(8,128)(2,1)S(1)}, bf16[1,4096,512]{2,1,0:T(8,128)(2,1)}, u32[]{:S(2)}) copy-start(bf16[1,4096,512]{2,1,0:T(8,128)(2,1)} %param.8) | copy-start | bytes 12582916
  37.2 2.2 %copy-start.2 = (bf16[1,4096,512]{2,1,0:T(8,128)(2,1)S(1)}, bf16[1,4096,512]{2,1,0:T(8,128)(2,1)}, u32[]{:S(2)}) copy-start(bf16[1,4096,512]{2,1,0:T(8,128)(2,1)} %param.9) | copy-start | bytes 12582916
  39.4 8.3 %copy-start.1 = (bf16[1,4096,512]{2,1,0:T(8,128)(2,1)S(1)}, bf16[1,4096,512]{2,1,0:T(8,128)(2,1)}, u32[]{:S(2)}) copy-start(bf16[1,4096,512]{2,1,0:T(8,128)(2,1)} %param.8) | copy-start | bytes 12582916
  39.4 8.3 %copy-start.3 = (bf16[1,4096,512]{2,1,0:T(8,128)(2,1)S(1)}, bf16[1,4096,512]{2,1,0:T(8,128)(2,1)}, u32[]{:S(2)}) copy-start(bf16[1,4096,512]{2,1,0:T(8,128)(2,1)} %param.9) | copy-start | bytes 12582916
  44.7 7.0 %collective-permute-start.10 = (bf16[64,1024]{1,0:T(8,128)(2,1)S(1)}, bf16[64,1024]{1,0:T(8,128)(2,1)S(1)}, u32[]{:S(2)}, u32[]{:S(2)}) collective-permute-start(bf16[64,1024]{1,0:T(8,128)(2,1)S(1)} %get-tuple-element.44.refs_14_), channel_id=1, source_target_pairs={{0,6},{2,0},{4,2},{6,4},{1,7},{3,1},{5,3},{7,5},{8,14},{10,8},{12,... | collective-permute-start | bytes 393224 | tf_op jit(solution)/shard_map/ppermute | solution.py:243
  47.7 6.2 %copy-start.5 = (bf16[1,1,512,512]{3,2,1,0:T(8,128)(2,1)S(1)}, bf16[1,1,512,512]{3,2,1,0:T(8,128)(2,1)}, u32[]{:S(2)}) copy-start(bf16[1,1,512,512]{3,2,1,0:T(8,128)(2,1)} %param.10) | copy-start | bytes 1572868
  47.7 6.2 %copy-start.6 = (bf16[1,1,512,512]{3,2,1,0:T(8,128)(2,1)S(1)}, bf16[1,1,512,512]{3,2,1,0:T(8,128)(2,1)}, u32[]{:S(2)}) copy-start(bf16[1,1,512,512]{3,2,1,0:T(8,128)(2,1)} %param.11) | copy-start | bytes 1572868
  47.7 6.2 %collective-permute-start.9 = (bf16[64,1024]{1,0:T(8,128)(2,1)S(1)}, bf16[64,1024]{1,0:T(8,128)(2,1)S(1)}, u32[]{:S(2)}, u32[]{:S(2)}) collective-permute-start(bf16[64,1024]{1,0:T(8,128)(2,1)S(1)} %get-tuple-element.43.refs_13_), channel_id=1, source_target_pairs={{0,2},{2,4},{4,6},{6,0},{1,3},{3,5},{5,7},{7,1},{8,10},{10,12},{12... | collective-permute-start | bytes 393224 | tf_op jit(solution)/shard_map/ppermute | solution.py:243
  60.5 10.7 %collective-permute-start.13 = (bf16[512,2048]{1,0:T(8,128)(2,1)S(1)}, bf16[512,2048]{1,0:T(8,128)(2,1)S(1)}, u32[]{:S(2)}, u32[]{:S(2)}) collective-permute-start(bf16[512,2048]{1,0:T(8,128)(2,1)S(1)} %shard_map.111), channel_id=1, source_target_pairs={{0,8},{8,0},{1,9},{9,1},{2,10},{10,2},{3,11},{11,3},{4,12},{12,4},... | collective-permute-start | bytes 6291464 | tf_op jit(solution)/shard_map/ppermute | solution.py:246
  60.6 10.6 %collective-permute-start.14 = (bf16[512,1024]{1,0:T(8,128)(2,1)S(1)}, bf16[512,1024]{1,0:T(8,128)(2,1)S(1)}, u32[]{:S(2)}, u32[]{:S(2)}) collective-permute-start(bf16[512,1024]{1,0:T(8,128)(2,1)S(1)} %get-tuple-element.47.act_ref.refs_2_), channel_id=1, source_target_pairs={{0,8},{8,0},{1,9},{9,1},{2,10},{10,2},{3,11},{11,3},{4,12},{12,4},... | collective-permute-start | bytes 3145736 | tf_op jit(solution)/shard_map/ppermute | solution.py:246
  63.3 12.4 %collective-permute-start.11 = (bf16[192,1024]{1,0:T(8,128)(2,1)S(1)}, bf16[192,1024]{1,0:T(8,128)(2,1)S(1)}, u32[]{:S(2)}, u32[]{:S(2)}) collective-permute-start(bf16[192,1024]{1,0:T(8,128)(2,1)S(1)} %get-tuple-element.49), channel_id=1, source_target_pairs={{0,2},{2,4},{4,6},{6,0},{1,3},{3,5},{5,7},{7,1},{8,10},{10,12},{12... | collective-permute-start | bytes 1179656 | tf_op jit(solution)/shard_map/ppermute | solution.py:243
  63.4 12.3 %collective-permute-start.12 = (bf16[192,1024]{1,0:T(8,128)(2,1)S(1)}, bf16[192,1024]{1,0:T(8,128)(2,1)S(1)}, u32[]{:S(2)}, u32[]{:S(2)}) collective-permute-start(bf16[192,1024]{1,0:T(8,128)(2,1)S(1)} %get-tuple-element.50), channel_id=1, source_target_pairs={{0,6},{2,0},{4,2},{6,4},{1,7},{3,1},{5,3},{7,5},{8,14},{10,8},{12,... | collective-permute-start | bytes 1179656 | tf_op jit(solution)/shard_map/ppermute | solution.py:243
  76.4 11.6 %collective-permute-start.15 = (bf16[192,1024]{1,0:T(8,128)(2,1)S(1)}, bf16[192,1024]{1,0:T(8,128)(2,1)S(1)}, u32[]{:S(2)}, u32[]{:S(2)}) collective-permute-start(bf16[192,1024]{1,0:T(8,128)(2,1)S(1)} %get-tuple-element.55.refs_4_), channel_id=1, source_target_pairs={{0,2},{2,4},{4,6},{6,0},{1,3},{3,5},{5,7},{7,1},{8,10},{10,12},{12... | collective-permute-start | bytes 1179656 | tf_op jit(solution)/shard_map/ppermute | solution.py:243
  76.5 11.5 %collective-permute-start.16 = (bf16[192,1024]{1,0:T(8,128)(2,1)S(1)}, bf16[192,1024]{1,0:T(8,128)(2,1)S(1)}, u32[]{:S(2)}, u32[]{:S(2)}) collective-permute-start(bf16[192,1024]{1,0:T(8,128)(2,1)S(1)} %get-tuple-element.56), channel_id=1, source_target_pairs={{0,6},{2,0},{4,2},{6,4},{1,7},{3,1},{5,3},{7,5},{8,14},{10,8},{12,... | collective-permute-start | bytes 1179656 | tf_op jit(solution)/shard_map/ppermute | solution.py:243
  79.8 33.7 %collective-permute-start.24 = (bf16[512,1024]{1,0:T(8,128)(2,1)S(1)}, bf16[512,1024]{1,0:T(8,128)(2,1)S(1)}, u32[]{:S(2)}, u32[]{:S(2)}) collective-permute-start(bf16[512,1024]{1,0:T(8,128)(2,1)S(1)} %get-tuple-element.65), channel_id=1, source_target_pairs={{0,16},{8,56},{16,32},{24,8},{32,48},{40,24},{48,0},{56,40},{1,17}... | collective-permute-start | bytes 3145736 | tf_op jit(solution)/shard_map/ppermute | solution.py:262
  88.8 13.5 %collective-permute-start.17 = (bf16[256,1024]{1,0:T(8,128)(2,1)S(1)}, bf16[256,1024]{1,0:T(8,128)(2,1)S(1)}, u32[]{:S(2)}, u32[]{:S(2)}) collective-permute-start(bf16[256,1024]{1,0:T(8,128)(2,1)S(1)} %get-tuple-element.57), channel_id=1, source_target_pairs={{0,2},{2,4},{4,6},{6,0},{1,3},{3,5},{5,7},{7,1},{8,10},{10,12},{12... | collective-permute-start | bytes 1572872 | tf_op jit(solution)/shard_map/ppermute | solution.py:243
  89.7 12.6 %collective-permute-start.18 = (bf16[256,1024]{1,0:T(8,128)(2,1)S(1)}, bf16[256,1024]{1,0:T(8,128)(2,1)S(1)}, u32[]{:S(2)}, u32[]{:S(2)}) collective-permute-start(bf16[256,1024]{1,0:T(8,128)(2,1)S(1)} %get-tuple-element.58), channel_id=1, source_target_pairs={{0,6},{2,0},{4,2},{6,4},{1,7},{3,1},{5,3},{7,5},{8,14},{10,8},{12,... | collective-permute-start | bytes 1572872 | tf_op jit(solution)/shard_map/ppermute | solution.py:243
  92.1 7.6 %collective-permute-start.19 = (bf16[128,1024]{1,0:T(8,128)(2,1)S(1)}, bf16[128,1024]{1,0:T(8,128)(2,1)S(1)}, u32[]{:S(2)}, u32[]{:S(2)}) collective-permute-start(bf16[128,1024]{1,0:T(8,128)(2,1)S(1)} %get-tuple-element.59), channel_id=1, source_target_pairs={{0,193},{1,64},{64,1},{65,128},{128,65},{129,192},{192,129},{193,0... | collective-permute-start | bytes 786440 | tf_op jit(solution)/shard_map/ppermute | solution.py:253
  103.1 12.9 %collective-permute-start.20 = (bf16[128,1024]{1,0:T(8,128)(2,1)S(1)}, bf16[128,1024]{1,0:T(8,128)(2,1)S(1)}, u32[]{:S(2)}, u32[]{:S(2)}) collective-permute-start(bf16[128,1024]{1,0:T(8,128)(2,1)S(1)} %get-tuple-element.60), channel_id=1, source_target_pairs={{0,2},{2,4},{4,6},{6,0},{1,3},{3,5},{5,7},{7,1},{8,10},{10,12},{12... | collective-permute-start | bytes 786440 | tf_op jit(solution)/shard_map/ppermute | solution.py:243
  104.0 12.0 %collective-permute-start.21 = (bf16[128,1024]{1,0:T(8,128)(2,1)S(1)}, bf16[128,1024]{1,0:T(8,128)(2,1)S(1)}, u32[]{:S(2)}, u32[]{:S(2)}) collective-permute-start(bf16[128,1024]{1,0:T(8,128)(2,1)S(1)} %get-tuple-element.61), channel_id=1, source_target_pairs={{0,6},{2,0},{4,2},{6,4},{1,7},{3,1},{5,3},{7,5},{8,14},{10,8},{12,... | collective-permute-start | bytes 786440 | tf_op jit(solution)/shard_map/ppermute | solution.py:243
  106.4 9.6 %collective-permute-start.22 = (bf16[128,1024]{1,0:T(8,128)(2,1)S(1)}, bf16[128,1024]{1,0:T(8,128)(2,1)S(1)}, u32[]{:S(2)}, u32[]{:S(2)}) collective-permute-start(bf16[128,1024]{1,0:T(8,128)(2,1)S(1)} %get-tuple-element.62), channel_id=1, source_target_pairs={{0,64},{1,193},{64,128},{65,1},{128,192},{129,65},{192,0},{193,129... | collective-permute-start | bytes 786440 | tf_op jit(solution)/shard_map/ppermute | solution.py:257
  106.7 11.6 %collective-permute-start.23 = (bf16[128,1024]{1,0:T(8,128)(2,1)S(1)}, bf16[128,1024]{1,0:T(8,128)(2,1)S(1)}, u32[]{:S(2)}, u32[]{:S(2)}) collective-permute-start(bf16[128,1024]{1,0:T(8,128)(2,1)S(1)} %get-tuple-element.63.refs_2_), channel_id=1, source_target_pairs={{0,193},{1,64},{64,1},{65,128},{128,65},{129,192},{192,129},{193,0... | collective-permute-start | bytes 786440 | tf_op jit(solution)/shard_map/ppermute | solution.py:253
  114.3 28.9 %collective-permute-start.30 = (bf16[512,1024]{1,0:T(8,128)(2,1)S(1)}, bf16[512,1024]{1,0:T(8,128)(2,1)S(1)}, u32[]{:S(2)}, u32[]{:S(2)}) collective-permute-start(bf16[512,1024]{1,0:T(8,128)(2,1)S(1)} %get-tuple-element.71), channel_id=1, source_target_pairs={{0,16},{8,56},{16,32},{24,8},{32,48},{40,24},{48,0},{56,40},{1,17}... | collective-permute-start | bytes 3145736 | tf_op jit(solution)/shard_map/ppermute | solution.py:262
  119.0 24.2 %collective-permute-start.31 = (bf16[512,1024]{1,0:T(8,128)(2,1)S(1)}, bf16[512,1024]{1,0:T(8,128)(2,1)S(1)}, u32[]{:S(2)}, u32[]{:S(2)}) collective-permute-start(bf16[512,1024]{1,0:T(8,128)(2,1)S(1)} %get-tuple-element.72), channel_id=1, source_target_pairs={{0,24},{8,48},{16,40},{24,0},{32,56},{40,16},{48,8},{56,32},{1,25}... | collective-permute-start | bytes 3145736 | tf_op jit(solution)/shard_map/ppermute | solution.py:262
  119.1 8.7 %collective-permute-start.25 = (bf16[128,1024]{1,0:T(8,128)(2,1)S(1)}, bf16[128,1024]{1,0:T(8,128)(2,1)S(1)}, u32[]{:S(2)}, u32[]{:S(2)}) collective-permute-start(bf16[128,1024]{1,0:T(8,128)(2,1)S(1)} %get-tuple-element.67.refs_0_), channel_id=1, source_target_pairs={{0,1},{1,0},{2,3},{3,2},{4,5},{5,4},{6,7},{7,6},{8,9},{9,8},{10,11... | collective-permute-start | bytes 786440 | tf_op jit(solution)/shard_map/ppermute | solution.py:249
  128.5 9.3 %collective-permute-start.27 = (bf16[128,1024]{1,0:T(8,128)(2,1)S(1)}, bf16[128,1024]{1,0:T(8,128)(2,1)S(1)}, u32[]{:S(2)}, u32[]{:S(2)}) collective-permute-start(bf16[128,1024]{1,0:T(8,128)(2,1)S(1)} %get-tuple-element.69.refs_0_), channel_id=1, source_target_pairs={{0,6},{2,0},{4,2},{6,4},{1,7},{3,1},{5,3},{7,5},{8,14},{10,8},{12,... | collective-permute-start | bytes 786440 | tf_op jit(solution)/shard_map/ppermute | solution.py:243
  130.1 11.6 %collective-permute-start.29 = (bf16[128,1024]{1,0:T(8,128)(2,1)S(1)}, bf16[128,1024]{1,0:T(8,128)(2,1)S(1)}, u32[]{:S(2)}, u32[]{:S(2)}) collective-permute-start(bf16[128,1024]{1,0:T(8,128)(2,1)S(1)} %get-tuple-element.69.refs_0_), channel_id=1, source_target_pairs={{0,2},{2,4},{4,6},{6,0},{1,3},{3,5},{5,7},{7,1},{8,10},{10,12},{12... | collective-permute-start | bytes 786440 | tf_op jit(solution)/shard_map/ppermute | solution.py:243
  130.6 14.4 %collective-permute-start.26 = (bf16[64,1024]{1,0:T(8,128)(2,1)S(1)}, bf16[64,1024]{1,0:T(8,128)(2,1)S(1)}, u32[]{:S(2)}, u32[]{:S(2)}) collective-permute-start(bf16[64,1024]{1,0:T(8,128)(2,1)S(1)} %get-tuple-element.68), channel_id=1, source_target_pairs={{0,4},{2,6},{4,0},{6,2},{1,5},{3,7},{5,1},{7,3},{8,12},{10,14},{12... | collective-permute-start | bytes 393224 | tf_op jit(solution)/shard_map/ppermute | solution.py:243
  138.4 6.7 %collective-permute-start.28 = (bf16[64,1024]{1,0:T(8,128)(2,1)S(1)}, bf16[64,1024]{1,0:T(8,128)(2,1)S(1)}, u32[]{:S(2)}, u32[]{:S(2)}) collective-permute-start(bf16[64,1024]{1,0:T(8,128)(2,1)S(1)} %shard_map.120.refs_3_), channel_id=1, source_target_pairs={{0,6},{2,0},{4,2},{6,4},{1,7},{3,1},{5,3},{7,5},{8,14},{10,8},{12,... | collective-permute-start | bytes 393224 | tf_op jit(solution)/shard_map/ppermute | solution.py:243

commit v7 on v6

--- a/solution.py
+++ b/solution.py
@@ -43,7 +43,7 @@
 LIGHT = pl.CostEstimate(flops=1, bytes_accessed=1, transcendentals=0)
 
 
-def project(quarters, enc, wk, wv, acc, info, n_sec, after=(), queries=None):
+def project(quarters, enc, wk, wv, acc, info, n_sec, after=(), queries=None, first=None):
     blk, width = enc.shape
     quarter = width // XS
     total = n_sec * blk
@@ -59,9 +59,13 @@
         part_refs = [refs.pop(0) for _ in parts]
         weight_refs = [refs.pop(0) for _ in range(2 * n)]
         acc_ref = refs.pop(0) if acc is not None else None
+        step = pl.program_id(0)
+        if queries is not None:
+            far_refs = refs[-3:]
+            del refs[-3:]
         rows_refs = refs[-n:]
 
-        @pl.when(pl.program_id(0) == 0)
+        @pl.when(step == 0)
         def _():
             left = list(part_refs)
             for rows_ref, enc_ref, (_, some) in zip(rows_refs, enc_refs, quarters):
@@ -72,54 +76,77 @@
                         to = block_of(info, block, n_sec) * blk + off
                         rows_ref[pl.ds(pl.multiple_of(to, count), count), :] = ref[at : at + count, :]
 
-        sums = [None if acc_ref is None else acc_ref[:, j * HEAD : (j + 1) * HEAD] for j in range(2)]
-        for i, rows_ref in enumerate(rows_refs):
-            rows = rows_ref[...]
-            for j in range(2):
-                term = dot(rows, weight_refs[2 * i + j][...])
-                sums[j] = term if sums[j] is None else sums[j] + term
+        def head_sums():
+            sums = [None if acc_ref is None else acc_ref[:, j * HEAD : (j + 1) * HEAD] for j in range(2)]
+            for i, rows_ref in enumerate(rows_refs):
+                rows = rows_ref[...]
+                for j in range(2):
+                    term = dot(rows, weight_refs[2 * i + j][...])
+                    sums[j] = term if sums[j] is None else sums[j] + term
+            return sums
+
         if queries is None:
+            sums = head_sums()
             refs[-n - 1][:, :HEAD] = sums[0]
             refs[-n - 1][:, HEAD:] = sums[1]
-        else:
-            k, v = (one.astype(bf16) for one in sums)
-            attend(k, v, refs[0][...], refs[1][...], info, refs[-n - 2], refs[-n - 1])
+            return
+        q_ref, g_ref, wk_ref, wv_ref = refs[:4]
+        ctx_ref, act_ref = refs[-n - 2], refs[-n - 1]
+
+        @pl.when(step < heads)
+        def _():
+            k, v = (one.astype(bf16) for one in head_sums())
+            at = pl.multiple_of(step * 2 * HEAD, 2 * HEAD)
+            here = act_ref.at[:, pl.ds(at, 2 * HEAD)]
+            attend(k, v, q_ref[...], g_ref[...], info, ctx_ref, here)
+
+        @pl.when(step >= heads)
+        def _():
+            far_terms(act_ref, wk_ref, wv_ref, info, (n_sec, blk, first), *far_refs)
 
     def head(rows, count):
-        return pl.BlockSpec((rows, count * HEAD), lambda h, info: (0, h))
+        return pl.BlockSpec((rows, count * HEAD), lambda h, info: (0, jnp.minimum(h, heads - 1)))
 
     def enc_block(m):
         return pl.BlockSpec((blk, quarter), lambda h, info: (0, mod4(info[X] - m)))
 
     def weight(m):
-        return pl.BlockSpec((quarter, HEAD), lambda h, info: (mod4(info[X] - m), h))
+        return pl.BlockSpec((quarter, HEAD), lambda h, info: (mod4(info[X] - m), jnp.minimum(h, heads - 1)))
 
     rows_out = jax.ShapeDtypeStruct((total, quarter), bf16)
     if queries is None:
+        far_shape, far_specs = [], []
         targets = 0
         out_shape, out_specs = [jax.ShapeDtypeStruct((total, 2 * cols), f32)], [head(total, 2)]
     else:
         targets = queries[0].shape[0]
-        out_shape = [
-            jax.ShapeDtypeStruct((targets, cols), bf16),
-            jax.ShapeDtypeStruct((total, 2 * cols), bf16),
-        ]
-        out_specs = [head(targets, 1), head(total, 2)]
+        act_out = jax.ShapeDtypeStruct((total, 2 * cols), bf16)
+        out_shape, out_specs = [jax.ShapeDtypeStruct((targets, cols), bf16), act_out], [head(targets, 1), whole(act_out)]
+        per = quarter // UNIT
+
+        def unit(h):
+            return jnp.maximum(h - heads, 0)
+
+        far_weight = pl.BlockSpec((UNIT, cols), lambda h, info: (mod4(info[X] - 2) * per + unit(h), 0))
+        far_rows = (total, blk // 2 * len(first), blk // 2 * len(first))
+        far_shape = [jax.ShapeDtypeStruct((r, quarter), bf16) for r in far_rows]
+        far_specs = [pl.BlockSpec((r, UNIT), lambda h, info: (0, unit(h))) for r in far_rows]
+        extra += [wk, wv]
     return pl.pallas_call(
         body,
         grid_spec=pltpu.PrefetchScalarGridSpec(
             num_scalar_prefetch=1,
-            grid=(heads,),
+            grid=(heads if queries is None else heads + per,),
             in_specs=[enc_block(m) for m, _ in quarters]
             + [whole(p) for p, _ in parts]
             + [weight(m) for m, _ in quarters for _ in range(2)]
             + ([] if acc is None else [head(total, 2)])
-            + ([] if queries is None else [head(targets, 1)] * 2)
+            + ([] if queries is None else [head(targets, 1)] * 2 + [far_weight] * 2)
             + [ANYWHERE] * len(after),
-            out_specs=out_specs + [whole(rows_out)] * n,
+            out_specs=out_specs + [whole(rows_out)] * n + far_specs,
         ),
-        out_shape=out_shape + [rows_out] * n,
-        compiler_params=params(24),
+        out_shape=out_shape + [rows_out] * n + far_shape,
+        compiler_params=params(28),
         cost_estimate=LIGHT,
     )(info, *[enc] * n, *[p for p, _ in parts], *[wk, wv] * n, *extra, *after)
 
@@ -147,10 +174,29 @@
     return lax.rem(info[SEC] - back + n_sec, n_sec)
 
 
-def partial_grad(act, wk, wv, info, quarters, dtype, after=(), first=None):
+def transposed(act_ref, wk_ref, wv_ref):
+    sums = None
+    for h in range(wk_ref.shape[1] // HEAD):
+        for j, w_ref in enumerate((wk_ref, wv_ref)):
+            at = (2 * h + j) * HEAD
+            term = dot_t(act_ref[:, at : at + HEAD], w_ref[:, h * HEAD : (h + 1) * HEAD])
+            sums = term if sums is None else sums + term
+    return sums
+
+
+def far_terms(act_ref, wk_ref, wv_ref, info, first, out_ref, up_ref, down_ref):
+    out_ref[...] = transposed(act_ref, wk_ref, wv_ref).astype(out_ref.dtype)
+    n_sec, blk, blocks = first
+    mid = blk // 2
+    for i, which in enumerate(blocks):
+        at = block_of(info, which, n_sec) * blk
+        up_ref[i * mid : (i + 1) * mid, :] = out_ref[pl.ds(pl.multiple_of(at, blk), mid), :]
+        down_ref[i * mid : (i + 1) * mid, :] = out_ref[pl.ds(pl.multiple_of(at + mid, mid), mid), :]
+
+
+def partial_grad(act, wk, wv, info, quarters, dtype, after=()):
     total, cols = act.shape[0], wk.shape[1]
     width = wk.shape[0]
-    heads = cols // HEAD
     per = width // XS // UNIT
     n = per * len(quarters)
 
@@ -162,31 +208,11 @@
         return mod4(info[X] - m) * per + i % per
 
     def body(info, act_ref, wk_ref, wv_ref, *refs):
-        sums = None
-        for h in range(heads):
-            for j, w_ref in enumerate((wk_ref, wv_ref)):
-                at = (2 * h + j) * HEAD
-                term = dot_t(act_ref[:, at : at + HEAD], w_ref[:, h * HEAD : (h + 1) * HEAD])
-                sums = term if sums is None else sums + term
-        if first is None:
-            refs[-1][...] = sums.astype(dtype)
-        else:
-            out_ref, up_ref, down_ref = refs[-3:]
-            out_ref[...] = sums.astype(dtype)
-            n_sec, blk, blocks = first
-            mid = blk // 2
-            for i, which in enumerate(blocks):
-                at = block_of(info, which, n_sec) * blk
-                up_ref[i * mid : (i + 1) * mid, :] = out_ref[pl.ds(pl.multiple_of(at, blk), mid), :]
-                down_ref[i * mid : (i + 1) * mid, :] = out_ref[pl.ds(pl.multiple_of(at + mid, mid), mid), :]
+        refs[-1][...] = transposed(act_ref, wk_ref, wv_ref).astype(dtype)
 
     weight = pl.BlockSpec((UNIT, cols), lambda i, info: (unit(i, info), 0))
     block = pl.BlockSpec((total, UNIT), lambda i, info: (0, i))
     out_specs, out_shape = [block], [jax.ShapeDtypeStruct((total, n * UNIT), dtype)]
-    if first is not None:
-        rows = first[1] // 2 * len(first[2])
-        out_specs += [pl.BlockSpec((rows, UNIT), lambda i, info: (0, i))] * 2
-        out_shape += [jax.ShapeDtypeStruct((rows, n * UNIT), dtype)] * 2
     return pl.pallas_call(
         body,
         grid_spec=pltpu.PrefetchScalarGridSpec(
@@ -324,7 +350,10 @@
         last = [(u3, [(blk, mid, 1, 0), (blk + mid, mid, 2, 0)]), (d3, [(blk, mid, 1, mid), (blk + mid, mid, 2, mid)])]
         last += [(u4, [(0, mid, 3, 0)]), (d4, [(0, mid, 3, mid)])]
         asked = (queries[0, 0], ctx_grad[0, 0])
-        context, act, rows[2] = project([(2, last)], enc, wk, wv, acc, info, n_sec, queries=asked)
+        first = (3, 0, 2)
+        context, act, rows[2], far, up, down = project(
+            [(2, last)], enc, wk, wv, acc, info, n_sec, queries=asked, first=first
+        )
         context = context[None, None]
         act_other = swap_core(act)
 
@@ -351,7 +380,6 @@
         sent = pack(False)
         got = swap_core(sent)
 
-        far, up, down = partial_grad(act, wk, wv, info, (2,), bf16, first=(n_sec, blk, (3, 0, 2)))
         halves = both(up, down)
         (near,) = partial_grad(act, wk, wv, info, (3, 1), bf16, (far,))
         kept = pack(True, (near,))

time: 147 us -> 147 us (level)
    pallas_call x3 -> x2, Pallas kernels: 8.15 us -> 5.89 us  [partial_grad(): pl.pallas_call(body, grid_spec=pltpu.PrefetchScalarGridSpec(num_scalar_pr...]
    pallas_call x3, Pallas kernels: 12.3 us -> 14.2 us  [project(): pl.pallas_call(body, grid_spec=pltpu.PrefetchScalarGridSpec(num_scalar_pr...]
  transfers between devices with their start and end apart: 32 -> 32, of which waited for: 15 -> 15; matrix products, arithmetic and copies ran while one was open for 0% -> 0% of each run, Pallas kernels for 20% -> 18%
where the time goes in v7:
time: 147 us; the launch traced here: 146 us
  waiting for transfers between devices  51.2 us (35%)
  starting transfers between devices  48.7 us (33%)
  Pallas kernels  38.2 us (26%)
  local copies, waits for them, and re-layouts  5.54 us (4%)
  between operations  2.19 us (1%)
    ppermute x20, starting transfers between devices, shift_x(): return lax.ppermute(v, 'x', [(i, (i + k) % XS) for i in range(XS)])  32 us
    ppermute x20, waiting for transfers between devices, shift_x(): return lax.ppermute(v, 'x', [(i, (i + k) % XS) for i in range(XS)])  26.2 us
    pallas_call x15, Pallas kernels, small(): pl.pallas_call(run, grid_spec=pltpu.PrefetchScalarGridSpec(num_scalar_pre...  16.9 us
    pallas_call x3, Pallas kernels, project(): pl.pallas_call(body, grid_spec=pltpu.PrefetchScalarGridSpec(num_scalar_pr...  14.2 us
    ppermute x4, waiting for transfers between devices, cross(): lax.ppermute(v, ('section', 'low'), [(z, (z + (1 if z % 2 else -1)) % n)...  9.58 us
    ppermute x1, waiting for transfers between devices, swap_low(): return lax.ppermute(v, 'low', [(0, 1), (1, 0)])  8.65 us
    ppermute x2, waiting for transfers between devices, jump(): lax.ppermute(v, ('section', 'low'), [(z, (z + (-2 * k if z % 2 else 2 * k...  6.71 us
    ppermute x2, starting transfers between devices, jump(): lax.ppermute(v, ('section', 'low'), [(z, (z + (-2 * k if z % 2 else 2 * k...  6.64 us
  transfers between devices with their start and end apart: 32, of which 15 were waited for; matrix products, arithmetic and copies ran while one was open for 0% of the time, Pallas kernels for 18%

profile of v7, /device:TPU:8, one launch (start us, length us, event | category | flops | bytes accessed | tf_op | source)
XLA Modules:
  0.0 145.9 jit_solution(14606805129260896849)
XLA Ops:
  0.6 1.1 dynamic-slice_bitcast_fusion
  1.7 6.4 %collective-permute-start = (bf16[128,1024]{1,0:T(8,128)(2,1)S(1)}, bf16[128,1024]{1,0:T(8,128)(2,1)S(1)}, u32[]{:S(2)}, u32[]{:S(2)}) collective-permute-start(bf16[128,1024]{1,0:T(8,128)(2,1)S(1)} %dynamic-slice_bitcast_fusion), channel_id=1, source_target_pairs={{0,192},{1,65},{64,0},{65,129},{128,64},{129,193},{192,128},{193,1... | collective-permute-start | bytes 786440 | tf_op jit(solution)/shard_map/ppermute | solution.py:283
  8.1 6.7 %collective-permute-done.refs_2_ = bf16[128,1024]{1,0:T(8,128)(2,1)S(1)} collective-permute-done((bf16[128,1024]{1,0:T(8,128)(2,1)S(1)}, bf16[128,1024]{1,0:T(8,128)(2,1)S(1)}, u32[]{:S(2)}, u32[]{:S(2)}) %collective-permute-start) | collective-permute-done | bytes 262176 | tf_op jit(solution)/shard_map/ppermute | solution.py:283
  14.8 2.9 %collective-permute-start.1 = (bf16[128,1024]{1,0:T(8,128)(2,1)S(1)}, bf16[128,1024]{1,0:T(8,128)(2,1)S(1)}, u32[]{:S(2)}, u32[]{:S(2)}) collective-permute-start(bf16[128,1024]{1,0:T(8,128)(2,1)S(1)} %collective-permute-done.refs_2_), channel_id=1, source_target_pairs={{0,193},{1,64},{64,1},{65,128},{128,65},{129,192},{192,129},{193,0... | collective-permute-start | bytes 786440 | tf_op jit(solution)/shard_map/ppermute | solution.py:279
  17.7 1.5 %collective-permute-start.4 = (bf16[128,1024]{1,0:T(8,128)(2,1)S(1)}, bf16[128,1024]{1,0:T(8,128)(2,1)S(1)}, u32[]{:S(2)}, u32[]{:S(2)}) collective-permute-start(bf16[128,1024]{1,0:T(8,128)(2,1)S(1)} %collective-permute-done.refs_2_), channel_id=1, source_target_pairs={{0,2},{2,4},{4,6},{6,0},{1,3},{3,5},{5,7},{7,1},{8,10},{10,12},{12... | collective-permute-start | bytes 786440 | tf_op jit(solution)/shard_map/ppermute | solution.py:269
  19.2 1.7 %collective-permute-start.6 = (bf16[128,1024]{1,0:T(8,128)(2,1)S(1)}, bf16[128,1024]{1,0:T(8,128)(2,1)S(1)}, u32[]{:S(2)}, u32[]{:S(2)}) collective-permute-start(bf16[128,1024]{1,0:T(8,128)(2,1)S(1)} %collective-permute-done.refs_2_), channel_id=1, source_target_pairs={{0,6},{2,0},{4,2},{6,4},{1,7},{3,1},{5,3},{7,5},{8,14},{10,8},{12,... | collective-permute-start | bytes 786440 | tf_op jit(solution)/shard_map/ppermute | solution.py:269
  21.0 0.9 collective-permute-start.3
  21.9 2.3 %collective-permute-start.5 = (bf16[128,1024]{1,0:T(8,128)(2,1)S(1)}, bf16[128,1024]{1,0:T(8,128)(2,1)S(1)}, u32[]{:S(2)}, u32[]{:S(2)}) collective-permute-start(bf16[128,1024]{1,0:T(8,128)(2,1)S(1)} %collective-permute-done.2.refs_1_), channel_id=1, source_target_pairs={{0,6},{2,0},{4,2},{6,4},{1,7},{3,1},{5,3},{7,5},{8,14},{10,8},{12,... | collective-permute-start | bytes 786440 | tf_op jit(solution)/shard_map/ppermute | solution.py:269
  25.6 2.4 %collective-permute-done.4.refs_2_.refs_3_ = bf16[128,1024]{1,0:T(8,128)(2,1)S(1)} collective-permute-done((bf16[128,1024]{1,0:T(8,128)(2,1)S(1)}, bf16[128,1024]{1,0:T(8,128)(2,1)S(1)}, u32[]{:S(2)}, u32[]{:S(2)}) %collective-permute-start.4) | collective-permute-done | bytes 262176 | tf_op jit(solution)/shard_map/ppermute | solution.py:269
  28.0 0.3 collective-permute-done.6.refs_4_.refs_6_
  28.3 2.7 %collective-permute-done.3.refs_1_.refs_2_ = bf16[128,1024]{1,0:T(8,128)(2,1)S(1)} collective-permute-done((bf16[128,1024]{1,0:T(8,128)(2,1)S(1)}, bf16[128,1024]{1,0:T(8,128)(2,1)S(1)}, u32[]{:S(2)}, u32[]{:S(2)}) %collective-permute-start.3) | collective-permute-done | bytes 262176 | tf_op jit(solution)/shard_map/ppermute | solution.py:269
  30.9 0.1 collective-permute-done.5.refs_3_.refs_5_
  31.1 0.6 shard_map.102
  31.7 1.6 %collective-permute-start.7 = (bf16[256,1024]{1,0:T(8,128)(2,1)S(1)}, bf16[256,1024]{1,0:T(8,128)(2,1)S(1)}, u32[]{:S(2)}, u32[]{:S(2)}) collective-permute-start(bf16[256,1024]{1,0:T(8,128)(2,1)S(1)} %get-tuple-element.40.refs_6_), channel_id=1, source_target_pairs={{0,2},{2,4},{4,6},{6,0},{1,3},{3,5},{5,7},{7,1},{8,10},{10,12},{12... | collective-permute-start | bytes 1572872 | tf_op jit(solution)/shard_map/ppermute | solution.py:269
  33.3 1.7 %collective-permute-start.8 = (bf16[256,1024]{1,0:T(8,128)(2,1)S(1)}, bf16[256,1024]{1,0:T(8,128)(2,1)S(1)}, u32[]{:S(2)}, u32[]{:S(2)}) collective-permute-start(bf16[256,1024]{1,0:T(8,128)(2,1)S(1)} %get-tuple-element.41.refs_7_), channel_id=1, source_target_pairs={{0,6},{2,0},{4,2},{6,4},{1,7},{3,1},{5,3},{7,5},{8,14},{10,8},{12,... | collective-permute-start | bytes 1572872 | tf_op jit(solution)/shard_map/ppermute | solution.py:269
  35.0 2.2 %copy-done = bf16[1,4096,512]{2,1,0:T(8,128)(2,1)S(1)} copy-done((bf16[1,4096,512]{2,1,0:T(8,128)(2,1)S(1)}, bf16[1,4096,512]{2,1,0:T(8,128)(2,1)}, u32[]{:S(2)}) %copy-start) | copy-done | bytes 4194328
  37.2 2.2 %copy-done.2 = bf16[1,4096,512]{2,1,0:T(8,128)(2,1)S(1)} copy-done((bf16[1,4096,512]{2,1,0:T(8,128)(2,1)S(1)}, bf16[1,4096,512]{2,1,0:T(8,128)(2,1)}, u32[]{:S(2)}) %copy-start.2) | copy-done | bytes 4194328
  39.4 2.5 %shard_map.103 = (f32[512,1024]{1,0:T(8,128)S(1)}, bf16[512,1024]{1,0:T(8,128)(2,1)S(1)}) custom-call(s32[7]{0:T(128)S(1)} %stack.25.info, bf16[128,4096]{1,0:T(8,128)(2,1)S(1)} %bitcast.30, bf16[128,1024]{1,0:T(8,128)(2,1)S(1)} %collective-permute-done.2.refs_1_, bf16[128,1024]{1,0:T(8,128)(2,1)S(1)} %collective-permute-done.refs_2_, ...), custom_call_target="tpu_custom_call" | custom-call | flops 1 | bytes 1 | tf_op jit(solution)/shard_map/pallas_call | solution.py:135
  41.9 2.2 %collective-permute-done.7.refs_0_.refs_4_.refs_1_ = bf16[256,1024]{1,0:T(8,128)(2,1)S(1)} collective-permute-done((bf16[256,1024]{1,0:T(8,128)(2,1)S(1)}, bf16[256,1024]{1,0:T(8,128)(2,1)S(1)}, u32[]{:S(2)}, u32[]{:S(2)}) %collective-permute-start.7) | collective-permute-done | bytes 524320 | tf_op jit(solution)/shard_map/ppermute | solution.py:269
  44.1 0.6 shard_map.104
  44.7 3.0 %collective-permute-start.10 = (bf16[64,1024]{1,0:T(8,128)(2,1)S(1)}, bf16[64,1024]{1,0:T(8,128)(2,1)S(1)}, u32[]{:S(2)}, u32[]{:S(2)}) collective-permute-start(bf16[64,1024]{1,0:T(8,128)(2,1)S(1)} %get-tuple-element.44.refs_14_), channel_id=1, source_target_pairs={{0,6},{2,0},{4,2},{6,4},{1,7},{3,1},{5,3},{7,5},{8,14},{10,8},{12,... | collective-permute-start | bytes 393224 | tf_op jit(solution)/shard_map/ppermute | solution.py:269
  47.7 4.0 %shard_map.105 = (f32[512,1024]{1,0:T(8,128)S(1)}, bf16[512,1024]{1,0:T(8,128)(2,1)S(1)}, bf16[512,1024]{1,0:T(8,128)(2,1)S(1)}) custom-call(s32[7]{0:T(128)S(1)} %stack.25.info, bf16[128,4096]{1,0:T(8,128)(2,1)S(1)} %bitcast.31, bf16[128,4096]{1,0:T(8,128)(2,1)S(1)} %bitcast.32, bf16[128,1024]{1,0:T(8,128)(2,1)S(1)} %collective-permute-done.3.refs_1_.refs_2_, ...), custom_call_target="tpu_custom_call" | custom-call | flops 1 | bytes 1 | tf_op jit(solution)/shard_map/pallas_call | solution.py:135
  51.8 2.1 %collective-permute-done.9.refs_3_ = bf16[64,1024]{1,0:T(8,128)(2,1)S(1)} collective-permute-done((bf16[64,1024]{1,0:T(8,128)(2,1)S(1)}, bf16[64,1024]{1,0:T(8,128)(2,1)S(1)}, u32[]{:S(2)}, u32[]{:S(2)}) %collective-permute-start.9) | collective-permute-done | bytes 131104 | tf_op jit(solution)/shard_map/ppermute | solution.py:269
  53.9 7.7 %shard_map.106 = (bf16[512,512]{1,0:T(8,128)(2,1)}, bf16[512,1024]{1,0:T(8,128)(2,1)S(1)}, bf16[512,1024]{1,0:T(8,128)(2,1)S(1)}, bf16[512,1024]{1,0:T(8,128)(2,...) custom-call(s32[7]{0:T(128)S(1)} %stack.25.info, bf16[128,4096]{1,0:T(8,128)(2,1)S(1)} %bitcast.33, ...), custom_call_target="tpu_custom_call" | custom-call | flops 1 | bytes 1 | tf_op jit(solution)/shard_map/pallas_call | solution.py:135
  61.6 0.8 shard_map.110
  62.4 0.5 collective-permute-start.14
  62.9 3.2 %collective-permute-start.12 = (bf16[192,1024]{1,0:T(8,128)(2,1)S(1)}, bf16[192,1024]{1,0:T(8,128)(2,1)S(1)}, u32[]{:S(2)}, u32[]{:S(2)}) collective-permute-start(bf16[192,1024]{1,0:T(8,128)(2,1)S(1)} %get-tuple-element.50), channel_id=1, source_target_pairs={{0,6},{2,0},{4,2},{6,4},{1,7},{3,1},{5,3},{7,5},{8,14},{10,8},{12,... | collective-permute-start | bytes 1179656 | tf_op jit(solution)/shard_map/ppermute | solution.py:269
  66.2 3.7 %shard_map.107.refs_0_.refs_4_.refs_3_.refs_6_.refs_7_ = bf16[512,2048]{1,0:T(8,128)(2,1)S(1)} custom-call(s32[7]{0:T(128)S(1)} %stack.25.info, bf16[512,1024]{1,0:T(8,128)(2,1)S(1)} %get-tuple-element.47.act_ref.refs_2_, bf16[4096,512]{1,0:T(8,128)(2,1)S(1)} %bitcast.21, bf16[4096,512]{1,0:T(8,128)(2,1)S(1)} %bitcast.28, ...), custom_call_target="tpu_custom_call" | custom-call | flops 1 | bytes 1 | tf_op jit(solution)/shard_map/pallas_call | solution.py:216
  69.9 0.8 shard_map.109.refs_0_
  70.7 1.8 %shard_map.111.refs_4_ = bf16[512,1024]{1,0:T(8,128)(2,1)S(1)} custom-call(s32[7]{0:T(128)S(1)} %stack.25.info, bf16[512,2048]{1,0:T(8,128)(2,1)S(1)} %shard_map.109.refs_0_, bf16[512,2048]{1,0:T(8,128)(2,1)S(1)} %collective-permute-done.13.refs_1_, bf16[512,1024]{1,0:T(8,128)(2,1)S(1)} %get-tuple-element.47.act_ref.refs_2_, ...), custom_call_target="tpu_custom_call" | custom-call | flops 1 | bytes 1 | tf_op jit(solution)/shard_map/pallas_call | solution.py:252
  72.5 2.8 %collective-permute-done.11.refs_1_.refs_4_.refs_8_ = bf16[192,1024]{1,0:T(8,128)(2,1)S(1)} collective-permute-done((bf16[192,1024]{1,0:T(8,128)(2,1)S(1)}, bf16[192,1024]{1,0:T(8,128)(2,1)S(1)}, u32[]{:S(2)}, u32[]{:S(2)}) %collective-permute-start.11) | collective-permute-done | bytes 393248 | tf_op jit(solution)/shard_map/ppermute | solution.py:269
  75.3 0.7 shard_map.112
  76.1 3.2 %collective-permute-start.16 = (bf16[192,1024]{1,0:T(8,128)(2,1)S(1)}, bf16[192,1024]{1,0:T(8,128)(2,1)S(1)}, u32[]{:S(2)}, u32[]{:S(2)}) collective-permute-start(bf16[192,1024]{1,0:T(8,128)(2,1)S(1)} %get-tuple-element.56), channel_id=1, source_target_pairs={{0,6},{2,0},{4,2},{6,4},{1,7},{3,1},{5,3},{7,5},{8,14},{10,8},{12,... | collective-permute-start | bytes 1179656 | tf_op jit(solution)/shard_map/ppermute | solution.py:269
  79.3 1.6 %collective-permute-start.24 = (bf16[512,1024]{1,0:T(8,128)(2,1)S(1)}, bf16[512,1024]{1,0:T(8,128)(2,1)S(1)}, u32[]{:S(2)}, u32[]{:S(2)}) collective-permute-start(bf16[512,1024]{1,0:T(8,128)(2,1)S(1)} %get-tuple-element.65), channel_id=1, source_target_pairs={{0,16},{8,56},{16,32},{24,8},{32,48},{40,24},{48,0},{56,40},{1,17}... | collective-permute-start | bytes 3145736 | tf_op jit(solution)/shard_map/ppermute | solution.py:288
  80.8 2.2 %shard_map.108.refs_0_.refs_4_ = f32[512,1024]{1,0:T(8,128)S(1)} custom-call(s32[7]{0:T(128)S(1)} %stack.25.info, bf16[512,1024]{1,0:T(8,128)(2,1)S(1)} %get-tuple-element.47.act_ref.refs_2_, bf16[4096,512]{1,0:T(8,128)(2,1)S(1)} %bitcast.22, bf16[4096,512]{1,0:T(8,128)(2,1)S(1)} %bitcast.29, ...), custom_call_target="tpu_custom_call" | custom-call | flops 1 | bytes 1 | tf_op jit(solution)/shard_map/pallas_call | solution.py:216
  83.0 4.5 %collective-permute-done.15.refs_1_.refs_7_ = bf16[192,1024]{1,0:T(8,128)(2,1)S(1)} collective-permute-done((bf16[192,1024]{1,0:T(8,128)(2,1)S(1)}, bf16[192,1024]{1,0:T(8,128)(2,1)S(1)}, u32[]{:S(2)}, u32[]{:S(2)}) %collective-permute-start.15) | collective-permute-done | bytes 393248 | tf_op jit(solution)/shard_map/ppermute | solution.py:269
  87.5 0.8 shard_map.113
  88.3 0.9 collective-permute-start.17
  89.2 2.4 %collective-permute-start.18 = (bf16[256,1024]{1,0:T(8,128)(2,1)S(1)}, bf16[256,1024]{1,0:T(8,128)(2,1)S(1)}, u32[]{:S(2)}, u32[]{:S(2)}) collective-permute-start(bf16[256,1024]{1,0:T(8,128)(2,1)S(1)} %get-tuple-element.58), channel_id=1, source_target_pairs={{0,6},{2,0},{4,2},{6,4},{1,7},{3,1},{5,3},{7,5},{8,14},{10,8},{12,... | collective-permute-start | bytes 1572872 | tf_op jit(solution)/shard_map/ppermute | solution.py:269
  91.6 0.3 collective-permute-start.19
  91.9 7.3 %collective-permute-done.19.refs_3_ = bf16[128,1024]{1,0:T(8,128)(2,1)S(1)} collective-permute-done((bf16[128,1024]{1,0:T(8,128)(2,1)S(1)}, bf16[128,1024]{1,0:T(8,128)(2,1)S(1)}, u32[]{:S(2)}, u32[]{:S(2)}) %collective-permute-start.19) | collective-permute-done | bytes 262176 | tf_op jit(solution)/shard_map/ppermute | solution.py:279
  99.2 2.6 %collective-permute-done.17.refs_1_.refs_5_ = bf16[256,1024]{1,0:T(8,128)(2,1)S(1)} collective-permute-done((bf16[256,1024]{1,0:T(8,128)(2,1)S(1)}, bf16[256,1024]{1,0:T(8,128)(2,1)S(1)}, u32[]{:S(2)}, u32[]{:S(2)}) %collective-permute-start.17) | collective-permute-done | bytes 524320 | tf_op jit(solution)/shard_map/ppermute | solution.py:269
  101.8 0.8 shard_map.114
  102.6 0.9 collective-permute-start.20
  103.5 2.4 %collective-permute-start.21 = (bf16[128,1024]{1,0:T(8,128)(2,1)S(1)}, bf16[128,1024]{1,0:T(8,128)(2,1)S(1)}, u32[]{:S(2)}, u32[]{:S(2)}) collective-permute-start(bf16[128,1024]{1,0:T(8,128)(2,1)S(1)} %get-tuple-element.61), channel_id=1, source_target_pairs={{0,6},{2,0},{4,2},{6,4},{1,7},{3,1},{5,3},{7,5},{8,14},{10,8},{12,... | collective-permute-start | bytes 786440 | tf_op jit(solution)/shard_map/ppermute | solution.py:269
  105.9 0.3 collective-permute-start.22
  106.2 2.8 %collective-permute-start.23 = (bf16[128,1024]{1,0:T(8,128)(2,1)S(1)}, bf16[128,1024]{1,0:T(8,128)(2,1)S(1)}, u32[]{:S(2)}, u32[]{:S(2)}) collective-permute-start(bf16[128,1024]{1,0:T(8,128)(2,1)S(1)} %get-tuple-element.63.refs_2_), channel_id=1, source_target_pairs={{0,193},{1,64},{64,1},{65,128},{128,65},{129,192},{192,129},{193,0... | collective-permute-start | bytes 786440 | tf_op jit(solution)/shard_map/ppermute | solution.py:279
  109.0 4.0 %shard_map.115 = (bf16[1024,1024]{1,0:T(8,128)(2,1)S(1)}, bf16[512,1024]{1,0:T(8,128)(2,1)S(1)}) custom-call(s32[7]{0:T(128)S(1)} %stack.25.info, bf16[512,2048]{1,0:T(8,128)(2,1)S(1)} %shard_map.109.refs_0_, bf16[512,2048]{1,0:T(8,128)(2,1)S(1)} %collective-permute-done.13.refs_1_, bf16[512,1024]{1,0:T(8,128)(2,1)S(1)} %get-tuple-element.47.act_ref.refs_2_, ...), custom_call_target="tpu_custom_call" | custom-call | flops 1 | bytes 1 | tf_op jit(solution)/shard_map/pallas_call | solution.py:252
  113.0 0.8 shard_map.116
  113.8 1.6 %collective-permute-start.30 = (bf16[512,1024]{1,0:T(8,128)(2,1)S(1)}, bf16[512,1024]{1,0:T(8,128)(2,1)S(1)}, u32[]{:S(2)}, u32[]{:S(2)}) collective-permute-start(bf16[512,1024]{1,0:T(8,128)(2,1)S(1)} %get-tuple-element.71), channel_id=1, source_target_pairs={{0,16},{8,56},{16,32},{24,8},{32,48},{40,24},{48,0},{56,40},{1,17}... | collective-permute-start | bytes 3145736 | tf_op jit(solution)/shard_map/ppermute | solution.py:288
  115.5 2.3 %collective-permute-done.23.refs_4_ = bf16[128,1024]{1,0:T(8,128)(2,1)S(1)} collective-permute-done((bf16[128,1024]{1,0:T(8,128)(2,1)S(1)}, bf16[128,1024]{1,0:T(8,128)(2,1)S(1)}, u32[]{:S(2)}, u32[]{:S(2)}) %collective-permute-start.23) | collective-permute-done | bytes 262176 | tf_op jit(solution)/shard_map/ppermute | solution.py:279
  117.8 0.7 shard_map.117
  118.7 8.7 %collective-permute-done.25.refs_1_ = bf16[128,1024]{1,0:T(8,128)(2,1)S(1)} collective-permute-done((bf16[128,1024]{1,0:T(8,128)(2,1)S(1)}, bf16[128,1024]{1,0:T(8,128)(2,1)S(1)}, u32[]{:S(2)}, u32[]{:S(2)}) %collective-permute-start.25) | collective-permute-done | bytes 262176 | tf_op jit(solution)/shard_map/ppermute | solution.py:275
  127.4 0.7 shard_map.118
  128.0 1.5 %collective-permute-start.27 = (bf16[128,1024]{1,0:T(8,128)(2,1)S(1)}, bf16[128,1024]{1,0:T(8,128)(2,1)S(1)}, u32[]{:S(2)}, u32[]{:S(2)}) collective-permute-start(bf16[128,1024]{1,0:T(8,128)(2,1)S(1)} %get-tuple-element.69.refs_0_), channel_id=1, source_target_pairs={{0,6},{2,0},{4,2},{6,4},{1,7},{3,1},{5,3},{7,5},{8,14},{10,8},{12,... | collective-permute-start | bytes 786440 | tf_op jit(solution)/shard_map/ppermute | solution.py:269
  129.6 0.6 collective-permute-start.29
  130.1 1.2 collective-permute-start.26
  131.3 6.0 %collective-permute-done.27.refs_0_.refs_2_ = bf16[128,1024]{1,0:T(8,128)(2,1)S(1)} collective-permute-done((bf16[128,1024]{1,0:T(8,128)(2,1)S(1)}, bf16[128,1024]{1,0:T(8,128)(2,1)S(1)}, u32[]{:S(2)}, u32[]{:S(2)}) %collective-permute-start.27) | collective-permute-done | bytes 262176 | tf_op jit(solution)/shard_map/ppermute | solution.py:269
  137.3 0.5 shard_map.119.refs_3_
  137.9 2.8 %collective-permute-start.28 = (bf16[64,1024]{1,0:T(8,128)(2,1)S(1)}, bf16[64,1024]{1,0:T(8,128)(2,1)S(1)}, u32[]{:S(2)}, u32[]{:S(2)}) collective-permute-start(bf16[64,1024]{1,0:T(8,128)(2,1)S(1)} %shard_map.119.refs_3_), channel_id=1, source_target_pairs={{0,6},{2,0},{4,2},{6,4},{1,7},{3,1},{5,3},{7,5},{8,14},{10,8},{12,... | collective-permute-start | bytes 393224 | tf_op jit(solution)/shard_map/ppermute | solution.py:269
  140.6 0.6 collective-permute-done.29.refs_1_
  141.2 1.6 %shard_map.120._ = bf16[128,4096]{1,0:T(8,128)(2,1)} custom-call(s32[7]{0:T(128)S(1)} %stack.25.info, bf16[128,1024]{1,0:T(8,128)(2,1)S(1)} %get-tuple-element.69.refs_0_, bf16[128,1024]{1,0:T(8,128)(2,1)S(1)} %collective-permute-done.29.refs_1_, bf16[128,1024]{1,0:T(8,128)(2,1)S(1)} %collective-permute-done.27.refs_0_.refs_2_, ...), custom_call_target="tpu_custom_call" | custom-call | flops 1 | bytes 1 | tf_op jit(solution)/shard_map/pallas_call | solution.py:252
  142.8 1.8 %shard_map.121 = (bf16[512,512]{1,0:T(8,128)(2,1)}, bf16[512,512]{1,0:T(8,128)(2,1)}, bf16[16,128]{1,0:T(8,128)(2,1)S(1)}) custom-call(s32[7]{0:T(128)S(1)} %stack.25.info, bf16[512,1024]{1,0:T(8,128)(2,1)S(1)} %get-tuple-element.70.refs_0_, bf16[512,1024]{1,0:T(8,128)(2,1)S(1)} %collective-permute-done.30.refs_1_, ...), custom_call_target="tpu_custom_call" | custom-call | flops 1 | bytes 1 | tf_op jit(solution)/shard_map/pallas_call | solution.py:252
  144.6 1.3 shard_map.122
  (37 shorter events, 0.6 us)
Async XLA Ops:
  0.6 34.4 %copy-start.4 = (bf16[1,128,4096]{2,1,0:T(8,128)(2,1)S(1)}, bf16[1,128,4096]{2,1,0:T(8,128)(2,1)}, u32[]{:S(2)}) copy-start(bf16[1,128,4096]{2,1,0:T(8,128)(2,1)} %param.7) | copy-start | bytes 3145732
  1.7 13.1 %collective-permute-start = (bf16[128,1024]{1,0:T(8,128)(2,1)S(1)}, bf16[128,1024]{1,0:T(8,128)(2,1)S(1)}, u32[]{:S(2)}, u32[]{:S(2)}) collective-permute-start(bf16[128,1024]{1,0:T(8,128)(2,1)S(1)} %dynamic-slice_bitcast_fusion), channel_id=1, source_target_pairs={{0,192},{1,65},{64,0},{65,129},{128,64},{129,193},{192,128},{193,1... | collective-permute-start | bytes 786440 | tf_op jit(solution)/shard_map/ppermute | solution.py:283
  8.1 12.9 %collective-permute-start.2 = (bf16[128,1024]{1,0:T(8,128)(2,1)S(1)}, bf16[128,1024]{1,0:T(8,128)(2,1)S(1)}, u32[]{:S(2)}, u32[]{:S(2)}) collective-permute-start(bf16[128,1024]{1,0:T(8,128)(2,1)S(1)} %dynamic-slice_bitcast_fusion), channel_id=1, source_target_pairs={{0,193},{1,64},{64,1},{65,128},{128,65},{129,192},{192,129},{193,0... | collective-permute-start | bytes 786440 | tf_op jit(solution)/shard_map/ppermute | solution.py:279
  14.8 10.8 %collective-permute-start.1 = (bf16[128,1024]{1,0:T(8,128)(2,1)S(1)}, bf16[128,1024]{1,0:T(8,128)(2,1)S(1)}, u32[]{:S(2)}, u32[]{:S(2)}) collective-permute-start(bf16[128,1024]{1,0:T(8,128)(2,1)S(1)} %collective-permute-done.refs_2_), channel_id=1, source_target_pairs={{0,193},{1,64},{64,1},{65,128},{128,65},{129,192},{192,129},{193,0... | collective-permute-start | bytes 786440 | tf_op jit(solution)/shard_map/ppermute | solution.py:279
  17.7 10.2 %collective-permute-start.4 = (bf16[128,1024]{1,0:T(8,128)(2,1)S(1)}, bf16[128,1024]{1,0:T(8,128)(2,1)S(1)}, u32[]{:S(2)}, u32[]{:S(2)}) collective-permute-start(bf16[128,1024]{1,0:T(8,128)(2,1)S(1)} %collective-permute-done.refs_2_), channel_id=1, source_target_pairs={{0,2},{2,4},{4,6},{6,0},{1,3},{3,5},{5,7},{7,1},{8,10},{10,12},{12... | collective-permute-start | bytes 786440 | tf_op jit(solution)/shard_map/ppermute | solution.py:269
  19.2 9.0 %collective-permute-start.6 = (bf16[128,1024]{1,0:T(8,128)(2,1)S(1)}, bf16[128,1024]{1,0:T(8,128)(2,1)S(1)}, u32[]{:S(2)}, u32[]{:S(2)}) collective-permute-start(bf16[128,1024]{1,0:T(8,128)(2,1)S(1)} %collective-permute-done.refs_2_), channel_id=1, source_target_pairs={{0,6},{2,0},{4,2},{6,4},{1,7},{3,1},{5,3},{7,5},{8,14},{10,8},{12,... | collective-permute-start | bytes 786440 | tf_op jit(solution)/shard_map/ppermute | solution.py:269
  21.0 10.0 %collective-permute-start.3 = (bf16[128,1024]{1,0:T(8,128)(2,1)S(1)}, bf16[128,1024]{1,0:T(8,128)(2,1)S(1)}, u32[]{:S(2)}, u32[]{:S(2)}) collective-permute-start(bf16[128,1024]{1,0:T(8,128)(2,1)S(1)} %collective-permute-done.2.refs_1_), channel_id=1, source_target_pairs={{0,2},{2,4},{4,6},{6,0},{1,3},{3,5},{5,7},{7,1},{8,10},{10,12},{12... | collective-permute-start | bytes 786440 | tf_op jit(solution)/shard_map/ppermute | solution.py:269
  21.9 9.2 %collective-permute-start.5 = (bf16[128,1024]{1,0:T(8,128)(2,1)S(1)}, bf16[128,1024]{1,0:T(8,128)(2,1)S(1)}, u32[]{:S(2)}, u32[]{:S(2)}) collective-permute-start(bf16[128,1024]{1,0:T(8,128)(2,1)S(1)} %collective-permute-done.2.refs_1_), channel_id=1, source_target_pairs={{0,6},{2,0},{4,2},{6,4},{1,7},{3,1},{5,3},{7,5},{8,14},{10,8},{12,... | collective-permute-start | bytes 786440 | tf_op jit(solution)/shard_map/ppermute | solution.py:269
  31.7 12.4 %collective-permute-start.7 = (bf16[256,1024]{1,0:T(8,128)(2,1)S(1)}, bf16[256,1024]{1,0:T(8,128)(2,1)S(1)}, u32[]{:S(2)}, u32[]{:S(2)}) collective-permute-start(bf16[256,1024]{1,0:T(8,128)(2,1)S(1)} %get-tuple-element.40.refs_6_), channel_id=1, source_target_pairs={{0,2},{2,4},{4,6},{6,0},{1,3},{3,5},{5,7},{7,1},{8,10},{10,12},{12... | collective-permute-start | bytes 1572872 | tf_op jit(solution)/shard_map/ppermute | solution.py:269
  33.3 10.9 %collective-permute-start.8 = (bf16[256,1024]{1,0:T(8,128)(2,1)S(1)}, bf16[256,1024]{1,0:T(8,128)(2,1)S(1)}, u32[]{:S(2)}, u32[]{:S(2)}) collective-permute-start(bf16[256,1024]{1,0:T(8,128)(2,1)S(1)} %get-tuple-element.41.refs_7_), channel_id=1, source_target_pairs={{0,6},{2,0},{4,2},{6,4},{1,7},{3,1},{5,3},{7,5},{8,14},{10,8},{12,... | collective-permute-start | bytes 1572872 | tf_op jit(solution)/shard_map/ppermute | solution.py:269
  35.0 2.2 %copy-start = (bf16[1,4096,512]{2,1,0:T(8,128)(2,1)S(1)}, bf16[1,4096,512]{2,1,0:T(8,128)(2,1)}, u32[]{:S(2)}) copy-start(bf16[1,4096,512]{2,1,0:T(8,128)(2,1)} %param.8) | copy-start | bytes 12582916
  37.2 2.2 %copy-start.2 = (bf16[1,4096,512]{2,1,0:T(8,128)(2,1)S(1)}, bf16[1,4096,512]{2,1,0:T(8,128)(2,1)}, u32[]{:S(2)}) copy-start(bf16[1,4096,512]{2,1,0:T(8,128)(2,1)} %param.9) | copy-start | bytes 12582916
  39.4 8.3 %copy-start.1 = (bf16[1,4096,512]{2,1,0:T(8,128)(2,1)S(1)}, bf16[1,4096,512]{2,1,0:T(8,128)(2,1)}, u32[]{:S(2)}) copy-start(bf16[1,4096,512]{2,1,0:T(8,128)(2,1)} %param.8) | copy-start | bytes 12582916
  39.4 8.3 %copy-start.3 = (bf16[1,4096,512]{2,1,0:T(8,128)(2,1)S(1)}, bf16[1,4096,512]{2,1,0:T(8,128)(2,1)}, u32[]{:S(2)}) copy-start(bf16[1,4096,512]{2,1,0:T(8,128)(2,1)} %param.9) | copy-start | bytes 12582916
  44.7 7.1 %collective-permute-start.10 = (bf16[64,1024]{1,0:T(8,128)(2,1)S(1)}, bf16[64,1024]{1,0:T(8,128)(2,1)S(1)}, u32[]{:S(2)}, u32[]{:S(2)}) collective-permute-start(bf16[64,1024]{1,0:T(8,128)(2,1)S(1)} %get-tuple-element.44.refs_14_), channel_id=1, source_target_pairs={{0,6},{2,0},{4,2},{6,4},{1,7},{3,1},{5,3},{7,5},{8,14},{10,8},{12,... | collective-permute-start | bytes 393224 | tf_op jit(solution)/shard_map/ppermute | solution.py:269
  47.7 6.2 %copy-start.5 = (bf16[1,1,512,512]{3,2,1,0:T(8,128)(2,1)S(1)}, bf16[1,1,512,512]{3,2,1,0:T(8,128)(2,1)}, u32[]{:S(2)}) copy-start(bf16[1,1,512,512]{3,2,1,0:T(8,128)(2,1)} %param.10) | copy-start | bytes 1572868
  47.7 6.2 %copy-start.6 = (bf16[1,1,512,512]{3,2,1,0:T(8,128)(2,1)S(1)}, bf16[1,1,512,512]{3,2,1,0:T(8,128)(2,1)}, u32[]{:S(2)}) copy-start(bf16[1,1,512,512]{3,2,1,0:T(8,128)(2,1)} %param.11) | copy-start | bytes 1572868
  47.7 6.2 %collective-permute-start.9 = (bf16[64,1024]{1,0:T(8,128)(2,1)S(1)}, bf16[64,1024]{1,0:T(8,128)(2,1)S(1)}, u32[]{:S(2)}, u32[]{:S(2)}) collective-permute-start(bf16[64,1024]{1,0:T(8,128)(2,1)S(1)} %get-tuple-element.43.refs_13_), channel_id=1, source_target_pairs={{0,2},{2,4},{4,6},{6,0},{1,3},{3,5},{5,7},{7,1},{8,10},{10,12},{12... | collective-permute-start | bytes 393224 | tf_op jit(solution)/shard_map/ppermute | solution.py:269
  62.3 8.3 %collective-permute-start.13 = (bf16[512,2048]{1,0:T(8,128)(2,1)S(1)}, bf16[512,2048]{1,0:T(8,128)(2,1)S(1)}, u32[]{:S(2)}, u32[]{:S(2)}) collective-permute-start(bf16[512,2048]{1,0:T(8,128)(2,1)S(1)} %shard_map.110), channel_id=1, source_target_pairs={{0,8},{8,0},{1,9},{9,1},{2,10},{10,2},{3,11},{11,3},{4,12},{12,4},... | collective-permute-start | bytes 6291464 | tf_op jit(solution)/shard_map/ppermute | solution.py:272
  62.4 8.2 %collective-permute-start.14 = (bf16[512,1024]{1,0:T(8,128)(2,1)S(1)}, bf16[512,1024]{1,0:T(8,128)(2,1)S(1)}, u32[]{:S(2)}, u32[]{:S(2)}) collective-permute-start(bf16[512,1024]{1,0:T(8,128)(2,1)S(1)} %get-tuple-element.47.act_ref.refs_2_), channel_id=1, source_target_pairs={{0,8},{8,0},{1,9},{9,1},{2,10},{10,2},{3,11},{11,3},{4,12},{12,4},... | collective-permute-start | bytes 3145736 | tf_op jit(solution)/shard_map/ppermute | solution.py:272
  62.9 12.3 %collective-permute-start.11 = (bf16[192,1024]{1,0:T(8,128)(2,1)S(1)}, bf16[192,1024]{1,0:T(8,128)(2,1)S(1)}, u32[]{:S(2)}, u32[]{:S(2)}) collective-permute-start(bf16[192,1024]{1,0:T(8,128)(2,1)S(1)} %get-tuple-element.49), channel_id=1, source_target_pairs={{0,2},{2,4},{4,6},{6,0},{1,3},{3,5},{5,7},{7,1},{8,10},{10,12},{12... | collective-permute-start | bytes 1179656 | tf_op jit(solution)/shard_map/ppermute | solution.py:269
  62.9 12.3 %collective-permute-start.12 = (bf16[192,1024]{1,0:T(8,128)(2,1)S(1)}, bf16[192,1024]{1,0:T(8,128)(2,1)S(1)}, u32[]{:S(2)}, u32[]{:S(2)}) collective-permute-start(bf16[192,1024]{1,0:T(8,128)(2,1)S(1)} %get-tuple-element.50), channel_id=1, source_target_pairs={{0,6},{2,0},{4,2},{6,4},{1,7},{3,1},{5,3},{7,5},{8,14},{10,8},{12,... | collective-permute-start | bytes 1179656 | tf_op jit(solution)/shard_map/ppermute | solution.py:269
  76.0 11.6 %collective-permute-start.15 = (bf16[192,1024]{1,0:T(8,128)(2,1)S(1)}, bf16[192,1024]{1,0:T(8,128)(2,1)S(1)}, u32[]{:S(2)}, u32[]{:S(2)}) collective-permute-start(bf16[192,1024]{1,0:T(8,128)(2,1)S(1)} %get-tuple-element.55.refs_4_), channel_id=1, source_target_pairs={{0,2},{2,4},{4,6},{6,0},{1,3},{3,5},{5,7},{7,1},{8,10},{10,12},{12... | collective-permute-start | bytes 1179656 | tf_op jit(solution)/shard_map/ppermute | solution.py:269
  76.1 11.5 %collective-permute-start.16 = (bf16[192,1024]{1,0:T(8,128)(2,1)S(1)}, bf16[192,1024]{1,0:T(8,128)(2,1)S(1)}, u32[]{:S(2)}, u32[]{:S(2)}) collective-permute-start(bf16[192,1024]{1,0:T(8,128)(2,1)S(1)} %get-tuple-element.56), channel_id=1, source_target_pairs={{0,6},{2,0},{4,2},{6,4},{1,7},{3,1},{5,3},{7,5},{8,14},{10,8},{12,... | collective-permute-start | bytes 1179656 | tf_op jit(solution)/shard_map/ppermute | solution.py:269
  79.3 33.7 %collective-permute-start.24 = (bf16[512,1024]{1,0:T(8,128)(2,1)S(1)}, bf16[512,1024]{1,0:T(8,128)(2,1)S(1)}, u32[]{:S(2)}, u32[]{:S(2)}) collective-permute-start(bf16[512,1024]{1,0:T(8,128)(2,1)S(1)} %get-tuple-element.65), channel_id=1, source_target_pairs={{0,16},{8,56},{16,32},{24,8},{32,48},{40,24},{48,0},{56,40},{1,17}... | collective-permute-start | bytes 3145736 | tf_op jit(solution)/shard_map/ppermute | solution.py:288
  88.3 13.5 %collective-permute-start.17 = (bf16[256,1024]{1,0:T(8,128)(2,1)S(1)}, bf16[256,1024]{1,0:T(8,128)(2,1)S(1)}, u32[]{:S(2)}, u32[]{:S(2)}) collective-permute-start(bf16[256,1024]{1,0:T(8,128)(2,1)S(1)} %get-tuple-element.57), channel_id=1, source_target_pairs={{0,2},{2,4},{4,6},{6,0},{1,3},{3,5},{5,7},{7,1},{8,10},{10,12},{12... | collective-permute-start | bytes 1572872 | tf_op jit(solution)/shard_map/ppermute | solution.py:269
  89.2 12.6 %collective-permute-start.18 = (bf16[256,1024]{1,0:T(8,128)(2,1)S(1)}, bf16[256,1024]{1,0:T(8,128)(2,1)S(1)}, u32[]{:S(2)}, u32[]{:S(2)}) collective-permute-start(bf16[256,1024]{1,0:T(8,128)(2,1)S(1)} %get-tuple-element.58), channel_id=1, source_target_pairs={{0,6},{2,0},{4,2},{6,4},{1,7},{3,1},{5,3},{7,5},{8,14},{10,8},{12,... | collective-permute-start | bytes 1572872 | tf_op jit(solution)/shard_map/ppermute | solution.py:269
  91.6 7.6 %collective-permute-start.19 = (bf16[128,1024]{1,0:T(8,128)(2,1)S(1)}, bf16[128,1024]{1,0:T(8,128)(2,1)S(1)}, u32[]{:S(2)}, u32[]{:S(2)}) collective-permute-start(bf16[128,1024]{1,0:T(8,128)(2,1)S(1)} %get-tuple-element.59), channel_id=1, source_target_pairs={{0,193},{1,64},{64,1},{65,128},{128,65},{129,192},{192,129},{193,0... | collective-permute-start | bytes 786440 | tf_op jit(solution)/shard_map/ppermute | solution.py:279
  102.6 12.9 %collective-permute-start.20 = (bf16[128,1024]{1,0:T(8,128)(2,1)S(1)}, bf16[128,1024]{1,0:T(8,128)(2,1)S(1)}, u32[]{:S(2)}, u32[]{:S(2)}) collective-permute-start(bf16[128,1024]{1,0:T(8,128)(2,1)S(1)} %get-tuple-element.60), channel_id=1, source_target_pairs={{0,2},{2,4},{4,6},{6,0},{1,3},{3,5},{5,7},{7,1},{8,10},{10,12},{12... | collective-permute-start | bytes 786440 | tf_op jit(solution)/shard_map/ppermute | solution.py:269
  103.5 12.0 %collective-permute-start.21 = (bf16[128,1024]{1,0:T(8,128)(2,1)S(1)}, bf16[128,1024]{1,0:T(8,128)(2,1)S(1)}, u32[]{:S(2)}, u32[]{:S(2)}) collective-permute-start(bf16[128,1024]{1,0:T(8,128)(2,1)S(1)} %get-tuple-element.61), channel_id=1, source_target_pairs={{0,6},{2,0},{4,2},{6,4},{1,7},{3,1},{5,3},{7,5},{8,14},{10,8},{12,... | collective-permute-start | bytes 786440 | tf_op jit(solution)/shard_map/ppermute | solution.py:269
  105.9 9.6 %collective-permute-start.22 = (bf16[128,1024]{1,0:T(8,128)(2,1)S(1)}, bf16[128,1024]{1,0:T(8,128)(2,1)S(1)}, u32[]{:S(2)}, u32[]{:S(2)}) collective-permute-start(bf16[128,1024]{1,0:T(8,128)(2,1)S(1)} %get-tuple-element.62), channel_id=1, source_target_pairs={{0,64},{1,193},{64,128},{65,1},{128,192},{129,65},{192,0},{193,129... | collective-permute-start | bytes 786440 | tf_op jit(solution)/shard_map/ppermute | solution.py:283
  106.2 11.6 %collective-permute-start.23 = (bf16[128,1024]{1,0:T(8,128)(2,1)S(1)}, bf16[128,1024]{1,0:T(8,128)(2,1)S(1)}, u32[]{:S(2)}, u32[]{:S(2)}) collective-permute-start(bf16[128,1024]{1,0:T(8,128)(2,1)S(1)} %get-tuple-element.63.refs_2_), channel_id=1, source_target_pairs={{0,193},{1,64},{64,1},{65,128},{128,65},{129,192},{192,129},{193,0... | collective-permute-start | bytes 786440 | tf_op jit(solution)/shard_map/ppermute | solution.py:279
  113.8 28.9 %collective-permute-start.30 = (bf16[512,1024]{1,0:T(8,128)(2,1)S(1)}, bf16[512,1024]{1,0:T(8,128)(2,1)S(1)}, u32[]{:S(2)}, u32[]{:S(2)}) collective-permute-start(bf16[512,1024]{1,0:T(8,128)(2,1)S(1)} %get-tuple-element.71), channel_id=1, source_target_pairs={{0,16},{8,56},{16,32},{24,8},{32,48},{40,24},{48,0},{56,40},{1,17}... | collective-permute-start | bytes 3145736 | tf_op jit(solution)/shard_map/ppermute | solution.py:288
  118.5 24.3 %collective-permute-start.31 = (bf16[512,1024]{1,0:T(8,128)(2,1)S(1)}, bf16[512,1024]{1,0:T(8,128)(2,1)S(1)}, u32[]{:S(2)}, u32[]{:S(2)}) collective-permute-start(bf16[512,1024]{1,0:T(8,128)(2,1)S(1)} %get-tuple-element.72), channel_id=1, source_target_pairs={{0,24},{8,48},{16,40},{24,0},{32,56},{40,16},{48,8},{56,32},{1,25}... | collective-permute-start | bytes 3145736 | tf_op jit(solution)/shard_map/ppermute | solution.py:288
  118.6 8.8 %collective-permute-start.25 = (bf16[128,1024]{1,0:T(8,128)(2,1)S(1)}, bf16[128,1024]{1,0:T(8,128)(2,1)S(1)}, u32[]{:S(2)}, u32[]{:S(2)}) collective-permute-start(bf16[128,1024]{1,0:T(8,128)(2,1)S(1)} %get-tuple-element.67.refs_0_), channel_id=1, source_target_pairs={{0,1},{1,0},{2,3},{3,2},{4,5},{5,4},{6,7},{7,6},{8,9},{9,8},{10,11... | collective-permute-start | bytes 786440 | tf_op jit(solution)/shard_map/ppermute | solution.py:275
  128.0 9.3 %collective-permute-start.27 = (bf16[128,1024]{1,0:T(8,128)(2,1)S(1)}, bf16[128,1024]{1,0:T(8,128)(2,1)S(1)}, u32[]{:S(2)}, u32[]{:S(2)}) collective-permute-start(bf16[128,1024]{1,0:T(8,128)(2,1)S(1)} %get-tuple-element.69.refs_0_), channel_id=1, source_target_pairs={{0,6},{2,0},{4,2},{6,4},{1,7},{3,1},{5,3},{7,5},{8,14},{10,8},{12,... | collective-permute-start | bytes 786440 | tf_op jit(solution)/shard_map/ppermute | solution.py:269
  129.6 11.6 %collective-permute-start.29 = (bf16[128,1024]{1,0:T(8,128)(2,1)S(1)}, bf16[128,1024]{1,0:T(8,128)(2,1)S(1)}, u32[]{:S(2)}, u32[]{:S(2)}) collective-permute-start(bf16[128,1024]{1,0:T(8,128)(2,1)S(1)} %get-tuple-element.69.refs_0_), channel_id=1, source_target_pairs={{0,2},{2,4},{4,6},{6,0},{1,3},{3,5},{5,7},{7,1},{8,10},{10,12},{12... | collective-permute-start | bytes 786440 | tf_op jit(solution)/shard_map/ppermute | solution.py:269
  130.1 14.5 %collective-permute-start.26 = (bf16[64,1024]{1,0:T(8,128)(2,1)S(1)}, bf16[64,1024]{1,0:T(8,128)(2,1)S(1)}, u32[]{:S(2)}, u32[]{:S(2)}) collective-permute-start(bf16[64,1024]{1,0:T(8,128)(2,1)S(1)} %get-tuple-element.68), channel_id=1, source_target_pairs={{0,4},{2,6},{4,0},{6,2},{1,5},{3,7},{5,1},{7,3},{8,12},{10,14},{12... | collective-permute-start | bytes 393224 | tf_op jit(solution)/shard_map/ppermute | solution.py:269
  137.9 6.7 %collective-permute-start.28 = (bf16[64,1024]{1,0:T(8,128)(2,1)S(1)}, bf16[64,1024]{1,0:T(8,128)(2,1)S(1)}, u32[]{:S(2)}, u32[]{:S(2)}) collective-permute-start(bf16[64,1024]{1,0:T(8,128)(2,1)S(1)} %shard_map.119.refs_3_), channel_id=1, source_target_pairs={{0,6},{2,0},{4,2},{6,4},{1,7},{3,1},{5,3},{7,5},{8,14},{10,8},{12,... | collective-permute-start | bytes 393224 | tf_op jit(solution)/shard_map/ppermute | solution.py:269

commit v8 on v7

--- a/solution.py
+++ b/solution.py
@@ -312,26 +312,31 @@
         def both(up, down):
             return shift_x(up, 1), shift_x(down, -1)
 
-        def with_halves(block, ups, downs, after=()):
-            out = jax.ShapeDtypeStruct((blk + mid * len(ups), quarter), bf16)
+        def with_halves(block, ups, downs):
+            part = jax.ShapeDtypeStruct((mid, quarter), bf16)
+            out = jax.ShapeDtypeStruct((mid + mid * len(ups), quarter), bf16)
 
             def body(info, block_ref, *refs):
-                up_out, down_out = refs[-2:]
-                up_out[:blk] = block_ref[...]
-                down_out[:blk] = block_ref[...]
+                up_out, down_out, top_out, low_out = refs[-4:]
+                top_out[...] = block_ref[:mid]
+                low_out[...] = block_ref[mid:]
+                up_out[:mid] = block_ref[mid:]
+                down_out[:mid] = block_ref[:mid]
                 for i in range(len(ups)):
-                    at = blk + i * mid
+                    at = mid + i * mid
                     up_out[at : at + mid] = refs[i][:mid]
                     down_out[at : at + mid] = refs[len(ups) + i][mid:blk]
 
-            return small(body, [block, *ups, *downs], [out, out], info, after)
+            return small(body, [block, *ups, *downs], [out, out, part, part], info)
 
         b1, b2 = cross(mine), jump(mine, -1)
         u1, d1 = both(b1, b1)
         u2, d2 = both(b2, b2)
         b3 = cross(b2)
         out3 = with_halves(b3, (u1, u2), (d1, d2))
-        u3, d3 = both(*out3)
+        ut, dt = both(*out3[2:])
+        u3, d3 = both(*out3[:2])
+        u4, d4 = both(ut, dt)
         rows = [None] * XS
 
         def parts(*got):
@@ -339,15 +344,12 @@
 
         acc, rows[0] = project([(0, parts(b1, b2, b3))], enc, wk, wv, None, info, n_sec, out3)
 
-        def cut(info, up_ref, down_ref, up_out, down_out):
-            up_out[...] = up_ref[:mid]
-            down_out[...] = down_ref[mid:blk]
-
-        out4 = small(cut, [u3, d3], [jax.ShapeDtypeStruct((mid, quarter), bf16)] * 2, info, (acc,))
-        u4, d4 = both(*out4)
-        beside = [(1, parts(u1, u2, u3)), (3, parts(d1, d2, d3))]
-        acc, rows[1], rows[3] = project(beside, enc, wk, wv, acc, info, n_sec, out4)
-        last = [(u3, [(blk, mid, 1, 0), (blk + mid, mid, 2, 0)]), (d3, [(blk, mid, 1, mid), (blk + mid, mid, 2, mid)])]
+        beside = [
+            (1, parts(u1, u2) + [(ut, [(0, mid, 3, 0)]), (u3, [(0, mid, 3, mid)])]),
+            (3, parts(d1, d2) + [(dt, [(0, mid, 3, mid)]), (d3, [(0, mid, 3, 0)])]),
+        ]
+        acc, rows[1], rows[3] = project(beside, enc, wk, wv, acc, info, n_sec)
+        last = [(u3, [(mid, mid, 1, 0), (blk, mid, 2, 0)]), (d3, [(mid, mid, 1, mid), (blk, mid, 2, mid)])]
         last += [(u4, [(0, mid, 3, 0)]), (d4, [(0, mid, 3, mid)])]
         asked = (queries[0, 0], ctx_grad[0, 0])
         first = (3, 0, 2)

time: 147 us -> 152 us (1.034)
  starting transfers between devices: 48.7 us -> 52.5 us
    ppermute x20 -> x22, starting transfers between devices: 32 us -> 35.5 us  [shift_x(): return lax.ppermute(v, 'x', [(i, (i + k) % XS) for i in range(XS)])]
    ppermute x20 -> x22, waiting for transfers between devices: 26.2 us -> 27.8 us  [shift_x(): return lax.ppermute(v, 'x', [(i, (i + k) % XS) for i in range(XS)])]
    pallas_call x15 -> x14, Pallas kernels: 16.9 us -> 16.3 us  [small(): pl.pallas_call(run, grid_spec=pltpu.PrefetchScalarGridSpec(num_scalar_pre...]
  transfers between devices with their start and end apart: 32 -> 34, of which waited for: 15 -> 14; matrix products, arithmetic and copies ran while one was open for 0% -> 0% of each run, Pallas kernels for 18% -> 18%
where the time goes in v8:
time: 152 us; the launch traced here: 151 us
  starting transfers between devices  52.5 us (35%)
  waiting for transfers between devices  52.4 us (34%)
  Pallas kernels  37.6 us (25%)
  local copies, waits for them, and re-layouts  6.48 us (4%)
  between operations  2.22 us (1%)
    ppermute x22, starting transfers between devices, shift_x(): return lax.ppermute(v, 'x', [(i, (i + k) % XS) for i in range(XS)])  35.5 us
    ppermute x22, waiting for transfers between devices, shift_x(): return lax.ppermute(v, 'x', [(i, (i + k) % XS) for i in range(XS)])  27.8 us
    pallas_call x14, Pallas kernels, small(): pl.pallas_call(run, grid_spec=pltpu.PrefetchScalarGridSpec(num_scalar_pre...  16.3 us
    pallas_call x3, Pallas kernels, project(): pl.pallas_call(body, grid_spec=pltpu.PrefetchScalarGridSpec(num_scalar_pr...  14.2 us
    ppermute x4, waiting for transfers between devices, cross(): lax.ppermute(v, ('section', 'low'), [(z, (z + (1 if z % 2 else -1)) % n)...  9.23 us
    ppermute x1, waiting for transfers between devices, swap_low(): return lax.ppermute(v, 'low', [(0, 1), (1, 0)])  8.67 us
    ppermute x2, waiting for transfers between devices, jump(): lax.ppermute(v, ('section', 'low'), [(z, (z + (-2 * k if z % 2 else 2 * k...  6.71 us
    ppermute x2, starting transfers between devices, jump(): lax.ppermute(v, ('section', 'low'), [(z, (z + (-2 * k if z % 2 else 2 * k...  6.57 us
  transfers between devices with their start and end apart: 34, of which 14 were waited for; matrix products, arithmetic and copies ran while one was open for 0% of the time, Pallas kernels for 18%

profile of v8, /device:TPU:8, one launch (start us, length us, event | category | flops | bytes accessed | tf_op | source)
XLA Modules:
  0.0 151.3 jit_solution(5196637274667161421)
XLA Ops:
  0.6 1.1 dynamic-slice_bitcast_fusion
  1.7 6.4 %collective-permute-start = (bf16[128,1024]{1,0:T(8,128)(2,1)S(1)}, bf16[128,1024]{1,0:T(8,128)(2,1)S(1)}, u32[]{:S(2)}, u32[]{:S(2)}) collective-permute-start(bf16[128,1024]{1,0:T(8,128)(2,1)S(1)} %dynamic-slice_bitcast_fusion), channel_id=1, source_target_pairs={{0,192},{1,65},{64,0},{65,129},{128,64},{129,193},{192,128},{193,1... | collective-permute-start | bytes 786440 | tf_op jit(solution)/shard_map/ppermute | solution.py:283
  8.1 6.7 %collective-permute-done.refs_2_ = bf16[128,1024]{1,0:T(8,128)(2,1)S(1)} collective-permute-done((bf16[128,1024]{1,0:T(8,128)(2,1)S(1)}, bf16[128,1024]{1,0:T(8,128)(2,1)S(1)}, u32[]{:S(2)}, u32[]{:S(2)}) %collective-permute-start) | collective-permute-done | bytes 262176 | tf_op jit(solution)/shard_map/ppermute | solution.py:283
  14.8 2.9 %collective-permute-start.1 = (bf16[128,1024]{1,0:T(8,128)(2,1)S(1)}, bf16[128,1024]{1,0:T(8,128)(2,1)S(1)}, u32[]{:S(2)}, u32[]{:S(2)}) collective-permute-start(bf16[128,1024]{1,0:T(8,128)(2,1)S(1)} %collective-permute-done.refs_2_), channel_id=1, source_target_pairs={{0,193},{1,64},{64,1},{65,128},{128,65},{129,192},{192,129},{193,0... | collective-permute-start | bytes 786440 | tf_op jit(solution)/shard_map/ppermute | solution.py:279
  17.7 1.5 collective-permute-start.4
  19.2 1.7 %collective-permute-start.6 = (bf16[128,1024]{1,0:T(8,128)(2,1)S(1)}, bf16[128,1024]{1,0:T(8,128)(2,1)S(1)}, u32[]{:S(2)}, u32[]{:S(2)}) collective-permute-start(bf16[128,1024]{1,0:T(8,128)(2,1)S(1)} %collective-permute-done.refs_2_), channel_id=1, source_target_pairs={{0,6},{2,0},{4,2},{6,4},{1,7},{3,1},{5,3},{7,5},{8,14},{10,8},{12,... | collective-permute-start | bytes 786440 | tf_op jit(solution)/shard_map/ppermute | solution.py:269
  21.0 0.9 collective-permute-start.3
  21.9 2.3 %collective-permute-start.5 = (bf16[128,1024]{1,0:T(8,128)(2,1)S(1)}, bf16[128,1024]{1,0:T(8,128)(2,1)S(1)}, u32[]{:S(2)}, u32[]{:S(2)}) collective-permute-start(bf16[128,1024]{1,0:T(8,128)(2,1)S(1)} %collective-permute-done.2.refs_1_), channel_id=1, source_target_pairs={{0,6},{2,0},{4,2},{6,4},{1,7},{3,1},{5,3},{7,5},{8,14},{10,8},{12,... | collective-permute-start | bytes 786440 | tf_op jit(solution)/shard_map/ppermute | solution.py:269
  25.6 2.4 %collective-permute-done.4.refs_2_.refs_3_ = bf16[128,1024]{1,0:T(8,128)(2,1)S(1)} collective-permute-done((bf16[128,1024]{1,0:T(8,128)(2,1)S(1)}, bf16[128,1024]{1,0:T(8,128)(2,1)S(1)}, u32[]{:S(2)}, u32[]{:S(2)}) %collective-permute-start.4) | collective-permute-done | bytes 262176 | tf_op jit(solution)/shard_map/ppermute | solution.py:269
  28.0 0.3 collective-permute-done.6.refs_4_.refs_7_
  28.3 2.7 %collective-permute-done.3.refs_1_.refs_2_ = bf16[128,1024]{1,0:T(8,128)(2,1)S(1)} collective-permute-done((bf16[128,1024]{1,0:T(8,128)(2,1)S(1)}, bf16[128,1024]{1,0:T(8,128)(2,1)S(1)}, u32[]{:S(2)}, u32[]{:S(2)}) %collective-permute-start.3) | collective-permute-done | bytes 262176 | tf_op jit(solution)/shard_map/ppermute | solution.py:269
  31.1 0.6 shard_map.102
  31.7 1.6 %collective-permute-start.7 = (bf16[192,1024]{1,0:T(8,128)(2,1)S(1)}, bf16[192,1024]{1,0:T(8,128)(2,1)S(1)}, u32[]{:S(2)}, u32[]{:S(2)}) collective-permute-start(bf16[192,1024]{1,0:T(8,128)(2,1)S(1)} %get-tuple-element.40.refs_6_), channel_id=1, source_target_pairs={{0,2},{2,4},{4,6},{6,0},{1,3},{3,5},{5,7},{7,1},{8,10},{10,12},{12... | collective-permute-start | bytes 1179656 | tf_op jit(solution)/shard_map/ppermute | solution.py:269
  33.3 1.7 %collective-permute-start.8 = (bf16[192,1024]{1,0:T(8,128)(2,1)S(1)}, bf16[192,1024]{1,0:T(8,128)(2,1)S(1)}, u32[]{:S(2)}, u32[]{:S(2)}) collective-permute-start(bf16[192,1024]{1,0:T(8,128)(2,1)S(1)} %get-tuple-element.41.refs_7_), channel_id=1, source_target_pairs={{0,6},{2,0},{4,2},{6,4},{1,7},{3,1},{5,3},{7,5},{8,14},{10,8},{12,... | collective-permute-start | bytes 1179656 | tf_op jit(solution)/shard_map/ppermute | solution.py:269
  35.0 0.3 collective-permute-start.9
  35.3 3.0 %collective-permute-start.11 = (bf16[64,1024]{1,0:T(8,128)(2,1)S(1)}, bf16[64,1024]{1,0:T(8,128)(2,1)S(1)}, u32[]{:S(2)}, u32[]{:S(2)}) collective-permute-start(bf16[64,1024]{1,0:T(8,128)(2,1)S(1)} %get-tuple-element.43.refs_9_), channel_id=1, source_target_pairs={{0,6},{2,0},{4,2},{6,4},{1,7},{3,1},{5,3},{7,5},{8,14},{10,8},{12,... | collective-permute-start | bytes 393224 | tf_op jit(solution)/shard_map/ppermute | solution.py:269
  38.2 5.9 %collective-permute-done.9.refs_4_ = bf16[64,1024]{1,0:T(8,128)(2,1)S(1)} collective-permute-done((bf16[64,1024]{1,0:T(8,128)(2,1)S(1)}, bf16[64,1024]{1,0:T(8,128)(2,1)S(1)}, u32[]{:S(2)}, u32[]{:S(2)}) %collective-permute-start.9) | collective-permute-done | bytes 131104 | tf_op jit(solution)/shard_map/ppermute | solution.py:269
  44.1 1.0 collective-permute-start.10
  45.1 2.3 %collective-permute-start.12 = (bf16[64,1024]{1,0:T(8,128)(2,1)S(1)}, bf16[64,1024]{1,0:T(8,128)(2,1)S(1)}, u32[]{:S(2)}, u32[]{:S(2)}) collective-permute-start(bf16[64,1024]{1,0:T(8,128)(2,1)S(1)} %collective-permute-done.11.refs_8_), channel_id=1, source_target_pairs={{0,6},{2,0},{4,2},{6,4},{1,7},{3,1},{5,3},{7,5},{8,14},{10,8},{12,... | collective-permute-start | bytes 393224 | tf_op jit(solution)/shard_map/ppermute | solution.py:269
  47.4 2.2 %copy-done = bf16[1,4096,512]{2,1,0:T(8,128)(2,1)S(1)} copy-done((bf16[1,4096,512]{2,1,0:T(8,128)(2,1)S(1)}, bf16[1,4096,512]{2,1,0:T(8,128)(2,1)}, u32[]{:S(2)}) %copy-start) | copy-done | bytes 4194328
  49.5 2.2 %copy-done.2 = bf16[1,4096,512]{2,1,0:T(8,128)(2,1)S(1)} copy-done((bf16[1,4096,512]{2,1,0:T(8,128)(2,1)S(1)}, bf16[1,4096,512]{2,1,0:T(8,128)(2,1)}, u32[]{:S(2)}) %copy-start.2) | copy-done | bytes 4194328
  51.7 2.5 %shard_map.103 = (f32[512,1024]{1,0:T(8,128)S(1)}, bf16[512,1024]{1,0:T(8,128)(2,1)S(1)}) custom-call(s32[7]{0:T(128)S(1)} %stack.25.info, bf16[128,4096]{1,0:T(8,128)(2,1)S(1)} %bitcast.30, bf16[128,1024]{1,0:T(8,128)(2,1)S(1)} %collective-permute-done.2.refs_1_, bf16[128,1024]{1,0:T(8,128)(2,1)S(1)} %collective-permute-done.refs_2_, ...), custom_call_target="tpu_custom_call" | custom-call | flops 1 | bytes 1 | tf_op jit(solution)/shard_map/pallas_call | solution.py:135
  54.3 0.9 copy-done.3
  55.2 4.0 %shard_map.104 = (f32[512,1024]{1,0:T(8,128)S(1)}, bf16[512,1024]{1,0:T(8,128)(2,1)S(1)}, bf16[512,1024]{1,0:T(8,128)(2,1)S(1)}) custom-call(s32[7]{0:T(128)S(1)} %stack.25.info, bf16[128,4096]{1,0:T(8,128)(2,1)S(1)} %bitcast.31, bf16[128,4096]{1,0:T(8,128)(2,1)S(1)} %bitcast.32, bf16[128,1024]{1,0:T(8,128)(2,1)S(1)} %collective-permute-done.3.refs_1_.refs_2_, ...), custom_call_target="tpu_custom_call" | custom-call | flops 1 | bytes 1 | tf_op jit(solution)/shard_map/pallas_call | solution.py:135
  59.3 7.7 %shard_map.105 = (bf16[512,512]{1,0:T(8,128)(2,1)}, bf16[512,1024]{1,0:T(8,128)(2,1)S(1)}, bf16[512,1024]{1,0:T(8,128)(2,1)S(1)}, bf16[512,1024]{1,0:T(8,128)(2,...) custom-call(s32[7]{0:T(128)S(1)} %stack.25.info, bf16[128,4096]{1,0:T(8,128)(2,1)S(1)} %bitcast.33, ...), custom_call_target="tpu_custom_call" | custom-call | flops 1 | bytes 1 | tf_op jit(solution)/shard_map/pallas_call | solution.py:135
  67.0 0.8 shard_map.109
  67.8 0.5 collective-permute-start.16
  68.3 3.2 %collective-permute-start.14 = (bf16[192,1024]{1,0:T(8,128)(2,1)S(1)}, bf16[192,1024]{1,0:T(8,128)(2,1)S(1)}, u32[]{:S(2)}, u32[]{:S(2)}) collective-permute-start(bf16[192,1024]{1,0:T(8,128)(2,1)S(1)} %get-tuple-element.50), channel_id=1, source_target_pairs={{0,6},{2,0},{4,2},{6,4},{1,7},{3,1},{5,3},{7,5},{8,14},{10,8},{12,... | collective-permute-start | bytes 1179656 | tf_op jit(solution)/shard_map/ppermute | solution.py:269
  71.6 3.7 %shard_map.106.refs_0_.refs_4_.refs_3_.refs_6_.refs_7_ = bf16[512,2048]{1,0:T(8,128)(2,1)S(1)} custom-call(s32[7]{0:T(128)S(1)} %stack.25.info, bf16[512,1024]{1,0:T(8,128)(2,1)S(1)} %get-tuple-element.47.act_ref.refs_2_, bf16[4096,512]{1,0:T(8,128)(2,1)S(1)} %bitcast.21, bf16[4096,512]{1,0:T(8,128)(2,1)S(1)} %bitcast.28, ...), custom_call_target="tpu_custom_call" | custom-call | flops 1 | bytes 1 | tf_op jit(solution)/shard_map/pallas_call | solution.py:216
  75.3 0.8 shard_map.108.refs_0_
  76.0 1.8 %shard_map.110.refs_4_ = bf16[512,1024]{1,0:T(8,128)(2,1)S(1)} custom-call(s32[7]{0:T(128)S(1)} %stack.25.info, bf16[512,2048]{1,0:T(8,128)(2,1)S(1)} %shard_map.108.refs_0_, bf16[512,2048]{1,0:T(8,128)(2,1)S(1)} %collective-permute-done.15.refs_1_, bf16[512,1024]{1,0:T(8,128)(2,1)S(1)} %get-tuple-element.47.act_ref.refs_2_, ...), custom_call_target="tpu_custom_call" | custom-call | flops 1 | bytes 1 | tf_op jit(solution)/shard_map/pallas_call | solution.py:252
  77.9 2.8 %collective-permute-done.13.refs_1_.refs_4_.refs_8_ = bf16[192,1024]{1,0:T(8,128)(2,1)S(1)} collective-permute-done((bf16[192,1024]{1,0:T(8,128)(2,1)S(1)}, bf16[192,1024]{1,0:T(8,128)(2,1)S(1)}, u32[]{:S(2)}, u32[]{:S(2)}) %collective-permute-start.13) | collective-permute-done | bytes 393248 | tf_op jit(solution)/shard_map/ppermute | solution.py:269
  80.7 0.7 shard_map.111
  81.4 3.2 %collective-permute-start.18 = (bf16[192,1024]{1,0:T(8,128)(2,1)S(1)}, bf16[192,1024]{1,0:T(8,128)(2,1)S(1)}, u32[]{:S(2)}, u32[]{:S(2)}) collective-permute-start(bf16[192,1024]{1,0:T(8,128)(2,1)S(1)} %get-tuple-element.56), channel_id=1, source_target_pairs={{0,6},{2,0},{4,2},{6,4},{1,7},{3,1},{5,3},{7,5},{8,14},{10,8},{12,... | collective-permute-start | bytes 1179656 | tf_op jit(solution)/shard_map/ppermute | solution.py:269
  84.6 1.6 %collective-permute-start.26 = (bf16[512,1024]{1,0:T(8,128)(2,1)S(1)}, bf16[512,1024]{1,0:T(8,128)(2,1)S(1)}, u32[]{:S(2)}, u32[]{:S(2)}) collective-permute-start(bf16[512,1024]{1,0:T(8,128)(2,1)S(1)} %get-tuple-element.65), channel_id=1, source_target_pairs={{0,16},{8,56},{16,32},{24,8},{32,48},{40,24},{48,0},{56,40},{1,17}... | collective-permute-start | bytes 3145736 | tf_op jit(solution)/shard_map/ppermute | solution.py:288
  86.2 2.2 %shard_map.107.refs_0_.refs_4_ = f32[512,1024]{1,0:T(8,128)S(1)} custom-call(s32[7]{0:T(128)S(1)} %stack.25.info, bf16[512,1024]{1,0:T(8,128)(2,1)S(1)} %get-tuple-element.47.act_ref.refs_2_, bf16[4096,512]{1,0:T(8,128)(2,1)S(1)} %bitcast.22, bf16[4096,512]{1,0:T(8,128)(2,1)S(1)} %bitcast.29, ...), custom_call_target="tpu_custom_call" | custom-call | flops 1 | bytes 1 | tf_op jit(solution)/shard_map/pallas_call | solution.py:216
  88.4 4.5 %collective-permute-done.17.refs_1_.refs_7_ = bf16[192,1024]{1,0:T(8,128)(2,1)S(1)} collective-permute-done((bf16[192,1024]{1,0:T(8,128)(2,1)S(1)}, bf16[192,1024]{1,0:T(8,128)(2,1)S(1)}, u32[]{:S(2)}, u32[]{:S(2)}) %collective-permute-start.17) | collective-permute-done | bytes 393248 | tf_op jit(solution)/shard_map/ppermute | solution.py:269
  92.9 0.8 shard_map.112
  93.7 0.9 collective-permute-start.19
  94.6 2.4 %collective-permute-start.20 = (bf16[256,1024]{1,0:T(8,128)(2,1)S(1)}, bf16[256,1024]{1,0:T(8,128)(2,1)S(1)}, u32[]{:S(2)}, u32[]{:S(2)}) collective-permute-start(bf16[256,1024]{1,0:T(8,128)(2,1)S(1)} %get-tuple-element.58), channel_id=1, source_target_pairs={{0,6},{2,0},{4,2},{6,4},{1,7},{3,1},{5,3},{7,5},{8,14},{10,8},{12,... | collective-permute-start | bytes 1572872 | tf_op jit(solution)/shard_map/ppermute | solution.py:269
  97.0 0.6 collective-permute-start.21
  97.6 6.9 %collective-permute-done.21.refs_3_ = bf16[128,1024]{1,0:T(8,128)(2,1)S(1)} collective-permute-done((bf16[128,1024]{1,0:T(8,128)(2,1)S(1)}, bf16[128,1024]{1,0:T(8,128)(2,1)S(1)}, u32[]{:S(2)}, u32[]{:S(2)}) %collective-permute-start.21) | collective-permute-done | bytes 262176 | tf_op jit(solution)/shard_map/ppermute | solution.py:279
  104.6 2.6 %collective-permute-done.19.refs_1_.refs_5_ = bf16[256,1024]{1,0:T(8,128)(2,1)S(1)} collective-permute-done((bf16[256,1024]{1,0:T(8,128)(2,1)S(1)}, bf16[256,1024]{1,0:T(8,128)(2,1)S(1)}, u32[]{:S(2)}, u32[]{:S(2)}) %collective-permute-start.19) | collective-permute-done | bytes 524320 | tf_op jit(solution)/shard_map/ppermute | solution.py:269
  107.1 0.8 shard_map.113
  107.9 0.9 collective-permute-start.22
  108.9 2.4 %collective-permute-start.23 = (bf16[128,1024]{1,0:T(8,128)(2,1)S(1)}, bf16[128,1024]{1,0:T(8,128)(2,1)S(1)}, u32[]{:S(2)}, u32[]{:S(2)}) collective-permute-start(bf16[128,1024]{1,0:T(8,128)(2,1)S(1)} %get-tuple-element.61), channel_id=1, source_target_pairs={{0,6},{2,0},{4,2},{6,4},{1,7},{3,1},{5,3},{7,5},{8,14},{10,8},{12,... | collective-permute-start | bytes 786440 | tf_op jit(solution)/shard_map/ppermute | solution.py:269
  111.5 2.9 %collective-permute-start.25 = (bf16[128,1024]{1,0:T(8,128)(2,1)S(1)}, bf16[128,1024]{1,0:T(8,128)(2,1)S(1)}, u32[]{:S(2)}, u32[]{:S(2)}) collective-permute-start(bf16[128,1024]{1,0:T(8,128)(2,1)S(1)} %get-tuple-element.63.refs_2_), channel_id=1, source_target_pairs={{0,193},{1,64},{64,1},{65,128},{128,65},{129,192},{192,129},{193,0... | collective-permute-start | bytes 786440 | tf_op jit(solution)/shard_map/ppermute | solution.py:279
  114.4 4.0 %shard_map.114 = (bf16[1024,1024]{1,0:T(8,128)(2,1)S(1)}, bf16[512,1024]{1,0:T(8,128)(2,1)S(1)}) custom-call(s32[7]{0:T(128)S(1)} %stack.25.info, bf16[512,2048]{1,0:T(8,128)(2,1)S(1)} %shard_map.108.refs_0_, bf16[512,2048]{1,0:T(8,128)(2,1)S(1)} %collective-permute-done.15.refs_1_, bf16[512,1024]{1,0:T(8,128)(2,1)S(1)} %get-tuple-element.47.act_ref.refs_2_, ...), custom_call_target="tpu_custom_call" | custom-call | flops 1 | bytes 1 | tf_op jit(solution)/shard_map/pallas_call | solution.py:252
  118.4 0.8 shard_map.115
  119.2 1.6 %collective-permute-start.32 = (bf16[512,1024]{1,0:T(8,128)(2,1)S(1)}, bf16[512,1024]{1,0:T(8,128)(2,1)S(1)}, u32[]{:S(2)}, u32[]{:S(2)}) collective-permute-start(bf16[512,1024]{1,0:T(8,128)(2,1)S(1)} %get-tuple-element.71), channel_id=1, source_target_pairs={{0,16},{8,56},{16,32},{24,8},{32,48},{40,24},{48,0},{56,40},{1,17}... | collective-permute-start | bytes 3145736 | tf_op jit(solution)/shard_map/ppermute | solution.py:288
  120.9 2.3 %collective-permute-done.25.refs_4_ = bf16[128,1024]{1,0:T(8,128)(2,1)S(1)} collective-permute-done((bf16[128,1024]{1,0:T(8,128)(2,1)S(1)}, bf16[128,1024]{1,0:T(8,128)(2,1)S(1)}, u32[]{:S(2)}, u32[]{:S(2)}) %collective-permute-start.25) | collective-permute-done | bytes 262176 | tf_op jit(solution)/shard_map/ppermute | solution.py:279
  123.2 0.7 shard_map.116
  124.1 8.7 %collective-permute-done.27.refs_1_ = bf16[128,1024]{1,0:T(8,128)(2,1)S(1)} collective-permute-done((bf16[128,1024]{1,0:T(8,128)(2,1)S(1)}, bf16[128,1024]{1,0:T(8,128)(2,1)S(1)}, u32[]{:S(2)}, u32[]{:S(2)}) %collective-permute-start.27) | collective-permute-done | bytes 262176 | tf_op jit(solution)/shard_map/ppermute | solution.py:275
  132.8 0.7 shard_map.117
  133.4 1.5 %collective-permute-start.29 = (bf16[128,1024]{1,0:T(8,128)(2,1)S(1)}, bf16[128,1024]{1,0:T(8,128)(2,1)S(1)}, u32[]{:S(2)}, u32[]{:S(2)}) collective-permute-start(bf16[128,1024]{1,0:T(8,128)(2,1)S(1)} %get-tuple-element.69.refs_0_), channel_id=1, source_target_pairs={{0,6},{2,0},{4,2},{6,4},{1,7},{3,1},{5,3},{7,5},{8,14},{10,8},{12,... | collective-permute-start | bytes 786440 | tf_op jit(solution)/shard_map/ppermute | solution.py:269
  135.0 0.6 collective-permute-start.31
  135.5 1.2 collective-permute-start.28
  136.7 6.0 %collective-permute-done.29.refs_0_.refs_2_ = bf16[128,1024]{1,0:T(8,128)(2,1)S(1)} collective-permute-done((bf16[128,1024]{1,0:T(8,128)(2,1)S(1)}, bf16[128,1024]{1,0:T(8,128)(2,1)S(1)}, u32[]{:S(2)}, u32[]{:S(2)}) %collective-permute-start.29) | collective-permute-done | bytes 262176 | tf_op jit(solution)/shard_map/ppermute | solution.py:269
  142.7 0.5 shard_map.118.refs_3_
  143.3 2.8 %collective-permute-start.30 = (bf16[64,1024]{1,0:T(8,128)(2,1)S(1)}, bf16[64,1024]{1,0:T(8,128)(2,1)S(1)}, u32[]{:S(2)}, u32[]{:S(2)}) collective-permute-start(bf16[64,1024]{1,0:T(8,128)(2,1)S(1)} %shard_map.118.refs_3_), channel_id=1, source_target_pairs={{0,6},{2,0},{4,2},{6,4},{1,7},{3,1},{5,3},{7,5},{8,14},{10,8},{12,... | collective-permute-start | bytes 393224 | tf_op jit(solution)/shard_map/ppermute | solution.py:269
  146.0 0.6 collective-permute-done.31.refs_1_
  146.6 1.6 %shard_map.119._ = bf16[128,4096]{1,0:T(8,128)(2,1)} custom-call(s32[7]{0:T(128)S(1)} %stack.25.info, bf16[128,1024]{1,0:T(8,128)(2,1)S(1)} %get-tuple-element.69.refs_0_, bf16[128,1024]{1,0:T(8,128)(2,1)S(1)} %collective-permute-done.31.refs_1_, bf16[128,1024]{1,0:T(8,128)(2,1)S(1)} %collective-permute-done.29.refs_0_.refs_2_, ...), custom_call_target="tpu_custom_call" | custom-call | flops 1 | bytes 1 | tf_op jit(solution)/shard_map/pallas_call | solution.py:252
  148.2 1.8 %shard_map.120 = (bf16[512,512]{1,0:T(8,128)(2,1)}, bf16[512,512]{1,0:T(8,128)(2,1)}, bf16[16,128]{1,0:T(8,128)(2,1)S(1)}) custom-call(s32[7]{0:T(128)S(1)} %stack.25.info, bf16[512,1024]{1,0:T(8,128)(2,1)S(1)} %get-tuple-element.70.refs_0_, bf16[512,1024]{1,0:T(8,128)(2,1)S(1)} %collective-permute-done.32.refs_1_, ...), custom_call_target="tpu_custom_call" | custom-call | flops 1 | bytes 1 | tf_op jit(solution)/shard_map/pallas_call | solution.py:252
  150.0 1.3 shard_map.121
  (40 shorter events, 0.9 us)
Async XLA Ops:
  0.6 46.7 %copy-start.4 = (bf16[1,128,4096]{2,1,0:T(8,128)(2,1)S(1)}, bf16[1,128,4096]{2,1,0:T(8,128)(2,1)}, u32[]{:S(2)}) copy-start(bf16[1,128,4096]{2,1,0:T(8,128)(2,1)} %param.7) | copy-start | bytes 3145732
  1.7 13.1 %collective-permute-start = (bf16[128,1024]{1,0:T(8,128)(2,1)S(1)}, bf16[128,1024]{1,0:T(8,128)(2,1)S(1)}, u32[]{:S(2)}, u32[]{:S(2)}) collective-permute-start(bf16[128,1024]{1,0:T(8,128)(2,1)S(1)} %dynamic-slice_bitcast_fusion), channel_id=1, source_target_pairs={{0,192},{1,65},{64,0},{65,129},{128,64},{129,193},{192,128},{193,1... | collective-permute-start | bytes 786440 | tf_op jit(solution)/shard_map/ppermute | solution.py:283
  8.1 12.9 %collective-permute-start.2 = (bf16[128,1024]{1,0:T(8,128)(2,1)S(1)}, bf16[128,1024]{1,0:T(8,128)(2,1)S(1)}, u32[]{:S(2)}, u32[]{:S(2)}) collective-permute-start(bf16[128,1024]{1,0:T(8,128)(2,1)S(1)} %dynamic-slice_bitcast_fusion), channel_id=1, source_target_pairs={{0,193},{1,64},{64,1},{65,128},{128,65},{129,192},{192,129},{193,0... | collective-permute-start | bytes 786440 | tf_op jit(solution)/shard_map/ppermute | solution.py:279
  14.8 10.8 %collective-permute-start.1 = (bf16[128,1024]{1,0:T(8,128)(2,1)S(1)}, bf16[128,1024]{1,0:T(8,128)(2,1)S(1)}, u32[]{:S(2)}, u32[]{:S(2)}) collective-permute-start(bf16[128,1024]{1,0:T(8,128)(2,1)S(1)} %collective-permute-done.refs_2_), channel_id=1, source_target_pairs={{0,193},{1,64},{64,1},{65,128},{128,65},{129,192},{192,129},{193,0... | collective-permute-start | bytes 786440 | tf_op jit(solution)/shard_map/ppermute | solution.py:279
  17.7 10.2 %collective-permute-start.4 = (bf16[128,1024]{1,0:T(8,128)(2,1)S(1)}, bf16[128,1024]{1,0:T(8,128)(2,1)S(1)}, u32[]{:S(2)}, u32[]{:S(2)}) collective-permute-start(bf16[128,1024]{1,0:T(8,128)(2,1)S(1)} %collective-permute-done.refs_2_), channel_id=1, source_target_pairs={{0,2},{2,4},{4,6},{6,0},{1,3},{3,5},{5,7},{7,1},{8,10},{10,12},{12... | collective-permute-start | bytes 786440 | tf_op jit(solution)/shard_map/ppermute | solution.py:269
  19.2 9.0 %collective-permute-start.6 = (bf16[128,1024]{1,0:T(8,128)(2,1)S(1)}, bf16[128,1024]{1,0:T(8,128)(2,1)S(1)}, u32[]{:S(2)}, u32[]{:S(2)}) collective-permute-start(bf16[128,1024]{1,0:T(8,128)(2,1)S(1)} %collective-permute-done.refs_2_), channel_id=1, source_target_pairs={{0,6},{2,0},{4,2},{6,4},{1,7},{3,1},{5,3},{7,5},{8,14},{10,8},{12,... | collective-permute-start | bytes 786440 | tf_op jit(solution)/shard_map/ppermute | solution.py:269
  21.0 10.0 %collective-permute-start.3 = (bf16[128,1024]{1,0:T(8,128)(2,1)S(1)}, bf16[128,1024]{1,0:T(8,128)(2,1)S(1)}, u32[]{:S(2)}, u32[]{:S(2)}) collective-permute-start(bf16[128,1024]{1,0:T(8,128)(2,1)S(1)} %collective-permute-done.2.refs_1_), channel_id=1, source_target_pairs={{0,2},{2,4},{4,6},{6,0},{1,3},{3,5},{5,7},{7,1},{8,10},{10,12},{12... | collective-permute-start | bytes 786440 | tf_op jit(solution)/shard_map/ppermute | solution.py:269
  21.9 9.2 %collective-permute-start.5 = (bf16[128,1024]{1,0:T(8,128)(2,1)S(1)}, bf16[128,1024]{1,0:T(8,128)(2,1)S(1)}, u32[]{:S(2)}, u32[]{:S(2)}) collective-permute-start(bf16[128,1024]{1,0:T(8,128)(2,1)S(1)} %collective-permute-done.2.refs_1_), channel_id=1, source_target_pairs={{0,6},{2,0},{4,2},{6,4},{1,7},{3,1},{5,3},{7,5},{8,14},{10,8},{12,... | collective-permute-start | bytes 786440 | tf_op jit(solution)/shard_map/ppermute | solution.py:269
  31.7 22.5 %collective-permute-start.7 = (bf16[192,1024]{1,0:T(8,128)(2,1)S(1)}, bf16[192,1024]{1,0:T(8,128)(2,1)S(1)}, u32[]{:S(2)}, u32[]{:S(2)}) collective-permute-start(bf16[192,1024]{1,0:T(8,128)(2,1)S(1)} %get-tuple-element.40.refs_6_), channel_id=1, source_target_pairs={{0,2},{2,4},{4,6},{6,0},{1,3},{3,5},{5,7},{7,1},{8,10},{10,12},{12... | collective-permute-start | bytes 1179656 | tf_op jit(solution)/shard_map/ppermute | solution.py:269
  33.3 21.0 %collective-permute-start.8 = (bf16[192,1024]{1,0:T(8,128)(2,1)S(1)}, bf16[192,1024]{1,0:T(8,128)(2,1)S(1)}, u32[]{:S(2)}, u32[]{:S(2)}) collective-permute-start(bf16[192,1024]{1,0:T(8,128)(2,1)S(1)} %get-tuple-element.41.refs_7_), channel_id=1, source_target_pairs={{0,6},{2,0},{4,2},{6,4},{1,7},{3,1},{5,3},{7,5},{8,14},{10,8},{12,... | collective-permute-start | bytes 1179656 | tf_op jit(solution)/shard_map/ppermute | solution.py:269
  35.0 9.1 %collective-permute-start.9 = (bf16[64,1024]{1,0:T(8,128)(2,1)S(1)}, bf16[64,1024]{1,0:T(8,128)(2,1)S(1)}, u32[]{:S(2)}, u32[]{:S(2)}) collective-permute-start(bf16[64,1024]{1,0:T(8,128)(2,1)S(1)} %get-tuple-element.42.refs_8_), channel_id=1, source_target_pairs={{0,2},{2,4},{4,6},{6,0},{1,3},{3,5},{5,7},{7,1},{8,10},{10,12},{12... | collective-permute-start | bytes 393224 | tf_op jit(solution)/shard_map/ppermute | solution.py:269
  35.3 9.8 %collective-permute-start.11 = (bf16[64,1024]{1,0:T(8,128)(2,1)S(1)}, bf16[64,1024]{1,0:T(8,128)(2,1)S(1)}, u32[]{:S(2)}, u32[]{:S(2)}) collective-permute-start(bf16[64,1024]{1,0:T(8,128)(2,1)S(1)} %get-tuple-element.43.refs_9_), channel_id=1, source_target_pairs={{0,6},{2,0},{4,2},{6,4},{1,7},{3,1},{5,3},{7,5},{8,14},{10,8},{12,... | collective-permute-start | bytes 393224 | tf_op jit(solution)/shard_map/ppermute | solution.py:269
  44.1 15.1 %collective-permute-start.10 = (bf16[64,1024]{1,0:T(8,128)(2,1)S(1)}, bf16[64,1024]{1,0:T(8,128)(2,1)S(1)}, u32[]{:S(2)}, u32[]{:S(2)}) collective-permute-start(bf16[64,1024]{1,0:T(8,128)(2,1)S(1)} %collective-permute-done.9.refs_4_), channel_id=1, source_target_pairs={{0,2},{2,4},{4,6},{6,0},{1,3},{3,5},{5,7},{7,1},{8,10},{10,12},{12... | collective-permute-start | bytes 393224 | tf_op jit(solution)/shard_map/ppermute | solution.py:269
  45.1 14.2 %collective-permute-start.12 = (bf16[64,1024]{1,0:T(8,128)(2,1)S(1)}, bf16[64,1024]{1,0:T(8,128)(2,1)S(1)}, u32[]{:S(2)}, u32[]{:S(2)}) collective-permute-start(bf16[64,1024]{1,0:T(8,128)(2,1)S(1)} %collective-permute-done.11.refs_8_), channel_id=1, source_target_pairs={{0,6},{2,0},{4,2},{6,4},{1,7},{3,1},{5,3},{7,5},{8,14},{10,8},{12,... | collective-permute-start | bytes 393224 | tf_op jit(solution)/shard_map/ppermute | solution.py:269
  47.4 2.2 %copy-start = (bf16[1,4096,512]{2,1,0:T(8,128)(2,1)S(1)}, bf16[1,4096,512]{2,1,0:T(8,128)(2,1)}, u32[]{:S(2)}) copy-start(bf16[1,4096,512]{2,1,0:T(8,128)(2,1)} %param.8) | copy-start | bytes 12582916
  49.5 2.2 %copy-start.2 = (bf16[1,4096,512]{2,1,0:T(8,128)(2,1)S(1)}, bf16[1,4096,512]{2,1,0:T(8,128)(2,1)}, u32[]{:S(2)}) copy-start(bf16[1,4096,512]{2,1,0:T(8,128)(2,1)} %param.9) | copy-start | bytes 12582916
  51.7 2.5 %copy-start.1 = (bf16[1,4096,512]{2,1,0:T(8,128)(2,1)S(1)}, bf16[1,4096,512]{2,1,0:T(8,128)(2,1)}, u32[]{:S(2)}) copy-start(bf16[1,4096,512]{2,1,0:T(8,128)(2,1)} %param.8) | copy-start | bytes 12582916
  51.7 3.5 %copy-start.3 = (bf16[1,4096,512]{2,1,0:T(8,128)(2,1)S(1)}, bf16[1,4096,512]{2,1,0:T(8,128)(2,1)}, u32[]{:S(2)}) copy-start(bf16[1,4096,512]{2,1,0:T(8,128)(2,1)} %param.9) | copy-start | bytes 12582916
  55.2 4.0 %copy-start.5 = (bf16[1,1,512,512]{3,2,1,0:T(8,128)(2,1)S(1)}, bf16[1,1,512,512]{3,2,1,0:T(8,128)(2,1)}, u32[]{:S(2)}) copy-start(bf16[1,1,512,512]{3,2,1,0:T(8,128)(2,1)} %param.10) | copy-start | bytes 1572868
  55.2 4.1 %copy-start.6 = (bf16[1,1,512,512]{3,2,1,0:T(8,128)(2,1)S(1)}, bf16[1,1,512,512]{3,2,1,0:T(8,128)(2,1)}, u32[]{:S(2)}) copy-start(bf16[1,1,512,512]{3,2,1,0:T(8,128)(2,1)} %param.11) | copy-start | bytes 1572868
  67.7 8.3 %collective-permute-start.15 = (bf16[512,2048]{1,0:T(8,128)(2,1)S(1)}, bf16[512,2048]{1,0:T(8,128)(2,1)S(1)}, u32[]{:S(2)}, u32[]{:S(2)}) collective-permute-start(bf16[512,2048]{1,0:T(8,128)(2,1)S(1)} %shard_map.109), channel_id=1, source_target_pairs={{0,8},{8,0},{1,9},{9,1},{2,10},{10,2},{3,11},{11,3},{4,12},{12,4},... | collective-permute-start | bytes 6291464 | tf_op jit(solution)/shard_map/ppermute | solution.py:272
  67.8 8.2 %collective-permute-start.16 = (bf16[512,1024]{1,0:T(8,128)(2,1)S(1)}, bf16[512,1024]{1,0:T(8,128)(2,1)S(1)}, u32[]{:S(2)}, u32[]{:S(2)}) collective-permute-start(bf16[512,1024]{1,0:T(8,128)(2,1)S(1)} %get-tuple-element.47.act_ref.refs_2_), channel_id=1, source_target_pairs={{0,8},{8,0},{1,9},{9,1},{2,10},{10,2},{3,11},{11,3},{4,12},{12,4},... | collective-permute-start | bytes 3145736 | tf_op jit(solution)/shard_map/ppermute | solution.py:272
  68.3 12.3 %collective-permute-start.13 = (bf16[192,1024]{1,0:T(8,128)(2,1)S(1)}, bf16[192,1024]{1,0:T(8,128)(2,1)S(1)}, u32[]{:S(2)}, u32[]{:S(2)}) collective-permute-start(bf16[192,1024]{1,0:T(8,128)(2,1)S(1)} %get-tuple-element.49), channel_id=1, source_target_pairs={{0,2},{2,4},{4,6},{6,0},{1,3},{3,5},{5,7},{7,1},{8,10},{10,12},{12... | collective-permute-start | bytes 1179656 | tf_op jit(solution)/shard_map/ppermute | solution.py:269
  68.3 12.3 %collective-permute-start.14 = (bf16[192,1024]{1,0:T(8,128)(2,1)S(1)}, bf16[192,1024]{1,0:T(8,128)(2,1)S(1)}, u32[]{:S(2)}, u32[]{:S(2)}) collective-permute-start(bf16[192,1024]{1,0:T(8,128)(2,1)S(1)} %get-tuple-element.50), channel_id=1, source_target_pairs={{0,6},{2,0},{4,2},{6,4},{1,7},{3,1},{5,3},{7,5},{8,14},{10,8},{12,... | collective-permute-start | bytes 1179656 | tf_op jit(solution)/shard_map/ppermute | solution.py:269
  81.3 11.6 %collective-permute-start.17 = (bf16[192,1024]{1,0:T(8,128)(2,1)S(1)}, bf16[192,1024]{1,0:T(8,128)(2,1)S(1)}, u32[]{:S(2)}, u32[]{:S(2)}) collective-permute-start(bf16[192,1024]{1,0:T(8,128)(2,1)S(1)} %get-tuple-element.55.refs_4_), channel_id=1, source_target_pairs={{0,2},{2,4},{4,6},{6,0},{1,3},{3,5},{5,7},{7,1},{8,10},{10,12},{12... | collective-permute-start | bytes 1179656 | tf_op jit(solution)/shard_map/ppermute | solution.py:269
  81.4 11.5 %collective-permute-start.18 = (bf16[192,1024]{1,0:T(8,128)(2,1)S(1)}, bf16[192,1024]{1,0:T(8,128)(2,1)S(1)}, u32[]{:S(2)}, u32[]{:S(2)}) collective-permute-start(bf16[192,1024]{1,0:T(8,128)(2,1)S(1)} %get-tuple-element.56), channel_id=1, source_target_pairs={{0,6},{2,0},{4,2},{6,4},{1,7},{3,1},{5,3},{7,5},{8,14},{10,8},{12,... | collective-permute-start | bytes 1179656 | tf_op jit(solution)/shard_map/ppermute | solution.py:269
  84.6 33.7 %collective-permute-start.26 = (bf16[512,1024]{1,0:T(8,128)(2,1)S(1)}, bf16[512,1024]{1,0:T(8,128)(2,1)S(1)}, u32[]{:S(2)}, u32[]{:S(2)}) collective-permute-start(bf16[512,1024]{1,0:T(8,128)(2,1)S(1)} %get-tuple-element.65), channel_id=1, source_target_pairs={{0,16},{8,56},{16,32},{24,8},{32,48},{40,24},{48,0},{56,40},{1,17}... | collective-permute-start | bytes 3145736 | tf_op jit(solution)/shard_map/ppermute | solution.py:288
  93.7 13.5 %collective-permute-start.19 = (bf16[256,1024]{1,0:T(8,128)(2,1)S(1)}, bf16[256,1024]{1,0:T(8,128)(2,1)S(1)}, u32[]{:S(2)}, u32[]{:S(2)}) collective-permute-start(bf16[256,1024]{1,0:T(8,128)(2,1)S(1)} %get-tuple-element.57), channel_id=1, source_target_pairs={{0,2},{2,4},{4,6},{6,0},{1,3},{3,5},{5,7},{7,1},{8,10},{10,12},{12... | collective-permute-start | bytes 1572872 | tf_op jit(solution)/shard_map/ppermute | solution.py:269
  94.6 12.6 %collective-permute-start.20 = (bf16[256,1024]{1,0:T(8,128)(2,1)S(1)}, bf16[256,1024]{1,0:T(8,128)(2,1)S(1)}, u32[]{:S(2)}, u32[]{:S(2)}) collective-permute-start(bf16[256,1024]{1,0:T(8,128)(2,1)S(1)} %get-tuple-element.58), channel_id=1, source_target_pairs={{0,6},{2,0},{4,2},{6,4},{1,7},{3,1},{5,3},{7,5},{8,14},{10,8},{12,... | collective-permute-start | bytes 1572872 | tf_op jit(solution)/shard_map/ppermute | solution.py:269
  97.0 7.6 %collective-permute-start.21 = (bf16[128,1024]{1,0:T(8,128)(2,1)S(1)}, bf16[128,1024]{1,0:T(8,128)(2,1)S(1)}, u32[]{:S(2)}, u32[]{:S(2)}) collective-permute-start(bf16[128,1024]{1,0:T(8,128)(2,1)S(1)} %get-tuple-element.59), channel_id=1, source_target_pairs={{0,193},{1,64},{64,1},{65,128},{128,65},{129,192},{192,129},{193,0... | collective-permute-start | bytes 786440 | tf_op jit(solution)/shard_map/ppermute | solution.py:279
  107.9 12.9 %collective-permute-start.22 = (bf16[128,1024]{1,0:T(8,128)(2,1)S(1)}, bf16[128,1024]{1,0:T(8,128)(2,1)S(1)}, u32[]{:S(2)}, u32[]{:S(2)}) collective-permute-start(bf16[128,1024]{1,0:T(8,128)(2,1)S(1)} %get-tuple-element.60), channel_id=1, source_target_pairs={{0,2},{2,4},{4,6},{6,0},{1,3},{3,5},{5,7},{7,1},{8,10},{10,12},{12... | collective-permute-start | bytes 786440 | tf_op jit(solution)/shard_map/ppermute | solution.py:269
  108.9 12.0 %collective-permute-start.23 = (bf16[128,1024]{1,0:T(8,128)(2,1)S(1)}, bf16[128,1024]{1,0:T(8,128)(2,1)S(1)}, u32[]{:S(2)}, u32[]{:S(2)}) collective-permute-start(bf16[128,1024]{1,0:T(8,128)(2,1)S(1)} %get-tuple-element.61), channel_id=1, source_target_pairs={{0,6},{2,0},{4,2},{6,4},{1,7},{3,1},{5,3},{7,5},{8,14},{10,8},{12,... | collective-permute-start | bytes 786440 | tf_op jit(solution)/shard_map/ppermute | solution.py:269
  111.3 9.6 %collective-permute-start.24 = (bf16[128,1024]{1,0:T(8,128)(2,1)S(1)}, bf16[128,1024]{1,0:T(8,128)(2,1)S(1)}, u32[]{:S(2)}, u32[]{:S(2)}) collective-permute-start(bf16[128,1024]{1,0:T(8,128)(2,1)S(1)} %get-tuple-element.62), channel_id=1, source_target_pairs={{0,64},{1,193},{64,128},{65,1},{128,192},{129,65},{192,0},{193,129... | collective-permute-start | bytes 786440 | tf_op jit(solution)/shard_map/ppermute | solution.py:283
  111.5 11.7 %collective-permute-start.25 = (bf16[128,1024]{1,0:T(8,128)(2,1)S(1)}, bf16[128,1024]{1,0:T(8,128)(2,1)S(1)}, u32[]{:S(2)}, u32[]{:S(2)}) collective-permute-start(bf16[128,1024]{1,0:T(8,128)(2,1)S(1)} %get-tuple-element.63.refs_2_), channel_id=1, source_target_pairs={{0,193},{1,64},{64,1},{65,128},{128,65},{129,192},{192,129},{193,0... | collective-permute-start | bytes 786440 | tf_op jit(solution)/shard_map/ppermute | solution.py:279
  119.2 29.0 %collective-permute-start.32 = (bf16[512,1024]{1,0:T(8,128)(2,1)S(1)}, bf16[512,1024]{1,0:T(8,128)(2,1)S(1)}, u32[]{:S(2)}, u32[]{:S(2)}) collective-permute-start(bf16[512,1024]{1,0:T(8,128)(2,1)S(1)} %get-tuple-element.71), channel_id=1, source_target_pairs={{0,16},{8,56},{16,32},{24,8},{32,48},{40,24},{48,0},{56,40},{1,17}... | collective-permute-start | bytes 3145736 | tf_op jit(solution)/shard_map/ppermute | solution.py:288
  123.9 24.3 %collective-permute-start.33 = (bf16[512,1024]{1,0:T(8,128)(2,1)S(1)}, bf16[512,1024]{1,0:T(8,128)(2,1)S(1)}, u32[]{:S(2)}, u32[]{:S(2)}) collective-permute-start(bf16[512,1024]{1,0:T(8,128)(2,1)S(1)} %get-tuple-element.72), channel_id=1, source_target_pairs={{0,24},{8,48},{16,40},{24,0},{32,56},{40,16},{48,8},{56,32},{1,25}... | collective-permute-start | bytes 3145736 | tf_op jit(solution)/shard_map/ppermute | solution.py:288
  124.0 8.8 %collective-permute-start.27 = (bf16[128,1024]{1,0:T(8,128)(2,1)S(1)}, bf16[128,1024]{1,0:T(8,128)(2,1)S(1)}, u32[]{:S(2)}, u32[]{:S(2)}) collective-permute-start(bf16[128,1024]{1,0:T(8,128)(2,1)S(1)} %get-tuple-element.67.refs_0_), channel_id=1, source_target_pairs={{0,1},{1,0},{2,3},{3,2},{4,5},{5,4},{6,7},{7,6},{8,9},{9,8},{10,11... | collective-permute-start | bytes 786440 | tf_op jit(solution)/shard_map/ppermute | solution.py:275
  133.4 9.3 %collective-permute-start.29 = (bf16[128,1024]{1,0:T(8,128)(2,1)S(1)}, bf16[128,1024]{1,0:T(8,128)(2,1)S(1)}, u32[]{:S(2)}, u32[]{:S(2)}) collective-permute-start(bf16[128,1024]{1,0:T(8,128)(2,1)S(1)} %get-tuple-element.69.refs_0_), channel_id=1, source_target_pairs={{0,6},{2,0},{4,2},{6,4},{1,7},{3,1},{5,3},{7,5},{8,14},{10,8},{12,... | collective-permute-start | bytes 786440 | tf_op jit(solution)/shard_map/ppermute | solution.py:269
  135.0 11.6 %collective-permute-start.31 = (bf16[128,1024]{1,0:T(8,128)(2,1)S(1)}, bf16[128,1024]{1,0:T(8,128)(2,1)S(1)}, u32[]{:S(2)}, u32[]{:S(2)}) collective-permute-start(bf16[128,1024]{1,0:T(8,128)(2,1)S(1)} %get-tuple-element.69.refs_0_), channel_id=1, source_target_pairs={{0,2},{2,4},{4,6},{6,0},{1,3},{3,5},{5,7},{7,1},{8,10},{10,12},{12... | collective-permute-start | bytes 786440 | tf_op jit(solution)/shard_map/ppermute | solution.py:269
  135.5 14.5 %collective-permute-start.28 = (bf16[64,1024]{1,0:T(8,128)(2,1)S(1)}, bf16[64,1024]{1,0:T(8,128)(2,1)S(1)}, u32[]{:S(2)}, u32[]{:S(2)}) collective-permute-start(bf16[64,1024]{1,0:T(8,128)(2,1)S(1)} %get-tuple-element.68), channel_id=1, source_target_pairs={{0,4},{2,6},{4,0},{6,2},{1,5},{3,7},{5,1},{7,3},{8,12},{10,14},{12... | collective-permute-start | bytes 393224 | tf_op jit(solution)/shard_map/ppermute | solution.py:269
  143.3 6.7 %collective-permute-start.30 = (bf16[64,1024]{1,0:T(8,128)(2,1)S(1)}, bf16[64,1024]{1,0:T(8,128)(2,1)S(1)}, u32[]{:S(2)}, u32[]{:S(2)}) collective-permute-start(bf16[64,1024]{1,0:T(8,128)(2,1)S(1)} %shard_map.118.refs_3_), channel_id=1, source_target_pairs={{0,6},{2,0},{4,2},{6,4},{1,7},{3,1},{5,3},{7,5},{8,14},{10,8},{12,... | collective-permute-start | bytes 393224 | tf_op jit(solution)/shard_map/ppermute | solution.py:269
